TPU v7x, 32 devices: a whole 2x2x4 slice. The times are simulated.
32 devices in a mesh: gx: 4 (over x, core), gy: 4 (over z), gz: 2 (over y).
Axes of the slice: x: 2, y: 2, z: 4, core: 2. Of those that a mesh axis runs over, the one named last changes fastest.
Arguments:
- orbitals: float32 [16, 8, 64, 512], P(None, 'gz', 'gy', 'gx'), may hold values from -6 to 6
- potential: float32 [8, 64, 512], P('gz', 'gy', 'gx'), may hold values from -1 to 0.5
- tile_proj: float32 [8192, 4, 128], P(('gx', 'gy', 'gz')), may hold values from -1 to 1
- tile_atom: int32 [8192], P(('gx', 'gy', 'gz')), may hold values from 0 to 2047, as said below
- tile_column: int32 [8192], P(('gx', 'gy', 'gz')), may hold values from 0 to 63
- tile_count: int32 [32], P(('gx', 'gy', 'gz')), may hold values from 64 to 256, as said below
- atom_home: int32 [2048], replicated, may hold values from 0 to 2047, each once
- coupling: float32 [2048, 4], P(('gx', 'gy', 'gz')), may hold values from 0.5 to 3
Outputs:
- filtered: float32 [16, 8, 64, 512], P(None, 'gz', 'gy', 'gx')
Inputs may be any that keep to these rules, and one draw needn't show every extreme that they name: `tile_atom`: each live or dead slot names an atom numbered d * 64 to d * 64 + 63 for a device d whose gx, gy and gz indices each differ from the slot's own device's by at most one. `tile_count`: some device has all 256 slots live. `atom_home`: each coupling row once.
All inputs are finite; a program needn't handle non-finite values.
Results may differ from a plain program's by a relative error of at most 0.00018.
Values sent between devices are 32-bit elements; how exact they have to be, the bound alone decides.
No kernel may reach another device: no remote copies, remote signals or barrier semaphores. Data moves between devices by JAX's collectives and lax.ppermute only.
A program may use at most 128 MiB of HBM per device.

v0:
```python
import jax
import jax.numpy as jnp
from jax import lax
from jax.sharding import PartitionSpec as P

DEGREE = 4


stencil_weights = (-205.0 / 72.0, 8.0 / 5.0, -1.0 / 5.0, 8.0 / 315.0, -1.0 / 560.0)
lower_edge = 4.0
upper_edge = 24.0


def padded_2(block, sides, width):
    for axis, dim in sides:
        count = lax.axis_size(axis)
        forward = [(i, i + 1) for i in range(count - 1)]
        backward = [(target, source) for source, target in forward]
        low = lax.ppermute(
            lax.slice_in_dim(block, block.shape[dim] - width, None, axis=dim), axis, forward
        )
        high = lax.ppermute(lax.slice_in_dim(block, 0, width, axis=dim), axis, backward)
        block = jnp.concatenate([low, block, high], axis=dim)
    return block


def along_axis(padded, dimension, length):
    result = None
    for offset in range(1, 5):
        upper = lax.slice_in_dim(padded, 4 + offset, 4 + offset + length, axis=dimension)
        lower = lax.slice_in_dim(padded, 4 - offset, 4 - offset + length, axis=dimension)
        term = stencil_weights[offset] * (upper + lower)
        result = term if offset == 1 else result + term
    return result


def laplacian(values):
    shape = values.shape
    result = 3.0 * stencil_weights[0] * values
    padded = padded_2(values, (("gx", 3), ("gy", 2), ("gz", 1)), 4)
    for dimension in (1, 2, 3):
        strip = padded
        for position in (1, 2, 3):
            if position != dimension:
                strip = lax.slice_in_dim(strip, 4, 4 + shape[position], axis=position)
        result = result + along_axis(strip, dimension, shape[dimension])
    return result


def three_sides(padded, dimension):
    return (
        lax.index_in_dim(padded, 0, dimension, False)
        + lax.index_in_dim(padded, 2, dimension, False)
        + lax.index_in_dim(padded, 4, dimension, False)
    )


def per_device(
    orbitals, potential, tile_proj, tile_atom, tile_column, tile_count, atom_home, coupling
):
    orbital_count, depth_z, depth_y, depth_x = orbitals.shape
    slot_count, proj_count, tile_length = tile_proj.shape
    owned_count = coupling.shape[0]
    feature_count = proj_count * orbital_count
    live = (jnp.arange(slot_count, dtype=jnp.int32) < tile_count[0]).astype(tile_proj.dtype)
    proj_live = tile_proj * live[:, None, None]
    full_coupling = lax.all_gather(coupling, ("gx", "gy", "gz"), axis=0, tiled=True)
    count_y = lax.axis_size("gy")
    count_z = lax.axis_size("gz")
    index_x = lax.axis_index("gx")
    index_y = lax.axis_index("gy")
    index_z = lax.axis_index("gz")
    own_index = (index_x * count_y + index_y) * count_z + index_z
    own_homes = lax.dynamic_slice_in_dim(atom_home, own_index * owned_count, owned_count)
    own_scale = full_coupling[own_homes]
    owner = tile_atom // owned_count
    rel_x = owner // (count_y * count_z) - index_x + 1
    rel_y = owner // count_z % count_y - index_y + 1
    rel_z = owner % count_z - index_z + 1
    near_key = ((rel_x * 3 + rel_y) * 3 + rel_z) * owned_count + tile_atom % owned_count
    center = 0.5 * (upper_edge + lower_edge)
    half_width = 0.5 * (upper_edge - lower_edge)

    def projected(values):
        lines = values.reshape(orbital_count, depth_z * depth_y, depth_x)
        tile_rows = lines[:, tile_column, :]
        partial_value = jnp.einsum(
            "tpx,otx->tpo", proj_live, tile_rows, precision=lax.Precision.HIGHEST
        )
        partial_value = partial_value.reshape(slot_count, feature_count)
        near_sums = jax.ops.segment_sum(partial_value, near_key, num_segments=27 * owned_count)
        near_sums = near_sums.reshape(3, 3, 3, owned_count, feature_count)
        padded_z = padded_2(near_sums, (("gz", 2),), 1)
        summed_z = three_sides(padded_z, 2)
        padded_y = padded_2(summed_z, (("gy", 1),), 1)
        summed_y = three_sides(padded_y, 1)
        padded_x = padded_2(summed_y, (("gx", 0),), 1)
        owned_sums = three_sides(padded_x, 0)
        scaled_own = (
            owned_sums.reshape(owned_count, proj_count, orbital_count) * own_scale[:, :, None]
        )
        spread = padded_2(
            scaled_own.reshape(1, 1, 1, owned_count, feature_count),
            (("gx", 0), ("gy", 1), ("gz", 2)),
            1,
        )
        per_tile = spread.reshape(27 * owned_count, proj_count, orbital_count)[near_key]
        returned = jnp.einsum("tpx,tpo->otx", proj_live, per_tile, precision=lax.Precision.HIGHEST)
        return jnp.zeros_like(lines).at[:, tile_column, :].add(returned).reshape(values.shape)

    def hamiltonian(values):
        return -0.5 * laplacian(values) + potential[None] * values + projected(values)

    previous = orbitals
    current = (hamiltonian(orbitals) - center * orbitals) / half_width
    for repeat in range(DEGREE - 1):
        following = 2.0 * (hamiltonian(current) - center * current) / half_width - previous
        previous = current
        current = following
    return current


def solution(mesh):
    return jax.shard_map(
        per_device,
        mesh=mesh,
        in_specs=(
            P(None, "gz", "gy", "gx"),
            P("gz", "gy", "gx"),
            P(("gx", "gy", "gz"), None, None),
            P(("gx", "gy", "gz")),
            P(("gx", "gy", "gz")),
            P(("gx", "gy", "gz")),
            P(),
            P(("gx", "gy", "gz"), None),
        ),
        out_specs=P(None, "gz", "gy", "gx"),
        check_vma=False,
    )
```

profile of v0, /device:TPU:0, one launch (start us, length us, event | category | flops | bytes accessed | tf_op | source)
XLA Modules:
  0.0 665.6 jit_solution(8564418587178644243)
XLA Ops:
  10.2 5.6 collective-permute-start.6
  36.7 67.6 %all-gather = f32[32,64,4]{1,2,0:T(4,128)S(1)} all-gather(f32[1,64,4]{1,2,0:T(4,128)S(1)} %bitcast.147), channel_id=1, replica_groups=mesh['gx'=4,'gy'=4,'gz'=2] {'gx','gy','gz'}, dimensions={0}, use_global_device_ids=true | all-gather | bytes 33792 | tf_op jit(solution)/shard_map/all_gather | solution.py:67
  124.6 6.9 %collective-permute-start.5 = (f32[16,4,24,136]{3,2,1,0:T(8,128)}, f32[16,4,24,136]{3,2,1,0:T(8,128)}, u32[]{:S(2)}, u32[]{:S(2)}) collective-permute-start(f32[16,4,24,136]{3,2,1,0:T(8,128)} %pad_maximum_fusion), channel_id=1, source_target_pairs={{0,1},{2,3},{4,5},{6,7},{8,9},{10,11},{12,13},{14,15},{16,17},{18,... | collective-permute-start | bytes 2506760 | tf_op jit(solution)/shard_map/ppermute | solution.py:19
  148.2 22.1 %collective-permute-done.16 = f32[3,3,1,64,64]{4,3,2,1,0:T(8,128)S(1)} collective-permute-done((f32[3,3,1,64,64]{4,3,2,1,0:T(8,128)S(1)}, f32[3,3,1,64,64]{4,3,2,1,0:T(8,128)S(1)}, u32[]{:S(2)}, u32[]{:S(2)}) %collective-permute-start.16) | collective-permute-done | bytes 147488 | tf_op jit(solution)/shard_map/ppermute | solution.py:19
  181.3 20.3 %scatter_fusion = f32[16,64,128]{2,0,1:T(8,128)S(1)} fusion(f32[16,64,128]{2,0,1:T(8,128)S(1)} %broadcast.100.clone, s32[256]{0:T(256)S(1)} %compare_select_fusion.1, f32[256,16,128]{2,1,0:T(8,128)} %fusion.204), kind=kCustom, calls=%fused_computation.10 | custom fusion | flops 524288 | bytes 6292480 | tf_op jit(solution)/shard_map/scatter-add | solution.py:109
  201.6 12.3 %broadcast_multiply_fusion = (f32[16,4,16,128]{3,2,1,0:T(8,128)S(1)}, f32[16,4,16,128]{3,2,1,0:T(8,128)}) fusion(f32[16,4,16,128]{3,2,1,0:T(8,128)S(1)} %copy-done, f32[16,4,16,128]{3,0,2,1:T(8,128)S(1)} %bitcast.124, f32[4,16,128]{2,1,0:T(8,128)S(1)} %copy-done.10, f32[16,4,16,4]{3,2,1,0:T(8,128)S(1)} %collective-permute-done, ...), kind=kLoop, calls=%fused_computation.345 | loop fusion | flops 10223616 | bytes 13049856 | tf_op jit(solution)/shard_map/div | solution.py:115
  262.6 6.9 %collective-permute-start.30 = (f32[1,1,1,64,64]{3,4,2,1,0:T(8,128)S(1)}, f32[1,1,1,64,64]{3,4,2,1,0:T(8,128)S(1)}, u32[]{:S(2)}, u32[]{:S(2)}) collective-permute-start(f32[1,1,1,64,64]{3,4,2,1,0:T(8,128)S(1)} %fusion.190), channel_id=1, source_target_pairs={{0,8},{8,16},{16,24},{1,9},{9,17},{17,25},{2,10},{10,18},{18,26},{... | collective-permute-start | bytes 49160 | tf_op jit(solution)/shard_map/ppermute | solution.py:19
  274.0 6.9 %collective-permute-start.23 = (f32[16,4,24,136]{3,2,1,0:T(8,128)}, f32[16,4,24,136]{3,2,1,0:T(8,128)}, u32[]{:S(2)}, u32[]{:S(2)}) collective-permute-start(f32[16,4,24,136]{3,2,1,0:T(8,128)} %pad_maximum_fusion.2), channel_id=1, source_target_pairs={{0,1},{2,3},{4,5},{6,7},{8,9},{10,11},{12,13},{14,15},{16,17},{18,... | collective-permute-start | bytes 2506760 | tf_op jit(solution)/shard_map/ppermute | solution.py:19
  297.5 22.2 %collective-permute-done.34 = f32[3,3,1,64,64]{3,4,2,1,0:T(8,128)S(1)} collective-permute-done((f32[3,3,1,64,64]{3,4,2,1,0:T(8,128)S(1)}, f32[3,3,1,64,64]{3,4,2,1,0:T(8,128)S(1)}, u32[]{:S(2)}, u32[]{:S(2)}) %collective-permute-start.34) | collective-permute-done | bytes 147488 | tf_op jit(solution)/shard_map/ppermute | solution.py:19
  335.3 20.3 %scatter_fusion.1 = f32[16,64,128]{2,0,1:T(8,128)S(1)} fusion(f32[16,64,128]{2,0,1:T(8,128)S(1)} %broadcast.100.clone.1, s32[256]{0:T(256)S(1)} %compare_select_fusion.1, f32[256,16,128]{2,1,0:T(8,128)} %fusion.203), kind=kCustom, calls=%fused_computation.12 | custom fusion | flops 524288 | bytes 6292480 | tf_op jit(solution)/shard_map/scatter-add | solution.py:109
  355.7 11.7 %fusion.63 = f32[16,4,16,128]{3,2,1,0:T(8,128)S(1)} fusion(f32[16,4,16,128]{3,2,1,0:T(8,128)S(1)} %copy-done, f32[16,4,16,4]{3,2,1,0:T(8,128)S(1)} %collective-permute-done.18, f32[16,4,16,128]{3,2,1,0:T(8,128)S(1)} %get-tuple-element.5, f32[16,4,16,4]{3,2,1,0:T(8,128)} %copy-done.4, f32[16,4,20,136]{3,2,1,0:T(8,128)} %get-tuple-element.18, ...), kind=kLoop, calls=%fused_computation.138 | loop fusion | flops 10878976 | bytes 11984896 | tf_op jit(solution)/shard_map/sub | solution.py:117
  383.2 5.6 collective-permute-done.42
  412.7 5.5 collective-permute-start.48
  422.9 6.9 %collective-permute-start.41 = (f32[16,4,24,136]{3,2,1,0:T(8,128)}, f32[16,4,24,136]{3,2,1,0:T(8,128)}, u32[]{:S(2)}, u32[]{:S(2)}) collective-permute-start(f32[16,4,24,136]{3,2,1,0:T(8,128)} %pad_maximum_fusion.4), channel_id=1, source_target_pairs={{0,1},{2,3},{4,5},{6,7},{8,9},{10,11},{12,13},{14,15},{16,17},{18,... | collective-permute-start | bytes 2506760 | tf_op jit(solution)/shard_map/ppermute | solution.py:19
  446.2 22.4 %collective-permute-done.52 = f32[3,3,1,64,64]{3,4,2,1,0:T(8,128)S(1)} collective-permute-done((f32[3,3,1,64,64]{3,4,2,1,0:T(8,128)S(1)}, f32[3,3,1,64,64]{3,4,2,1,0:T(8,128)S(1)}, u32[]{:S(2)}, u32[]{:S(2)}) %collective-permute-start.52) | collective-permute-done | bytes 147488 | tf_op jit(solution)/shard_map/ppermute | solution.py:19
  484.2 20.3 %scatter_fusion.2 = f32[16,64,128]{2,0,1:T(8,128)S(1)} fusion(f32[16,64,128]{2,0,1:T(8,128)S(1)} %broadcast.100.clone.2, s32[256]{0:T(256)S(1)} %compare_select_fusion.1, f32[256,16,128]{2,1,0:T(8,128)} %fusion.202), kind=kCustom, calls=%fused_computation.14 | custom fusion | flops 524288 | bytes 6292480 | tf_op jit(solution)/shard_map/scatter-add | solution.py:109
  504.6 10.8 %fusion.41 = f32[16,4,16,128]{3,2,1,0:T(8,128)S(1)} fusion(f32[16,4,16,4]{3,2,1,0:T(8,128)S(1)} %collective-permute-done.36, f32[16,4,16,128]{3,2,1,0:T(8,128)S(1)} %fusion.63, f32[16,4,16,4]{3,2,1,0:T(8,128)S(1)} %collective-permute-done.37, f32[16,4,20,136]{3,2,1,0:T(8,128)} %get-tuple-element.14, f32[16,4,20,136]{3,2,1,0:T(8,128)} %get-tuple-element.13, ...), kind=kLoop, calls=%fused_computation.116 | loop fusion | flops 11010048 | bytes 10952704 | tf_op jit(solution)/shard_map/sub | solution.py:117
  531.2 5.6 collective-permute-done.60
  560.6 5.5 collective-permute-start.66
  570.8 6.9 %collective-permute-start.59 = (f32[16,4,24,136]{3,2,1,0:T(8,128)}, f32[16,4,24,136]{3,2,1,0:T(8,128)}, u32[]{:S(2)}, u32[]{:S(2)}) collective-permute-start(f32[16,4,24,136]{3,2,1,0:T(8,128)} %pad_maximum_fusion.6), channel_id=1, source_target_pairs={{0,1},{2,3},{4,5},{6,7},{8,9},{10,11},{12,13},{14,15},{16,17},{18,... | collective-permute-start | bytes 2506760 | tf_op jit(solution)/shard_map/ppermute | solution.py:19
  593.7 22.9 %collective-permute-done.70 = f32[3,3,1,64,64]{3,4,2,1,0:T(8,128)S(1)} collective-permute-done((f32[3,3,1,64,64]{3,4,2,1,0:T(8,128)S(1)}, f32[3,3,1,64,64]{3,4,2,1,0:T(8,128)S(1)}, u32[]{:S(2)}, u32[]{:S(2)}) %collective-permute-start.70) | collective-permute-done | bytes 147488 | tf_op jit(solution)/shard_map/ppermute | solution.py:19
  627.9 6.1 fusion.201
  634.0 20.3 %scatter_fusion.3 = f32[16,64,128]{2,0,1:T(8,128)S(1)} fusion(f32[16,64,128]{2,0,1:T(8,128)S(1)} %broadcast.100, s32[256]{0:T(256)S(1)} %compare_select_fusion.1, f32[256,16,128]{2,1,0:T(8,128)} %fusion.201), kind=kCustom, calls=%fused_computation.16 | custom fusion | flops 524288 | bytes 6292480 | tf_op jit(solution)/shard_map/scatter-add | solution.py:109
  654.4 10.8 %fusion.19 = f32[16,4,16,128]{3,2,1,0:T(8,128)} fusion(f32[16,4,16,128]{3,2,1,0:T(8,128)S(1)} %fusion.63, f32[16,4,16,4]{3,2,1,0:T(8,128)} %copy-done.2, f32[16,4,16,128]{3,2,1,0:T(8,128)S(1)} %fusion.41, f32[16,4,16,4]{3,2,1,0:T(8,128)} %copy-done.3, f32[16,4,20,136]{3,2,1,0:T(8,128)} %get-tuple-element.10, f32[16,4,20,136]{3,2,1,0:T(8,128)S(1)} %get-tuple-element.9, ...), kind=kLoop, calls=%fused_computation.94 | loop fusion | flops 10878976 | bytes 11968512 | tf_op jit(solution)/shard_map/sub | solution.py:117
  (278 shorter events, 310.6 us)
Async XLA Ops:
  19.1 92.2 %collective-permute-start.1 = (f32[16,4,16,4]{3,2,1,0:T(8,128)}, f32[16,4,16,4]{3,2,1,0:T(8,128)S(1)}, u32[]{:S(2)}, u32[]{:S(2)}) collective-permute-start(f32[16,4,16,4]{3,2,1,0:T(8,128)} %get-tuple-element.43), channel_id=1, source_target_pairs={{8,0},{16,8},{24,16},{9,1},{17,9},{25,17},{10,2},{18,10},{26,18},{... | collective-permute-start | bytes 49160 | tf_op jit(solution)/shard_map/ppermute | solution.py:22
  20.3 90.9 %collective-permute-start = (f32[16,4,16,4]{3,2,1,0:T(8,128)}, f32[16,4,16,4]{3,2,1,0:T(8,128)S(1)}, u32[]{:S(2)}, u32[]{:S(2)}) collective-permute-start(f32[16,4,16,4]{3,2,1,0:T(8,128)} %get-tuple-element.44), channel_id=1, source_target_pairs={{0,8},{8,16},{16,24},{1,9},{9,17},{17,25},{2,10},{10,18},{18,26},{... | collective-permute-start | bytes 49160 | tf_op jit(solution)/shard_map/ppermute | solution.py:19
  31.3 76.3 %collective-permute-start.8 = (f32[3,1,64,64]{3,2,1,0:T(8,128)}, f32[3,1,64,64]{3,2,1,0:T(8,128)}, u32[]{:S(2)}, u32[]{:S(2)}) collective-permute-start(f32[3,1,64,64]{3,2,1,0:T(8,128)} %get-tuple-element.51), channel_id=1, source_target_pairs={{0,2},{2,4},{4,6},{1,3},{3,5},{5,7},{8,10},{10,12},{12,14},{9,11},... | collective-permute-start | bytes 147464 | tf_op jit(solution)/shard_map/ppermute | solution.py:19
  35.4 72.3 %collective-permute-start.9 = (f32[3,1,64,64]{3,2,1,0:T(8,128)}, f32[3,1,64,64]{3,2,1,0:T(8,128)}, u32[]{:S(2)}, u32[]{:S(2)}) collective-permute-start(f32[3,1,64,64]{3,2,1,0:T(8,128)} %get-tuple-element.52), channel_id=1, source_target_pairs={{2,0},{4,2},{6,4},{3,1},{5,3},{7,5},{10,8},{12,10},{14,12},{11,9},... | collective-permute-start | bytes 147464 | tf_op jit(solution)/shard_map/ppermute | solution.py:22
  115.5 16.0 %collective-permute-start.12 = (f32[1,1,1,64,64]{4,3,2,1,0:T(8,128)S(1)}, f32[1,1,1,64,64]{4,3,2,1,0:T(8,128)S(1)}, u32[]{:S(2)}, u32[]{:S(2)}) collective-permute-start(f32[1,1,1,64,64]{4,3,2,1,0:T(8,128)S(1)} %fusion.194), channel_id=1, source_target_pairs={{0,8},{8,16},{16,24},{1,9},{9,17},{17,25},{2,10},{10,18},{18,26},{... | collective-permute-start | bytes 49160 | tf_op jit(solution)/shard_map/ppermute | solution.py:19
  123.3 78.3 %collective-permute-start.4 = (f32[16,4,24,136]{3,2,1,0:T(8,128)}, f32[16,4,24,136]{3,2,1,0:T(8,128)}, u32[]{:S(2)}, u32[]{:S(2)}) collective-permute-start(f32[16,4,24,136]{3,2,1,0:T(8,128)} %pad_maximum_fusion), channel_id=1, source_target_pairs={{1,0},{3,2},{5,4},{7,6},{9,8},{11,10},{13,12},{15,14},{17,16},{19,... | collective-permute-start | bytes 2506760 | tf_op jit(solution)/shard_map/ppermute | solution.py:22
  124.6 77.0 %collective-permute-start.5 = (f32[16,4,24,136]{3,2,1,0:T(8,128)}, f32[16,4,24,136]{3,2,1,0:T(8,128)}, u32[]{:S(2)}, u32[]{:S(2)}) collective-permute-start(f32[16,4,24,136]{3,2,1,0:T(8,128)} %pad_maximum_fusion), channel_id=1, source_target_pairs={{0,1},{2,3},{4,5},{6,7},{8,9},{10,11},{12,13},{14,15},{16,17},{18,... | collective-permute-start | bytes 2506760 | tf_op jit(solution)/shard_map/ppermute | solution.py:19
  142.4 27.9 %collective-permute-start.16 = (f32[3,3,1,64,64]{4,3,2,1,0:T(8,128)S(1)}, f32[3,3,1,64,64]{4,3,2,1,0:T(8,128)S(1)}, u32[]{:S(2)}, u32[]{:S(2)}) collective-permute-start(f32[3,3,1,64,64]{4,3,2,1,0:T(8,128)S(1)} %pad_maximum_fusion.59), channel_id=1, source_target_pairs={{0,1},{2,3},{4,5},{6,7},{8,9},{10,11},{12,13},{14,15},{16,17},{18,... | collective-permute-start | bytes 442376 | tf_op jit(solution)/shard_map/ppermute | solution.py:19
  143.7 26.6 %collective-permute-start.17 = (f32[3,3,1,64,64]{4,3,2,1,0:T(8,128)S(1)}, f32[3,3,1,64,64]{4,3,2,1,0:T(8,128)S(1)}, u32[]{:S(2)}, u32[]{:S(2)}) collective-permute-start(f32[3,3,1,64,64]{4,3,2,1,0:T(8,128)S(1)} %pad_maximum_fusion.59), channel_id=1, source_target_pairs={{1,0},{3,2},{5,4},{7,6},{9,8},{11,10},{13,12},{15,14},{17,16},{19,... | collective-permute-start | bytes 442376 | tf_op jit(solution)/shard_map/ppermute | solution.py:22
  262.6 18.3 %collective-permute-start.30 = (f32[1,1,1,64,64]{3,4,2,1,0:T(8,128)S(1)}, f32[1,1,1,64,64]{3,4,2,1,0:T(8,128)S(1)}, u32[]{:S(2)}, u32[]{:S(2)}) collective-permute-start(f32[1,1,1,64,64]{3,4,2,1,0:T(8,128)S(1)} %fusion.190), channel_id=1, source_target_pairs={{0,8},{8,16},{16,24},{1,9},{9,17},{17,25},{2,10},{10,18},{18,26},{... | collective-permute-start | bytes 49160 | tf_op jit(solution)/shard_map/ppermute | solution.py:19
  272.7 82.9 %collective-permute-start.22 = (f32[16,4,24,136]{3,2,1,0:T(8,128)}, f32[16,4,24,136]{3,2,1,0:T(8,128)}, u32[]{:S(2)}, u32[]{:S(2)}) collective-permute-start(f32[16,4,24,136]{3,2,1,0:T(8,128)} %pad_maximum_fusion.2), channel_id=1, source_target_pairs={{1,0},{3,2},{5,4},{7,6},{9,8},{11,10},{13,12},{15,14},{17,16},{19,... | collective-permute-start | bytes 2506760 | tf_op jit(solution)/shard_map/ppermute | solution.py:22
  274.0 81.6 %collective-permute-start.23 = (f32[16,4,24,136]{3,2,1,0:T(8,128)}, f32[16,4,24,136]{3,2,1,0:T(8,128)}, u32[]{:S(2)}, u32[]{:S(2)}) collective-permute-start(f32[16,4,24,136]{3,2,1,0:T(8,128)} %pad_maximum_fusion.2), channel_id=1, source_target_pairs={{0,1},{2,3},{4,5},{6,7},{8,9},{10,11},{12,13},{14,15},{16,17},{18,... | collective-permute-start | bytes 2506760 | tf_op jit(solution)/shard_map/ppermute | solution.py:19
  292.1 27.5 %collective-permute-start.34 = (f32[3,3,1,64,64]{3,4,2,1,0:T(8,128)S(1)}, f32[3,3,1,64,64]{3,4,2,1,0:T(8,128)S(1)}, u32[]{:S(2)}, u32[]{:S(2)}) collective-permute-start(f32[3,3,1,64,64]{3,4,2,1,0:T(8,128)S(1)} %pad_maximum_fusion.60), channel_id=1, source_target_pairs={{0,1},{2,3},{4,5},{6,7},{8,9},{10,11},{12,13},{14,15},{16,17},{18,... | collective-permute-start | bytes 442376 | tf_op jit(solution)/shard_map/ppermute | solution.py:19
  293.4 26.2 %collective-permute-start.35 = (f32[3,3,1,64,64]{3,4,2,1,0:T(8,128)S(1)}, f32[3,3,1,64,64]{3,4,2,1,0:T(8,128)S(1)}, u32[]{:S(2)}, u32[]{:S(2)}) collective-permute-start(f32[3,3,1,64,64]{3,4,2,1,0:T(8,128)S(1)} %pad_maximum_fusion.60), channel_id=1, source_target_pairs={{1,0},{3,2},{5,4},{7,6},{9,8},{11,10},{13,12},{15,14},{17,16},{19,... | collective-permute-start | bytes 442376 | tf_op jit(solution)/shard_map/ppermute | solution.py:22
  412.7 17.1 %collective-permute-start.48 = (f32[1,1,1,64,64]{3,4,2,1,0:T(8,128)S(1)}, f32[1,1,1,64,64]{3,4,2,1,0:T(8,128)S(1)}, u32[]{:S(2)}, u32[]{:S(2)}) collective-permute-start(f32[1,1,1,64,64]{3,4,2,1,0:T(8,128)S(1)} %fusion.186), channel_id=1, source_target_pairs={{0,8},{8,16},{16,24},{1,9},{9,17},{17,25},{2,10},{10,18},{18,26},{... | collective-permute-start | bytes 49160 | tf_op jit(solution)/shard_map/ppermute | solution.py:19
  421.6 82.9 %collective-permute-start.40 = (f32[16,4,24,136]{3,2,1,0:T(8,128)}, f32[16,4,24,136]{3,2,1,0:T(8,128)}, u32[]{:S(2)}, u32[]{:S(2)}) collective-permute-start(f32[16,4,24,136]{3,2,1,0:T(8,128)} %pad_maximum_fusion.4), channel_id=1, source_target_pairs={{1,0},{3,2},{5,4},{7,6},{9,8},{11,10},{13,12},{15,14},{17,16},{19,... | collective-permute-start | bytes 2506760 | tf_op jit(solution)/shard_map/ppermute | solution.py:22
  422.9 81.6 %collective-permute-start.41 = (f32[16,4,24,136]{3,2,1,0:T(8,128)}, f32[16,4,24,136]{3,2,1,0:T(8,128)}, u32[]{:S(2)}, u32[]{:S(2)}) collective-permute-start(f32[16,4,24,136]{3,2,1,0:T(8,128)} %pad_maximum_fusion.4), channel_id=1, source_target_pairs={{0,1},{2,3},{4,5},{6,7},{8,9},{10,11},{12,13},{14,15},{16,17},{18,... | collective-permute-start | bytes 2506760 | tf_op jit(solution)/shard_map/ppermute | solution.py:19
  440.9 27.7 %collective-permute-start.52 = (f32[3,3,1,64,64]{3,4,2,1,0:T(8,128)S(1)}, f32[3,3,1,64,64]{3,4,2,1,0:T(8,128)S(1)}, u32[]{:S(2)}, u32[]{:S(2)}) collective-permute-start(f32[3,3,1,64,64]{3,4,2,1,0:T(8,128)S(1)} %pad_maximum_fusion.61), channel_id=1, source_target_pairs={{0,1},{2,3},{4,5},{6,7},{8,9},{10,11},{12,13},{14,15},{16,17},{18,... | collective-permute-start | bytes 442376 | tf_op jit(solution)/shard_map/ppermute | solution.py:19
  442.2 26.4 %collective-permute-start.53 = (f32[3,3,1,64,64]{3,4,2,1,0:T(8,128)S(1)}, f32[3,3,1,64,64]{3,4,2,1,0:T(8,128)S(1)}, u32[]{:S(2)}, u32[]{:S(2)}) collective-permute-start(f32[3,3,1,64,64]{3,4,2,1,0:T(8,128)S(1)} %pad_maximum_fusion.61), channel_id=1, source_target_pairs={{1,0},{3,2},{5,4},{7,6},{9,8},{11,10},{13,12},{15,14},{17,16},{19,... | collective-permute-start | bytes 442376 | tf_op jit(solution)/shard_map/ppermute | solution.py:22
  560.6 17.1 %collective-permute-start.66 = (f32[1,1,1,64,64]{3,4,2,1,0:T(8,128)S(1)}, f32[1,1,1,64,64]{3,4,2,1,0:T(8,128)S(1)}, u32[]{:S(2)}, u32[]{:S(2)}) collective-permute-start(f32[1,1,1,64,64]{3,4,2,1,0:T(8,128)S(1)} %fusion.182), channel_id=1, source_target_pairs={{0,8},{8,16},{16,24},{1,9},{9,17},{17,25},{2,10},{10,18},{18,26},{... | collective-permute-start | bytes 49160 | tf_op jit(solution)/shard_map/ppermute | solution.py:19
  569.5 84.8 %collective-permute-start.58 = (f32[16,4,24,136]{3,2,1,0:T(8,128)}, f32[16,4,24,136]{3,2,1,0:T(8,128)}, u32[]{:S(2)}, u32[]{:S(2)}) collective-permute-start(f32[16,4,24,136]{3,2,1,0:T(8,128)} %pad_maximum_fusion.6), channel_id=1, source_target_pairs={{1,0},{3,2},{5,4},{7,6},{9,8},{11,10},{13,12},{15,14},{17,16},{19,... | collective-permute-start | bytes 2506760 | tf_op jit(solution)/shard_map/ppermute | solution.py:22
  570.8 83.5 %collective-permute-start.59 = (f32[16,4,24,136]{3,2,1,0:T(8,128)}, f32[16,4,24,136]{3,2,1,0:T(8,128)}, u32[]{:S(2)}, u32[]{:S(2)}) collective-permute-start(f32[16,4,24,136]{3,2,1,0:T(8,128)} %pad_maximum_fusion.6), channel_id=1, source_target_pairs={{0,1},{2,3},{4,5},{6,7},{8,9},{10,11},{12,13},{14,15},{16,17},{18,... | collective-permute-start | bytes 2506760 | tf_op jit(solution)/shard_map/ppermute | solution.py:19
  588.7 27.9 %collective-permute-start.70 = (f32[3,3,1,64,64]{3,4,2,1,0:T(8,128)S(1)}, f32[3,3,1,64,64]{3,4,2,1,0:T(8,128)S(1)}, u32[]{:S(2)}, u32[]{:S(2)}) collective-permute-start(f32[3,3,1,64,64]{3,4,2,1,0:T(8,128)S(1)} %pad_maximum_fusion.62), channel_id=1, source_target_pairs={{0,1},{2,3},{4,5},{6,7},{8,9},{10,11},{12,13},{14,15},{16,17},{18,... | collective-permute-start | bytes 442376 | tf_op jit(solution)/shard_map/ppermute | solution.py:19
  590.0 26.6 %collective-permute-start.71 = (f32[3,3,1,64,64]{3,4,2,1,0:T(8,128)S(1)}, f32[3,3,1,64,64]{3,4,2,1,0:T(8,128)S(1)}, u32[]{:S(2)}, u32[]{:S(2)}) collective-permute-start(f32[3,3,1,64,64]{3,4,2,1,0:T(8,128)S(1)} %pad_maximum_fusion.62), channel_id=1, source_target_pairs={{1,0},{3,2},{5,4},{7,6},{9,8},{11,10},{13,12},{15,14},{17,16},{19,... | collective-permute-start | bytes 442376 | tf_op jit(solution)/shard_map/ppermute | solution.py:22
  (61 other events, 686.3 us)
where the time goes:
time: 678 us; the launch traced here: 666 us
  starting transfers between devices  181 us (27%)
  other arithmetic  162 us (24%)
  waiting for transfers between devices  154 us (23%)
  blocking collectives  67.6 us (10%)
  local copies, waits for them, and re-layouts  59 us (9%)
  matrix products  39.9 us (6%)
    ppermute x36, starting transfers between devices, padded_2(): lax.ppermute(lax.slice_in_dim(block, block.shape[dim] - width, None, axis...  134 us
    ppermute x36, waiting for transfers between devices, padded_2(): lax.ppermute(lax.slice_in_dim(block, block.shape[dim] - width, None, axis...  111 us
    scatter-add x4, other arithmetic, projected(): jnp.zeros_like(lines).at[:, tile_column, :].add(returned)  81.1 us
    all_gather x1, blocking collectives, per_device(): lax.all_gather(coupling, ('gx', 'gy', 'gz'), axis=0, tiled=True)  67.6 us
    ppermute x36, starting transfers between devices, padded_2(): lax.ppermute(lax.slice_in_dim(block, 0, width, axis=dim), axis, backward)  46.9 us
    ppermute x36, waiting for transfers between devices, padded_2(): lax.ppermute(lax.slice_in_dim(block, 0, width, axis=dim), axis, backward)  42.6 us
    sub x3, other arithmetic, per_device(): 2.0 * (hamiltonian(current) - center * current) / half_width - previous  33.3 us
    concatenate x24, other arithmetic, padded_2(): block = jnp.concatenate([low, block, high], axis=dim)  22.9 us
  transfers between devices with their start and end apart: 72, of which 26 were waited for; matrix products, arithmetic and copies ran while one was open for 26% of the time, Pallas kernels for 0%

commit v1 on v0

--- a/solution.py
+++ b/solution.py
@@ -1,14 +1,23 @@
+import functools
+
 import jax
 import jax.numpy as jnp
 from jax import lax
+from jax.experimental import pallas as pl
+from jax.experimental.pallas import tpu as pltpu
 from jax.sharding import PartitionSpec as P
 
 DEGREE = 4
 
 
 stencil_weights = (-205.0 / 72.0, 8.0 / 5.0, -1.0 / 5.0, 8.0 / 315.0, -1.0 / 560.0)
+REACH = len(stencil_weights) - 1
 lower_edge = 4.0
 upper_edge = 24.0
+CENTER = 0.5 * (upper_edge + lower_edge)
+HALF_WIDTH = 0.5 * (upper_edge - lower_edge)
+SUB = 8
+LANE = 128
 
 
 def padded_2(block, sides, width):
@@ -55,7 +64,7 @@
     )
 
 
-def per_device(
+def general_path(
     orbitals, potential, tile_proj, tile_atom, tile_column, tile_count, atom_home, coupling
 ):
     orbital_count, depth_z, depth_y, depth_x = orbitals.shape
@@ -78,8 +87,6 @@
     rel_y = owner // count_z % count_y - index_y + 1
     rel_z = owner % count_z - index_z + 1
     near_key = ((rel_x * 3 + rel_y) * 3 + rel_z) * owned_count + tile_atom % owned_count
-    center = 0.5 * (upper_edge + lower_edge)
-    half_width = 0.5 * (upper_edge - lower_edge)
 
     def projected(values):
         lines = values.reshape(orbital_count, depth_z * depth_y, depth_x)
@@ -112,12 +119,491 @@
         return -0.5 * laplacian(values) + potential[None] * values + projected(values)
 
     previous = orbitals
-    current = (hamiltonian(orbitals) - center * orbitals) / half_width
+    current = (hamiltonian(orbitals) - CENTER * orbitals) / HALF_WIDTH
     for repeat in range(DEGREE - 1):
-        following = 2.0 * (hamiltonian(current) - center * current) / half_width - previous
+        following = 2.0 * (hamiltonian(current) - CENTER * current) / HALF_WIDTH - previous
         previous = current
         current = following
     return current
+
+
+def hi_lo(value):
+    hi = value.astype(jnp.bfloat16)
+    lo = (value - hi.astype(jnp.float32)).astype(jnp.bfloat16)
+    return hi, lo
+
+
+def dot_nn(left, right):
+    return lax.dot_general(left, right, (((1,), (0,)), ((), ())), preferred_element_type=jnp.float32)
+
+
+def dot_nt(left, right):
+    return lax.dot_general(left, right, (((1,), (1,)), ((), ())), preferred_element_type=jnp.float32)
+
+
+def forward_block(plan, y_block, stack, hot, columns):
+    on, points, slots, projs = plan.on, plan.points, plan.slots, plan.projs
+    hi, lo = hi_lo(y_block)
+    left = jnp.concatenate(
+        [jnp.concatenate([hi, hi], axis=1), jnp.concatenate([lo, lo], axis=1)], axis=0
+    )
+    both = dot_nt(left, stack)
+    rows = on * points
+    product = both[:rows] + both[rows:]
+    mask = columns == lax.broadcasted_iota(jnp.int32, (points, slots), 0)
+    lines = []
+    for p in range(projs):
+        for o in range(on):
+            piece = product[o * points : (o + 1) * points, p * slots : (p + 1) * slots]
+            lines.append(jnp.sum(jnp.where(mask, piece, 0.0), axis=0, keepdims=True))
+    partial = jnp.concatenate(lines, axis=0)
+    part_hi, part_lo = hi_lo(partial)
+    sums = dot_nt(jnp.concatenate([part_hi, part_lo], axis=0), hot)
+    return sums[: plan.features] + sums[plan.features :]
+
+
+def backward_block(plan, coef_split, stack, hot, columns):
+    on, points, slots, projs = plan.on, plan.points, plan.slots, plan.projs
+    near = dot_nn(coef_split, hot)
+    near = near[: plan.features] + near[plan.features :]
+    mask = columns == lax.broadcasted_iota(jnp.int32, (points, slots), 0)
+    bands = []
+    for o in range(on):
+        pieces = []
+        for p in range(projs):
+            line = near[p * on + o : p * on + o + 1, :]
+            pieces.append(jnp.where(mask, line, 0.0))
+        bands.append(jnp.concatenate(pieces, axis=1))
+    weights = jnp.concatenate(bands, axis=0)
+    hi, lo = hi_lo(weights)
+    four = dot_nn(jnp.concatenate([hi, lo], axis=0), stack)
+    rows = on * points
+    cx = plan.cx
+    return (four[:rows, :cx] + four[rows:, cx:]) + (four[:rows, cx:] + four[rows:, :cx])
+
+
+def emit_halo(plan, y_new, g, up_ref, down_ref):
+    on, cz, cy = plan.on, plan.cz, plan.cy
+    tops, bottoms = [], []
+    for o in range(on):
+        for z in range(cz):
+            start = (o * cz + z) * cy
+            bottoms.append(y_new[start : start + REACH])
+            tops.append(y_new[start + cy - REACH : start + cy])
+    rows = on * cz * REACH
+    where = pl.ds(pl.multiple_of(g * rows, SUB), rows)
+    up_ref[where, :] = jnp.concatenate(tops, axis=0)
+    down_ref[where, :] = jnp.concatenate(bottoms, axis=0)
+
+
+def emit_sums(plan, total, own_ref, up_ref, down_ref, up2_ref, down2_ref):
+    f, third, halo = plan.features, plan.third, plan.halo_rows
+    for j in range(3 * third):
+        block = total[:, j * LANE : (j + 1) * LANE]
+        own_ref[j * f : (j + 1) * f, :] = block
+        if j >= third:
+            row = halo + (j - third) * f
+            up_ref[row : row + f, :] = block
+        if j < 2 * third:
+            row = halo + j * f
+            down_ref[row : row + f, :] = block
+        if j >= 2 * third:
+            row = (j - 2 * third) * f
+            up2_ref[row : row + f, :] = block
+        if j < third:
+            down2_ref[j * f : (j + 1) * f, :] = block
+
+
+def load_coefs(plan, own_ref, low_ref, high_ref, low2_ref, high2_ref, scale_ref):
+    f, third, halo = plan.features, plan.third, plan.halo_rows
+    blocks = []
+    for j in range(3 * third):
+        block = own_ref[j * f : (j + 1) * f, :]
+        if j < 2 * third:
+            row = halo + j * f
+            block = block + low_ref[row : row + f, :]
+        if j >= third:
+            row = halo + (j - third) * f
+            block = block + high_ref[row : row + f, :]
+        if j < third:
+            block = block + low2_ref[j * f : (j + 1) * f, :]
+        if j >= 2 * third:
+            row = (j - 2 * third) * f
+            block = block + high2_ref[row : row + f, :]
+        blocks.append(block)
+    return jnp.concatenate(blocks, axis=1) * scale_ref[...]
+
+
+def fill_padded(plan, y_ref, low_ref, high_ref, pad_ref):
+    on, cz, cy, gx, gz = plan.on, plan.cz, plan.cy, plan.gx, plan.gz
+    depth = cz * gz
+    zero_plane = jnp.zeros((1,) + pad_ref.shape[1:], jnp.float32)
+    pad_ref[0:1] = zero_plane
+    pad_ref[gx + 1 : gx + 2] = zero_plane
+    zero_ends = jnp.zeros((gx, on, REACH) + pad_ref.shape[3:], jnp.float32)
+    pad_ref[1 : gx + 1, :, 0:REACH] = zero_ends
+    pad_ref[1 : gx + 1, :, REACH + depth :] = zero_ends
+    rows = on * cz * REACH
+    for ix in range(gx):
+        for iz in range(gz):
+            g = ix * gz + iz
+            for o in range(on):
+                at = REACH + iz * cz
+                lead = (o * cz) * cy
+                pad_ref[ix + 1, o, at : at + cz, SUB : SUB + cy, :] = y_ref[
+                    g, lead : lead + cz * cy, :
+                ].reshape(cz, cy, plan.cx)
+                for z in range(cz):
+                    row = g * rows + (o * cz + z) * REACH
+                    pad_ref[ix + 1, o, at + z, SUB - REACH : SUB, :] = low_ref[row : row + REACH, :]
+                    pad_ref[ix + 1, o, at + z, SUB + cy : SUB + cy + REACH, :] = high_ref[
+                        row : row + REACH, :
+                    ]
+
+
+def local_block(plan, g, pad_ref, potential, previous, first):
+    on, cz, cy, cx, gz = plan.on, plan.cz, plan.cy, plan.cx, plan.gz
+    ix = g // gz
+    iz = g - ix * gz
+    at = REACH + iz * cz
+    own = slice(SUB, SUB + cy)
+    factor = (1.0 if first else 2.0) / HALF_WIDTH
+    rows = on * cz * cy
+    shape = (rows, cx)
+    lane = lax.broadcasted_iota(jnp.int32, shape, 1)
+    center = pad_ref[ix + 1, :, pl.ds(at, cz), own, :].reshape(shape)
+    left = pad_ref[ix, :, pl.ds(at, cz), own, :].reshape(shape)
+    right = pad_ref[ix + 2, :, pl.ds(at, cz), own, :].reshape(shape)
+    diagonal = potential - (CENTER + 1.5 * stencil_weights[0])
+    diagonal = jnp.concatenate([factor * diagonal] * on, axis=0)
+    total = diagonal * center
+    for k in range(1, REACH + 1):
+        near = pltpu.roll(jnp.where(lane >= cx - k, left, center), k, 1)
+        near = near + pltpu.roll(jnp.where(lane < k, right, center), cx - k, 1)
+        for sign in (k, -k):
+            near = near + pad_ref[ix + 1, :, pl.ds(at + sign, cz), own, :].reshape(shape)
+            moved = slice(SUB + sign, SUB + sign + cy)
+            near = near + pad_ref[ix + 1, :, pl.ds(at, cz), moved, :].reshape(shape)
+        total = total + (-0.5 * factor * stencil_weights[k]) * near
+    if not first:
+        total = total - previous
+    return total, factor
+
+
+def opening_kernel(
+    plan, me_ref, near_ref, far_ref, y_ref,
+    stack_ref, hot_ref, columns_ref, potential_ref, own_ref, up_ref, down_ref, up2_ref, down2_ref,
+    total_ref,
+):
+    step = pl.program_id(0)
+    half = plan.blocks // 2
+    g = plan.block_of(step, me_ref[0])
+
+    def unpack(source):
+        tiles = plan.projs * plan.slots
+        hi, lo = hi_lo(source[0, :tiles, :])
+        stack_ref[0, :, : plan.cx] = hi
+        stack_ref[0, :, plan.cx :] = lo
+        potential_ref[0] = source[0, tiles : tiles + plan.points, :]
+        meta = tiles + plan.points
+        per = plan.slots // LANE
+        keys = jnp.concatenate([source[0, meta + i : meta + i + 1, :] for i in range(per)], axis=1)
+        cols = jnp.concatenate(
+            [source[0, meta + per + i : meta + per + i + 1, :] for i in range(per)], axis=1
+        )
+        keys = keys.astype(jnp.int32)
+        columns_ref[0] = jnp.broadcast_to(cols.astype(jnp.int32), (SUB, plan.slots))
+        chunk = 256
+        index = lax.broadcasted_iota(jnp.int32, (chunk, plan.slots), 0)
+        for start in range(0, plan.keys, chunk):
+            hot_ref[0, start : start + chunk, :] = jnp.where(
+                index == keys - start, 1.0, 0.0
+            ).astype(jnp.bfloat16)
+
+    @pl.when(step < half)
+    def _():
+        unpack(near_ref)
+
+    @pl.when(step >= half)
+    def _():
+        unpack(far_ref)
+
+    y_block = y_ref[0]
+    sums = forward_block(plan, y_block, stack_ref[0], hot_ref[0], columns_ref[0, 0:1, :])
+    emit_halo(plan, y_block, g, up_ref, down_ref)
+
+    @pl.when(step == 0)
+    def _():
+        total_ref[...] = sums
+
+    @pl.when(step > 0)
+    def _():
+        total_ref[...] += sums
+
+    @pl.when(step == plan.blocks - 1)
+    def _():
+        emit_sums(plan, total_ref[...], own_ref, up_ref, down_ref, up2_ref, down2_ref)
+
+
+def middle_kernel(plan, first, last, *refs):
+    me_ref, y_ref = refs[:2]
+    refs = refs[2:]
+    if first:
+        previous = None
+    else:
+        previous, refs = refs[0], refs[1:]
+    (own_in, low_ref, high_ref, low2_ref, high2_ref, scale_ref) = refs[:6]
+    stack_ref, hot_ref, columns_ref, potential_ref, out_ref = refs[6:11]
+    refs = refs[11:]
+    if not last:
+        own_ref, up_ref, down_ref, up2_ref, down2_ref = refs[:5]
+        refs = refs[5:]
+    pad_ref, coef_ref = refs[:2]
+    step = pl.program_id(0)
+    g = plan.block_of(step, me_ref[0])
+
+    @pl.when(step == 0)
+    def _():
+        coefs = load_coefs(plan, own_in, low_ref, high_ref, low2_ref, high2_ref, scale_ref)
+        hi, lo = hi_lo(coefs)
+        coef_ref[...] = jnp.concatenate([hi, lo], axis=0)
+        fill_padded(plan, y_ref, low_ref, high_ref, pad_ref)
+
+    columns = columns_ref[0, 0:1, :]
+    projected = backward_block(plan, coef_ref[...], stack_ref[0], hot_ref[0], columns)
+    before = None if first else previous[0]
+    local, factor = local_block(plan, g, pad_ref, potential_ref[0], before, first)
+    y_new = local + factor * projected
+    out_ref[0] = y_new
+    if last:
+        return
+    sums = forward_block(plan, y_new, stack_ref[0], hot_ref[0], columns)
+    emit_halo(plan, y_new, g, up_ref, down_ref)
+    total_ref = refs[2]
+
+    @pl.when(step == 0)
+    def _():
+        total_ref[...] = sums
+
+    @pl.when(step > 0)
+    def _():
+        total_ref[...] += sums
+
+    @pl.when(step == plan.blocks - 1)
+    def _():
+        emit_sums(plan, total_ref[...], own_ref, up_ref, down_ref, up2_ref, down2_ref)
+
+
+class Plan:
+    pass
+
+
+def log2(value):
+    return value.bit_length() - 1
+
+
+def exchange(value, axis, bit):
+    count = lax.axis_size(axis)
+    return lax.ppermute(value, axis, [(i, i ^ bit) for i in range(count)])
+
+
+def turned_path(
+    orbitals, potential, tile_proj, tile_atom, tile_column, tile_count, atom_home, coupling
+):
+    norb, cz, cy, cx = orbitals.shape
+    slots, projs, _ = tile_proj.shape
+    owned = coupling.shape[0]
+    gx, gy, gz = (lax.axis_size(name) for name in ("gx", "gy", "gz"))
+    ix, iy, iz = (lax.axis_index(name) for name in ("gx", "gy", "gz"))
+    blocks = gx * gz
+    on = norb // blocks
+    points = cz * cy
+    plan = Plan()
+    plan.on, plan.cz, plan.cy, plan.cx, plan.gx, plan.gz = on, cz, cy, cx, gx, gz
+    plan.points, plan.slots, plan.projs, plan.blocks = points, slots, projs, blocks
+    plan.features = projs * on
+    plan.keys = 3 * blocks * owned
+    plan.third = blocks * owned // LANE
+    plan.halo_rows = blocks * on * cz * REACH
+    rounds = [("gz", 1 << b) for b in range(log2(gz))]
+    rounds += [("gx", 1 << b) for b in reversed(range(log2(gx)))]
+    weights = [bit if axis == "gz" else bit * gz for axis, bit in rounds]
+
+    def block_of(step, me):
+        moved = sum(((step >> j) & 1) * w for j, w in enumerate(weights))
+        return moved ^ me
+
+    plan.block_of = block_of
+
+    live = jnp.arange(slots, dtype=jnp.int32) < tile_count[0]
+    column = jnp.where(live, tile_column, -1)
+    owner = tile_atom // owned
+    owner_x = owner // (gy * gz)
+    owner_y = owner // gz % gy
+    owner_z = owner % gz
+    key = (
+        (owner_y - iy + 1) * (blocks * owned)
+        + (owner_x * gz + owner_z) * owned
+        + tile_atom % owned
+    )
+    lanes = lambda value: value.astype(jnp.float32).reshape(-1, LANE)
+    tiles = tile_proj.transpose(1, 0, 2).reshape(projs * slots, cx)
+    meta = jnp.concatenate([lanes(key), lanes(column), lanes(coupling)], axis=0)
+    meta_rows = -(-meta.shape[0] // SUB) * SUB
+    meta = jnp.pad(meta, ((0, meta_rows - meta.shape[0]), (0, 0)))
+    payload = jnp.concatenate([tiles, potential.reshape(points, cx), meta], axis=0)
+    rows = payload.shape[0]
+    cut = rows // 2 // SUB * SUB
+    part_a, part_b = payload[None, :cut], payload[None, cut:]
+    swapped = [rounds[1], rounds[0]] + rounds[2:]
+    for (axis_a, bit_a), (axis_b, bit_b) in zip(rounds[:2], swapped[:2]):
+        far_a = exchange(part_a, axis_a, bit_a)
+        far_b = exchange(part_b, axis_b, bit_b)
+        part_a = jnp.concatenate([part_a, far_a], axis=0)
+        part_b = jnp.concatenate([part_b, far_b], axis=0)
+    part_b = jnp.stack([part_b[0], part_b[2], part_b[1], part_b[3]])
+    near = jnp.concatenate([part_a, part_b], axis=1)
+    for axis, bit in rounds[2:-1]:
+        near = jnp.concatenate([near, exchange(near, axis, bit)], axis=0)
+    far = exchange(near, *rounds[-1])
+
+    meta_at = projs * slots + points + 2 * (slots // LANE)
+    coupling_rows = owned * projs // LANE
+    take = lambda value: value[:, meta_at : meta_at + coupling_rows]
+    table = jnp.concatenate([take(near), take(far)], axis=0).reshape(
+        (1, blocks, coupling_rows, LANE)
+    )
+    for b in range(log2(gy)):
+        table = jnp.concatenate([table, exchange(table, "gy", 1 << b)], axis=0)
+    me = ix * gz + iz
+    home = atom_home.reshape(gx, gy, gz, owned).transpose(1, 0, 2, 3).reshape(gy, blocks * owned)
+    home = jnp.pad(home, ((1, 1), (0, 0)))
+    home = lax.dynamic_slice_in_dim(home, iy, 3, axis=0).reshape(plan.keys)
+    home_device = home // owned
+    home_y = home_device // gz % gy
+    home_g = home_device // (gy * gz) * gz + home_device % gz
+    moved_g = home_g ^ me
+    place = sum(((moved_g >> log2(w)) & 1) * (1 << j) for j, w in enumerate(weights))
+    row = ((home_y ^ iy) * blocks + place) * owned + home % owned
+    scale = table.reshape(gy * blocks * owned, projs)[row]
+    scale = jnp.repeat(scale.T, on, axis=0)
+
+    y0 = lax.all_to_all(
+        orbitals.reshape(blocks, on * points, cx), ("gx", "gz"), 0, 0, tiled=True
+    )
+
+    f32 = jnp.float32
+    spec_me = me.reshape(1).astype(jnp.int32)
+    message_rows = plan.halo_rows + 2 * plan.third * plan.features
+    message2_rows = plan.third * plan.features
+    own_rows = 3 * plan.third * plan.features
+    half = blocks // 2
+    whole = lambda *shape: pl.BlockSpec(shape, lambda i, m: (0,) * len(shape))
+    per_step = lambda *shape: pl.BlockSpec((1,) + shape, lambda i, m: (i, 0, 0))
+    per_block = lambda *shape: pl.BlockSpec((1,) + shape, lambda i, m: (block_of(i, m[0]), 0, 0))
+    tile_rows = projs * slots
+    y_rows = on * points
+    send_shapes = [
+        jax.ShapeDtypeStruct((own_rows, LANE), f32),
+        jax.ShapeDtypeStruct((message_rows, LANE), f32),
+        jax.ShapeDtypeStruct((message_rows, LANE), f32),
+        jax.ShapeDtypeStruct((message2_rows, LANE), f32),
+        jax.ShapeDtypeStruct((message2_rows, LANE), f32),
+    ]
+    send_specs = [whole(*shape.shape) for shape in send_shapes]
+    constant_specs = [
+        per_step(tile_rows, 2 * cx),
+        per_step(plan.keys, slots),
+        per_step(SUB, slots),
+        per_step(points, cx),
+    ]
+    params = pltpu.CompilerParams(vmem_limit_bytes=48 * 1024 * 1024)
+    sums_scratch = pltpu.VMEM((plan.features, plan.keys), f32)
+
+    opened = pl.pallas_call(
+        functools.partial(opening_kernel, plan),
+        out_shape=[
+            jax.ShapeDtypeStruct((blocks, tile_rows, 2 * cx), jnp.bfloat16),
+            jax.ShapeDtypeStruct((blocks, plan.keys, slots), jnp.bfloat16),
+            jax.ShapeDtypeStruct((blocks, SUB, slots), jnp.int32),
+            jax.ShapeDtypeStruct((blocks, points, cx), f32),
+        ]
+        + send_shapes,
+        grid_spec=pltpu.PrefetchScalarGridSpec(
+            num_scalar_prefetch=1,
+            grid=(blocks,),
+            in_specs=[
+                pl.BlockSpec((1, rows, cx), lambda i, m: (jnp.minimum(i, half - 1), 0, 0)),
+                pl.BlockSpec((1, rows, cx), lambda i, m: (jnp.maximum(i - half, 0), 0, 0)),
+                per_block(y_rows, cx),
+            ],
+            out_specs=constant_specs + send_specs,
+            scratch_shapes=[sums_scratch],
+        ),
+        compiler_params=params,
+        name="opening",
+    )(spec_me, near, far, y0)
+    constants, sends = list(opened[:4]), list(opened[4:])
+
+    def shift(value, by):
+        pairs = [(i, i + by) for i in range(gy) if 0 <= i + by < gy]
+        return lax.ppermute(value, "gy", pairs)
+
+    def swap(sends):
+        own, up, down, up2, down2 = sends
+        return own, shift(up, 1), shift(down, -1), shift(up2, 2), shift(down2, -2)
+
+    current, previous = y0, None
+    for repeat in range(DEGREE):
+        first, last = repeat == 0, repeat == DEGREE - 1
+        received = swap(sends)
+        arrays = [spec_me, current] + ([] if first else [previous])
+        arrays += [*received, scale] + constants
+        in_specs = [whole(blocks, y_rows, cx)] + ([] if first else [per_block(y_rows, cx)])
+        in_specs += send_specs + [whole(plan.features, plan.keys)] + constant_specs
+        scratch = [
+            pltpu.VMEM((gx + 2, on, cz * gz + 2 * REACH, 2 * SUB + cy, cx), f32),
+            pltpu.VMEM((2 * plan.features, plan.keys), jnp.bfloat16),
+        ]
+        result = pl.pallas_call(
+            functools.partial(middle_kernel, plan, first, last),
+            out_shape=[jax.ShapeDtypeStruct((blocks, y_rows, cx), f32)]
+            + ([] if last else send_shapes),
+            grid_spec=pltpu.PrefetchScalarGridSpec(
+                num_scalar_prefetch=1,
+                grid=(blocks,),
+                in_specs=in_specs,
+                out_specs=[per_block(y_rows, cx)] + ([] if last else send_specs),
+                scratch_shapes=scratch + ([] if last else [sums_scratch]),
+            ),
+            compiler_params=params,
+            name="step",
+        )(*arrays)
+        previous, current = current, result[0]
+        sends = result[1:]
+
+    turned = lax.all_to_all(current, ("gx", "gz"), 0, 0, tiled=True)
+    return turned.reshape(norb, cz, cy, cx)
+
+
+def power_of_two(value):
+    return value & (value - 1) == 0
+
+
+def per_device(*arguments):
+    orbitals, coupling = arguments[0], arguments[-1]
+    norb, cz, cy, cx = orbitals.shape
+    slots, projs, _ = arguments[2].shape
+    owned = coupling.shape[0]
+    gx, gy, gz = (lax.axis_size(name) for name in ("gx", "gy", "gz"))
+    blocks = gx * gz
+    turned = all(power_of_two(size) for size in (gx, gy, gz)) and gx > 1 and gz > 1
+    turned = turned and norb % blocks == 0 and cx == LANE and slots % LANE == 0
+    if turned:
+        turned = (norb // blocks * projs) % SUB == 0 and (owned * projs) % LANE == 0
+        turned = turned and (blocks * owned) % LANE == 0 and cy % SUB == 0 and cy >= REACH
+        turned = turned and cz % 2 == 0 and (3 * blocks * owned) % 256 == 0
+    return turned_path(*arguments) if turned else general_path(*arguments)
 
 
 def solution(mesh):

time: 678 us -> 174 us (0.26); the launches traced: 666 us -> 172 us
  other arithmetic: 162 us -> 2.71 us
  starting transfers between devices: 181 us -> 55.4 us
  waiting for transfers between devices: 154 us -> 39 us
  blocking collectives: 67.6 us -> 11.4 us
  Pallas kernels: 0 us -> 54.6 us
  local copies, waits for them, and re-layouts: 59 us -> 7.75 us
  matrix products: 39.9 us -> 0 us
    ppermute x72 -> x23, starting transfers between devices: 181 us -> 51.9 us  [the longest x16 38.6 us: shift(): return lax.ppermute(value, 'gy', pairs)]
    ppermute x72 -> x23, waiting for transfers between devices: 154 us -> 34.4 us  [the longest x7 18.6 us: exchange(): return lax.ppermute(value, axis, [(i, i ^ bit) for i in range(count)])]
    scatter-add x8 -> x0, other arithmetic: 87.7 us -> none  [the longest x4 81.1 us: projected(): jnp.zeros_like(lines).at[:, tile_column, :].add(returned)]
    all_gather x1 -> x0, blocking collectives: 67.6 us -> none  [per_device(): lax.all_gather(coupling, ('gx', 'gy', 'gz'), axis=0, tiled=True)]
    pallas_call x0 -> x5, Pallas kernels: none -> 54.6 us  [the longest x4 44 us: turned_path(): pl.pallas_call(functools.partial(middle_kernel, plan, first, last), out_s...]
    dot_general x8 -> x0, matrix products: 39.9 us -> none  [the longest x4 21.4 us: projected(): jnp.einsum('tpx,tpo->otx', proj_live, per_tile, precision=lax.Precision.H...]
    sub x3 -> x0, other arithmetic: 33.3 us -> none  [per_device(): 2.0 * (hamiltonian(current) - center * current) / half_width - previous]
    concatenate x24 -> x6, other arithmetic: 22.9 us -> 0.33 us  [the longest x1 0.18 us: turned_path(): near = jnp.concatenate([part_a, part_b], axis=1)]
  transfers between devices with their start and end apart: 72 -> 24, of which waited for: 26 -> 13; matrix products, arithmetic and copies ran while one was open for 26% -> 3% of each run, Pallas kernels for 0% -> 6%
where the time goes in v1:
time: 174 us; the launch traced here: 172 us
  starting transfers between devices  55.4 us (32%)
  Pallas kernels  54.6 us (31%)
  waiting for transfers between devices  39 us (22%)
  blocking collectives  11.4 us (7%)
  local copies, waits for them, and re-layouts  7.75 us (4%)
  other arithmetic  2.71 us (2%)
    pallas_call x4, Pallas kernels, turned_path(): pl.pallas_call(functools.partial(middle_kernel, plan, first, last), out_s...  44 us
    ppermute x16, starting transfers between devices, shift(): return lax.ppermute(value, 'gy', pairs)  38.6 us
    ppermute x7, waiting for transfers between devices, exchange(): return lax.ppermute(value, axis, [(i, i ^ bit) for i in range(count)])  18.6 us
    ppermute x16, waiting for transfers between devices, shift(): return lax.ppermute(value, 'gy', pairs)  15.8 us
    ppermute x7, starting transfers between devices, exchange(): return lax.ppermute(value, axis, [(i, i ^ bit) for i in range(count)])  13.3 us
    all_to_all x1, blocking collectives, turned_path(): turned = lax.all_to_all(current, ('gx', 'gz'), 0, 0, tiled=True)  11.4 us
    pallas_call x1, Pallas kernels, turned_path(): pl.pallas_call(functools.partial(opening_kernel, plan), out_shape=[jax.Sh...  10.6 us
    all_to_all x1, waiting for transfers between devices, turned_path(): lax.all_to_all(orbitals.reshape(blocks, on * points, cx), ('gx', 'gz'), 0...  4.64 us
  transfers between devices with their start and end apart: 24, of which 13 were waited for; matrix products, arithmetic and copies ran while one was open for 3% of the time, Pallas kernels for 6%

profile of v1, /device:TPU:0, one launch (start us, length us, event | category | flops | bytes accessed | tf_op | source)
XLA Modules:
  0.0 171.9 jit_solution(3584907771876142549)
XLA Ops:
  4.1 3.0 %collective-permute-start.2 = (f32[1,552,128]{2,1,0:T(8,128)S(1)}, f32[1,552,128]{2,1,0:T(8,128)S(1)}, u32[]{:S(2)}, u32[]{:S(2)}) collective-permute-start(f32[1,552,128]{2,1,0:T(8,128)S(1)} %fusion), channel_id=1, source_target_pairs={{0,16},{8,24},{16,0},{24,8},{1,17},{9,25},{17,1},{25,9},{2,18},{10... | collective-permute-start | bytes 847880 | tf_op jit(solution)/shard_map/ppermute | solution.py:407
  8.8 5.1 %collective-permute-done.2 = f32[1,552,128]{2,1,0:T(8,128)S(1)} collective-permute-done((f32[1,552,128]{2,1,0:T(8,128)S(1)}, f32[1,552,128]{2,1,0:T(8,128)S(1)}, u32[]{:S(2)}, u32[]{:S(2)}) %collective-permute-start.2) | collective-permute-done | bytes 282656 | tf_op jit(solution)/shard_map/ppermute | solution.py:407
  17.4 10.6 %collective-permute-done.3 = f32[2,552,128]{2,1,0:T(8,128)S(1)} collective-permute-done((f32[2,552,128]{2,1,0:T(8,128)S(1)}, f32[2,552,128]{2,1,0:T(8,128)S(1)}, u32[]{:S(2)}, u32[]{:S(2)}) %collective-permute-start.3) | collective-permute-done | bytes 565280 | tf_op jit(solution)/shard_map/ppermute | solution.py:407
  29.4 3.5 %all-to-all-start = ((f32[8,128,128]{2,1,0:T(8,128)}), f32[8,128,128]{2,1,0:T(8,128)S(1)}, u32[]{:S(2)}, u32[]{:S(2)}) async-start(f32[8,128,128]{2,1,0:T(8,128)} %bitcast.30), calls=%async_computation | async-start | bytes 1048576 | tf_op jit(solution)/shard_map/all_to_all | solution.py:491
  37.0 4.6 %all-to-all-done.y_ref.refs_1_.refs_2_ = f32[8,128,128]{2,1,0:T(8,128)S(1)} async-done(((f32[8,128,128]{2,1,0:T(8,128)}), f32[8,128,128]{2,1,0:T(8,128)S(1)}, u32[]{:S(2)}, u32[]{:S(2)}) %all-to-all-start) | async-done | bytes 524320 | tf_op jit(solution)/shard_map/all_to_all | solution.py:491
  41.7 10.6 %opening.1 = (bf16[8,1024,256]{2,1,0:T(8,128)(2,1)}, bf16[8,1536,256]{2,1,0:T(8,128)(2,1)}, s32[8,8,256]{2,1,0:T(8,128)S(1)}, f32[8,64,128]{2,1,0:T(8,128)S(1)},...) custom-call(s32[1]{0:T(128)} %bitcast.me_ref.refs_0_, ...), custom_call_target="tpu_custom_call" | custom-call | tf_op jit(solution)/shard_map/opening/pallas_call | solution.py:523
  52.3 3.5 %collective-permute-start.5 = (f32[320,128]{1,0:T(8,128)S(1)}, f32[320,128]{1,0:T(8,128)S(1)}, u32[]{:S(2)}, u32[]{:S(2)}) collective-permute-start(f32[320,128]{1,0:T(8,128)S(1)} %get-tuple-element.33), channel_id=1, source_target_pairs={{0,2},{2,4},{4,6},{1,3},{3,5},{5,7},{8,10},{10,12},{12,14},{9,11},... | collective-permute-start | bytes 491528 | tf_op jit(solution)/shard_map/ppermute | solution.py:550
  57.1 3.7 %collective-permute-start.10 = (f32[2,8,2,128]{3,2,1,0:T(2,128)S(1)}, f32[2,8,2,128]{3,2,1,0:T(2,128)S(1)}, u32[]{:S(2)}, u32[]{:S(2)}) collective-permute-start(f32[2,8,2,128]{3,2,1,0:T(2,128)S(1)} %pad_maximum_fusion.5), channel_id=1, source_target_pairs={{0,4},{2,6},{4,0},{6,2},{1,5},{3,7},{5,1},{7,3},{8,12},{10,14},{12... | collective-permute-start | bytes 49160 | tf_op jit(solution)/shard_map/ppermute | solution.py:407
  60.8 1.9 %collective-permute-start.7 = (f32[32,128]{1,0:T(8,128)S(1)}, f32[32,128]{1,0:T(8,128)S(1)}, u32[]{:S(2)}, u32[]{:S(2)}) collective-permute-start(f32[32,128]{1,0:T(8,128)S(1)} %get-tuple-element.35), channel_id=1, source_target_pairs={{0,4},{2,6},{1,5},{3,7},{8,12},{10,14},{9,13},{11,15},{16,20},{18,... | collective-permute-start | bytes 49160 | tf_op jit(solution)/shard_map/ppermute | solution.py:550
  66.2 2.6 %gather_fusion = f32[1536,4]{1,0:T(8,128)S(1)} fusion(f32[2048,4]{1,0:T(8,128)S(1)} %reshape.335, s32[2048]{0:T(1024)S(1)} %pad_clamp_fusion), kind=kCustom, calls=%fused_computation | custom fusion | bytes 55296 | tf_op jit(solution)/shard_map/gather | solution.py:488
  69.3 11.6 %step.4 = (f32[8,128,128]{2,1,0:T(8,128)S(1)}, f32[96,128]{1,0:T(8,128)S(1)}, f32[320,128]{1,0:T(8,128)S(1)}, f32[320,128]{1,0:T(8,128)S(1)}, f32[32,128]{1,0:T(8,128)S(1)}, /*index=5*/f32[32,128]{1,0:T(8,128)S(1)}) custom-call(s32[1]{0:T(128)} %bitcast.me_ref.refs_0_, f32[8,128,128]{2,1,0:T(8,128)S(1)} %all-to-all-done.y_ref.refs_1_.refs_2_, ...), custom_call_target="tpu_custom_call" | custom-call | tf_op jit(solution)/shard_map/step/pallas_call | solution.py:568
  80.9 3.8 %collective-permute-start.11 = (f32[320,128]{1,0:T(8,128)S(1)}, f32[320,128]{1,0:T(8,128)S(1)}, u32[]{:S(2)}, u32[]{:S(2)}) collective-permute-start(f32[320,128]{1,0:T(8,128)S(1)} %get-tuple-element.43), channel_id=1, source_target_pairs={{0,2},{2,4},{4,6},{1,3},{3,5},{5,7},{8,10},{10,12},{12,14},{9,11},... | collective-permute-start | bytes 491528 | tf_op jit(solution)/shard_map/ppermute | solution.py:550
  86.0 5.1 %collective-permute-start.13 = (f32[32,128]{1,0:T(8,128)S(1)}, f32[32,128]{1,0:T(8,128)S(1)}, u32[]{:S(2)}, u32[]{:S(2)}) collective-permute-start(f32[32,128]{1,0:T(8,128)S(1)} %get-tuple-element.45), channel_id=1, source_target_pairs={{0,4},{2,6},{1,5},{3,7},{8,12},{10,14},{9,13},{11,15},{16,20},{18,... | collective-permute-start | bytes 49160 | tf_op jit(solution)/shard_map/ppermute | solution.py:550
  92.5 5.1 %collective-permute-done.14.refs_7_ = f32[32,128]{1,0:T(8,128)S(1)} collective-permute-done((f32[32,128]{1,0:T(8,128)S(1)}, f32[32,128]{1,0:T(8,128)S(1)}, u32[]{:S(2)}, u32[]{:S(2)}) %collective-permute-start.14) | collective-permute-done | bytes 16416 | tf_op jit(solution)/shard_map/ppermute | solution.py:550
  97.6 11.6 %step.5 = (f32[8,128,128]{2,1,0:T(8,128)S(1)}, f32[96,128]{1,0:T(8,128)S(1)}, f32[320,128]{1,0:T(8,128)S(1)}, f32[320,128]{1,0:T(8,128)S(1)}, f32[32,128]{1,0:T(8,128)S(1)}, /*index=5*/f32[32,128]{1,0:T(8,128)S(1)}) custom-call(s32[1]{0:T(128)} %bitcast.me_ref.refs_0_, f32[8,128,128]{2,1,0:T(8,128)S(1)} %get-tuple-element.41.refs_1_.refs_2_, ...), custom_call_target="tpu_custom_call" | custom-call | tf_op jit(solution)/shard_map/step/pallas_call | solution.py:568
  109.2 3.8 %collective-permute-start.15 = (f32[320,128]{1,0:T(8,128)S(1)}, f32[320,128]{1,0:T(8,128)S(1)}, u32[]{:S(2)}, u32[]{:S(2)}) collective-permute-start(f32[320,128]{1,0:T(8,128)S(1)} %get-tuple-element.49), channel_id=1, source_target_pairs={{0,2},{2,4},{4,6},{1,3},{3,5},{5,7},{8,10},{10,12},{12,14},{9,11},... | collective-permute-start | bytes 491528 | tf_op jit(solution)/shard_map/ppermute | solution.py:550
  114.3 4.0 %collective-permute-start.17 = (f32[32,128]{1,0:T(8,128)S(1)}, f32[32,128]{1,0:T(8,128)S(1)}, u32[]{:S(2)}, u32[]{:S(2)}) collective-permute-start(f32[32,128]{1,0:T(8,128)S(1)} %get-tuple-element.51), channel_id=1, source_target_pairs={{0,4},{2,6},{1,5},{3,7},{8,12},{10,14},{9,13},{11,15},{16,20},{18,... | collective-permute-start | bytes 49160 | tf_op jit(solution)/shard_map/ppermute | solution.py:550
  119.7 5.1 %collective-permute-done.18.refs_7_ = f32[32,128]{1,0:T(8,128)S(1)} collective-permute-done((f32[32,128]{1,0:T(8,128)S(1)}, f32[32,128]{1,0:T(8,128)S(1)}, u32[]{:S(2)}, u32[]{:S(2)}) %collective-permute-start.18) | collective-permute-done | bytes 16416 | tf_op jit(solution)/shard_map/ppermute | solution.py:550
  124.9 11.6 %step.6 = (f32[8,128,128]{2,1,0:T(8,128)S(1)}, f32[96,128]{1,0:T(8,128)S(1)}, f32[320,128]{1,0:T(8,128)S(1)}, f32[320,128]{1,0:T(8,128)S(1)}, f32[32,128]{1,0:T(8,128)S(1)}, /*index=5*/f32[32,128]{1,0:T(8,128)S(1)}) custom-call(s32[1]{0:T(128)} %bitcast.me_ref.refs_0_, f32[8,128,128]{2,1,0:T(8,128)S(1)} %get-tuple-element.47.refs_1_.refs_2_, ...), custom_call_target="tpu_custom_call" | custom-call | tf_op jit(solution)/shard_map/step/pallas_call | solution.py:568
  136.4 2.2 %collective-permute-start.19 = (f32[320,128]{1,0:T(8,128)S(1)}, f32[320,128]{1,0:T(8,128)S(1)}, u32[]{:S(2)}, u32[]{:S(2)}) collective-permute-start(f32[320,128]{1,0:T(8,128)S(1)} %get-tuple-element.55), channel_id=1, source_target_pairs={{0,2},{2,4},{4,6},{1,3},{3,5},{5,7},{8,10},{10,12},{12,14},{9,11},... | collective-permute-start | bytes 491528 | tf_op jit(solution)/shard_map/ppermute | solution.py:550
  139.9 4.0 %collective-permute-start.21 = (f32[32,128]{1,0:T(8,128)S(1)}, f32[32,128]{1,0:T(8,128)S(1)}, u32[]{:S(2)}, u32[]{:S(2)}) collective-permute-start(f32[32,128]{1,0:T(8,128)S(1)} %get-tuple-element.57), channel_id=1, source_target_pairs={{0,4},{2,6},{1,5},{3,7},{8,12},{10,14},{9,13},{11,15},{16,20},{18,... | collective-permute-start | bytes 49160 | tf_op jit(solution)/shard_map/ppermute | solution.py:550
  145.4 5.1 %collective-permute-done.22.refs_7_ = f32[32,128]{1,0:T(8,128)S(1)} collective-permute-done((f32[32,128]{1,0:T(8,128)S(1)}, f32[32,128]{1,0:T(8,128)S(1)}, u32[]{:S(2)}, u32[]{:S(2)}) %collective-permute-start.22) | collective-permute-done | bytes 16416 | tf_op jit(solution)/shard_map/ppermute | solution.py:550
  150.5 9.2 %step.7 = f32[8,128,128]{2,1,0:T(8,128)S(1)} custom-call(s32[1]{0:T(128)} %bitcast.me_ref.refs_0_, f32[8,128,128]{2,1,0:T(8,128)S(1)} %get-tuple-element.53.refs_1_, f32[8,128,128]{2,1,0:T(8,128)S(1)} %get-tuple-element.47.refs_1_.refs_2_, f32[96,128]{1,0:T(8,128)S(1)} %get-tuple-element.54.refs_3_, f32[320,128]{1,0:T(8,128)S(1)} %collective-permute-done.19.refs_4_, ...), custom_call_target="tpu_custom_call" | custom-call | tf_op jit(solution)/shard_map/step/pallas_call | solution.py:568
  159.7 11.4 %all_to_all.10 = f32[8,128,128]{2,1,0:T(8,128)S(1)} all-to-all(f32[8,128,128]{2,1,0:T(8,128)S(1)} %step.7), channel_id=1, replica_groups=mesh['gx'=4,'gy'=4,'gz'=2] {'gx','gz'}, dimensions={0} | all-to-all | bytes 1048576 | tf_op jit(solution)/shard_map/all_to_all | solution.py:585
  (64 shorter events, 28.2 us)
Async XLA Ops:
  4.1 9.7 %collective-permute-start.2 = (f32[1,552,128]{2,1,0:T(8,128)S(1)}, f32[1,552,128]{2,1,0:T(8,128)S(1)}, u32[]{:S(2)}, u32[]{:S(2)}) collective-permute-start(f32[1,552,128]{2,1,0:T(8,128)S(1)} %fusion), channel_id=1, source_target_pairs={{0,16},{8,24},{16,0},{24,8},{1,17},{9,25},{17,1},{25,9},{2,18},{10... | collective-permute-start | bytes 847880 | tf_op jit(solution)/shard_map/ppermute | solution.py:407
  7.2 8.6 %collective-permute-start = (f32[1,544,128]{2,1,0:T(8,128)S(1)}, f32[1,544,128]{2,1,0:T(8,128)S(1)}, u32[]{:S(2)}, u32[]{:S(2)}) collective-permute-start(f32[1,544,128]{2,1,0:T(8,128)S(1)} %slice_bitcast_fusion), channel_id=1, source_target_pairs={{0,1},{1,0},{2,3},{3,2},{4,5},{5,4},{6,7},{7,6},{8,9},{9,8},{10,11... | collective-permute-start | bytes 835592 | tf_op jit(solution)/shard_map/ppermute | solution.py:407
  14.0 14.0 %collective-permute-start.3 = (f32[2,552,128]{2,1,0:T(8,128)S(1)}, f32[2,552,128]{2,1,0:T(8,128)S(1)}, u32[]{:S(2)}, u32[]{:S(2)}) collective-permute-start(f32[2,552,128]{2,1,0:T(8,128)S(1)} %pad_maximum_fusion), channel_id=1, source_target_pairs={{0,1},{1,0},{2,3},{3,2},{4,5},{5,4},{6,7},{7,6},{8,9},{9,8},{10,11... | collective-permute-start | bytes 1695752 | tf_op jit(solution)/shard_map/ppermute | solution.py:407
  15.8 13.3 %collective-permute-start.1 = (f32[2,544,128]{2,1,0:T(8,128)S(1)}, f32[2,544,128]{2,1,0:T(8,128)S(1)}, u32[]{:S(2)}, u32[]{:S(2)}) collective-permute-start(f32[2,544,128]{2,1,0:T(8,128)S(1)} %pad_maximum_fusion.1), channel_id=1, source_target_pairs={{0,16},{8,24},{16,0},{24,8},{1,17},{9,25},{17,1},{25,9},{2,18},{10... | collective-permute-start | bytes 1671176 | tf_op jit(solution)/shard_map/ppermute | solution.py:407
  29.3 4.6 %collective-permute-start.4 = (f32[4,1096,128]{2,1,0:T(8,128)S(1)}, f32[4,1096,128]{2,1,0:T(8,128)}, u32[]{:S(2)}, u32[]{:S(2)}) collective-permute-start(f32[4,1096,128]{2,1,0:T(8,128)S(1)} %maximum_maximum_fusion.near_ref), channel_id=1, source_target_pairs={{0,8},{8,0},{16,24},{24,16},{1,9},{9,1},{17,25},{25,17},{2,10},{10... | collective-permute-start | bytes 6733832 | tf_op jit(solution)/shard_map/ppermute | solution.py:407
  29.4 12.3 %all-to-all-start = ((f32[8,128,128]{2,1,0:T(8,128)}), f32[8,128,128]{2,1,0:T(8,128)S(1)}, u32[]{:S(2)}, u32[]{:S(2)}) async-start(f32[8,128,128]{2,1,0:T(8,128)} %bitcast.30), calls=%async_computation | async-start | bytes 1048576 | tf_op jit(solution)/shard_map/all_to_all | solution.py:491
  35.3 21.8 %collective-permute-start.9 = (f32[1,8,2,128]{3,2,1,0:T(2,128)S(1)}, f32[1,8,2,128]{3,2,1,0:T(2,128)S(1)}, u32[]{:S(2)}, u32[]{:S(2)}) collective-permute-start(f32[1,8,2,128]{3,2,1,0:T(2,128)S(1)} %fusion.3), channel_id=1, source_target_pairs={{0,2},{2,0},{4,6},{6,4},{1,3},{3,1},{5,7},{7,5},{8,10},{10,8},{12,... | collective-permute-start | bytes 24584 | tf_op jit(solution)/shard_map/ppermute | solution.py:407
  52.3 17.0 %collective-permute-start.5 = (f32[320,128]{1,0:T(8,128)S(1)}, f32[320,128]{1,0:T(8,128)S(1)}, u32[]{:S(2)}, u32[]{:S(2)}) collective-permute-start(f32[320,128]{1,0:T(8,128)S(1)} %get-tuple-element.33), channel_id=1, source_target_pairs={{0,2},{2,4},{4,6},{1,3},{3,5},{5,7},{8,10},{10,12},{12,14},{9,11},... | collective-permute-start | bytes 491528 | tf_op jit(solution)/shard_map/ppermute | solution.py:550
  55.8 13.5 %collective-permute-start.6 = (f32[320,128]{1,0:T(8,128)S(1)}, f32[320,128]{1,0:T(8,128)S(1)}, u32[]{:S(2)}, u32[]{:S(2)}) collective-permute-start(f32[320,128]{1,0:T(8,128)S(1)} %get-tuple-element.34), channel_id=1, source_target_pairs={{2,0},{4,2},{6,4},{3,1},{5,3},{7,5},{10,8},{12,10},{14,12},{11,9},... | collective-permute-start | bytes 491528 | tf_op jit(solution)/shard_map/ppermute | solution.py:550
  57.1 8.0 %collective-permute-start.10 = (f32[2,8,2,128]{3,2,1,0:T(2,128)S(1)}, f32[2,8,2,128]{3,2,1,0:T(2,128)S(1)}, u32[]{:S(2)}, u32[]{:S(2)}) collective-permute-start(f32[2,8,2,128]{3,2,1,0:T(2,128)S(1)} %pad_maximum_fusion.5), channel_id=1, source_target_pairs={{0,4},{2,6},{4,0},{6,2},{1,5},{3,7},{5,1},{7,3},{8,12},{10,14},{12... | collective-permute-start | bytes 49160 | tf_op jit(solution)/shard_map/ppermute | solution.py:407
  60.8 8.4 %collective-permute-start.7 = (f32[32,128]{1,0:T(8,128)S(1)}, f32[32,128]{1,0:T(8,128)S(1)}, u32[]{:S(2)}, u32[]{:S(2)}) collective-permute-start(f32[32,128]{1,0:T(8,128)S(1)} %get-tuple-element.35), channel_id=1, source_target_pairs={{0,4},{2,6},{1,5},{3,7},{8,12},{10,14},{9,13},{11,15},{16,20},{18,... | collective-permute-start | bytes 49160 | tf_op jit(solution)/shard_map/ppermute | solution.py:550
  62.8 6.5 %collective-permute-start.8 = (f32[32,128]{1,0:T(8,128)S(1)}, f32[32,128]{1,0:T(8,128)S(1)}, u32[]{:S(2)}, u32[]{:S(2)}) collective-permute-start(f32[32,128]{1,0:T(8,128)S(1)} %get-tuple-element.36), channel_id=1, source_target_pairs={{4,0},{6,2},{5,1},{7,3},{12,8},{14,10},{13,9},{15,11},{20,16},{22,... | collective-permute-start | bytes 49160 | tf_op jit(solution)/shard_map/ppermute | solution.py:550
  80.9 16.8 %collective-permute-start.11 = (f32[320,128]{1,0:T(8,128)S(1)}, f32[320,128]{1,0:T(8,128)S(1)}, u32[]{:S(2)}, u32[]{:S(2)}) collective-permute-start(f32[320,128]{1,0:T(8,128)S(1)} %get-tuple-element.43), channel_id=1, source_target_pairs={{0,2},{2,4},{4,6},{1,3},{3,5},{5,7},{8,10},{10,12},{12,14},{9,11},... | collective-permute-start | bytes 491528 | tf_op jit(solution)/shard_map/ppermute | solution.py:550
  84.7 12.9 %collective-permute-start.12 = (f32[320,128]{1,0:T(8,128)S(1)}, f32[320,128]{1,0:T(8,128)S(1)}, u32[]{:S(2)}, u32[]{:S(2)}) collective-permute-start(f32[320,128]{1,0:T(8,128)S(1)} %get-tuple-element.44), channel_id=1, source_target_pairs={{2,0},{4,2},{6,4},{3,1},{5,3},{7,5},{10,8},{12,10},{14,12},{11,9},... | collective-permute-start | bytes 491528 | tf_op jit(solution)/shard_map/ppermute | solution.py:550
  86.0 6.5 %collective-permute-start.13 = (f32[32,128]{1,0:T(8,128)S(1)}, f32[32,128]{1,0:T(8,128)S(1)}, u32[]{:S(2)}, u32[]{:S(2)}) collective-permute-start(f32[32,128]{1,0:T(8,128)S(1)} %get-tuple-element.45), channel_id=1, source_target_pairs={{0,4},{2,6},{1,5},{3,7},{8,12},{10,14},{9,13},{11,15},{16,20},{18,... | collective-permute-start | bytes 49160 | tf_op jit(solution)/shard_map/ppermute | solution.py:550
  91.1 6.5 %collective-permute-start.14 = (f32[32,128]{1,0:T(8,128)S(1)}, f32[32,128]{1,0:T(8,128)S(1)}, u32[]{:S(2)}, u32[]{:S(2)}) collective-permute-start(f32[32,128]{1,0:T(8,128)S(1)} %get-tuple-element.46), channel_id=1, source_target_pairs={{4,0},{6,2},{5,1},{7,3},{12,8},{14,10},{13,9},{15,11},{20,16},{22,... | collective-permute-start | bytes 49160 | tf_op jit(solution)/shard_map/ppermute | solution.py:550
  109.2 15.6 %collective-permute-start.15 = (f32[320,128]{1,0:T(8,128)S(1)}, f32[320,128]{1,0:T(8,128)S(1)}, u32[]{:S(2)}, u32[]{:S(2)}) collective-permute-start(f32[320,128]{1,0:T(8,128)S(1)} %get-tuple-element.49), channel_id=1, source_target_pairs={{0,2},{2,4},{4,6},{1,3},{3,5},{5,7},{8,10},{10,12},{12,14},{9,11},... | collective-permute-start | bytes 491528 | tf_op jit(solution)/shard_map/ppermute | solution.py:550
  113.0 11.8 %collective-permute-start.16 = (f32[320,128]{1,0:T(8,128)S(1)}, f32[320,128]{1,0:T(8,128)S(1)}, u32[]{:S(2)}, u32[]{:S(2)}) collective-permute-start(f32[320,128]{1,0:T(8,128)S(1)} %get-tuple-element.50), channel_id=1, source_target_pairs={{2,0},{4,2},{6,4},{3,1},{5,3},{7,5},{10,8},{12,10},{14,12},{11,9},... | collective-permute-start | bytes 491528 | tf_op jit(solution)/shard_map/ppermute | solution.py:550
  114.3 5.4 %collective-permute-start.17 = (f32[32,128]{1,0:T(8,128)S(1)}, f32[32,128]{1,0:T(8,128)S(1)}, u32[]{:S(2)}, u32[]{:S(2)}) collective-permute-start(f32[32,128]{1,0:T(8,128)S(1)} %get-tuple-element.51), channel_id=1, source_target_pairs={{0,4},{2,6},{1,5},{3,7},{8,12},{10,14},{9,13},{11,15},{16,20},{18,... | collective-permute-start | bytes 49160 | tf_op jit(solution)/shard_map/ppermute | solution.py:550
  118.3 6.5 %collective-permute-start.18 = (f32[32,128]{1,0:T(8,128)S(1)}, f32[32,128]{1,0:T(8,128)S(1)}, u32[]{:S(2)}, u32[]{:S(2)}) collective-permute-start(f32[32,128]{1,0:T(8,128)S(1)} %get-tuple-element.52), channel_id=1, source_target_pairs={{4,0},{6,2},{5,1},{7,3},{12,8},{14,10},{13,9},{15,11},{20,16},{22,... | collective-permute-start | bytes 49160 | tf_op jit(solution)/shard_map/ppermute | solution.py:550
  136.4 14.0 %collective-permute-start.19 = (f32[320,128]{1,0:T(8,128)S(1)}, f32[320,128]{1,0:T(8,128)S(1)}, u32[]{:S(2)}, u32[]{:S(2)}) collective-permute-start(f32[320,128]{1,0:T(8,128)S(1)} %get-tuple-element.55), channel_id=1, source_target_pairs={{0,2},{2,4},{4,6},{1,3},{3,5},{5,7},{8,10},{10,12},{12,14},{9,11},... | collective-permute-start | bytes 491528 | tf_op jit(solution)/shard_map/ppermute | solution.py:550
  138.6 11.8 %collective-permute-start.20 = (f32[320,128]{1,0:T(8,128)S(1)}, f32[320,128]{1,0:T(8,128)S(1)}, u32[]{:S(2)}, u32[]{:S(2)}) collective-permute-start(f32[320,128]{1,0:T(8,128)S(1)} %get-tuple-element.56), channel_id=1, source_target_pairs={{2,0},{4,2},{6,4},{3,1},{5,3},{7,5},{10,8},{12,10},{14,12},{11,9},... | collective-permute-start | bytes 491528 | tf_op jit(solution)/shard_map/ppermute | solution.py:550
  139.9 5.4 %collective-permute-start.21 = (f32[32,128]{1,0:T(8,128)S(1)}, f32[32,128]{1,0:T(8,128)S(1)}, u32[]{:S(2)}, u32[]{:S(2)}) collective-permute-start(f32[32,128]{1,0:T(8,128)S(1)} %get-tuple-element.57), channel_id=1, source_target_pairs={{0,4},{2,6},{1,5},{3,7},{8,12},{10,14},{9,13},{11,15},{16,20},{18,... | collective-permute-start | bytes 49160 | tf_op jit(solution)/shard_map/ppermute | solution.py:550
  143.9 6.5 %collective-permute-start.22 = (f32[32,128]{1,0:T(8,128)S(1)}, f32[32,128]{1,0:T(8,128)S(1)}, u32[]{:S(2)}, u32[]{:S(2)}) collective-permute-start(f32[32,128]{1,0:T(8,128)S(1)} %get-tuple-element.58), channel_id=1, source_target_pairs={{4,0},{6,2},{5,1},{7,3},{12,8},{14,10},{13,9},{15,11},{20,16},{22,... | collective-permute-start | bytes 49160 | tf_op jit(solution)/shard_map/ppermute | solution.py:550
  (3 other events, 6.2 us)

commit v2 on v1

--- a/solution.py
+++ b/solution.py
@@ -182,122 +182,139 @@
     return (four[:rows, :cx] + four[rows:, cx:]) + (four[:rows, cx:] + four[rows:, :cx])
 
 
-def emit_halo(plan, y_new, g, up_ref, down_ref):
+def halo_rows(plan, y_block, low):
     on, cz, cy = plan.on, plan.cz, plan.cy
-    tops, bottoms = [], []
-    for o in range(on):
-        for z in range(cz):
-            start = (o * cz + z) * cy
-            bottoms.append(y_new[start : start + REACH])
-            tops.append(y_new[start + cy - REACH : start + cy])
-    rows = on * cz * REACH
-    where = pl.ds(pl.multiple_of(g * rows, SUB), rows)
-    up_ref[where, :] = jnp.concatenate(tops, axis=0)
-    down_ref[where, :] = jnp.concatenate(bottoms, axis=0)
-
-
-def emit_sums(plan, total, own_ref, up_ref, down_ref, up2_ref, down2_ref):
+    pieces = []
+    for line in range(on * cz):
+        start = line * cy if low else line * cy + cy - REACH
+        pieces.append(y_block[start : start + REACH])
+    return jnp.concatenate(pieces, axis=0)
+
+
+def emit_halo(plan, y_block, slot, odd, even_ref, odd_ref):
+    up = halo_rows(plan, y_block, False)
+    down = halo_rows(plan, y_block, True)
+    rows = up.shape[0]
+    where = pl.ds(pl.multiple_of(slot * rows, SUB), rows)
+    even_ref[where, :] = jnp.where(odd, down, up)
+    odd_ref[where, :] = jnp.where(odd, up, down)
+
+
+def emit_sums(plan, total, odd, upper, own_ref, even_ref, odd_ref, far_ref):
     f, third, halo = plan.features, plan.third, plan.halo_rows
+    blocks = [total[:, j * LANE : (j + 1) * LANE] for j in range(3 * third)]
     for j in range(3 * third):
-        block = total[:, j * LANE : (j + 1) * LANE]
-        own_ref[j * f : (j + 1) * f, :] = block
-        if j >= third:
-            row = halo + (j - third) * f
-            up_ref[row : row + f, :] = block
-        if j < 2 * third:
-            row = halo + j * f
-            down_ref[row : row + f, :] = block
-        if j >= 2 * third:
-            row = (j - 2 * third) * f
-            up2_ref[row : row + f, :] = block
-        if j < third:
-            down2_ref[j * f : (j + 1) * f, :] = block
-
-
-def load_coefs(plan, own_ref, low_ref, high_ref, low2_ref, high2_ref, scale_ref):
+        own_ref[j * f : (j + 1) * f, :] = blocks[j]
+    for j in range(2 * third):
+        row = halo + j * f
+        up, down = blocks[j + third], blocks[j]
+        even_ref[row : row + f, :] = jnp.where(odd, down, up)
+        odd_ref[row : row + f, :] = jnp.where(odd, up, down)
+    for j in range(third):
+        far_ref[j * f : (j + 1) * f, :] = jnp.where(upper, blocks[j], blocks[j + 2 * third])
+
+
+def load_coefs(plan, odd, upper, own_ref, even_ref, odd_ref, far_ref, scale_ref):
     f, third, halo = plan.features, plan.third, plan.halo_rows
     blocks = []
     for j in range(3 * third):
         block = own_ref[j * f : (j + 1) * f, :]
         if j < 2 * third:
             row = halo + j * f
-            block = block + low_ref[row : row + f, :]
+            at = slice(row, row + f)
+            block = block + jnp.where(odd, even_ref[at, :], odd_ref[at, :])
         if j >= third:
             row = halo + (j - third) * f
-            block = block + high_ref[row : row + f, :]
+            at = slice(row, row + f)
+            block = block + jnp.where(odd, odd_ref[at, :], even_ref[at, :])
         if j < third:
-            block = block + low2_ref[j * f : (j + 1) * f, :]
+            block = block + jnp.where(upper, far_ref[j * f : (j + 1) * f, :], 0.0)
         if j >= 2 * third:
             row = (j - 2 * third) * f
-            block = block + high2_ref[row : row + f, :]
+            block = block + jnp.where(upper, 0.0, far_ref[row : row + f, :])
         blocks.append(block)
     return jnp.concatenate(blocks, axis=1) * scale_ref[...]
 
 
-def fill_padded(plan, y_ref, low_ref, high_ref, pad_ref):
-    on, cz, cy, gx, gz = plan.on, plan.cz, plan.cy, plan.gx, plan.gz
+def local_kernel(plan, first, info_ref, y_ref, *refs):
+    if first:
+        potential_ref, out_ref, pad_ref = refs
+    else:
+        previous_ref, potential_ref, out_ref, pad_ref = refs
+    on, cz, cy, cx, gx, gz = plan.on, plan.cz, plan.cy, plan.cx, plan.gx, plan.gz
+    step = pl.program_id(0)
+    me = info_ref[0]
+    own = slice(SUB, SUB + cy)
     depth = cz * gz
-    zero_plane = jnp.zeros((1,) + pad_ref.shape[1:], jnp.float32)
-    pad_ref[0:1] = zero_plane
-    pad_ref[gx + 1 : gx + 2] = zero_plane
-    zero_ends = jnp.zeros((gx, on, REACH) + pad_ref.shape[3:], jnp.float32)
-    pad_ref[1 : gx + 1, :, 0:REACH] = zero_ends
-    pad_ref[1 : gx + 1, :, REACH + depth :] = zero_ends
-    rows = on * cz * REACH
-    for ix in range(gx):
-        for iz in range(gz):
-            g = ix * gz + iz
-            for o in range(on):
-                at = REACH + iz * cz
-                lead = (o * cz) * cy
-                pad_ref[ix + 1, o, at : at + cz, SUB : SUB + cy, :] = y_ref[
-                    g, lead : lead + cz * cy, :
-                ].reshape(cz, cy, plan.cx)
-                for z in range(cz):
-                    row = g * rows + (o * cz + z) * REACH
-                    pad_ref[ix + 1, o, at + z, SUB - REACH : SUB, :] = low_ref[row : row + REACH, :]
-                    pad_ref[ix + 1, o, at + z, SUB + cy : SUB + cy + REACH, :] = high_ref[
-                        row : row + REACH, :
-                    ]
-
-
-def local_block(plan, g, pad_ref, potential, previous, first):
-    on, cz, cy, cx, gz = plan.on, plan.cz, plan.cy, plan.cx, plan.gz
-    ix = g // gz
-    iz = g - ix * gz
-    at = REACH + iz * cz
-    own = slice(SUB, SUB + cy)
-    factor = (1.0 if first else 2.0) / HALF_WIDTH
-    rows = on * cz * cy
-    shape = (rows, cx)
+
+    @pl.when(step == 0)
+    def _():
+        zeros = jnp.zeros((1, on, depth, cy, cx), jnp.float32)
+        inside = slice(REACH, REACH + depth)
+        pad_ref[0:1, :, inside, own, :] = zeros
+        pad_ref[gx + 1 : gx + 2, :, inside, own, :] = zeros
+        zeros = jnp.zeros((gx, on, REACH, cy, cx), jnp.float32)
+        pad_ref[1 : gx + 1, :, 0:REACH, own, :] = zeros
+        pad_ref[1 : gx + 1, :, REACH + depth :, own, :] = zeros
+        zeros = jnp.zeros((gx, on, depth, SUB, cx), jnp.float32)
+        pad_ref[1 : gx + 1, :, inside, 0:SUB, :] = zeros
+        pad_ref[1 : gx + 1, :, inside, SUB + cy :, :] = zeros
+        for slot in range(plan.blocks):
+            g = plan.block_of(slot, me)
+            ix = g // gz
+            at = REACH + (g - ix * gz) * cz
+            pad_ref[ix + 1, :, pl.ds(at, cz), own, :] = y_ref[slot].reshape(on, cz, cy, cx)
+
+    factor = plan.factor(first)
+    shape = (on * cz * cy, cx)
     lane = lax.broadcasted_iota(jnp.int32, shape, 1)
-    center = pad_ref[ix + 1, :, pl.ds(at, cz), own, :].reshape(shape)
-    left = pad_ref[ix, :, pl.ds(at, cz), own, :].reshape(shape)
-    right = pad_ref[ix + 2, :, pl.ds(at, cz), own, :].reshape(shape)
-    diagonal = potential - (CENTER + 1.5 * stencil_weights[0])
-    diagonal = jnp.concatenate([factor * diagonal] * on, axis=0)
-    total = diagonal * center
+    for part in range(plan.per):
+        g = plan.block_of(step * plan.per + part, me)
+        ix = g // gz
+        at = REACH + (g - ix * gz) * cz
+        planes = pl.ds(at, cz)
+        center = pad_ref[ix + 1, :, planes, own, :].reshape(shape)
+        left = pad_ref[ix, :, planes, own, :].reshape(shape)
+        right = pad_ref[ix + 2, :, planes, own, :].reshape(shape)
+        diagonal = factor * (potential_ref[part] - (CENTER + 1.5 * stencil_weights[0]))
+        total = jnp.concatenate([diagonal] * on, axis=0) * center
+        for k in range(1, REACH + 1):
+            near = pltpu.roll(jnp.where(lane >= cx - k, left, center), k, 1)
+            near = near + pltpu.roll(jnp.where(lane < k, right, center), cx - k, 1)
+            for sign in (k, -k):
+                near = near + pad_ref[ix + 1, :, pl.ds(at + sign, cz), own, :].reshape(shape)
+                moved = slice(SUB + sign, SUB + sign + cy)
+                near = near + pad_ref[ix + 1, :, planes, moved, :].reshape(shape)
+            total = total + plan.weight(first, k) * near
+        if not first:
+            total = total - previous_ref[part]
+        out_ref[part] = total
+
+
+def halo_part(plan, first, low_rows, high_rows, low_ref, high_ref):
+    on, cz, cy, cx = plan.on, plan.cz, plan.cy, plan.cx
+    lines = on * cz
+    low_ref[:, SUB - REACH : SUB, :] = low_rows.reshape(lines, REACH, cx)
+    high_ref[:, SUB : SUB + REACH, :] = high_rows.reshape(lines, REACH, cx)
+    low = high = None
     for k in range(1, REACH + 1):
-        near = pltpu.roll(jnp.where(lane >= cx - k, left, center), k, 1)
-        near = near + pltpu.roll(jnp.where(lane < k, right, center), cx - k, 1)
-        for sign in (k, -k):
-            near = near + pad_ref[ix + 1, :, pl.ds(at + sign, cz), own, :].reshape(shape)
-            moved = slice(SUB + sign, SUB + sign + cy)
-            near = near + pad_ref[ix + 1, :, pl.ds(at, cz), moved, :].reshape(shape)
-        total = total + (-0.5 * factor * stencil_weights[k]) * near
-    if not first:
-        total = total - previous
-    return total, factor
+        weight = plan.weight(first, k)
+        below = weight * low_ref[:, SUB - k : 2 * SUB - k, :]
+        above = weight * high_ref[:, k : SUB + k, :]
+        low = below if low is None else low + below
+        high = above if high is None else high + above
+    middle = [jnp.zeros((lines, cy - 2 * SUB, cx), jnp.float32)] if cy > 2 * SUB else []
+    return jnp.concatenate([low] + middle + [high], axis=1).reshape(lines * cy, cx)
 
 
 def opening_kernel(
-    plan, me_ref, near_ref, far_ref, y_ref,
-    stack_ref, hot_ref, columns_ref, potential_ref, own_ref, up_ref, down_ref, up2_ref, down2_ref,
-    total_ref,
+    plan, info_ref, near_ref, far_ref, y_ref,
+    stack_ref, hot_ref, columns_ref, potential_ref, y_out_ref,
+    own_ref, even_ref, odd_ref, far_sums_ref, total_ref,
 ):
     step = pl.program_id(0)
     half = plan.blocks // 2
-    g = plan.block_of(step, me_ref[0])
+    odd, upper = info_ref[1] == 1, info_ref[2] == 1
 
     def unpack(source):
         tiles = plan.projs * plan.slots
@@ -329,8 +346,9 @@
         unpack(far_ref)
 
     y_block = y_ref[0]
+    y_out_ref[0] = y_block
     sums = forward_block(plan, y_block, stack_ref[0], hot_ref[0], columns_ref[0, 0:1, :])
-    emit_halo(plan, y_block, g, up_ref, down_ref)
+    emit_halo(plan, y_block, step, odd, even_ref, odd_ref)
 
     @pl.when(step == 0)
     def _():
@@ -342,44 +360,53 @@
 
     @pl.when(step == plan.blocks - 1)
     def _():
-        emit_sums(plan, total_ref[...], own_ref, up_ref, down_ref, up2_ref, down2_ref)
-
-
-def middle_kernel(plan, first, last, *refs):
-    me_ref, y_ref = refs[:2]
-    refs = refs[2:]
-    if first:
-        previous = None
-    else:
-        previous, refs = refs[0], refs[1:]
-    (own_in, low_ref, high_ref, low2_ref, high2_ref, scale_ref) = refs[:6]
-    stack_ref, hot_ref, columns_ref, potential_ref, out_ref = refs[6:11]
-    refs = refs[11:]
+        emit_sums(plan, total_ref[...], odd, upper, own_ref, even_ref, odd_ref, far_sums_ref)
+
+
+def step_kernel(plan, first, last, info_ref, local_ref, *refs):
+    received, refs = refs[:5], refs[5:]
+    own_in, even_in, odd_in, far_in, scale_ref = received
+    stack_ref, hot_ref, columns_ref, out_ref = refs[:4]
+    refs = refs[4:]
     if not last:
-        own_ref, up_ref, down_ref, up2_ref, down2_ref = refs[:5]
-        refs = refs[5:]
-    pad_ref, coef_ref = refs[:2]
+        own_ref, even_ref, odd_ref, far_ref = refs[:4]
+        refs = refs[4:]
+    coef_ref, low_ref, high_ref = refs[:3]
     step = pl.program_id(0)
-    g = plan.block_of(step, me_ref[0])
+    odd, upper = info_ref[1] == 1, info_ref[2] == 1
+    factor = plan.factor(first)
 
     @pl.when(step == 0)
     def _():
-        coefs = load_coefs(plan, own_in, low_ref, high_ref, low2_ref, high2_ref, scale_ref)
+        coefs = factor * load_coefs(
+            plan, odd, upper, own_in, even_in, odd_in, far_in, scale_ref
+        )
         hi, lo = hi_lo(coefs)
         coef_ref[...] = jnp.concatenate([hi, lo], axis=0)
-        fill_padded(plan, y_ref, low_ref, high_ref, pad_ref)
-
-    columns = columns_ref[0, 0:1, :]
-    projected = backward_block(plan, coef_ref[...], stack_ref[0], hot_ref[0], columns)
-    before = None if first else previous[0]
-    local, factor = local_block(plan, g, pad_ref, potential_ref[0], before, first)
-    y_new = local + factor * projected
-    out_ref[0] = y_new
+        low_ref[...] = jnp.zeros_like(low_ref)
+        high_ref[...] = jnp.zeros_like(high_ref)
+
+    rows = plan.on * plan.cz * REACH
+    sums = None
+    for part in range(plan.per):
+        slot = step * plan.per + part
+        columns = columns_ref[part, 0:1, :]
+        where = pl.ds(pl.multiple_of(slot * rows, SUB), rows)
+        from_even, from_odd = even_in[where, :], odd_in[where, :]
+        low_rows = jnp.where(odd, from_even, from_odd)
+        high_rows = jnp.where(odd, from_odd, from_even)
+        halo = halo_part(plan, first, low_rows, high_rows, low_ref.at[part], high_ref.at[part])
+        projected = backward_block(plan, coef_ref[...], stack_ref[part], hot_ref[part], columns)
+        y_new = (local_ref[part] + halo) + projected
+        out_ref[part] = y_new
+        if last:
+            continue
+        more = forward_block(plan, y_new, stack_ref[part], hot_ref[part], columns)
+        sums = more if sums is None else sums + more
+        emit_halo(plan, y_new, slot, odd, even_ref, odd_ref)
     if last:
         return
-    sums = forward_block(plan, y_new, stack_ref[0], hot_ref[0], columns)
-    emit_halo(plan, y_new, g, up_ref, down_ref)
-    total_ref = refs[2]
+    total_ref = refs[3]
 
     @pl.when(step == 0)
     def _():
@@ -389,9 +416,15 @@
     def _():
         total_ref[...] += sums
 
-    @pl.when(step == plan.blocks - 1)
-    def _():
-        emit_sums(plan, total_ref[...], own_ref, up_ref, down_ref, up2_ref, down2_ref)
+    @pl.when(step == plan.blocks // plan.per - 1)
+    def _():
+        emit_sums(plan, total_ref[...], odd, upper, own_ref, even_ref, odd_ref, far_ref)
+
+
+def place_kernel(plan, info_ref, *refs):
+    out_ref = refs[-1]
+    for slot in range(plan.blocks):
+        out_ref[plan.block_of(slot, info_ref[0])] = refs[slot][0]
 
 
 class Plan:
@@ -434,6 +467,9 @@
         return moved ^ me
 
     plan.block_of = block_of
+    plan.per = 2
+    plan.factor = lambda first: (1.0 if first else 2.0) / HALF_WIDTH
+    plan.weight = lambda first, k: -0.5 * plan.factor(first) * stencil_weights[k]
 
     live = jnp.arange(slots, dtype=jnp.int32) < tile_count[0]
     column = jnp.where(live, tile_column, -1)
@@ -493,30 +529,22 @@
     )
 
     f32 = jnp.float32
-    spec_me = me.reshape(1).astype(jnp.int32)
+    info = jnp.stack([me, iy & 1, (iy >> 1) & 1]).astype(jnp.int32)
     message_rows = plan.halo_rows + 2 * plan.third * plan.features
-    message2_rows = plan.third * plan.features
+    far_rows = plan.third * plan.features
     own_rows = 3 * plan.third * plan.features
     half = blocks // 2
+    per = plan.per
     whole = lambda *shape: pl.BlockSpec(shape, lambda i, m: (0,) * len(shape))
-    per_step = lambda *shape: pl.BlockSpec((1,) + shape, lambda i, m: (i, 0, 0))
-    per_block = lambda *shape: pl.BlockSpec((1,) + shape, lambda i, m: (block_of(i, m[0]), 0, 0))
+    each = lambda count, *shape: pl.BlockSpec((count,) + shape, lambda i, m: (i, 0, 0))
     tile_rows = projs * slots
     y_rows = on * points
+    y_shape = jax.ShapeDtypeStruct((blocks, y_rows, cx), f32)
     send_shapes = [
-        jax.ShapeDtypeStruct((own_rows, LANE), f32),
-        jax.ShapeDtypeStruct((message_rows, LANE), f32),
-        jax.ShapeDtypeStruct((message_rows, LANE), f32),
-        jax.ShapeDtypeStruct((message2_rows, LANE), f32),
-        jax.ShapeDtypeStruct((message2_rows, LANE), f32),
+        jax.ShapeDtypeStruct((count, LANE), f32)
+        for count in (own_rows, message_rows, message_rows, far_rows)
     ]
     send_specs = [whole(*shape.shape) for shape in send_shapes]
-    constant_specs = [
-        per_step(tile_rows, 2 * cx),
-        per_step(plan.keys, slots),
-        per_step(SUB, slots),
-        per_step(points, cx),
-    ]
     params = pltpu.CompilerParams(vmem_limit_bytes=48 * 1024 * 1024)
     sums_scratch = pltpu.VMEM((plan.features, plan.keys), f32)
 
@@ -527,6 +555,7 @@
             jax.ShapeDtypeStruct((blocks, plan.keys, slots), jnp.bfloat16),
             jax.ShapeDtypeStruct((blocks, SUB, slots), jnp.int32),
             jax.ShapeDtypeStruct((blocks, points, cx), f32),
+            y_shape,
         ]
         + send_shapes,
         grid_spec=pltpu.PrefetchScalarGridSpec(
@@ -535,54 +564,112 @@
             in_specs=[
                 pl.BlockSpec((1, rows, cx), lambda i, m: (jnp.minimum(i, half - 1), 0, 0)),
                 pl.BlockSpec((1, rows, cx), lambda i, m: (jnp.maximum(i - half, 0), 0, 0)),
-                per_block(y_rows, cx),
+                pl.BlockSpec((1, y_rows, cx), lambda i, m: (block_of(i, m[0]), 0, 0)),
             ],
-            out_specs=constant_specs + send_specs,
+            out_specs=[
+                each(1, tile_rows, 2 * cx),
+                each(1, plan.keys, slots),
+                each(1, SUB, slots),
+                each(1, points, cx),
+                each(1, y_rows, cx),
+            ]
+            + send_specs,
             scratch_shapes=[sums_scratch],
         ),
         compiler_params=params,
         name="opening",
-    )(spec_me, near, far, y0)
-    constants, sends = list(opened[:4]), list(opened[4:])
-
-    def shift(value, by):
-        pairs = [(i, i + by) for i in range(gy) if 0 <= i + by < gy]
-        return lax.ppermute(value, "gy", pairs)
+    )(info, near, far, y0)
+    stack, hot, columns, plane_potential, current = opened[:5]
+    sends = list(opened[5:])
+
+    def pairwise(value, pairs):
+        pairs = [(a, b) for a, b in pairs if b < gy]
+        if not pairs:
+            return jnp.zeros_like(value)
+        return lax.ppermute(value, "gy", pairs + [(b, a) for a, b in pairs])
 
     def swap(sends):
-        own, up, down, up2, down2 = sends
-        return own, shift(up, 1), shift(down, -1), shift(up2, 2), shift(down2, -2)
-
-    current, previous = y0, None
+        own, even, odd, distant = sends
+        return (
+            own,
+            pairwise(even, [(i, i + 1) for i in range(0, gy, 2)]),
+            pairwise(odd, [(i, i + 1) for i in range(1, gy, 2)]),
+            pairwise(distant, [(i, i + 2) for i in range(gy) if i & 2 == 0]),
+        )
+
+    previous = None
     for repeat in range(DEGREE):
         first, last = repeat == 0, repeat == DEGREE - 1
         received = swap(sends)
-        arrays = [spec_me, current] + ([] if first else [previous])
-        arrays += [*received, scale] + constants
-        in_specs = [whole(blocks, y_rows, cx)] + ([] if first else [per_block(y_rows, cx)])
-        in_specs += send_specs + [whole(plan.features, plan.keys)] + constant_specs
+        local = pl.pallas_call(
+            functools.partial(local_kernel, plan, first),
+            out_shape=y_shape,
+            grid_spec=pltpu.PrefetchScalarGridSpec(
+                num_scalar_prefetch=1,
+                grid=(blocks // per,),
+                in_specs=[whole(blocks, y_rows, cx)]
+                + ([] if first else [each(per, y_rows, cx)])
+                + [each(per, points, cx)],
+                out_specs=each(per, y_rows, cx),
+                scratch_shapes=[
+                    pltpu.VMEM((gx + 2, on, cz * gz + 2 * REACH, 2 * SUB + cy, cx), f32)
+                ],
+            ),
+            compiler_params=params,
+            cost_estimate=pl.CostEstimate(
+                flops=60 * blocks * y_rows * cx,
+                bytes_accessed=16 * blocks * y_rows * cx,
+                transcendentals=0,
+            ),
+            name="local",
+        )(info, current, *([] if first else [previous]), plane_potential)
+        lines = on * cz
         scratch = [
-            pltpu.VMEM((gx + 2, on, cz * gz + 2 * REACH, 2 * SUB + cy, cx), f32),
             pltpu.VMEM((2 * plan.features, plan.keys), jnp.bfloat16),
+            pltpu.VMEM((per, lines, 2 * SUB, cx), f32),
+            pltpu.VMEM((per, lines, 2 * SUB, cx), f32),
         ]
         result = pl.pallas_call(
-            functools.partial(middle_kernel, plan, first, last),
-            out_shape=[jax.ShapeDtypeStruct((blocks, y_rows, cx), f32)]
-            + ([] if last else send_shapes),
+            functools.partial(step_kernel, plan, first, last),
+            out_shape=[y_shape] + ([] if last else send_shapes),
             grid_spec=pltpu.PrefetchScalarGridSpec(
                 num_scalar_prefetch=1,
-                grid=(blocks,),
-                in_specs=in_specs,
-                out_specs=[per_block(y_rows, cx)] + ([] if last else send_specs),
+                grid=(blocks // per,),
+                in_specs=[each(per, y_rows, cx)]
+                + send_specs
+                + [
+                    whole(plan.features, plan.keys),
+                    each(per, tile_rows, 2 * cx),
+                    each(per, plan.keys, slots),
+                    each(per, SUB, slots),
+                ],
+                out_specs=[each(per, y_rows, cx)] + ([] if last else send_specs),
                 scratch_shapes=scratch + ([] if last else [sums_scratch]),
             ),
             compiler_params=params,
             name="step",
-        )(*arrays)
+        )(info, local, *received, scale, stack, hot, columns)
         previous, current = current, result[0]
         sends = result[1:]
 
-    turned = lax.all_to_all(current, ("gx", "gz"), 0, 0, tiled=True)
+    pieces = []
+    for slot in range(blocks):
+        block = current[slot : slot + 1]
+        if slot:
+            moved = block_of(slot, 0)
+            block = lax.ppermute(block, ("gx", "gz"), [(i, i ^ moved) for i in range(blocks)])
+        pieces.append(block)
+    turned = pl.pallas_call(
+        functools.partial(place_kernel, plan),
+        out_shape=y_shape,
+        grid_spec=pltpu.PrefetchScalarGridSpec(
+            num_scalar_prefetch=1,
+            grid=(1,),
+            in_specs=[whole(1, y_rows, cx)] * blocks,
+            out_specs=whole(blocks, y_rows, cx),
+        ),
+        name="place",
+    )(info, *pieces)
     return turned.reshape(norb, cz, cy, cx)
 
 
@@ -597,11 +684,11 @@
     owned = coupling.shape[0]
     gx, gy, gz = (lax.axis_size(name) for name in ("gx", "gy", "gz"))
     blocks = gx * gz
-    turned = all(power_of_two(size) for size in (gx, gy, gz)) and gx > 1 and gz > 1
+    turned = all(power_of_two(size) for size in (gx, gy, gz)) and gx > 1 and gz > 1 and gy <= 4
     turned = turned and norb % blocks == 0 and cx == LANE and slots % LANE == 0
     if turned:
         turned = (norb // blocks * projs) % SUB == 0 and (owned * projs) % LANE == 0
-        turned = turned and (blocks * owned) % LANE == 0 and cy % SUB == 0 and cy >= REACH
+        turned = turned and (blocks * owned) % LANE == 0 and cy % SUB == 0 and cy >= 2 * SUB
         turned = turned and cz % 2 == 0 and (3 * blocks * owned) % 256 == 0
     return turned_path(*arguments) if turned else general_path(*arguments)
 

time: 174 us -> 159 us (0.914)
  starting transfers between devices: 55.4 us -> 43 us
  blocking collectives: 11.4 us -> 0 us
  Pallas kernels: 54.6 us -> 64.8 us
  waiting for transfers between devices: 39 us -> 28.9 us
  local copies, waits for them, and re-layouts: 7.75 us -> 13.9 us
  other arithmetic: 2.71 us -> 5.92 us
    ppermute x16 -> x19, starting transfers between devices: 38.6 us -> 26 us  [the longest x12 19.2 us: pairwise(): return lax.ppermute(value, 'gy', pairs + [(b, a) for a, b in pairs])]
    all_to_all x1 -> x0, blocking collectives: 11.4 us -> none  [turned_path(): turned = lax.all_to_all(current, ('gx', 'gz'), 0, 0, tiled=True)]
    pallas_call x4 -> x9, Pallas kernels: 44 us -> 53.6 us  [the longest x4 41.6 us: turned_path(): pl.pallas_call(functools.partial(step_kernel, plan, first, last), out_sha...]
    ppermute x16 -> x19, waiting for transfers between devices: 15.8 us -> 6.59 us  [the longest x7 3.47 us: turned_path(): lax.ppermute(block, ('gx', 'gz'), [(i, i ^ moved) for i in range(blocks)])]
    unnamed x10 -> x41, local copies, waits for them, and re-layouts: 1.6 us -> 4.86 us
  transfers between devices with their start and end apart: 24 -> 27, of which waited for: 13 -> 11; matrix products, arithmetic and copies ran while one was open for 3% -> 7% of each run, Pallas kernels for 6% -> 13%
where the time goes in v2:
time: 159 us; the launch traced here: 158 us
  Pallas kernels  64.8 us (41%)
  starting transfers between devices  43 us (27%)
  waiting for transfers between devices  28.9 us (18%)
  local copies, waits for them, and re-layouts  13.9 us (9%)
  other arithmetic  5.92 us (4%)
    pallas_call x4, Pallas kernels, turned_path(): pl.pallas_call(functools.partial(step_kernel, plan, first, last), out_sha...  41.6 us
    ppermute x12, starting transfers between devices, pairwise(): return lax.ppermute(value, 'gy', pairs + [(b, a) for a, b in pairs])  19.2 us
    ppermute x7, waiting for transfers between devices, exchange(): return lax.ppermute(value, axis, [(i, i ^ bit) for i in range(count)])  18.8 us
    ppermute x7, starting transfers between devices, exchange(): return lax.ppermute(value, axis, [(i, i ^ bit) for i in range(count)])  13.5 us
    pallas_call x1, Pallas kernels, turned_path(): pl.pallas_call(functools.partial(opening_kernel, plan), out_shape=[jax.Sh...  11.2 us
    pallas_call x4, Pallas kernels, turned_path(): pl.pallas_call(functools.partial(local_kernel, plan, first), out_shape=y_...  9.48 us
    ppermute x7, starting transfers between devices, turned_path(): lax.ppermute(block, ('gx', 'gz'), [(i, i ^ moved) for i in range(blocks)])  6.77 us
    unnamed x41, local copies, waits for them, and re-layouts  4.86 us
  transfers between devices with their start and end apart: 27, of which 11 were waited for; matrix products, arithmetic and copies ran while one was open for 7% of the time, Pallas kernels for 13%

profile of v2, /device:TPU:0, one launch (start us, length us, event | category | flops | bytes accessed | tf_op | source)
XLA Modules:
  0.0 157.6 jit_solution(1446741705114372137)
XLA Ops:
  4.1 3.0 %collective-permute-start.2 = (f32[1,552,128]{2,1,0:T(8,128)S(1)}, f32[1,552,128]{2,1,0:T(8,128)S(1)}, u32[]{:S(2)}, u32[]{:S(2)}) collective-permute-start(f32[1,552,128]{2,1,0:T(8,128)S(1)} %fusion), channel_id=1, source_target_pairs={{0,16},{8,24},{16,0},{24,8},{1,17},{9,25},{17,1},{25,9},{2,18},{10... | collective-permute-start | bytes 847880 | tf_op jit(solution)/shard_map/ppermute | solution.py:440
  8.8 5.1 %collective-permute-done.2 = f32[1,552,128]{2,1,0:T(8,128)S(1)} collective-permute-done((f32[1,552,128]{2,1,0:T(8,128)S(1)}, f32[1,552,128]{2,1,0:T(8,128)S(1)}, u32[]{:S(2)}, u32[]{:S(2)}) %collective-permute-start.2) | collective-permute-done | bytes 282656 | tf_op jit(solution)/shard_map/ppermute | solution.py:440
  17.4 10.6 %collective-permute-done.3 = f32[2,552,128]{2,1,0:T(8,128)S(1)} collective-permute-done((f32[2,552,128]{2,1,0:T(8,128)S(1)}, f32[2,552,128]{2,1,0:T(8,128)S(1)}, u32[]{:S(2)}, u32[]{:S(2)}) %collective-permute-start.3) | collective-permute-done | bytes 565280 | tf_op jit(solution)/shard_map/ppermute | solution.py:440
  29.4 3.5 %all-to-all-start = ((f32[8,128,128]{2,1,0:T(8,128)}), f32[8,128,128]{2,1,0:T(8,128)S(1)}, u32[]{:S(2)}, u32[]{:S(2)}) async-start(f32[8,128,128]{2,1,0:T(8,128)} %bitcast.31), calls=%async_computation | async-start | bytes 1048576 | tf_op jit(solution)/shard_map/all_to_all | solution.py:527
  38.1 3.5 %all-to-all-done.y_ref = f32[8,128,128]{2,1,0:T(8,128)S(1)} async-done(((f32[8,128,128]{2,1,0:T(8,128)}), f32[8,128,128]{2,1,0:T(8,128)S(1)}, u32[]{:S(2)}, u32[]{:S(2)}) %all-to-all-start) | async-done | bytes 524320 | tf_op jit(solution)/shard_map/all_to_all | solution.py:527
  42.3 11.2 %opening.1 = (bf16[8,1024,256]{2,1,0:T(8,128)(2,1)}, bf16[8,1536,256]{2,1,0:T(8,128)(2,1)}, s32[8,8,256]{2,1,0:T(8,128)S(1)}, f32[8,64,128]{2,1,0:T(8,128)S(1)},...) custom-call(s32[3]{0:T(128)S(1)} %copy-done.4, ...), custom_call_target="tpu_custom_call" | custom-call | tf_op jit(solution)/shard_map/opening/pallas_call | solution.py:551
  57.1 3.9 %collective-permute-start.9 = (f32[2,8,2,128]{3,2,1,0:T(2,128)S(1)}, f32[2,8,2,128]{3,2,1,0:T(2,128)S(1)}, u32[]{:S(2)}, u32[]{:S(2)}) collective-permute-start(f32[2,8,2,128]{3,2,1,0:T(2,128)S(1)} %pad_maximum_fusion.5), channel_id=1, source_target_pairs={{0,4},{2,6},{4,0},{6,2},{1,5},{3,7},{5,1},{7,3},{8,12},{10,14},{12... | collective-permute-start | bytes 49160 | tf_op jit(solution)/shard_map/ppermute | solution.py:440
  61.1 2.4 %local.4.local_ref = f32[8,128,128]{2,1,0:T(8,128)S(1)} custom-call(s32[3]{0:T(128)S(1)} %copy-done.4, f32[8,128,128]{2,1,0:T(8,128)S(1)} %get-tuple-element.29.y_ref.refs_0_, f32[8,64,128]{2,1,0:T(8,128)S(1)} %get-tuple-element.30.refs_0_.refs_1_), custom_call_target="tpu_custom_call" | custom-call | flops 7864320 | bytes 2097152 | tf_op jit(solution)/shard_map/local/pallas_call | solution.py:604
  63.5 1.9 %collective-permute-done.9 = f32[2,8,2,128]{3,2,1,0:T(2,128)S(1)} collective-permute-done((f32[2,8,2,128]{3,2,1,0:T(2,128)S(1)}, f32[2,8,2,128]{3,2,1,0:T(2,128)S(1)}, u32[]{:S(2)}, u32[]{:S(2)}) %collective-permute-start.9) | collective-permute-done | bytes 16416 | tf_op jit(solution)/shard_map/ppermute | solution.py:440
  67.3 3.7 %gather_fusion = f32[1536,4]{1,0:T(8,128)} fusion(f32[2048,4]{1,0:T(8,128)S(1)} %reshape.331, s32[2048]{0:T(1024)S(1)} %pad_clamp_fusion), kind=kCustom, calls=%fused_computation | custom fusion | bytes 55296 | tf_op jit(solution)/shard_map/gather | solution.py:524
  72.5 2.2 %copy-done = bf16[8,1024,256]{2,1,0:T(8,128)(2,1)S(1)} copy-done((bf16[8,1024,256]{2,1,0:T(8,128)(2,1)S(1)}, bf16[8,1024,256]{2,1,0:T(8,128)(2,1)}, u32[]{:S(2)}) %copy-start) | copy-done | bytes 4194328
  74.7 11.8 %step.4 = (f32[8,128,128]{2,1,0:T(8,128)S(1)}, f32[96,128]{1,0:T(8,128)S(1)}, f32[320,128]{1,0:T(8,128)S(1)}, f32[320,128]{1,0:T(8,128)S(1)}, f32[32,128]{1,0:T(8,128)S(1)}) custom-call(s32[3]{0:T(128)S(1)} %copy-done.5, f32[8,128,128]{2,1,0:T(8,128)S(1)} %local.4.local_ref, f32[96,128]{1,0:T(8,128)S(1)} %copy-done.7, ...), custom_call_target="tpu_custom_call" | custom-call | tf_op jit(solution)/shard_map/step/pallas_call | solution.py:632
  88.7 3.4 %collective-permute-start.12 = (f32[32,128]{1,0:T(8,128)S(1)}, f32[32,128]{1,0:T(8,128)S(1)}, u32[]{:S(2)}, u32[]{:S(2)}) collective-permute-start(f32[32,128]{1,0:T(8,128)S(1)} %get-tuple-element.42), channel_id=1, source_target_pairs={{0,4},{2,6},{4,0},{6,2},{1,5},{3,7},{5,1},{7,3},{8,12},{10,14},{12... | collective-permute-start | bytes 49160 | tf_op jit(solution)/shard_map/ppermute | solution.py:589
  92.1 2.4 %local.5.local_ref = f32[8,128,128]{2,1,0:T(8,128)S(1)} custom-call(s32[3]{0:T(128)S(1)} %copy-done.5, f32[8,128,128]{2,1,0:T(8,128)S(1)} %get-tuple-element.38.y_ref.refs_0_, f32[8,128,128]{2,1,0:T(8,128)S(1)} %get-tuple-element.29.y_ref.refs_0_, f32[8,64,128]{2,1,0:T(8,128)S(1)} %get-tuple-element.30.refs_0_.refs_1_), custom_call_target="tpu_custom_call" | custom-call | flops 7864320 | bytes 2097152 | tf_op jit(solution)/shard_map/local/pallas_call | solution.py:604
  95.6 11.5 %step.5 = (f32[8,128,128]{2,1,0:T(8,128)S(1)}, f32[96,128]{1,0:T(8,128)S(1)}, f32[320,128]{1,0:T(8,128)S(1)}, f32[320,128]{1,0:T(8,128)S(1)}, f32[32,128]{1,0:T(8,128)S(1)}) custom-call(s32[3]{0:T(128)S(1)} %copy-done.5, f32[8,128,128]{2,1,0:T(8,128)S(1)} %local.5.local_ref, f32[96,128]{1,0:T(8,128)S(1)} %get-tuple-element.39.refs_0_, ...), custom_call_target="tpu_custom_call" | custom-call | tf_op jit(solution)/shard_map/step/pallas_call | solution.py:632
  109.5 3.2 %collective-permute-start.15 = (f32[32,128]{1,0:T(8,128)S(1)}, f32[32,128]{1,0:T(8,128)S(1)}, u32[]{:S(2)}, u32[]{:S(2)}) collective-permute-start(f32[32,128]{1,0:T(8,128)S(1)} %get-tuple-element.47), channel_id=1, source_target_pairs={{0,4},{2,6},{4,0},{6,2},{1,5},{3,7},{5,1},{7,3},{8,12},{10,14},{12... | collective-permute-start | bytes 49160 | tf_op jit(solution)/shard_map/ppermute | solution.py:589
  112.7 2.4 %local.6.local_ref = f32[8,128,128]{2,1,0:T(8,128)S(1)} custom-call(s32[3]{0:T(128)S(1)} %copy-done.5, f32[8,128,128]{2,1,0:T(8,128)S(1)} %get-tuple-element.43.y_ref.refs_0_, f32[8,128,128]{2,1,0:T(8,128)S(1)} %get-tuple-element.38.y_ref.refs_0_, f32[8,64,128]{2,1,0:T(8,128)S(1)} %get-tuple-element.30.refs_0_.refs_1_), custom_call_target="tpu_custom_call" | custom-call | flops 7864320 | bytes 2097152 | tf_op jit(solution)/shard_map/local/pallas_call | solution.py:604
  116.1 11.5 %step.6 = (f32[8,128,128]{2,1,0:T(8,128)S(1)}, f32[96,128]{1,0:T(8,128)S(1)}, f32[320,128]{1,0:T(8,128)S(1)}, f32[320,128]{1,0:T(8,128)S(1)}, f32[32,128]{1,0:T(8,128)S(1)}) custom-call(s32[3]{0:T(128)S(1)} %copy-done.5, f32[8,128,128]{2,1,0:T(8,128)S(1)} %local.6.local_ref, f32[96,128]{1,0:T(8,128)S(1)} %get-tuple-element.44.refs_0_, ...), custom_call_target="tpu_custom_call" | custom-call | tf_op jit(solution)/shard_map/step/pallas_call | solution.py:632
  130.1 3.2 %collective-permute-start.18 = (f32[32,128]{1,0:T(8,128)S(1)}, f32[32,128]{1,0:T(8,128)S(1)}, u32[]{:S(2)}, u32[]{:S(2)}) collective-permute-start(f32[32,128]{1,0:T(8,128)S(1)} %get-tuple-element.52), channel_id=1, source_target_pairs={{0,4},{2,6},{4,0},{6,2},{1,5},{3,7},{5,1},{7,3},{8,12},{10,14},{12... | collective-permute-start | bytes 49160 | tf_op jit(solution)/shard_map/ppermute | solution.py:589
  133.3 2.4 %local.7.local_ref = f32[8,128,128]{2,1,0:T(8,128)S(1)} custom-call(s32[3]{0:T(128)S(1)} %copy-done.5, f32[8,128,128]{2,1,0:T(8,128)S(1)} %get-tuple-element.48.y_ref, f32[8,128,128]{2,1,0:T(8,128)S(1)} %get-tuple-element.43.y_ref.refs_0_, f32[8,64,128]{2,1,0:T(8,128)S(1)} %get-tuple-element.30.refs_0_.refs_1_), custom_call_target="tpu_custom_call" | custom-call | flops 7864320 | bytes 2097152 | tf_op jit(solution)/shard_map/local/pallas_call | solution.py:604
  136.7 6.8 %step.7 = f32[8,128,128]{2,1,0:T(8,128)S(1)} custom-call(s32[3]{0:T(128)S(1)} %copy-done.5, f32[8,128,128]{2,1,0:T(8,128)S(1)} %local.7.local_ref, f32[96,128]{1,0:T(8,128)S(1)} %get-tuple-element.49.refs_0_, f32[320,128]{1,0:T(8,128)S(1)} %collective-permute-done.16.refs_1_, f32[320,128]{1,0:T(8,128)S(1)} %collective-permute-done.17.refs_2_, ...), custom_call_target="tpu_custom_call" | custom-call | tf_op jit(solution)/shard_map/step/pallas_call | solution.py:632
  144.2 2.2 %collective-permute-start.24 = (f32[1,128,128]{2,1,0:T(8,128)S(1)}, f32[1,128,128]{2,1,0:T(8,128)S(1)}, u32[]{:S(2)}, u32[]{:S(2)}) collective-permute-start(f32[1,128,128]{2,1,0:T(8,128)S(1)} %get-tuple-element.56), channel_id=1, source_target_pairs={{0,24},{1,25},{8,16},{9,17},{16,8},{17,9},{24,0},{25,1},{2,26},{3,... | collective-permute-start | bytes 196616 | tf_op jit(solution)/shard_map/ppermute | solution.py:660
  151.0 2.2 %collective-permute-done.21.refs_3_ = f32[1,128,128]{2,1,0:T(8,128)S(1)} collective-permute-done((f32[1,128,128]{2,1,0:T(8,128)S(1)}, f32[1,128,128]{2,1,0:T(8,128)S(1)}, u32[]{:S(2)}, u32[]{:S(2)}) %collective-permute-start.21) | collective-permute-done | bytes 65568 | tf_op jit(solution)/shard_map/ppermute | solution.py:660
  155.1 2.6 %place.1 = f32[8,128,128]{2,1,0:T(8,128)} custom-call(s32[3]{0:T(128)} %pad_add_fusion.info_ref, f32[1,128,128]{2,1,0:T(8,128)} %get-tuple-element.62.refs_0_, f32[1,128,128]{2,1,0:T(8,128)} %copy-done.16, f32[1,128,128]{2,1,0:T(8,128)} %copy-done.15, f32[1,128,128]{2,1,0:T(8,128)} %copy-done.14, f32[1,128,128]{2,1,0:T(8,128)} %copy-done.13, ...), custom_call_target="tpu_custom_call" | custom-call | tf_op jit(solution)/shard_map/place/pallas_call | solution.py:662
  (107 shorter events, 40.1 us)
Async XLA Ops:
  4.1 9.7 %collective-permute-start.2 = (f32[1,552,128]{2,1,0:T(8,128)S(1)}, f32[1,552,128]{2,1,0:T(8,128)S(1)}, u32[]{:S(2)}, u32[]{:S(2)}) collective-permute-start(f32[1,552,128]{2,1,0:T(8,128)S(1)} %fusion), channel_id=1, source_target_pairs={{0,16},{8,24},{16,0},{24,8},{1,17},{9,25},{17,1},{25,9},{2,18},{10... | collective-permute-start | bytes 847880 | tf_op jit(solution)/shard_map/ppermute | solution.py:440
  7.2 8.6 %collective-permute-start = (f32[1,544,128]{2,1,0:T(8,128)S(1)}, f32[1,544,128]{2,1,0:T(8,128)S(1)}, u32[]{:S(2)}, u32[]{:S(2)}) collective-permute-start(f32[1,544,128]{2,1,0:T(8,128)S(1)} %slice_bitcast_fusion), channel_id=1, source_target_pairs={{0,1},{1,0},{2,3},{3,2},{4,5},{5,4},{6,7},{7,6},{8,9},{9,8},{10,11... | collective-permute-start | bytes 835592 | tf_op jit(solution)/shard_map/ppermute | solution.py:440
  14.0 14.0 %collective-permute-start.3 = (f32[2,552,128]{2,1,0:T(8,128)S(1)}, f32[2,552,128]{2,1,0:T(8,128)S(1)}, u32[]{:S(2)}, u32[]{:S(2)}) collective-permute-start(f32[2,552,128]{2,1,0:T(8,128)S(1)} %pad_maximum_fusion), channel_id=1, source_target_pairs={{0,1},{1,0},{2,3},{3,2},{4,5},{5,4},{6,7},{7,6},{8,9},{9,8},{10,11... | collective-permute-start | bytes 1695752 | tf_op jit(solution)/shard_map/ppermute | solution.py:440
  15.8 13.3 %collective-permute-start.1 = (f32[2,544,128]{2,1,0:T(8,128)S(1)}, f32[2,544,128]{2,1,0:T(8,128)S(1)}, u32[]{:S(2)}, u32[]{:S(2)}) collective-permute-start(f32[2,544,128]{2,1,0:T(8,128)S(1)} %pad_maximum_fusion.1), channel_id=1, source_target_pairs={{0,16},{8,24},{16,0},{24,8},{1,17},{9,25},{17,1},{25,9},{2,18},{10... | collective-permute-start | bytes 1671176 | tf_op jit(solution)/shard_map/ppermute | solution.py:440
  29.3 4.6 %collective-permute-start.4 = (f32[4,1096,128]{2,1,0:T(8,128)S(1)}, f32[4,1096,128]{2,1,0:T(8,128)}, u32[]{:S(2)}, u32[]{:S(2)}) collective-permute-start(f32[4,1096,128]{2,1,0:T(8,128)S(1)} %maximum_maximum_fusion.near_ref), channel_id=1, source_target_pairs={{0,8},{8,0},{16,24},{24,16},{1,9},{9,1},{17,25},{25,17},{2,10},{10... | collective-permute-start | bytes 6733832 | tf_op jit(solution)/shard_map/ppermute | solution.py:440
  29.4 12.3 %all-to-all-start = ((f32[8,128,128]{2,1,0:T(8,128)}), f32[8,128,128]{2,1,0:T(8,128)S(1)}, u32[]{:S(2)}, u32[]{:S(2)}) async-start(f32[8,128,128]{2,1,0:T(8,128)} %bitcast.31), calls=%async_computation | async-start | bytes 1048576 | tf_op jit(solution)/shard_map/all_to_all | solution.py:527
  35.9 20.5 %collective-permute-start.8 = (f32[1,8,2,128]{3,2,1,0:T(2,128)}, f32[1,8,2,128]{3,2,1,0:T(2,128)}, u32[]{:S(2)}, u32[]{:S(2)}) collective-permute-start(f32[1,8,2,128]{3,2,1,0:T(2,128)} %fusion.3), channel_id=1, source_target_pairs={{0,2},{2,0},{4,6},{6,4},{1,3},{3,1},{5,7},{7,5},{8,10},{10,8},{12,... | collective-permute-start | bytes 24584 | tf_op jit(solution)/shard_map/ppermute | solution.py:440
  54.1 18.3 %collective-permute-start.5 = (f32[320,128]{1,0:T(8,128)}, f32[320,128]{1,0:T(8,128)S(1)}, u32[]{:S(2)}, u32[]{:S(2)}) collective-permute-start(f32[320,128]{1,0:T(8,128)} %get-tuple-element.32), channel_id=1, source_target_pairs={{0,2},{4,6},{2,0},{6,4},{1,3},{5,7},{3,1},{7,5},{8,10},{12,14},{10... | collective-permute-start | bytes 491528 | tf_op jit(solution)/shard_map/ppermute | solution.py:589
  55.7 16.8 %collective-permute-start.6 = (f32[320,128]{1,0:T(8,128)}, f32[320,128]{1,0:T(8,128)S(1)}, u32[]{:S(2)}, u32[]{:S(2)}) collective-permute-start(f32[320,128]{1,0:T(8,128)} %get-tuple-element.33), channel_id=1, source_target_pairs={{2,4},{4,2},{3,5},{5,3},{10,12},{12,10},{11,13},{13,11},{18,20},{2... | collective-permute-start | bytes 491528 | tf_op jit(solution)/shard_map/ppermute | solution.py:589
  57.1 8.3 %collective-permute-start.9 = (f32[2,8,2,128]{3,2,1,0:T(2,128)S(1)}, f32[2,8,2,128]{3,2,1,0:T(2,128)S(1)}, u32[]{:S(2)}, u32[]{:S(2)}) collective-permute-start(f32[2,8,2,128]{3,2,1,0:T(2,128)S(1)} %pad_maximum_fusion.5), channel_id=1, source_target_pairs={{0,4},{2,6},{4,0},{6,2},{1,5},{3,7},{5,1},{7,3},{8,12},{10,14},{12... | collective-permute-start | bytes 49160 | tf_op jit(solution)/shard_map/ppermute | solution.py:440
  61.0 11.4 %collective-permute-start.7 = (f32[32,128]{1,0:T(8,128)}, f32[32,128]{1,0:T(8,128)S(1)}, u32[]{:S(2)}, u32[]{:S(2)}) collective-permute-start(f32[32,128]{1,0:T(8,128)} %get-tuple-element.34), channel_id=1, source_target_pairs={{0,4},{2,6},{4,0},{6,2},{1,5},{3,7},{5,1},{7,3},{8,12},{10,14},{12... | collective-permute-start | bytes 49160 | tf_op jit(solution)/shard_map/ppermute | solution.py:589
  86.5 9.1 %collective-permute-start.10 = (f32[320,128]{1,0:T(8,128)S(1)}, f32[320,128]{1,0:T(8,128)S(1)}, u32[]{:S(2)}, u32[]{:S(2)}) collective-permute-start(f32[320,128]{1,0:T(8,128)S(1)} %get-tuple-element.40), channel_id=1, source_target_pairs={{0,2},{4,6},{2,0},{6,4},{1,3},{5,7},{3,1},{7,5},{8,10},{12,14},{10... | collective-permute-start | bytes 491528 | tf_op jit(solution)/shard_map/ppermute | solution.py:589
  88.0 7.5 %collective-permute-start.11 = (f32[320,128]{1,0:T(8,128)S(1)}, f32[320,128]{1,0:T(8,128)S(1)}, u32[]{:S(2)}, u32[]{:S(2)}) collective-permute-start(f32[320,128]{1,0:T(8,128)S(1)} %get-tuple-element.41), channel_id=1, source_target_pairs={{2,4},{4,2},{3,5},{5,3},{10,12},{12,10},{11,13},{13,11},{18,20},{2... | collective-permute-start | bytes 491528 | tf_op jit(solution)/shard_map/ppermute | solution.py:589
  88.7 6.8 %collective-permute-start.12 = (f32[32,128]{1,0:T(8,128)S(1)}, f32[32,128]{1,0:T(8,128)S(1)}, u32[]{:S(2)}, u32[]{:S(2)}) collective-permute-start(f32[32,128]{1,0:T(8,128)S(1)} %get-tuple-element.42), channel_id=1, source_target_pairs={{0,4},{2,6},{4,0},{6,2},{1,5},{3,7},{5,1},{7,3},{8,12},{10,14},{12... | collective-permute-start | bytes 49160 | tf_op jit(solution)/shard_map/ppermute | solution.py:589
  107.1 9.0 %collective-permute-start.13 = (f32[320,128]{1,0:T(8,128)S(1)}, f32[320,128]{1,0:T(8,128)S(1)}, u32[]{:S(2)}, u32[]{:S(2)}) collective-permute-start(f32[320,128]{1,0:T(8,128)S(1)} %get-tuple-element.45), channel_id=1, source_target_pairs={{0,2},{4,6},{2,0},{6,4},{1,3},{5,7},{3,1},{7,5},{8,10},{12,14},{10... | collective-permute-start | bytes 491528 | tf_op jit(solution)/shard_map/ppermute | solution.py:589
  108.9 7.2 %collective-permute-start.14 = (f32[320,128]{1,0:T(8,128)S(1)}, f32[320,128]{1,0:T(8,128)S(1)}, u32[]{:S(2)}, u32[]{:S(2)}) collective-permute-start(f32[320,128]{1,0:T(8,128)S(1)} %get-tuple-element.46), channel_id=1, source_target_pairs={{2,4},{4,2},{3,5},{5,3},{10,12},{12,10},{11,13},{13,11},{18,20},{2... | collective-permute-start | bytes 491528 | tf_op jit(solution)/shard_map/ppermute | solution.py:589
  109.5 6.5 %collective-permute-start.15 = (f32[32,128]{1,0:T(8,128)S(1)}, f32[32,128]{1,0:T(8,128)S(1)}, u32[]{:S(2)}, u32[]{:S(2)}) collective-permute-start(f32[32,128]{1,0:T(8,128)S(1)} %get-tuple-element.47), channel_id=1, source_target_pairs={{0,4},{2,6},{4,0},{6,2},{1,5},{3,7},{5,1},{7,3},{8,12},{10,14},{12... | collective-permute-start | bytes 49160 | tf_op jit(solution)/shard_map/ppermute | solution.py:589
  127.6 9.1 %collective-permute-start.16 = (f32[320,128]{1,0:T(8,128)S(1)}, f32[320,128]{1,0:T(8,128)S(1)}, u32[]{:S(2)}, u32[]{:S(2)}) collective-permute-start(f32[320,128]{1,0:T(8,128)S(1)} %get-tuple-element.50), channel_id=1, source_target_pairs={{0,2},{4,6},{2,0},{6,4},{1,3},{5,7},{3,1},{7,5},{8,10},{12,14},{10... | collective-permute-start | bytes 491528 | tf_op jit(solution)/shard_map/ppermute | solution.py:589
  129.5 7.2 %collective-permute-start.17 = (f32[320,128]{1,0:T(8,128)S(1)}, f32[320,128]{1,0:T(8,128)S(1)}, u32[]{:S(2)}, u32[]{:S(2)}) collective-permute-start(f32[320,128]{1,0:T(8,128)S(1)} %get-tuple-element.51), channel_id=1, source_target_pairs={{2,4},{4,2},{3,5},{5,3},{10,12},{12,10},{11,13},{13,11},{18,20},{2... | collective-permute-start | bytes 491528 | tf_op jit(solution)/shard_map/ppermute | solution.py:589
  130.1 6.5 %collective-permute-start.18 = (f32[32,128]{1,0:T(8,128)S(1)}, f32[32,128]{1,0:T(8,128)S(1)}, u32[]{:S(2)}, u32[]{:S(2)}) collective-permute-start(f32[32,128]{1,0:T(8,128)S(1)} %get-tuple-element.52), channel_id=1, source_target_pairs={{0,4},{2,6},{4,0},{6,2},{1,5},{3,7},{5,1},{7,3},{8,12},{10,14},{12... | collective-permute-start | bytes 49160 | tf_op jit(solution)/shard_map/ppermute | solution.py:589
  144.2 6.0 %collective-permute-start.24 = (f32[1,128,128]{2,1,0:T(8,128)S(1)}, f32[1,128,128]{2,1,0:T(8,128)S(1)}, u32[]{:S(2)}, u32[]{:S(2)}) collective-permute-start(f32[1,128,128]{2,1,0:T(8,128)S(1)} %get-tuple-element.56), channel_id=1, source_target_pairs={{0,24},{1,25},{8,16},{9,17},{16,8},{17,9},{24,0},{25,1},{2,26},{3,... | collective-permute-start | bytes 196616 | tf_op jit(solution)/shard_map/ppermute | solution.py:660
  146.4 4.6 %collective-permute-start.23 = (f32[1,128,128]{2,1,0:T(8,128)S(1)}, f32[1,128,128]{2,1,0:T(8,128)S(1)}, u32[]{:S(2)}, u32[]{:S(2)}) collective-permute-start(f32[1,128,128]{2,1,0:T(8,128)S(1)} %get-tuple-element.57), channel_id=1, source_target_pairs={{0,9},{1,8},{8,1},{9,0},{16,25},{17,24},{24,17},{25,16},{2,11},{3,... | collective-permute-start | bytes 196616 | tf_op jit(solution)/shard_map/ppermute | solution.py:660
  147.5 5.7 %collective-permute-start.21 = (f32[1,128,128]{2,1,0:T(8,128)S(1)}, f32[1,128,128]{2,1,0:T(8,128)S(1)}, u32[]{:S(2)}, u32[]{:S(2)}) collective-permute-start(f32[1,128,128]{2,1,0:T(8,128)S(1)} %get-tuple-element.59), channel_id=1, source_target_pairs={{0,17},{1,16},{8,25},{9,24},{16,1},{17,0},{24,9},{25,8},{2,19},{3,... | collective-permute-start | bytes 196616 | tf_op jit(solution)/shard_map/ppermute | solution.py:660
  148.7 4.6 %collective-permute-start.20 = (f32[1,128,128]{2,1,0:T(8,128)S(1)}, f32[1,128,128]{2,1,0:T(8,128)S(1)}, u32[]{:S(2)}, u32[]{:S(2)}) collective-permute-start(f32[1,128,128]{2,1,0:T(8,128)S(1)} %get-tuple-element.60), channel_id=1, source_target_pairs={{0,16},{1,17},{8,24},{9,25},{16,0},{17,1},{24,8},{25,9},{2,18},{3,... | collective-permute-start | bytes 196616 | tf_op jit(solution)/shard_map/ppermute | solution.py:660
  (22 other events, 107.0 us)

commit v3 on v2

--- a/solution.py
+++ b/solution.py
@@ -141,7 +141,7 @@
     return lax.dot_general(left, right, (((1,), (1,)), ((), ())), preferred_element_type=jnp.float32)
 
 
-def forward_block(plan, y_block, stack, hot, columns):
+def tile_sums(plan, y_block, stack, columns):
     on, points, slots, projs = plan.on, plan.points, plan.slots, plan.projs
     hi, lo = hi_lo(y_block)
     left = jnp.concatenate(
@@ -149,23 +149,37 @@
     )
     both = dot_nt(left, stack)
     rows = on * points
-    product = both[:rows] + both[rows:]
     mask = columns == lax.broadcasted_iota(jnp.int32, (points, slots), 0)
     lines = []
     for p in range(projs):
         for o in range(on):
-            piece = product[o * points : (o + 1) * points, p * slots : (p + 1) * slots]
-            lines.append(jnp.sum(jnp.where(mask, piece, 0.0), axis=0, keepdims=True))
-    partial = jnp.concatenate(lines, axis=0)
-    part_hi, part_lo = hi_lo(partial)
-    sums = dot_nt(jnp.concatenate([part_hi, part_lo], axis=0), hot)
-    return sums[: plan.features] + sums[plan.features :]
-
-
-def backward_block(plan, coef_split, stack, hot, columns):
-    on, points, slots, projs = plan.on, plan.points, plan.slots, plan.projs
-    near = dot_nn(coef_split, hot)
-    near = near[: plan.features] + near[plan.features :]
+            top = both[o * points : (o + 1) * points, p * slots : (p + 1) * slots]
+            low = both[rows + o * points : rows + (o + 1) * points, p * slots : (p + 1) * slots]
+            lines.append(jnp.sum(jnp.where(mask, top + low, 0.0), axis=0, keepdims=True))
+    return jnp.concatenate(lines, axis=0)
+
+
+def key_sums(plan, partial, hot, group):
+    hi, lo = hi_lo(partial)
+    pieces = []
+    for half in (hi, lo):
+        half = half.astype(jnp.float32)
+        pieces += [jnp.where(group == j, half, 0.0) for j in range(plan.groups)]
+    left = jnp.concatenate(pieces, axis=0).astype(jnp.bfloat16)
+    sums = dot_nt(left, hot)
+    rows = plan.groups * plan.features
+    return sums[:rows] + sums[rows:]
+
+
+def backward_block(plan, coef_split, stack, hot, group, columns):
+    on, points, slots, projs, f = plan.on, plan.points, plan.slots, plan.projs, plan.features
+    every = dot_nn(coef_split, hot)
+    rows = plan.groups * f
+    near = None
+    for j in range(plan.groups):
+        piece = every[j * f : (j + 1) * f] + every[rows + j * f : rows + (j + 1) * f]
+        piece = jnp.where(group == j, piece, 0.0)
+        near = piece if near is None else near + piece
     mask = columns == lax.broadcasted_iota(jnp.int32, (points, slots), 0)
     bands = []
     for o in range(on):
@@ -201,44 +215,31 @@
 
 
 def emit_sums(plan, total, odd, upper, own_ref, even_ref, odd_ref, far_ref):
-    f, third, halo = plan.features, plan.third, plan.halo_rows
-    blocks = [total[:, j * LANE : (j + 1) * LANE] for j in range(3 * third)]
-    for j in range(3 * third):
-        own_ref[j * f : (j + 1) * f, :] = blocks[j]
-    for j in range(2 * third):
-        row = halo + j * f
-        up, down = blocks[j + third], blocks[j]
-        even_ref[row : row + f, :] = jnp.where(odd, down, up)
-        odd_ref[row : row + f, :] = jnp.where(odd, up, down)
-    for j in range(third):
-        far_ref[j * f : (j + 1) * f, :] = jnp.where(upper, blocks[j], blocks[j + 2 * third])
+    third, halo = plan.third, plan.halo_rows
+    own_ref[...] = total
+    up, down = total[third:], total[: 2 * third]
+    even_ref[halo : halo + 2 * third, :] = jnp.where(odd, down, up)
+    odd_ref[halo : halo + 2 * third, :] = jnp.where(odd, up, down)
+    far_ref[:third, :] = jnp.where(upper, total[:third], total[2 * third :])
 
 
 def load_coefs(plan, odd, upper, own_ref, even_ref, odd_ref, far_ref, scale_ref):
-    f, third, halo = plan.features, plan.third, plan.halo_rows
-    blocks = []
-    for j in range(3 * third):
-        block = own_ref[j * f : (j + 1) * f, :]
-        if j < 2 * third:
-            row = halo + j * f
-            at = slice(row, row + f)
-            block = block + jnp.where(odd, even_ref[at, :], odd_ref[at, :])
-        if j >= third:
-            row = halo + (j - third) * f
-            at = slice(row, row + f)
-            block = block + jnp.where(odd, odd_ref[at, :], even_ref[at, :])
-        if j < third:
-            block = block + jnp.where(upper, far_ref[j * f : (j + 1) * f, :], 0.0)
-        if j >= 2 * third:
-            row = (j - 2 * third) * f
-            block = block + jnp.where(upper, 0.0, far_ref[row : row + f, :])
-        blocks.append(block)
-    return jnp.concatenate(blocks, axis=1) * scale_ref[...]
+    third, halo = plan.third, plan.halo_rows
+    from_even = even_ref[halo : halo + 2 * third, :]
+    from_odd = odd_ref[halo : halo + 2 * third, :]
+    low = jnp.where(odd, from_even, from_odd)
+    high = jnp.where(odd, from_odd, from_even)
+    far = far_ref[:third, :]
+    own = own_ref[...]
+    first = own[:third] + low[:third] + jnp.where(upper, far, 0.0)
+    second = own[third : 2 * third] + low[third:] + high[:third]
+    last = own[2 * third :] + high[third:] + jnp.where(upper, 0.0, far)
+    return jnp.concatenate([first, second, last], axis=0) * scale_ref[...]
 
 
 def local_kernel(plan, first, info_ref, y_ref, *refs):
     if first:
-        potential_ref, out_ref, pad_ref = refs
+        out_ref, pad_ref = refs
     else:
         previous_ref, potential_ref, out_ref, pad_ref = refs
     on, cz, cy, cx, gx, gz = plan.on, plan.cz, plan.cy, plan.cx, plan.gx, plan.gz
@@ -276,8 +277,12 @@
         center = pad_ref[ix + 1, :, planes, own, :].reshape(shape)
         left = pad_ref[ix, :, planes, own, :].reshape(shape)
         right = pad_ref[ix + 2, :, planes, own, :].reshape(shape)
-        diagonal = factor * (potential_ref[part] - (CENTER + 1.5 * stencil_weights[0]))
-        total = jnp.concatenate([diagonal] * on, axis=0) * center
+        constant = CENTER + 1.5 * stencil_weights[0]
+        if first:
+            total = (-factor * constant) * center
+        else:
+            diagonal = factor * (potential_ref[part] - constant)
+            total = jnp.concatenate([diagonal] * on, axis=0) * center
         for k in range(1, REACH + 1):
             near = pltpu.roll(jnp.where(lane >= cx - k, left, center), k, 1)
             near = near + pltpu.roll(jnp.where(lane < k, right, center), cx - k, 1)
@@ -307,67 +312,148 @@
     return jnp.concatenate([low] + middle + [high], axis=1).reshape(lines * cy, cx)
 
 
-def opening_kernel(
-    plan, info_ref, near_ref, far_ref, y_ref,
-    stack_ref, hot_ref, columns_ref, potential_ref, y_out_ref,
-    own_ref, even_ref, odd_ref, far_sums_ref, total_ref,
+def pack_kernel(plan, tile_ref, potential_ref, part_a_ref, part_b_ref):
+    half = plan.projs // 2
+    slots = plan.slots
+    for p in range(half):
+        part_a_ref[0, p * slots : (p + 1) * slots, :] = tile_ref[:, p, :]
+        part_b_ref[0, p * slots : (p + 1) * slots, :] = tile_ref[:, half + p, :]
+    part_b_ref[0, half * slots :, :] = potential_ref[...]
+
+
+def fill_stack(plan, stack_ref, first_rows, second_rows):
+    rows = first_rows.shape[0]
+    for start, value in ((0, first_rows), (rows, second_rows)):
+        hi, lo = hi_lo(value)
+        stack_ref[start : start + rows, : plan.cx] = hi
+        stack_ref[start : start + rows, plan.cx :] = lo
+
+
+def own_tiles_kernel(plan, part_a_ref, part_b_ref, meta_ref, y_ref, out_ref, stack_ref):
+    @pl.when(pl.program_id(0) == 0)
+    def _():
+        rows = part_a_ref.shape[1]
+        fill_stack(plan, stack_ref, part_a_ref[0], part_b_ref[0, :rows, :])
+
+    meta = meta_ref[...]
+    columns = meta_line(plan, meta, 1).astype(jnp.int32)
+    y_rows, f = plan.y_rows, plan.features
+    for part in range(plan.per):
+        y_block = y_ref[part]
+        partial = tile_sums(plan, y_block, stack_ref[...], columns)
+        out_ref[part, :y_rows, :] = y_block
+        for j in range(plan.slots // LANE):
+            row = y_rows + j * f
+            out_ref[part, row : row + f, :] = partial[:, j * LANE : (j + 1) * LANE]
+        out_ref[part, plan.meta_at :, :] = meta
+
+
+def meta_line(plan, meta, which):
+    count = plan.slots // LANE
+    return jnp.concatenate(
+        [meta[which * count + i : which * count + i + 1, :] for i in range(count)], axis=1
+    )
+
+
+def sums_kernel(
+    plan, info_ref, in_ref, hot_ref, place_ref, y_ref, own_ref, even_ref, odd_ref, far_ref, total_ref
 ):
     step = pl.program_id(0)
-    half = plan.blocks // 2
-    odd, upper = info_ref[1] == 1, info_ref[2] == 1
-
-    def unpack(source):
-        tiles = plan.projs * plan.slots
-        hi, lo = hi_lo(source[0, :tiles, :])
-        stack_ref[0, :, : plan.cx] = hi
-        stack_ref[0, :, plan.cx :] = lo
-        potential_ref[0] = source[0, tiles : tiles + plan.points, :]
-        meta = tiles + plan.points
-        per = plan.slots // LANE
-        keys = jnp.concatenate([source[0, meta + i : meta + i + 1, :] for i in range(per)], axis=1)
-        cols = jnp.concatenate(
-            [source[0, meta + per + i : meta + per + i + 1, :] for i in range(per)], axis=1
-        )
-        keys = keys.astype(jnp.int32)
-        columns_ref[0] = jnp.broadcast_to(cols.astype(jnp.int32), (SUB, plan.slots))
-        chunk = 256
-        index = lax.broadcasted_iota(jnp.int32, (chunk, plan.slots), 0)
-        for start in range(0, plan.keys, chunk):
-            hot_ref[0, start : start + chunk, :] = jnp.where(
-                index == keys - start, 1.0, 0.0
-            ).astype(jnp.bfloat16)
-
-    @pl.when(step < half)
-    def _():
-        unpack(near_ref)
-
-    @pl.when(step >= half)
-    def _():
-        unpack(far_ref)
-
-    y_block = y_ref[0]
-    y_out_ref[0] = y_block
-    sums = forward_block(plan, y_block, stack_ref[0], hot_ref[0], columns_ref[0, 0:1, :])
-    emit_halo(plan, y_block, step, odd, even_ref, odd_ref)
+    me, odd, upper = info_ref[0], info_ref[1] == 1, info_ref[2] == 1
+    f, y_rows = plan.features, plan.y_rows
+    count = plan.slots // LANE
+    index = lax.broadcasted_iota(jnp.int32, (LANE, plan.slots), 0)
+    total = None
+    table_at = plan.halo_rows + 2 * plan.third
+    for part in range(plan.per):
+        slot = step * plan.per + part
+        g = plan.block_of(slot, me)
+        meta = in_ref[g, plan.meta_at :, :]
+        keys = meta_line(plan, meta, 0).astype(jnp.int32)
+        columns = meta_line(plan, meta, 1).astype(jnp.int32)
+        group = lax.shift_right_logical(keys, LANE.bit_length() - 1)
+        place = keys & (LANE - 1)
+        hot = jnp.where(index == place, 1.0, 0.0).astype(jnp.bfloat16)
+        hot_ref[part] = hot
+        place_ref[part] = jnp.concatenate(
+            [columns, group, jnp.zeros((SUB - 2, plan.slots), jnp.int32)], axis=0
+        )
+        y_block = in_ref[g, :y_rows, :]
+        y_ref[part] = y_block
+        partial = jnp.concatenate(
+            [in_ref[g, y_rows + j * f : y_rows + (j + 1) * f, :] for j in range(count)], axis=1
+        )
+        more = key_sums(plan, partial, hot, group)
+        total = more if total is None else total + more
+        emit_halo(plan, y_block, slot, odd, even_ref, odd_ref)
+        for j in range(plan.coupling_rows):
+            line = meta[2 * count + j : 2 * count + j + 1, :]
+            even_ref[pl.ds(table_at + j * plan.blocks + slot, 1), :] = line
+            far_ref[pl.ds(plan.third + j * plan.blocks + slot, 1), :] = line
 
     @pl.when(step == 0)
     def _():
-        total_ref[...] = sums
+        total_ref[...] = total
 
     @pl.when(step > 0)
     def _():
-        total_ref[...] += sums
-
-    @pl.when(step == plan.blocks - 1)
+        total_ref[...] += total
+
+    @pl.when(step == plan.blocks // plan.per - 1)
     def _():
-        emit_sums(plan, total_ref[...], odd, upper, own_ref, even_ref, odd_ref, far_sums_ref)
+        emit_sums(plan, total_ref[...], odd, upper, own_ref, even_ref, odd_ref, far_ref)
+
+
+def scale_kernel(plan, device_ref, within_ref, *refs):
+    table_refs, out_ref = refs[:-1], refs[-1]
+    blocks, owned = plan.blocks, plan.owned
+    tables = []
+    for table_ref in table_refs:
+        tables.append(
+            jnp.concatenate(
+                [
+                    table_ref[j * blocks : (j + 1) * blocks, :]
+                    for j in range(plan.coupling_rows)
+                ],
+                axis=1,
+            )
+        )
+    table = jnp.concatenate(tables, axis=0).T
+    high, rest = hi_lo(table)
+    middle = table - high.astype(jnp.float32)
+    lowest = (middle - rest.astype(jnp.float32)).astype(jnp.bfloat16)
+    parts = (high, rest, lowest)
+    devices = table.shape[1]
+    device_index = lax.broadcasted_iota(jnp.int32, (devices, LANE), 0)
+    within_index = lax.broadcasted_iota(jnp.int32, (owned, LANE), 0)
+    for j in range(plan.groups):
+        lanes = slice(j * LANE, (j + 1) * LANE)
+        pick = jnp.where(device_index == device_ref[0:1, lanes], 1.0, 0.0).astype(jnp.bfloat16)
+        rows = None
+        for value in parts:
+            product = dot_nn(value, pick)
+            rows = product if rows is None else rows + product
+        mask = within_index == within_ref[0:1, lanes]
+        lines = []
+        for p in range(plan.projs):
+            piece = jnp.where(mask, rows[p * owned : (p + 1) * owned], 0.0)
+            lines += [jnp.sum(piece, axis=0, keepdims=True)] * plan.on
+        out_ref[j * plan.features : (j + 1) * plan.features, :] = jnp.concatenate(lines, axis=0)
 
 
 def step_kernel(plan, first, last, info_ref, local_ref, *refs):
     received, refs = refs[:5], refs[5:]
     own_in, even_in, odd_in, far_in, scale_ref = received
-    stack_ref, hot_ref, columns_ref, out_ref = refs[:4]
-    refs = refs[4:]
+    if first:
+        y_ref, near_a_ref, near_b_ref, far_a_ref, far_b_ref = refs[:5]
+        refs = refs[5:]
+    else:
+        stack_ref, refs = refs[0], refs[1:]
+    hot_ref, place_ref, out_ref = refs[:3]
+    refs = refs[3:]
+    if first:
+        stack_ref, potential_ref = refs[:2]
+        refs = refs[2:]
     if not last:
         own_ref, even_ref, odd_ref, far_ref = refs[:4]
         refs = refs[4:]
@@ -386,22 +472,45 @@
         low_ref[...] = jnp.zeros_like(low_ref)
         high_ref[...] = jnp.zeros_like(high_ref)
 
+    if first:
+        def unpack(part_a_ref, part_b_ref):
+            tiles = part_a_ref.shape[1]
+            for part in range(plan.per):
+                fill_stack(
+                    plan, stack_ref.at[part], part_a_ref[part], part_b_ref[part, :tiles, :]
+                )
+                potential_ref[part] = part_b_ref[part, tiles:, :]
+
+        @pl.when(step * plan.per < plan.blocks // 2)
+        def _():
+            unpack(near_a_ref, near_b_ref)
+
+        @pl.when(step * plan.per >= plan.blocks // 2)
+        def _():
+            unpack(far_a_ref, far_b_ref)
+
     rows = plan.on * plan.cz * REACH
     sums = None
     for part in range(plan.per):
         slot = step * plan.per + part
-        columns = columns_ref[part, 0:1, :]
+        columns, group = place_ref[part, 0:1, :], place_ref[part, 1:2, :]
         where = pl.ds(pl.multiple_of(slot * rows, SUB), rows)
         from_even, from_odd = even_in[where, :], odd_in[where, :]
         low_rows = jnp.where(odd, from_even, from_odd)
         high_rows = jnp.where(odd, from_odd, from_even)
         halo = halo_part(plan, first, low_rows, high_rows, low_ref.at[part], high_ref.at[part])
-        projected = backward_block(plan, coef_ref[...], stack_ref[part], hot_ref[part], columns)
+        projected = backward_block(
+            plan, coef_ref[...], stack_ref[part], hot_ref[part], group, columns
+        )
         y_new = (local_ref[part] + halo) + projected
+        if first:
+            potential = factor * potential_ref[part]
+            y_new = y_new + jnp.concatenate([potential] * plan.on, axis=0) * y_ref[part]
         out_ref[part] = y_new
         if last:
             continue
-        more = forward_block(plan, y_new, stack_ref[part], hot_ref[part], columns)
+        partial = tile_sums(plan, y_new, stack_ref[part], columns)
+        more = key_sums(plan, partial, hot_ref[part], group)
         sums = more if sums is None else sums + more
         emit_halo(plan, y_new, slot, odd, even_ref, odd_ref)
     if last:
@@ -456,8 +565,13 @@
     plan.points, plan.slots, plan.projs, plan.blocks = points, slots, projs, blocks
     plan.features = projs * on
     plan.keys = 3 * blocks * owned
-    plan.third = blocks * owned // LANE
+    plan.owned = owned
+    plan.groups = plan.keys // LANE
+    plan.third = plan.groups // 3 * plan.features
     plan.halo_rows = blocks * on * cz * REACH
+    plan.y_rows = on * points
+    plan.coupling_rows = owned * projs // LANE
+    plan.meta_at = plan.y_rows + plan.features * slots // LANE
     rounds = [("gz", 1 << b) for b in range(log2(gz))]
     rounds += [("gx", 1 << b) for b in reversed(range(log2(gx)))]
     weights = [bit if axis == "gz" else bit * gz for axis, bit in rounds]
@@ -483,104 +597,104 @@
         + tile_atom % owned
     )
     lanes = lambda value: value.astype(jnp.float32).reshape(-1, LANE)
-    tiles = tile_proj.transpose(1, 0, 2).reshape(projs * slots, cx)
-    meta = jnp.concatenate([lanes(key), lanes(column), lanes(coupling)], axis=0)
+    meta = jnp.concatenate([lanes(key), lanes(column), lanes(coupling.T)], axis=0)
     meta_rows = -(-meta.shape[0] // SUB) * SUB
     meta = jnp.pad(meta, ((0, meta_rows - meta.shape[0]), (0, 0)))
-    payload = jnp.concatenate([tiles, potential.reshape(points, cx), meta], axis=0)
-    rows = payload.shape[0]
-    cut = rows // 2 // SUB * SUB
-    part_a, part_b = payload[None, :cut], payload[None, cut:]
-    swapped = [rounds[1], rounds[0]] + rounds[2:]
-    for (axis_a, bit_a), (axis_b, bit_b) in zip(rounds[:2], swapped[:2]):
-        far_a = exchange(part_a, axis_a, bit_a)
-        far_b = exchange(part_b, axis_b, bit_b)
-        part_a = jnp.concatenate([part_a, far_a], axis=0)
-        part_b = jnp.concatenate([part_b, far_b], axis=0)
-    part_b = jnp.stack([part_b[0], part_b[2], part_b[1], part_b[3]])
-    near = jnp.concatenate([part_a, part_b], axis=1)
+
+    f32 = jnp.float32
+    per = plan.per
+    tile_rows = projs * slots
+    y_rows = plan.y_rows
+    full = lambda *shape: pl.BlockSpec(shape, lambda *_: (0,) * len(shape))
+    each = lambda count, *shape: pl.BlockSpec((count,) + shape, lambda i, *_: (i, 0, 0))
+    params = pltpu.CompilerParams(vmem_limit_bytes=48 * 1024 * 1024)
+    half_rows = tile_rows // 2
+    part_a, part_b = pl.pallas_call(
+        functools.partial(pack_kernel, plan),
+        out_shape=[
+            jax.ShapeDtypeStruct((1, half_rows, cx), f32),
+            jax.ShapeDtypeStruct((1, half_rows + points, cx), f32),
+        ],
+        compiler_params=params,
+        name="pack",
+    )(tile_proj, potential.reshape(points, cx))
+
+    messages = pl.pallas_call(
+        functools.partial(own_tiles_kernel, plan),
+        out_shape=jax.ShapeDtypeStruct((blocks, plan.meta_at + meta_rows, cx), f32),
+        grid=(blocks // per,),
+        in_specs=[
+            full(1, half_rows, cx),
+            full(1, half_rows + points, cx),
+            full(meta_rows, LANE),
+            each(per, y_rows, cx),
+        ],
+        out_specs=each(per, plan.meta_at + meta_rows, cx),
+        scratch_shapes=[pltpu.VMEM((tile_rows, 2 * cx), jnp.bfloat16)],
+        compiler_params=params,
+        name="own_tiles",
+    )(part_a, part_b, meta, orbitals.reshape(blocks, y_rows, cx))
+    arrived = lax.all_to_all(messages, ("gx", "gz"), 0, 0, tiled=True)
+
+    far_a = exchange(part_a, *rounds[0])
+    far_b = exchange(part_b, *rounds[1])
+    part_a = jnp.concatenate([part_a, far_a], axis=0)
+    part_b = jnp.concatenate([part_b, far_b], axis=0)
+    far_a = exchange(part_a, *rounds[1])
+    far_b = exchange(part_b, *rounds[0])
+    part_a = jnp.concatenate([part_a, far_a], axis=0)
+    part_b = jnp.stack([part_b, far_b], axis=1).reshape((4,) + part_b.shape[1:])
     for axis, bit in rounds[2:-1]:
-        near = jnp.concatenate([near, exchange(near, axis, bit)], axis=0)
-    far = exchange(near, *rounds[-1])
-
-    meta_at = projs * slots + points + 2 * (slots // LANE)
-    coupling_rows = owned * projs // LANE
-    take = lambda value: value[:, meta_at : meta_at + coupling_rows]
-    table = jnp.concatenate([take(near), take(far)], axis=0).reshape(
-        (1, blocks, coupling_rows, LANE)
-    )
-    for b in range(log2(gy)):
-        table = jnp.concatenate([table, exchange(table, "gy", 1 << b)], axis=0)
+        part_a = jnp.concatenate([part_a, exchange(part_a, axis, bit)], axis=0)
+        part_b = jnp.concatenate([part_b, exchange(part_b, axis, bit)], axis=0)
+    far_a = exchange(part_a, *rounds[-1])
+    far_b = exchange(part_b, *rounds[-1])
+
     me = ix * gz + iz
     home = atom_home.reshape(gx, gy, gz, owned).transpose(1, 0, 2, 3).reshape(gy, blocks * owned)
     home = jnp.pad(home, ((1, 1), (0, 0)))
-    home = lax.dynamic_slice_in_dim(home, iy, 3, axis=0).reshape(plan.keys)
+    home = lax.dynamic_slice_in_dim(home, iy, 3, axis=0).reshape(1, plan.keys)
     home_device = home // owned
     home_y = home_device // gz % gy
     home_g = home_device // (gy * gz) * gz + home_device % gz
     moved_g = home_g ^ me
     place = sum(((moved_g >> log2(w)) & 1) * (1 << j) for j, w in enumerate(weights))
-    row = ((home_y ^ iy) * blocks + place) * owned + home % owned
-    scale = table.reshape(gy * blocks * owned, projs)[row]
-    scale = jnp.repeat(scale.T, on, axis=0)
-
-    y0 = lax.all_to_all(
-        orbitals.reshape(blocks, on * points, cx), ("gx", "gz"), 0, 0, tiled=True
-    )
-
-    f32 = jnp.float32
+    home_device = (home_y ^ iy) * blocks + place
+    home_within = home % owned
+
     info = jnp.stack([me, iy & 1, (iy >> 1) & 1]).astype(jnp.int32)
-    message_rows = plan.halo_rows + 2 * plan.third * plan.features
-    far_rows = plan.third * plan.features
-    own_rows = 3 * plan.third * plan.features
+    table_rows = plan.coupling_rows * blocks
+    message_rows = plan.halo_rows + 2 * plan.third
     half = blocks // 2
-    per = plan.per
-    whole = lambda *shape: pl.BlockSpec(shape, lambda i, m: (0,) * len(shape))
-    each = lambda count, *shape: pl.BlockSpec((count,) + shape, lambda i, m: (i, 0, 0))
-    tile_rows = projs * slots
-    y_rows = on * points
     y_shape = jax.ShapeDtypeStruct((blocks, y_rows, cx), f32)
-    send_shapes = [
-        jax.ShapeDtypeStruct((count, LANE), f32)
-        for count in (own_rows, message_rows, message_rows, far_rows)
-    ]
-    send_specs = [whole(*shape.shape) for shape in send_shapes]
-    params = pltpu.CompilerParams(vmem_limit_bytes=48 * 1024 * 1024)
-    sums_scratch = pltpu.VMEM((plan.features, plan.keys), f32)
-
-    opened = pl.pallas_call(
-        functools.partial(opening_kernel, plan),
+
+    def send_shapes(extra):
+        counts = (3 * plan.third, message_rows + extra, message_rows, plan.third + extra)
+        return [jax.ShapeDtypeStruct((count, LANE), f32) for count in counts]
+
+    def send_specs(extra):
+        return [full(*shape.shape) for shape in send_shapes(extra)]
+
+    sums_scratch = pltpu.VMEM((3 * plan.third, LANE), f32)
+    hot, places, current, *sends = pl.pallas_call(
+        functools.partial(sums_kernel, plan),
         out_shape=[
-            jax.ShapeDtypeStruct((blocks, tile_rows, 2 * cx), jnp.bfloat16),
-            jax.ShapeDtypeStruct((blocks, plan.keys, slots), jnp.bfloat16),
+            jax.ShapeDtypeStruct((blocks, LANE, slots), jnp.bfloat16),
             jax.ShapeDtypeStruct((blocks, SUB, slots), jnp.int32),
-            jax.ShapeDtypeStruct((blocks, points, cx), f32),
             y_shape,
         ]
-        + send_shapes,
+        + send_shapes(table_rows),
         grid_spec=pltpu.PrefetchScalarGridSpec(
             num_scalar_prefetch=1,
-            grid=(blocks,),
-            in_specs=[
-                pl.BlockSpec((1, rows, cx), lambda i, m: (jnp.minimum(i, half - 1), 0, 0)),
-                pl.BlockSpec((1, rows, cx), lambda i, m: (jnp.maximum(i - half, 0), 0, 0)),
-                pl.BlockSpec((1, y_rows, cx), lambda i, m: (block_of(i, m[0]), 0, 0)),
-            ],
-            out_specs=[
-                each(1, tile_rows, 2 * cx),
-                each(1, plan.keys, slots),
-                each(1, SUB, slots),
-                each(1, points, cx),
-                each(1, y_rows, cx),
-            ]
-            + send_specs,
+            grid=(blocks // per,),
+            in_specs=[full(*arrived.shape)],
+            out_specs=[each(per, LANE, slots), each(per, SUB, slots), each(per, y_rows, cx)]
+            + send_specs(table_rows),
             scratch_shapes=[sums_scratch],
         ),
         compiler_params=params,
-        name="opening",
-    )(info, near, far, y0)
-    stack, hot, columns, plane_potential, current = opened[:5]
-    sends = list(opened[5:])
+        name="first_sums",
+    )(info, arrived)
 
     def pairwise(value, pairs):
         pairs = [(a, b) for a, b in pairs if b < gy]
@@ -601,15 +715,29 @@
     for repeat in range(DEGREE):
         first, last = repeat == 0, repeat == DEGREE - 1
         received = swap(sends)
+        if first:
+            own_table = sends[3][plan.third :]
+            across = [own_table] * (gy > 1) + [received[1][message_rows:]] * (gy > 1)
+            across += [received[3][plan.third :]] * (gy > 2)
+            if gy > 2:
+                pairs = [(i, i ^ 3) for i in range(gy)]
+                across.append(lax.ppermute(own_table, "gy", pairs))
+            across = across or [own_table]
+            scale = pl.pallas_call(
+                functools.partial(scale_kernel, plan),
+                out_shape=jax.ShapeDtypeStruct((3 * plan.third, LANE), f32),
+                compiler_params=params,
+                name="scale",
+            )(home_device, home_within, *across)
+        extra = table_rows if first else 0
         local = pl.pallas_call(
             functools.partial(local_kernel, plan, first),
             out_shape=y_shape,
             grid_spec=pltpu.PrefetchScalarGridSpec(
                 num_scalar_prefetch=1,
                 grid=(blocks // per,),
-                in_specs=[whole(blocks, y_rows, cx)]
-                + ([] if first else [each(per, y_rows, cx)])
-                + [each(per, points, cx)],
+                in_specs=[full(blocks, y_rows, cx)]
+                + ([] if first else [each(per, y_rows, cx), each(per, points, cx)]),
                 out_specs=each(per, y_rows, cx),
                 scratch_shapes=[
                     pltpu.VMEM((gx + 2, on, cz * gz + 2 * REACH, 2 * SUB + cy, cx), f32)
@@ -622,35 +750,56 @@
                 transcendentals=0,
             ),
             name="local",
-        )(info, current, *([] if first else [previous]), plane_potential)
+        )(info, current, *([] if first else [previous, plane_potential]))
         lines = on * cz
         scratch = [
-            pltpu.VMEM((2 * plan.features, plan.keys), jnp.bfloat16),
+            pltpu.VMEM((6 * plan.third, LANE), jnp.bfloat16),
             pltpu.VMEM((per, lines, 2 * SUB, cx), f32),
             pltpu.VMEM((per, lines, 2 * SUB, cx), f32),
         ]
+        in_specs = [each(per, y_rows, cx)] + send_specs(extra) + [full(3 * plan.third, LANE)]
+        arrays = [local, *received, scale]
+        out_shapes, out_specs = [y_shape], [each(per, y_rows, cx)]
+        if first:
+            arrays += [current, part_a, part_b, far_a, far_b]
+            in_specs.append(each(per, y_rows, cx))
+            near_index = lambda i, m: (jnp.minimum(i, half // per - 1), 0, 0)
+            far_index = lambda i, m: (jnp.maximum(i - half // per, 0), 0, 0)
+            for index in (near_index, far_index):
+                for array in (part_a, part_b):
+                    in_specs.append(pl.BlockSpec((per,) + array.shape[1:], index))
+            out_shapes += [
+                jax.ShapeDtypeStruct((blocks, tile_rows, 2 * cx), jnp.bfloat16),
+                jax.ShapeDtypeStruct((blocks, points, cx), f32),
+            ]
+            out_specs += [each(per, tile_rows, 2 * cx), each(per, points, cx)]
+        else:
+            arrays.append(stack)
+            in_specs.append(each(per, tile_rows, 2 * cx))
+        arrays += [hot, places]
+        in_specs += [each(per, LANE, slots), each(per, SUB, slots)]
+        if not last:
+            out_shapes += send_shapes(0)
+            out_specs += send_specs(0)
+            scratch.append(sums_scratch)
         result = pl.pallas_call(
             functools.partial(step_kernel, plan, first, last),
-            out_shape=[y_shape] + ([] if last else send_shapes),
+            out_shape=out_shapes,
             grid_spec=pltpu.PrefetchScalarGridSpec(
                 num_scalar_prefetch=1,
                 grid=(blocks // per,),
-                in_specs=[each(per, y_rows, cx)]
-                + send_specs
-                + [
-                    whole(plan.features, plan.keys),
-                    each(per, tile_rows, 2 * cx),
-                    each(per, plan.keys, slots),
-                    each(per, SUB, slots),
-                ],
-                out_specs=[each(per, y_rows, cx)] + ([] if last else send_specs),
-                scratch_shapes=scratch + ([] if last else [sums_scratch]),
+                in_specs=in_specs,
+                out_specs=out_specs,
+                scratch_shapes=scratch,
             ),
             compiler_params=params,
             name="step",
-        )(info, local, *received, scale, stack, hot, columns)
+        )(info, *arrays)
         previous, current = current, result[0]
-        sends = result[1:]
+        result = result[1:]
+        if first:
+            stack, plane_potential, *result = result
+        sends = result
 
     pieces = []
     for slot in range(blocks):
@@ -665,8 +814,8 @@
         grid_spec=pltpu.PrefetchScalarGridSpec(
             num_scalar_prefetch=1,
             grid=(1,),
-            in_specs=[whole(1, y_rows, cx)] * blocks,
-            out_specs=whole(blocks, y_rows, cx),
+            in_specs=[full(1, y_rows, cx)] * blocks,
+            out_specs=full(blocks, y_rows, cx),
         ),
         name="place",
     )(info, *pieces)
@@ -688,8 +837,9 @@
     turned = turned and norb % blocks == 0 and cx == LANE and slots % LANE == 0
     if turned:
         turned = (norb // blocks * projs) % SUB == 0 and (owned * projs) % LANE == 0
+        turned = turned and owned % SUB == 0 and blocks % SUB == 0
         turned = turned and (blocks * owned) % LANE == 0 and cy % SUB == 0 and cy >= 2 * SUB
-        turned = turned and cz % 2 == 0 and (3 * blocks * owned) % 256 == 0
+        turned = turned and cz % 2 == 0 and projs % 2 == 0 and blocks % 4 == 0
     return turned_path(*arguments) if turned else general_path(*arguments)
 
 

time: 159 us -> 126 us (0.79)
  Pallas kernels: 64.8 us -> 53.5 us
  waiting for transfers between devices: 28.9 us -> 20.3 us
  local copies, waits for them, and re-layouts: 13.9 us -> 5.65 us
  other arithmetic: 5.92 us -> 1.18 us
    ppermute x7 -> x6, waiting for transfers between devices: 18.8 us -> 9.78 us  [exchange(): return lax.ppermute(value, axis, [(i, i ^ bit) for i in range(count)])]
    pallas_call x4, Pallas kernels: 41.6 us -> 35.8 us  [turned_path(): pl.pallas_call(functools.partial(step_kernel, plan, first, last), out_sha...]
    pallas_call x1 -> x4, Pallas kernels: 11.2 us -> 5.62 us  [the longest x1 2.92 us: turned_path(): pl.pallas_call(functools.partial(own_tiles_kernel, plan), out_shape=jax.S...]
    ppermute x7 -> x6, starting transfers between devices: 13.5 us -> 8.42 us  [exchange(): return lax.ppermute(value, axis, [(i, i ^ bit) for i in range(count)])]
    ppermute x12, starting transfers between devices: 19.2 us -> 23.3 us  [pairwise(): return lax.ppermute(value, 'gy', pairs + [(b, a) for a, b in pairs])]
    gather x1 -> x0, local copies, waits for them, and re-layouts: 3.67 us -> none  [turned_path(): scale = table.reshape(gy * blocks * owned, projs)[row]]
    transpose x2 -> x0, local copies, waits for them, and re-layouts: 2.47 us -> none  [the longest x1 1.39 us: turned_path(): scale = jnp.repeat(scale.T, on, axis=0)]
    unnamed x41 -> x35, local copies, waits for them, and re-layouts: 4.86 us -> 2.51 us
  transfers between devices with their start and end apart: 27 -> 27, of which waited for: 11 -> 10; matrix products, arithmetic and copies ran while one was open for 7% -> 3% of each run, Pallas kernels for 13% -> 12%
where the time goes in v3:
time: 126 us; the launch traced here: 125 us
  Pallas kernels  53.5 us (42%)
  starting transfers between devices  43.5 us (35%)
  waiting for transfers between devices  20.3 us (16%)
  local copies, waits for them, and re-layouts  5.65 us (4%)
    pallas_call x4, Pallas kernels, turned_path(): pl.pallas_call(functools.partial(step_kernel, plan, first, last), out_sha...  35.8 us
    ppermute x12, starting transfers between devices, pairwise(): return lax.ppermute(value, 'gy', pairs + [(b, a) for a, b in pairs])  23.3 us
    ppermute x6, waiting for transfers between devices, exchange(): return lax.ppermute(value, axis, [(i, i ^ bit) for i in range(count)])  9.78 us
    pallas_call x4, Pallas kernels, turned_path(): pl.pallas_call(functools.partial(local_kernel, plan, first), out_shape=y_...  9.51 us
    ppermute x6, starting transfers between devices, exchange(): return lax.ppermute(value, axis, [(i, i ^ bit) for i in range(count)])  8.42 us
    ppermute x7, starting transfers between devices, turned_path(): lax.ppermute(block, ('gx', 'gz'), [(i, i ^ moved) for i in range(blocks)])  6.81 us
    ppermute x12, waiting for transfers between devices, pairwise(): return lax.ppermute(value, 'gy', pairs + [(b, a) for a, b in pairs])  3.88 us
    all_to_all x1, starting transfers between devices, turned_path(): arrived = lax.all_to_all(messages, ('gx', 'gz'), 0, 0, tiled=True)  3.54 us
  transfers between devices with their start and end apart: 27, of which 10 were waited for; matrix products, arithmetic and copies ran while one was open for 3% of the time, Pallas kernels for 12%

profile of v3, /device:TPU:0, one launch (start us, length us, event | category | flops | bytes accessed | tf_op | source)
XLA Modules:
  0.0 125.1 jit_solution(6788393282083002239)
XLA Ops:
  2.1 3.0 %collective-permute-start.6 = (f32[1,576,128]{2,1,0:T(8,128)S(1)}, f32[1,576,128]{2,1,0:T(8,128)S(1)}, u32[]{:S(2)}, u32[]{:S(2)}) collective-permute-start(f32[1,576,128]{2,1,0:T(8,128)S(1)} %get-tuple-element.32.part_b_ref), channel_id=1, source_target_pairs={{0,16},{8,24},{16,0},{24,8},{1,17},{9,25},{17,1},{25,9},{2,18},{10... | collective-permute-start | bytes 884744 | tf_op jit(solution)/shard_map/ppermute | solution.py:549
  7.3 4.8 %collective-permute-done.6 = f32[1,576,128]{2,1,0:T(8,128)S(1)} collective-permute-done((f32[1,576,128]{2,1,0:T(8,128)S(1)}, f32[1,576,128]{2,1,0:T(8,128)S(1)}, u32[]{:S(2)}, u32[]{:S(2)}) %collective-permute-start.6) | collective-permute-done | bytes 294944 | tf_op jit(solution)/shard_map/ppermute | solution.py:549
  12.2 1.8 %collective-permute-start.7 = (f32[2,576,128]{2,1,0:T(8,128)S(1)}, f32[2,576,128]{2,1,0:T(8,128)S(1)}, u32[]{:S(2)}, u32[]{:S(2)}) collective-permute-start(f32[2,576,128]{2,1,0:T(8,128)S(1)} %constant_dynamic-update-slice_fusion.3), channel_id=1, source_target_pairs={{0,1},{1,0},{2,3},{3,2},{4,5},{5,4},{6,7},{7,6},{8,9},{9,8},{10,11... | collective-permute-start | bytes 1769480 | tf_op jit(solution)/shard_map/ppermute | solution.py:549
  16.5 2.9 %own_tiles.1 = f32[8,152,128]{2,1,0:T(8,128)} custom-call(f32[1,512,128]{2,1,0:T(8,128)S(1)} %get-tuple-element.31.part_a_ref, f32[1,576,128]{2,1,0:T(8,128)S(1)} %get-tuple-element.32.part_b_ref, f32[8,128]{1,0:T(8,128)S(1)} %select_maximum_fusion.meta_ref, f32[8,128,128]{2,1,0:T(8,128)S(1)} %bitcast.21), custom_call_target="tpu_custom_call" | custom-call | tf_op jit(solution)/shard_map/own_tiles/pallas_call | solution.py:622
  19.4 3.5 %all-to-all-start = ((f32[8,152,128]{2,1,0:T(8,128)}), f32[8,152,128]{2,1,0:T(8,128)S(1)}, u32[]{:S(2)}, u32[]{:S(2)}) async-start(f32[8,152,128]{2,1,0:T(8,128)} %own_tiles.1), calls=%async_computation | async-start | bytes 1245184 | tf_op jit(solution)/shard_map/all_to_all | solution.py:637
  23.2 5.0 %collective-permute-done.7 = f32[2,576,128]{2,1,0:T(8,128)S(1)} collective-permute-done((f32[2,576,128]{2,1,0:T(8,128)S(1)}, f32[2,576,128]{2,1,0:T(8,128)S(1)}, u32[]{:S(2)}, u32[]{:S(2)}) %collective-permute-start.7) | collective-permute-done | bytes 589856 | tf_op jit(solution)/shard_map/ppermute | solution.py:549
  31.1 3.1 %all-to-all-done.in_ref = f32[8,152,128]{2,1,0:T(8,128)S(1)} async-done(((f32[8,152,128]{2,1,0:T(8,128)}), f32[8,152,128]{2,1,0:T(8,128)S(1)}, u32[]{:S(2)}, u32[]{:S(2)}) %all-to-all-start) | async-done | bytes 622624 | tf_op jit(solution)/shard_map/all_to_all | solution.py:637
  35.9 2.7 %collective-permute-start.2 = (f32[48,128]{1,0:T(8,128)S(1)}, f32[48,128]{1,0:T(8,128)S(1)}, u32[]{:S(2)}, u32[]{:S(2)}) collective-permute-start(f32[48,128]{1,0:T(8,128)S(1)} %get-tuple-element.37), channel_id=1, source_target_pairs={{0,4},{2,6},{4,0},{6,2},{1,5},{3,7},{5,1},{7,3},{8,12},{10,14},{12... | collective-permute-start | bytes 73736 | tf_op jit(solution)/shard_map/ppermute | solution.py:703
  40.7 3.6 %collective-permute-start = (f32[336,128]{1,0:T(8,128)S(1)}, f32[336,128]{1,0:T(8,128)S(1)}, u32[]{:S(2)}, u32[]{:S(2)}) collective-permute-start(f32[336,128]{1,0:T(8,128)S(1)} %get-tuple-element.35), channel_id=1, source_target_pairs={{0,2},{4,6},{2,0},{6,4},{1,3},{5,7},{3,1},{7,5},{8,10},{12,14},{10... | collective-permute-start | bytes 516104 | tf_op jit(solution)/shard_map/ppermute | solution.py:703
  44.3 2.4 %local.4.local_ref = f32[8,128,128]{2,1,0:T(8,128)S(1)} custom-call(s32[3]{0:T(128)S(1)} %pad_add_fusion.info_ref, f32[8,128,128]{2,1,0:T(8,128)S(1)} %get-tuple-element.33.y_ref.refs_5_.refs_0_), custom_call_target="tpu_custom_call" | custom-call | flops 7864320 | bytes 2097152 | tf_op jit(solution)/shard_map/local/pallas_call | solution.py:733
  48.5 11.6 %step.4 = (f32[8,128,128]{2,1,0:T(8,128)S(1)}, bf16[8,1024,256]{2,1,0:T(8,128)(2,1)}, f32[8,64,128]{2,1,0:T(8,128)S(1)}, f32[96,128]{1,0:T(8,128)S(1)}, f32[320,...) custom-call(s32[3]{0:T(128)S(1)} %pad_add_fusion.info_ref, f32[8,128,128]{2,1,0:T(8,128)S(1)} %local.4.local_ref, ...), custom_call_target="tpu_custom_call" | custom-call | tf_op jit(solution)/shard_map/step/pallas_call | solution.py:785
  60.1 2.0 %collective-permute-start.10 = (f32[320,128]{1,0:T(8,128)S(1)}, f32[320,128]{1,0:T(8,128)S(1)}, u32[]{:S(2)}, u32[]{:S(2)}) collective-permute-start(f32[320,128]{1,0:T(8,128)S(1)} %get-tuple-element.43), channel_id=1, source_target_pairs={{0,2},{4,6},{2,0},{6,4},{1,3},{5,7},{3,1},{7,5},{8,10},{12,14},{10... | collective-permute-start | bytes 491528 | tf_op jit(solution)/shard_map/ppermute | solution.py:703
  62.7 2.8 %collective-permute-start.12 = (f32[32,128]{1,0:T(8,128)S(1)}, f32[32,128]{1,0:T(8,128)S(1)}, u32[]{:S(2)}, u32[]{:S(2)}) collective-permute-start(f32[32,128]{1,0:T(8,128)S(1)} %get-tuple-element.45), channel_id=1, source_target_pairs={{0,4},{2,6},{4,0},{6,2},{1,5},{3,7},{5,1},{7,3},{8,12},{10,14},{12... | collective-permute-start | bytes 49160 | tf_op jit(solution)/shard_map/ppermute | solution.py:703
  65.5 2.4 %local.5.local_ref = f32[8,128,128]{2,1,0:T(8,128)S(1)} custom-call(s32[3]{0:T(128)S(1)} %pad_add_fusion.info_ref, f32[8,128,128]{2,1,0:T(8,128)S(1)} %get-tuple-element.40.y_ref.refs_0_, f32[8,128,128]{2,1,0:T(8,128)S(1)} %get-tuple-element.33.y_ref.refs_5_.refs_0_, f32[8,64,128]{2,1,0:T(8,128)S(1)} %get-tuple-element.41.refs_1_), custom_call_target="tpu_custom_call" | custom-call | flops 7864320 | bytes 2097152 | tf_op jit(solution)/shard_map/local/pallas_call | solution.py:733
  68.9 9.6 %step.5 = (f32[8,128,128]{2,1,0:T(8,128)S(1)}, f32[96,128]{1,0:T(8,128)S(1)}, f32[320,128]{1,0:T(8,128)S(1)}, f32[320,128]{1,0:T(8,128)S(1)}, f32[32,128]{1,0:T(8,128)S(1)}) custom-call(s32[3]{0:T(128)S(1)} %pad_add_fusion.info_ref, f32[8,128,128]{2,1,0:T(8,128)S(1)} %local.5.local_ref, f32[96,128]{1,0:T(8,128)S(1)} %get-tuple-element.42.refs_0_, ...), custom_call_target="tpu_custom_call" | custom-call | tf_op jit(solution)/shard_map/step/pallas_call | solution.py:785
  80.3 3.7 %collective-permute-start.15 = (f32[32,128]{1,0:T(8,128)S(1)}, f32[32,128]{1,0:T(8,128)S(1)}, u32[]{:S(2)}, u32[]{:S(2)}) collective-permute-start(f32[32,128]{1,0:T(8,128)S(1)} %get-tuple-element.51), channel_id=1, source_target_pairs={{0,4},{2,6},{4,0},{6,2},{1,5},{3,7},{5,1},{7,3},{8,12},{10,14},{12... | collective-permute-start | bytes 49160 | tf_op jit(solution)/shard_map/ppermute | solution.py:703
  84.0 2.4 %local.6.local_ref = f32[8,128,128]{2,1,0:T(8,128)S(1)} custom-call(s32[3]{0:T(128)S(1)} %pad_add_fusion.info_ref, f32[8,128,128]{2,1,0:T(8,128)S(1)} %get-tuple-element.47.y_ref.refs_0_, f32[8,128,128]{2,1,0:T(8,128)S(1)} %get-tuple-element.40.y_ref.refs_0_, f32[8,64,128]{2,1,0:T(8,128)S(1)} %get-tuple-element.41.refs_1_), custom_call_target="tpu_custom_call" | custom-call | flops 7864320 | bytes 2097152 | tf_op jit(solution)/shard_map/local/pallas_call | solution.py:733
  87.4 9.6 %step.6 = (f32[8,128,128]{2,1,0:T(8,128)S(1)}, f32[96,128]{1,0:T(8,128)S(1)}, f32[320,128]{1,0:T(8,128)S(1)}, f32[320,128]{1,0:T(8,128)S(1)}, f32[32,128]{1,0:T(8,128)S(1)}) custom-call(s32[3]{0:T(128)S(1)} %pad_add_fusion.info_ref, f32[8,128,128]{2,1,0:T(8,128)S(1)} %local.6.local_ref, f32[96,128]{1,0:T(8,128)S(1)} %get-tuple-element.48.refs_0_, ...), custom_call_target="tpu_custom_call" | custom-call | tf_op jit(solution)/shard_map/step/pallas_call | solution.py:785
  99.0 3.5 %collective-permute-start.18 = (f32[32,128]{1,0:T(8,128)S(1)}, f32[32,128]{1,0:T(8,128)S(1)}, u32[]{:S(2)}, u32[]{:S(2)}) collective-permute-start(f32[32,128]{1,0:T(8,128)S(1)} %get-tuple-element.56), channel_id=1, source_target_pairs={{0,4},{2,6},{4,0},{6,2},{1,5},{3,7},{5,1},{7,3},{8,12},{10,14},{12... | collective-permute-start | bytes 49160 | tf_op jit(solution)/shard_map/ppermute | solution.py:703
  102.5 2.4 %local.7.local_ref = f32[8,128,128]{2,1,0:T(8,128)S(1)} custom-call(s32[3]{0:T(128)S(1)} %pad_add_fusion.info_ref, f32[8,128,128]{2,1,0:T(8,128)S(1)} %get-tuple-element.52.y_ref, f32[8,128,128]{2,1,0:T(8,128)S(1)} %get-tuple-element.47.y_ref.refs_0_, f32[8,64,128]{2,1,0:T(8,128)S(1)} %get-tuple-element.41.refs_1_), custom_call_target="tpu_custom_call" | custom-call | flops 7864320 | bytes 2097152 | tf_op jit(solution)/shard_map/local/pallas_call | solution.py:733
  105.9 5.0 %step.7 = f32[8,128,128]{2,1,0:T(8,128)S(1)} custom-call(s32[3]{0:T(128)S(1)} %pad_add_fusion.info_ref, f32[8,128,128]{2,1,0:T(8,128)S(1)} %local.7.local_ref, f32[96,128]{1,0:T(8,128)S(1)} %get-tuple-element.53.refs_0_, f32[320,128]{1,0:T(8,128)S(1)} %collective-permute-done.16.refs_1_, f32[320,128]{1,0:T(8,128)S(1)} %collective-permute-done.17.refs_2_, ...), custom_call_target="tpu_custom_call" | custom-call | tf_op jit(solution)/shard_map/step/pallas_call | solution.py:785
  111.6 1.8 %collective-permute-start.24 = (f32[1,128,128]{2,1,0:T(8,128)S(1)}, f32[1,128,128]{2,1,0:T(8,128)S(1)}, u32[]{:S(2)}, u32[]{:S(2)}) collective-permute-start(f32[1,128,128]{2,1,0:T(8,128)S(1)} %get-tuple-element.60), channel_id=1, source_target_pairs={{0,24},{1,25},{8,16},{9,17},{16,8},{17,9},{24,0},{25,1},{2,26},{3,... | collective-permute-start | bytes 196616 | tf_op jit(solution)/shard_map/ppermute | solution.py:809
  118.5 2.1 %collective-permute-done.21.refs_3_ = f32[1,128,128]{2,1,0:T(8,128)S(1)} collective-permute-done((f32[1,128,128]{2,1,0:T(8,128)S(1)}, f32[1,128,128]{2,1,0:T(8,128)S(1)}, u32[]{:S(2)}, u32[]{:S(2)}) %collective-permute-start.21) | collective-permute-done | bytes 65568 | tf_op jit(solution)/shard_map/ppermute | solution.py:809
  122.6 2.6 %place.1 = f32[8,128,128]{2,1,0:T(8,128)} custom-call(s32[3]{0:T(128)} %copy-done.2, f32[1,128,128]{2,1,0:T(8,128)} %get-tuple-element.66.refs_0_, f32[1,128,128]{2,1,0:T(8,128)} %copy-done.10, f32[1,128,128]{2,1,0:T(8,128)} %copy-done.9, f32[1,128,128]{2,1,0:T(8,128)} %copy-done.8, f32[1,128,128]{2,1,0:T(8,128)} %copy-done.7, f32[1,128,128]{2,1,0:T(8,128)} %copy-done.6, ...), custom_call_target="tpu_custom_call" | custom-call | tf_op jit(solution)/shard_map/place/pallas_call | solution.py:811
  (96 shorter events, 29.9 us)
Async XLA Ops:
  2.1 10.0 %collective-permute-start.6 = (f32[1,576,128]{2,1,0:T(8,128)S(1)}, f32[1,576,128]{2,1,0:T(8,128)S(1)}, u32[]{:S(2)}, u32[]{:S(2)}) collective-permute-start(f32[1,576,128]{2,1,0:T(8,128)S(1)} %get-tuple-element.32.part_b_ref), channel_id=1, source_target_pairs={{0,16},{8,24},{16,0},{24,8},{1,17},{9,25},{17,1},{25,9},{2,18},{10... | collective-permute-start | bytes 884744 | tf_op jit(solution)/shard_map/ppermute | solution.py:549
  5.1 8.9 %collective-permute-start.4 = (f32[1,512,128]{2,1,0:T(8,128)S(1)}, f32[1,512,128]{2,1,0:T(8,128)S(1)}, u32[]{:S(2)}, u32[]{:S(2)}) collective-permute-start(f32[1,512,128]{2,1,0:T(8,128)S(1)} %get-tuple-element.31.part_a_ref), channel_id=1, source_target_pairs={{0,1},{1,0},{2,3},{3,2},{4,5},{5,4},{6,7},{7,6},{8,9},{9,8},{10,11... | collective-permute-start | bytes 786440 | tf_op jit(solution)/shard_map/ppermute | solution.py:549
  12.2 16.0 %collective-permute-start.7 = (f32[2,576,128]{2,1,0:T(8,128)S(1)}, f32[2,576,128]{2,1,0:T(8,128)S(1)}, u32[]{:S(2)}, u32[]{:S(2)}) collective-permute-start(f32[2,576,128]{2,1,0:T(8,128)S(1)} %constant_dynamic-update-slice_fusion.3), channel_id=1, source_target_pairs={{0,1},{1,0},{2,3},{3,2},{4,5},{5,4},{6,7},{7,6},{8,9},{9,8},{10,11... | collective-permute-start | bytes 1769480 | tf_op jit(solution)/shard_map/ppermute | solution.py:549
  14.8 14.5 %collective-permute-start.5 = (f32[2,512,128]{2,1,0:T(8,128)}, f32[2,512,128]{2,1,0:T(8,128)}, u32[]{:S(2)}, u32[]{:S(2)}) collective-permute-start(f32[2,512,128]{2,1,0:T(8,128)} %pad_maximum_fusion.1), channel_id=1, source_target_pairs={{0,16},{8,24},{16,0},{24,8},{1,17},{9,25},{17,1},{25,9},{2,18},{10... | collective-permute-start | bytes 1572872 | tf_op jit(solution)/shard_map/ppermute | solution.py:549
  19.4 14.9 %all-to-all-start = ((f32[8,152,128]{2,1,0:T(8,128)}), f32[8,152,128]{2,1,0:T(8,128)S(1)}, u32[]{:S(2)}, u32[]{:S(2)}) async-start(f32[8,152,128]{2,1,0:T(8,128)} %own_tiles.1), calls=%async_computation | async-start | bytes 1245184 | tf_op jit(solution)/shard_map/all_to_all | solution.py:637
  29.3 19.1 %collective-permute-start.9 = (f32[4,576,128]{2,1,0:T(8,128)}, f32[4,576,128]{2,1,0:T(8,128)}, u32[]{:S(2)}, u32[]{:S(2)}) collective-permute-start(f32[4,576,128]{2,1,0:T(8,128)} %bitcast.12.refs_7_), channel_id=1, source_target_pairs={{0,8},{8,0},{16,24},{24,16},{1,9},{9,1},{17,25},{25,17},{2,10},{10... | collective-permute-start | bytes 3538952 | tf_op jit(solution)/shard_map/ppermute | solution.py:549
  30.4 18.0 %collective-permute-start.8 = (f32[4,512,128]{2,1,0:T(8,128)S(1)}, f32[4,512,128]{2,1,0:T(8,128)S(1)}, u32[]{:S(2)}, u32[]{:S(2)}) collective-permute-start(f32[4,512,128]{2,1,0:T(8,128)S(1)} %constant_dynamic-update-slice_fusion.refs_6_), channel_id=1, source_target_pairs={{0,8},{8,0},{16,24},{24,16},{1,9},{9,1},{17,25},{25,17},{2,10},{10... | collective-permute-start | bytes 3145736 | tf_op jit(solution)/shard_map/ppermute | solution.py:549
  35.9 4.8 %collective-permute-start.2 = (f32[48,128]{1,0:T(8,128)S(1)}, f32[48,128]{1,0:T(8,128)S(1)}, u32[]{:S(2)}, u32[]{:S(2)}) collective-permute-start(f32[48,128]{1,0:T(8,128)S(1)} %get-tuple-element.37), channel_id=1, source_target_pairs={{0,4},{2,6},{4,0},{6,2},{1,5},{3,7},{5,1},{7,3},{8,12},{10,14},{12... | collective-permute-start | bytes 73736 | tf_op jit(solution)/shard_map/ppermute | solution.py:703
  38.6 9.0 %collective-permute-start.3 = (f32[16,128]{1,0:T(8,128)S(1)}, f32[16,128]{1,0:T(8,128)S(1)}, u32[]{:S(2)}, u32[]{:S(2)}) collective-permute-start(f32[16,128]{1,0:T(8,128)S(1)} %slice.33.refs_0_), channel_id=1, source_target_pairs={{0,6},{2,4},{4,2},{6,0},{1,7},{3,5},{5,3},{7,1},{8,14},{10,12},{12... | collective-permute-start | bytes 24584 | tf_op jit(solution)/shard_map/ppermute | solution.py:724
  40.0 8.5 %collective-permute-start.1 = (f32[320,128]{1,0:T(8,128)S(1)}, f32[320,128]{1,0:T(8,128)S(1)}, u32[]{:S(2)}, u32[]{:S(2)}) collective-permute-start(f32[320,128]{1,0:T(8,128)S(1)} %get-tuple-element.36), channel_id=1, source_target_pairs={{2,4},{4,2},{3,5},{5,3},{10,12},{12,10},{11,13},{13,11},{18,20},{2... | collective-permute-start | bytes 491528 | tf_op jit(solution)/shard_map/ppermute | solution.py:703
  40.7 6.9 %collective-permute-start = (f32[336,128]{1,0:T(8,128)S(1)}, f32[336,128]{1,0:T(8,128)S(1)}, u32[]{:S(2)}, u32[]{:S(2)}) collective-permute-start(f32[336,128]{1,0:T(8,128)S(1)} %get-tuple-element.35), channel_id=1, source_target_pairs={{0,2},{4,6},{2,0},{6,4},{1,3},{5,7},{3,1},{7,5},{8,10},{12,14},{10... | collective-permute-start | bytes 516104 | tf_op jit(solution)/shard_map/ppermute | solution.py:703
  60.1 8.8 %collective-permute-start.10 = (f32[320,128]{1,0:T(8,128)S(1)}, f32[320,128]{1,0:T(8,128)S(1)}, u32[]{:S(2)}, u32[]{:S(2)}) collective-permute-start(f32[320,128]{1,0:T(8,128)S(1)} %get-tuple-element.43), channel_id=1, source_target_pairs={{0,2},{4,6},{2,0},{6,4},{1,3},{5,7},{3,1},{7,5},{8,10},{12,14},{10... | collective-permute-start | bytes 491528 | tf_op jit(solution)/shard_map/ppermute | solution.py:703
  62.1 6.8 %collective-permute-start.11 = (f32[320,128]{1,0:T(8,128)S(1)}, f32[320,128]{1,0:T(8,128)S(1)}, u32[]{:S(2)}, u32[]{:S(2)}) collective-permute-start(f32[320,128]{1,0:T(8,128)S(1)} %get-tuple-element.44), channel_id=1, source_target_pairs={{2,4},{4,2},{3,5},{5,3},{10,12},{12,10},{11,13},{13,11},{18,20},{2... | collective-permute-start | bytes 491528 | tf_op jit(solution)/shard_map/ppermute | solution.py:703
  62.7 6.2 %collective-permute-start.12 = (f32[32,128]{1,0:T(8,128)S(1)}, f32[32,128]{1,0:T(8,128)S(1)}, u32[]{:S(2)}, u32[]{:S(2)}) collective-permute-start(f32[32,128]{1,0:T(8,128)S(1)} %get-tuple-element.45), channel_id=1, source_target_pairs={{0,4},{2,6},{4,0},{6,2},{1,5},{3,7},{5,1},{7,3},{8,12},{10,14},{12... | collective-permute-start | bytes 49160 | tf_op jit(solution)/shard_map/ppermute | solution.py:703
  78.5 8.9 %collective-permute-start.13 = (f32[320,128]{1,0:T(8,128)S(1)}, f32[320,128]{1,0:T(8,128)S(1)}, u32[]{:S(2)}, u32[]{:S(2)}) collective-permute-start(f32[320,128]{1,0:T(8,128)S(1)} %get-tuple-element.49), channel_id=1, source_target_pairs={{0,2},{4,6},{2,0},{6,4},{1,3},{5,7},{3,1},{7,5},{8,10},{12,14},{10... | collective-permute-start | bytes 491528 | tf_op jit(solution)/shard_map/ppermute | solution.py:703
  79.7 7.7 %collective-permute-start.14 = (f32[320,128]{1,0:T(8,128)S(1)}, f32[320,128]{1,0:T(8,128)S(1)}, u32[]{:S(2)}, u32[]{:S(2)}) collective-permute-start(f32[320,128]{1,0:T(8,128)S(1)} %get-tuple-element.50), channel_id=1, source_target_pairs={{2,4},{4,2},{3,5},{5,3},{10,12},{12,10},{11,13},{13,11},{18,20},{2... | collective-permute-start | bytes 491528 | tf_op jit(solution)/shard_map/ppermute | solution.py:703
  80.3 7.0 %collective-permute-start.15 = (f32[32,128]{1,0:T(8,128)S(1)}, f32[32,128]{1,0:T(8,128)S(1)}, u32[]{:S(2)}, u32[]{:S(2)}) collective-permute-start(f32[32,128]{1,0:T(8,128)S(1)} %get-tuple-element.51), channel_id=1, source_target_pairs={{0,4},{2,6},{4,0},{6,2},{1,5},{3,7},{5,1},{7,3},{8,12},{10,14},{12... | collective-permute-start | bytes 49160 | tf_op jit(solution)/shard_map/ppermute | solution.py:703
  97.0 8.9 %collective-permute-start.16 = (f32[320,128]{1,0:T(8,128)S(1)}, f32[320,128]{1,0:T(8,128)S(1)}, u32[]{:S(2)}, u32[]{:S(2)}) collective-permute-start(f32[320,128]{1,0:T(8,128)S(1)} %get-tuple-element.54), channel_id=1, source_target_pairs={{0,2},{4,6},{2,0},{6,4},{1,3},{5,7},{3,1},{7,5},{8,10},{12,14},{10... | collective-permute-start | bytes 491528 | tf_op jit(solution)/shard_map/ppermute | solution.py:703
  98.4 7.6 %collective-permute-start.17 = (f32[320,128]{1,0:T(8,128)S(1)}, f32[320,128]{1,0:T(8,128)S(1)}, u32[]{:S(2)}, u32[]{:S(2)}) collective-permute-start(f32[320,128]{1,0:T(8,128)S(1)} %get-tuple-element.55), channel_id=1, source_target_pairs={{2,4},{4,2},{3,5},{5,3},{10,12},{12,10},{11,13},{13,11},{18,20},{2... | collective-permute-start | bytes 491528 | tf_op jit(solution)/shard_map/ppermute | solution.py:703
  99.0 6.9 %collective-permute-start.18 = (f32[32,128]{1,0:T(8,128)S(1)}, f32[32,128]{1,0:T(8,128)S(1)}, u32[]{:S(2)}, u32[]{:S(2)}) collective-permute-start(f32[32,128]{1,0:T(8,128)S(1)} %get-tuple-element.56), channel_id=1, source_target_pairs={{0,4},{2,6},{4,0},{6,2},{1,5},{3,7},{5,1},{7,3},{8,12},{10,14},{12... | collective-permute-start | bytes 49160 | tf_op jit(solution)/shard_map/ppermute | solution.py:703
  111.6 4.8 %collective-permute-start.25 = (f32[1,128,128]{2,1,0:T(8,128)S(1)}, f32[1,128,128]{2,1,0:T(8,128)S(1)}, u32[]{:S(2)}, u32[]{:S(2)}) collective-permute-start(f32[1,128,128]{2,1,0:T(8,128)S(1)} %get-tuple-element.59), channel_id=1, source_target_pairs={{0,25},{1,24},{8,17},{9,16},{16,9},{17,8},{24,1},{25,0},{2,27},{3,... | collective-permute-start | bytes 196616 | tf_op jit(solution)/shard_map/ppermute | solution.py:809
  111.6 6.0 %collective-permute-start.24 = (f32[1,128,128]{2,1,0:T(8,128)S(1)}, f32[1,128,128]{2,1,0:T(8,128)S(1)}, u32[]{:S(2)}, u32[]{:S(2)}) collective-permute-start(f32[1,128,128]{2,1,0:T(8,128)S(1)} %get-tuple-element.60), channel_id=1, source_target_pairs={{0,24},{1,25},{8,16},{9,17},{16,8},{17,9},{24,0},{25,1},{2,26},{3,... | collective-permute-start | bytes 196616 | tf_op jit(solution)/shard_map/ppermute | solution.py:809
  113.4 5.0 %collective-permute-start.23 = (f32[1,128,128]{2,1,0:T(8,128)S(1)}, f32[1,128,128]{2,1,0:T(8,128)S(1)}, u32[]{:S(2)}, u32[]{:S(2)}) collective-permute-start(f32[1,128,128]{2,1,0:T(8,128)S(1)} %get-tuple-element.61), channel_id=1, source_target_pairs={{0,9},{1,8},{8,1},{9,0},{16,25},{17,24},{24,17},{25,16},{2,11},{3,... | collective-permute-start | bytes 196616 | tf_op jit(solution)/shard_map/ppermute | solution.py:809
  115.0 5.7 %collective-permute-start.21 = (f32[1,128,128]{2,1,0:T(8,128)S(1)}, f32[1,128,128]{2,1,0:T(8,128)S(1)}, u32[]{:S(2)}, u32[]{:S(2)}) collective-permute-start(f32[1,128,128]{2,1,0:T(8,128)S(1)} %get-tuple-element.63), channel_id=1, source_target_pairs={{0,17},{1,16},{8,25},{9,24},{16,1},{17,0},{24,9},{25,8},{2,19},{3,... | collective-permute-start | bytes 196616 | tf_op jit(solution)/shard_map/ppermute | solution.py:809
  (18 other events, 172.8 us)

commit v4 on v3

--- a/solution.py
+++ b/solution.py
@@ -141,59 +141,73 @@
     return lax.dot_general(left, right, (((1,), (1,)), ((), ())), preferred_element_type=jnp.float32)
 
 
-def tile_sums(plan, y_block, stack, columns):
+def tile_sums(plan, y_blocks, stacks, columns):
     on, points, slots, projs = plan.on, plan.points, plan.slots, plan.projs
-    hi, lo = hi_lo(y_block)
-    left = jnp.concatenate(
-        [jnp.concatenate([hi, hi], axis=1), jnp.concatenate([lo, lo], axis=1)], axis=0
-    )
-    both = dot_nt(left, stack)
     rows = on * points
-    mask = columns == lax.broadcasted_iota(jnp.int32, (points, slots), 0)
-    lines = []
-    for p in range(projs):
-        for o in range(on):
-            top = both[o * points : (o + 1) * points, p * slots : (p + 1) * slots]
-            low = both[rows + o * points : rows + (o + 1) * points, p * slots : (p + 1) * slots]
-            lines.append(jnp.sum(jnp.where(mask, top + low, 0.0), axis=0, keepdims=True))
-    return jnp.concatenate(lines, axis=0)
-
-
-def key_sums(plan, partial, hot, group):
-    hi, lo = hi_lo(partial)
-    pieces = []
-    for half in (hi, lo):
-        half = half.astype(jnp.float32)
-        pieces += [jnp.where(group == j, half, 0.0) for j in range(plan.groups)]
-    left = jnp.concatenate(pieces, axis=0).astype(jnp.bfloat16)
-    sums = dot_nt(left, hot)
+    boths = []
+    for y_block, stack in zip(y_blocks, stacks):
+        hi, lo = hi_lo(y_block)
+        left = jnp.concatenate(
+            [jnp.concatenate([hi, hi], axis=1), jnp.concatenate([lo, lo], axis=1)], axis=0
+        )
+        boths.append(dot_nt(left, stack))
+    partials = []
+    for both, column in zip(boths, columns):
+        mask = column == lax.broadcasted_iota(jnp.int32, (points, slots), 0)
+        lines = []
+        for p in range(projs):
+            for o in range(on):
+                here = slice(p * slots, (p + 1) * slots)
+                top = both[o * points : (o + 1) * points, here]
+                low = both[rows + o * points : rows + (o + 1) * points, here]
+                lines.append(jnp.sum(jnp.where(mask, top + low, 0.0), axis=0, keepdims=True))
+        partials.append(jnp.concatenate(lines, axis=0))
+    return partials
+
+
+def key_sums(plan, partials, hots, groups):
+    lefts = []
+    for partial, group in zip(partials, groups):
+        hi, lo = hi_lo(partial)
+        pieces = []
+        for half in (hi, lo):
+            half = half.astype(jnp.float32)
+            pieces += [jnp.where(group == j, half, 0.0) for j in range(plan.groups)]
+        lefts.append(jnp.concatenate(pieces, axis=0).astype(jnp.bfloat16))
+    sums = dot_nt(jnp.concatenate(lefts, axis=1), jnp.concatenate(hots, axis=1))
     rows = plan.groups * plan.features
     return sums[:rows] + sums[rows:]
 
 
-def backward_block(plan, coef_split, stack, hot, group, columns):
+def backward_blocks(plan, coef_split, stacks, hots, groups, columns):
     on, points, slots, projs, f = plan.on, plan.points, plan.slots, plan.projs, plan.features
-    every = dot_nn(coef_split, hot)
+    every = dot_nn(coef_split, jnp.concatenate(hots, axis=1))
     rows = plan.groups * f
-    near = None
-    for j in range(plan.groups):
-        piece = every[j * f : (j + 1) * f] + every[rows + j * f : rows + (j + 1) * f]
-        piece = jnp.where(group == j, piece, 0.0)
-        near = piece if near is None else near + piece
-    mask = columns == lax.broadcasted_iota(jnp.int32, (points, slots), 0)
-    bands = []
-    for o in range(on):
-        pieces = []
-        for p in range(projs):
-            line = near[p * on + o : p * on + o + 1, :]
-            pieces.append(jnp.where(mask, line, 0.0))
-        bands.append(jnp.concatenate(pieces, axis=1))
-    weights = jnp.concatenate(bands, axis=0)
-    hi, lo = hi_lo(weights)
-    four = dot_nn(jnp.concatenate([hi, lo], axis=0), stack)
-    rows = on * points
-    cx = plan.cx
-    return (four[:rows, :cx] + four[rows:, cx:]) + (four[:rows, cx:] + four[rows:, :cx])
+    splits = []
+    for index, (group, column) in enumerate(zip(groups, columns)):
+        here = slice(index * slots, (index + 1) * slots)
+        near = None
+        for j in range(plan.groups):
+            piece = every[j * f : (j + 1) * f, here]
+            piece = piece + every[rows + j * f : rows + (j + 1) * f, here]
+            piece = jnp.where(group == j, piece, 0.0)
+            near = piece if near is None else near + piece
+        mask = column == lax.broadcasted_iota(jnp.int32, (points, slots), 0)
+        bands = []
+        for o in range(on):
+            pieces = []
+            for p in range(projs):
+                line = near[p * on + o : p * on + o + 1, :]
+                pieces.append(jnp.where(mask, line, 0.0))
+            bands.append(jnp.concatenate(pieces, axis=1))
+        hi, lo = hi_lo(jnp.concatenate(bands, axis=0))
+        splits.append(jnp.concatenate([hi, lo], axis=0))
+    fours = [dot_nn(split, stack) for split, stack in zip(splits, stacks)]
+    rows, cx = on * points, plan.cx
+    return [
+        (four[:rows, :cx] + four[rows:, cx:]) + (four[:rows, cx:] + four[rows:, :cx])
+        for four in fours
+    ]
 
 
 def halo_rows(plan, y_block, low):
@@ -338,9 +352,9 @@
     meta = meta_ref[...]
     columns = meta_line(plan, meta, 1).astype(jnp.int32)
     y_rows, f = plan.y_rows, plan.features
-    for part in range(plan.per):
-        y_block = y_ref[part]
-        partial = tile_sums(plan, y_block, stack_ref[...], columns)
+    y_blocks = [y_ref[part] for part in range(plan.per)]
+    partials = tile_sums(plan, y_blocks, [stack_ref[...]] * plan.per, [columns] * plan.per)
+    for part, (y_block, partial) in enumerate(zip(y_blocks, partials)):
         out_ref[part, :y_rows, :] = y_block
         for j in range(plan.slots // LANE):
             row = y_rows + j * f
@@ -363,7 +377,7 @@
     f, y_rows = plan.features, plan.y_rows
     count = plan.slots // LANE
     index = lax.broadcasted_iota(jnp.int32, (LANE, plan.slots), 0)
-    total = None
+    partials, hots, groups = [], [], []
     table_at = plan.halo_rows + 2 * plan.third
     for part in range(plan.per):
         slot = step * plan.per + part
@@ -383,13 +397,15 @@
         partial = jnp.concatenate(
             [in_ref[g, y_rows + j * f : y_rows + (j + 1) * f, :] for j in range(count)], axis=1
         )
-        more = key_sums(plan, partial, hot, group)
-        total = more if total is None else total + more
+        partials.append(partial)
+        hots.append(hot)
+        groups.append(group)
         emit_halo(plan, y_block, slot, odd, even_ref, odd_ref)
         for j in range(plan.coupling_rows):
             line = meta[2 * count + j : 2 * count + j + 1, :]
             even_ref[pl.ds(table_at + j * plan.blocks + slot, 1), :] = line
             far_ref[pl.ds(plan.third + j * plan.blocks + slot, 1), :] = line
+    total = key_sums(plan, partials, hots, groups)
 
     @pl.when(step == 0)
     def _():
@@ -441,7 +457,7 @@
         out_ref[j * plan.features : (j + 1) * plan.features, :] = jnp.concatenate(lines, axis=0)
 
 
-def step_kernel(plan, first, last, info_ref, local_ref, *refs):
+def step_kernel(plan, first, last, base, info_ref, local_ref, *refs):
     received, refs = refs[:5], refs[5:]
     own_in, even_in, odd_in, far_in, scale_ref = received
     if first:
@@ -449,8 +465,9 @@
         refs = refs[5:]
     else:
         stack_ref, refs = refs[0], refs[1:]
-    hot_ref, place_ref, out_ref = refs[:3]
-    refs = refs[3:]
+    hot_ref, place_ref = refs[:2]
+    count = plan.blocks // 2 if last else 1
+    out_refs, refs = refs[2 : 2 + count], refs[2 + count :]
     if first:
         stack_ref, potential_ref = refs[:2]
         refs = refs[2:]
@@ -490,31 +507,37 @@
             unpack(far_a_ref, far_b_ref)
 
     rows = plan.on * plan.cz * REACH
-    sums = None
-    for part in range(plan.per):
-        slot = step * plan.per + part
-        columns, group = place_ref[part, 0:1, :], place_ref[part, 1:2, :]
+    parts = range(plan.per)
+    columns = [place_ref[part, 0:1, :] for part in parts]
+    groups = [place_ref[part, 1:2, :] for part in parts]
+    hots = [hot_ref[part] for part in parts]
+    stacks = [stack_ref[part] for part in parts]
+    projected = backward_blocks(plan, coef_ref[...], stacks, hots, groups, columns)
+    y_blocks = []
+    for part in parts:
+        slot = (base + step) * plan.per + part
         where = pl.ds(pl.multiple_of(slot * rows, SUB), rows)
         from_even, from_odd = even_in[where, :], odd_in[where, :]
         low_rows = jnp.where(odd, from_even, from_odd)
         high_rows = jnp.where(odd, from_odd, from_even)
         halo = halo_part(plan, first, low_rows, high_rows, low_ref.at[part], high_ref.at[part])
-        projected = backward_block(
-            plan, coef_ref[...], stack_ref[part], hot_ref[part], group, columns
-        )
-        y_new = (local_ref[part] + halo) + projected
+        y_new = (local_ref[part] + halo) + projected[part]
         if first:
             potential = factor * potential_ref[part]
             y_new = y_new + jnp.concatenate([potential] * plan.on, axis=0) * y_ref[part]
-        out_ref[part] = y_new
+        y_blocks.append(y_new)
         if last:
-            continue
-        partial = tile_sums(plan, y_new, stack_ref[part], columns)
-        more = key_sums(plan, partial, hot_ref[part], group)
-        sums = more if sums is None else sums + more
-        emit_halo(plan, y_new, slot, odd, even_ref, odd_ref)
+            for other in range(len(out_refs) // plan.per):
+                @pl.when(step == other)
+                def _(other=other, y_new=y_new, part=part):
+                    out_refs[other * plan.per + part][0] = y_new
+        else:
+            out_refs[0][part] = y_new
+            emit_halo(plan, y_new, slot, odd, even_ref, odd_ref)
     if last:
         return
+    partials = tile_sums(plan, y_blocks, stacks, columns)
+    sums = key_sums(plan, partials, hots, groups)
     total_ref = refs[3]
 
     @pl.when(step == 0)
@@ -531,9 +554,17 @@
 
 
 def place_kernel(plan, info_ref, *refs):
-    out_ref = refs[-1]
+    pieces, out_ref, sem = refs[: plan.blocks], refs[plan.blocks], refs[plan.blocks + 1]
+    copies = []
     for slot in range(plan.blocks):
-        out_ref[plan.block_of(slot, info_ref[0])] = refs[slot][0]
+        where = plan.block_of(slot, info_ref[0])
+        copies.append(
+            pltpu.make_async_copy(pieces[slot], out_ref.at[pl.ds(where, 1)], sem.at[slot])
+        )
+    for copy in copies:
+        copy.start()
+    for copy in copies:
+        copy.wait()
 
 
 class Plan:
@@ -581,7 +612,7 @@
         return moved ^ me
 
     plan.block_of = block_of
-    plan.per = 2
+    plan.per = 4
     plan.factor = lambda first: (1.0 if first else 2.0) / HALF_WIDTH
     plan.weight = lambda first, k: -0.5 * plan.factor(first) * stencil_weights[k]
 
@@ -634,22 +665,15 @@
         compiler_params=params,
         name="own_tiles",
     )(part_a, part_b, meta, orbitals.reshape(blocks, y_rows, cx))
-    arrived = lax.all_to_all(messages, ("gx", "gz"), 0, 0, tiled=True)
 
     far_a = exchange(part_a, *rounds[0])
     far_b = exchange(part_b, *rounds[1])
+    far_a, far_b, messages = lax.optimization_barrier((far_a, far_b, messages))
+    arrived = lax.all_to_all(messages, ("gx", "gz"), 0, 0, tiled=True)
     part_a = jnp.concatenate([part_a, far_a], axis=0)
     part_b = jnp.concatenate([part_b, far_b], axis=0)
     far_a = exchange(part_a, *rounds[1])
     far_b = exchange(part_b, *rounds[0])
-    part_a = jnp.concatenate([part_a, far_a], axis=0)
-    part_b = jnp.stack([part_b, far_b], axis=1).reshape((4,) + part_b.shape[1:])
-    for axis, bit in rounds[2:-1]:
-        part_a = jnp.concatenate([part_a, exchange(part_a, axis, bit)], axis=0)
-        part_b = jnp.concatenate([part_b, exchange(part_b, axis, bit)], axis=0)
-    far_a = exchange(part_a, *rounds[-1])
-    far_b = exchange(part_b, *rounds[-1])
-
     me = ix * gz + iz
     home = atom_home.reshape(gx, gy, gz, owned).transpose(1, 0, 2, 3).reshape(gy, blocks * owned)
     home = jnp.pad(home, ((1, 1), (0, 0)))
@@ -696,6 +720,15 @@
         name="first_sums",
     )(info, arrived)
 
+    far_a, far_b, sends[0] = lax.optimization_barrier((far_a, far_b, sends[0]))
+    part_a = jnp.concatenate([part_a, far_a], axis=0)
+    part_b = jnp.stack([part_b, far_b], axis=1).reshape((4,) + part_b.shape[1:])
+    for axis, bit in rounds[2:-1]:
+        part_a = jnp.concatenate([part_a, exchange(part_a, axis, bit)], axis=0)
+        part_b = jnp.concatenate([part_b, exchange(part_b, axis, bit)], axis=0)
+    far_a = exchange(part_a, *rounds[-1])
+    far_b = exchange(part_b, *rounds[-1])
+
     def pairwise(value, pairs):
         pairs = [(a, b) for a, b in pairs if b < gy]
         if not pairs:
@@ -711,7 +744,7 @@
             pairwise(distant, [(i, i + 2) for i in range(gy) if i & 2 == 0]),
         )
 
-    previous = None
+    previous, pieces = None, []
     for repeat in range(DEGREE):
         first, last = repeat == 0, repeat == DEGREE - 1
         received = swap(sends)
@@ -757,66 +790,72 @@
             pltpu.VMEM((per, lines, 2 * SUB, cx), f32),
             pltpu.VMEM((per, lines, 2 * SUB, cx), f32),
         ]
-        in_specs = [each(per, y_rows, cx)] + send_specs(extra) + [full(3 * plan.third, LANE)]
-        arrays = [local, *received, scale]
-        out_shapes, out_specs = [y_shape], [each(per, y_rows, cx)]
-        if first:
-            arrays += [current, part_a, part_b, far_a, far_b]
-            in_specs.append(each(per, y_rows, cx))
-            near_index = lambda i, m: (jnp.minimum(i, half // per - 1), 0, 0)
-            far_index = lambda i, m: (jnp.maximum(i - half // per, 0), 0, 0)
-            for index in (near_index, far_index):
-                for array in (part_a, part_b):
-                    in_specs.append(pl.BlockSpec((per,) + array.shape[1:], index))
-            out_shapes += [
-                jax.ShapeDtypeStruct((blocks, tile_rows, 2 * cx), jnp.bfloat16),
-                jax.ShapeDtypeStruct((blocks, points, cx), f32),
-            ]
-            out_specs += [each(per, tile_rows, 2 * cx), each(per, points, cx)]
-        else:
-            arrays.append(stack)
-            in_specs.append(each(per, tile_rows, 2 * cx))
-        arrays += [hot, places]
-        in_specs += [each(per, LANE, slots), each(per, SUB, slots)]
-        if not last:
-            out_shapes += send_shapes(0)
-            out_specs += send_specs(0)
-            scratch.append(sums_scratch)
-        result = pl.pallas_call(
-            functools.partial(step_kernel, plan, first, last),
-            out_shape=out_shapes,
-            grid_spec=pltpu.PrefetchScalarGridSpec(
-                num_scalar_prefetch=1,
-                grid=(blocks // per,),
-                in_specs=in_specs,
-                out_specs=out_specs,
-                scratch_shapes=scratch,
-            ),
-            compiler_params=params,
-            name="step",
-        )(info, *arrays)
+        for base in (half // per, 0) if last else (0,):
+            slots_at = lambda i, *_, base=base: (i + base, 0, 0)
+            each = lambda count, *shape: pl.BlockSpec((count,) + shape, slots_at)
+            in_specs = [each(per, y_rows, cx)] + send_specs(extra) + [full(3 * plan.third, LANE)]
+            arrays = [local, *received, scale]
+            if first:
+                arrays += [current, part_a, part_b, far_a, far_b]
+                in_specs.append(each(per, y_rows, cx))
+                near_index = lambda i, m: (jnp.minimum(i, half // per - 1), 0, 0)
+                far_index = lambda i, m: (jnp.maximum(i - half // per, 0), 0, 0)
+                for index in (near_index, far_index):
+                    for array in (part_a, part_b):
+                        in_specs.append(pl.BlockSpec((per,) + array.shape[1:], index))
+            else:
+                arrays.append(stack)
+                in_specs.append(each(per, tile_rows, 2 * cx))
+            arrays += [hot, places]
+            in_specs += [each(per, LANE, slots), each(per, SUB, slots)]
+            if last:
+                out_shapes = [jax.ShapeDtypeStruct((1, y_rows, cx), f32)] * half
+                out_specs = [full(1, y_rows, cx)] * half
+            else:
+                out_shapes, out_specs = [y_shape], [each(per, y_rows, cx)]
+            if first:
+                out_shapes += [
+                    jax.ShapeDtypeStruct((blocks, tile_rows, 2 * cx), jnp.bfloat16),
+                    jax.ShapeDtypeStruct((blocks, points, cx), f32),
+                ]
+                out_specs += [each(per, tile_rows, 2 * cx), each(per, points, cx)]
+            if not last:
+                out_shapes += send_shapes(0)
+                out_specs += send_specs(0)
+            result = pl.pallas_call(
+                functools.partial(step_kernel, plan, first, last, base),
+                out_shape=out_shapes,
+                grid_spec=pltpu.PrefetchScalarGridSpec(
+                    num_scalar_prefetch=1,
+                    grid=((half if last else blocks) // per,),
+                    in_specs=in_specs,
+                    out_specs=out_specs,
+                    scratch_shapes=scratch + ([] if last else [sums_scratch]),
+                ),
+                compiler_params=params,
+                name="step",
+            )(info, *arrays)
+            if last:
+                pieces = list(result) + pieces
+        if last:
+            break
         previous, current = current, result[0]
         result = result[1:]
         if first:
             stack, plane_potential, *result = result
         sends = result
 
-    pieces = []
-    for slot in range(blocks):
-        block = current[slot : slot + 1]
-        if slot:
-            moved = block_of(slot, 0)
-            block = lax.ppermute(block, ("gx", "gz"), [(i, i ^ moved) for i in range(blocks)])
-        pieces.append(block)
+    for slot in range(1, blocks):
+        moved = block_of(slot, 0)
+        pairs = [(i, i ^ moved) for i in range(blocks)]
+        pieces[slot] = lax.ppermute(pieces[slot], ("gx", "gz"), pairs)
     turned = pl.pallas_call(
         functools.partial(place_kernel, plan),
         out_shape=y_shape,
-        grid_spec=pltpu.PrefetchScalarGridSpec(
-            num_scalar_prefetch=1,
-            grid=(1,),
-            in_specs=[full(1, y_rows, cx)] * blocks,
-            out_specs=full(blocks, y_rows, cx),
-        ),
+        in_specs=[pl.BlockSpec(memory_space=pltpu.SMEM)]
+        + [pl.BlockSpec(memory_space=pl.ANY)] * blocks,
+        out_specs=pl.BlockSpec(memory_space=pl.ANY),
+        scratch_shapes=[pltpu.SemaphoreType.DMA((blocks,))],
         name="place",
     )(info, *pieces)
     return turned.reshape(norb, cz, cy, cx)

time: 126 us -> 137 us (1.087)
  waiting for transfers between devices: 20.3 us -> 25.2 us
  local copies, waits for them, and re-layouts: 5.65 us -> 8.76 us
  other arithmetic: 1.18 us -> 3.15 us
  Pallas kernels: 53.5 us -> 54.9 us
    pallas_call x1, Pallas kernels: 2.55 us -> 17.7 us  [turned_path(): pl.pallas_call(functools.partial(place_kernel, plan), out_shape=y_shape,...]
    pallas_call x4 -> x5, Pallas kernels: 35.8 us -> 23.5 us  [turned_path(): pl.pallas_call(functools.partial(step_kernel, plan, first, last, base), o...]
    unnamed x35 -> x33, local copies, waits for them, and re-layouts: 2.51 us -> 4.88 us
    all_to_all x1, waiting for transfers between devices: 3.14 us -> 5.22 us  [turned_path(): arrived = lax.all_to_all(messages, ('gx', 'gz'), 0, 0, tiled=True)]
    ppermute x6, waiting for transfers between devices: 9.78 us -> 11.6 us  [exchange(): return lax.ppermute(value, axis, [(i, i ^ bit) for i in range(count)])]
  transfers between devices with their start and end apart: 27 -> 27, of which waited for: 10 -> 12; matrix products, arithmetic and copies ran while one was open for 3% -> 4% of each run, Pallas kernels for 12% -> 11%
where the time goes in v4:
time: 137 us
  Pallas kernels  54.9 us (40%)
  starting transfers between devices  43.6 us (32%)
  waiting for transfers between devices  25.2 us (18%)
  local copies, waits for them, and re-layouts  8.76 us (6%)
  other arithmetic  3.15 us (2%)
    pallas_call x5, Pallas kernels, turned_path(): pl.pallas_call(functools.partial(step_kernel, plan, first, last, base), o...  23.5 us
    ppermute x12, starting transfers between devices, pairwise(): return lax.ppermute(value, 'gy', pairs + [(b, a) for a, b in pairs])  23.3 us
    pallas_call x1, Pallas kernels, turned_path(): pl.pallas_call(functools.partial(place_kernel, plan), out_shape=y_shape,...  17.7 us
    ppermute x6, waiting for transfers between devices, exchange(): return lax.ppermute(value, axis, [(i, i ^ bit) for i in range(count)])  11.6 us
    pallas_call x4, Pallas kernels, turned_path(): pl.pallas_call(functools.partial(local_kernel, plan, first), out_shape=y_...  8.93 us
    ppermute x6, starting transfers between devices, exchange(): return lax.ppermute(value, axis, [(i, i ^ bit) for i in range(count)])  8.51 us
    ppermute x7, starting transfers between devices, turned_path(): pieces[slot] = lax.ppermute(pieces[slot], ('gx', 'gz'), pairs)  6.88 us
    all_to_all x1, waiting for transfers between devices, turned_path(): arrived = lax.all_to_all(messages, ('gx', 'gz'), 0, 0, tiled=True)  5.22 us
  transfers between devices with their start and end apart: 27, of which 12 were waited for; matrix products, arithmetic and copies ran while one was open for 4% of the time, Pallas kernels for 11%

profile of v4, /device:TPU:0, one launch (start us, length us, event | category | flops | bytes accessed | tf_op | source)
XLA Modules:
  0.0 136.7 jit_solution(4623104423630100535)
XLA Ops:
  2.1 3.0 %collective-permute-start = (f32[1,512,128]{2,1,0:T(8,128)S(1)}, f32[1,512,128]{2,1,0:T(8,128)S(1)}, u32[]{:S(2)}, u32[]{:S(2)}) collective-permute-start(f32[1,512,128]{2,1,0:T(8,128)S(1)} %get-tuple-element.45.part_a_ref), channel_id=1, source_target_pairs={{0,1},{1,0},{2,3},{3,2},{4,5},{5,4},{6,7},{7,6},{8,9},{9,8},{10,11... | collective-permute-start | bytes 786440 | tf_op jit(solution)/shard_map/ppermute | solution.py:580
  9.8 2.4 %own_tiles.1 = f32[8,152,128]{2,1,0:T(8,128)} custom-call(f32[1,512,128]{2,1,0:T(8,128)S(1)} %get-tuple-element.45.part_a_ref, f32[1,576,128]{2,1,0:T(8,128)S(1)} %get-tuple-element.46.part_b_ref, f32[8,128]{1,0:T(8,128)S(1)} %select_maximum_fusion.meta_ref, f32[8,128,128]{2,1,0:T(8,128)S(1)} %bitcast.21), custom_call_target="tpu_custom_call" | custom-call | tf_op jit(solution)/shard_map/own_tiles/pallas_call | solution.py:653
  13.6 3.5 %all-to-all-start = ((f32[8,152,128]{2,1,0:T(8,128)}), f32[8,152,128]{2,1,0:T(8,128)S(1)}, u32[]{:S(2)}, u32[]{:S(2)}) async-start(f32[8,152,128]{2,1,0:T(8,128)} %own_tiles.1), calls=%async_computation | async-start | bytes 1245184 | tf_op jit(solution)/shard_map/all_to_all | solution.py:672
  17.9 1.9 %collective-permute-start.3 = (f32[2,576,128]{2,1,0:T(8,128)}, f32[2,576,128]{2,1,0:T(8,128)}, u32[]{:S(2)}, u32[]{:S(2)}) collective-permute-start(f32[2,576,128]{2,1,0:T(8,128)} %constant_dynamic-update-slice_fusion), channel_id=1, source_target_pairs={{0,1},{1,0},{2,3},{3,2},{4,5},{5,4},{6,7},{7,6},{8,9},{9,8},{10,11... | collective-permute-start | bytes 1769480 | tf_op jit(solution)/shard_map/ppermute | solution.py:580
  22.2 5.2 %all-to-all-done.in_ref = f32[8,152,128]{2,1,0:T(8,128)S(1)} async-done(((f32[8,152,128]{2,1,0:T(8,128)}), f32[8,152,128]{2,1,0:T(8,128)S(1)}, u32[]{:S(2)}, u32[]{:S(2)}) %all-to-all-start) | async-done | bytes 622624 | tf_op jit(solution)/shard_map/all_to_all | solution.py:672
  28.7 9.6 %collective-permute-done.2 = f32[2,512,128]{2,1,0:T(8,128)} collective-permute-done((f32[2,512,128]{2,1,0:T(8,128)}, f32[2,512,128]{2,1,0:T(8,128)}, u32[]{:S(2)}, u32[]{:S(2)}) %collective-permute-start.2) | collective-permute-done | bytes 524320 | tf_op jit(solution)/shard_map/ppermute | solution.py:580
  44.0 2.7 %collective-permute-start.6 = (f32[48,128]{1,0:T(8,128)S(1)}, f32[48,128]{1,0:T(8,128)S(1)}, u32[]{:S(2)}, u32[]{:S(2)}) collective-permute-start(f32[48,128]{1,0:T(8,128)S(1)} %get-tuple-element.55), channel_id=1, source_target_pairs={{0,4},{2,6},{4,0},{6,2},{1,5},{3,7},{5,1},{7,3},{8,12},{10,14},{12... | collective-permute-start | bytes 73736 | tf_op jit(solution)/shard_map/ppermute | solution.py:736
  49.0 3.3 %collective-permute-start.4 = (f32[336,128]{1,0:T(8,128)S(1)}, f32[336,128]{1,0:T(8,128)S(1)}, u32[]{:S(2)}, u32[]{:S(2)}) collective-permute-start(f32[336,128]{1,0:T(8,128)S(1)} %get-tuple-element.53), channel_id=1, source_target_pairs={{0,2},{4,6},{2,0},{6,4},{1,3},{5,7},{3,1},{7,5},{8,10},{12,14},{10... | collective-permute-start | bytes 516104 | tf_op jit(solution)/shard_map/ppermute | solution.py:736
  52.5 2.2 %local.4.local_ref = f32[8,128,128]{2,1,0:T(8,128)S(1)} custom-call(s32[3]{0:T(128)S(1)} %pad_add_fusion.info_ref, f32[8,128,128]{2,1,0:T(8,128)S(1)} %get-tuple-element.48.y_ref.refs_5_.refs_0_), custom_call_target="tpu_custom_call" | custom-call | flops 7864320 | bytes 2097152 | tf_op jit(solution)/shard_map/local/pallas_call | solution.py:766
  56.9 8.4 %step.5 = (f32[8,128,128]{2,1,0:T(8,128)S(1)}, bf16[8,1024,256]{2,1,0:T(8,128)(2,1)}, f32[8,64,128]{2,1,0:T(8,128)S(1)}, f32[96,128]{1,0:T(8,128)S(1)}, f32[320,...) custom-call(s32[3]{0:T(128)S(1)} %pad_add_fusion.info_ref, f32[8,128,128]{2,1,0:T(8,128)S(1)} %local.4.local_ref, ...), custom_call_target="tpu_custom_call" | custom-call | tf_op jit(solution)/shard_map/step/pallas_call | solution.py:825
  65.4 1.7 %collective-permute-start.10 = (f32[320,128]{1,0:T(8,128)S(1)}, f32[320,128]{1,0:T(8,128)S(1)}, u32[]{:S(2)}, u32[]{:S(2)}) collective-permute-start(f32[320,128]{1,0:T(8,128)S(1)} %get-tuple-element.63), channel_id=1, source_target_pairs={{0,2},{4,6},{2,0},{6,4},{1,3},{5,7},{3,1},{7,5},{8,10},{12,14},{10... | collective-permute-start | bytes 491528 | tf_op jit(solution)/shard_map/ppermute | solution.py:736
  67.8 3.1 %collective-permute-start.12 = (f32[32,128]{1,0:T(8,128)S(1)}, f32[32,128]{1,0:T(8,128)S(1)}, u32[]{:S(2)}, u32[]{:S(2)}) collective-permute-start(f32[32,128]{1,0:T(8,128)S(1)} %get-tuple-element.65), channel_id=1, source_target_pairs={{0,4},{2,6},{4,0},{6,2},{1,5},{3,7},{5,1},{7,3},{8,12},{10,14},{12... | collective-permute-start | bytes 49160 | tf_op jit(solution)/shard_map/ppermute | solution.py:736
  70.8 2.2 %local.5.local_ref = f32[8,128,128]{2,1,0:T(8,128)S(1)} custom-call(s32[3]{0:T(128)S(1)} %pad_add_fusion.info_ref, f32[8,128,128]{2,1,0:T(8,128)S(1)} %get-tuple-element.60.y_ref.refs_0_, f32[8,128,128]{2,1,0:T(8,128)S(1)} %get-tuple-element.48.y_ref.refs_5_.refs_0_, f32[8,64,128]{2,1,0:T(8,128)S(1)} %get-tuple-element.61.refs_1_), custom_call_target="tpu_custom_call" | custom-call | flops 7864320 | bytes 2097152 | tf_op jit(solution)/shard_map/local/pallas_call | solution.py:766
  74.2 5.8 %step.6 = (f32[8,128,128]{2,1,0:T(8,128)S(1)}, f32[96,128]{1,0:T(8,128)S(1)}, f32[320,128]{1,0:T(8,128)S(1)}, f32[320,128]{1,0:T(8,128)S(1)}, f32[32,128]{1,0:T(8,128)S(1)}) custom-call(s32[3]{0:T(128)S(1)} %pad_add_fusion.info_ref, f32[8,128,128]{2,1,0:T(8,128)S(1)} %local.5.local_ref, f32[96,128]{1,0:T(8,128)S(1)} %get-tuple-element.62.refs_0_, ...), custom_call_target="tpu_custom_call" | custom-call | tf_op jit(solution)/shard_map/step/pallas_call | solution.py:825
  81.8 3.9 %collective-permute-start.15 = (f32[32,128]{1,0:T(8,128)S(1)}, f32[32,128]{1,0:T(8,128)S(1)}, u32[]{:S(2)}, u32[]{:S(2)}) collective-permute-start(f32[32,128]{1,0:T(8,128)S(1)} %get-tuple-element.71), channel_id=1, source_target_pairs={{0,4},{2,6},{4,0},{6,2},{1,5},{3,7},{5,1},{7,3},{8,12},{10,14},{12... | collective-permute-start | bytes 49160 | tf_op jit(solution)/shard_map/ppermute | solution.py:736
  85.7 2.2 %local.6.local_ref = f32[8,128,128]{2,1,0:T(8,128)S(1)} custom-call(s32[3]{0:T(128)S(1)} %pad_add_fusion.info_ref, f32[8,128,128]{2,1,0:T(8,128)S(1)} %get-tuple-element.67.y_ref.refs_0_, f32[8,128,128]{2,1,0:T(8,128)S(1)} %get-tuple-element.60.y_ref.refs_0_, f32[8,64,128]{2,1,0:T(8,128)S(1)} %get-tuple-element.61.refs_1_), custom_call_target="tpu_custom_call" | custom-call | flops 7864320 | bytes 2097152 | tf_op jit(solution)/shard_map/local/pallas_call | solution.py:766
  88.9 6.1 %step.7 = (f32[8,128,128]{2,1,0:T(8,128)S(1)}, f32[96,128]{1,0:T(8,128)S(1)}, f32[320,128]{1,0:T(8,128)S(1)}, f32[320,128]{1,0:T(8,128)S(1)}, f32[32,128]{1,0:T(8,128)S(1)}) custom-call(s32[3]{0:T(128)S(1)} %pad_add_fusion.info_ref, f32[8,128,128]{2,1,0:T(8,128)S(1)} %local.6.local_ref, f32[96,128]{1,0:T(8,128)S(1)} %get-tuple-element.68.refs_0_, ...), custom_call_target="tpu_custom_call" | custom-call | tf_op jit(solution)/shard_map/step/pallas_call | solution.py:825
  96.8 3.7 %collective-permute-start.18 = (f32[32,128]{1,0:T(8,128)S(1)}, f32[32,128]{1,0:T(8,128)S(1)}, u32[]{:S(2)}, u32[]{:S(2)}) collective-permute-start(f32[32,128]{1,0:T(8,128)S(1)} %get-tuple-element.76), channel_id=1, source_target_pairs={{0,4},{2,6},{4,0},{6,2},{1,5},{3,7},{5,1},{7,3},{8,12},{10,14},{12... | collective-permute-start | bytes 49160 | tf_op jit(solution)/shard_map/ppermute | solution.py:736
  100.5 2.2 %local.7.local_ref = f32[8,128,128]{2,1,0:T(8,128)S(1)} custom-call(s32[3]{0:T(128)S(1)} %pad_add_fusion.info_ref, f32[8,128,128]{2,1,0:T(8,128)S(1)} %get-tuple-element.72.y_ref, f32[8,128,128]{2,1,0:T(8,128)S(1)} %get-tuple-element.67.y_ref.refs_0_, f32[8,64,128]{2,1,0:T(8,128)S(1)} %get-tuple-element.61.refs_1_), custom_call_target="tpu_custom_call" | custom-call | flops 7864320 | bytes 2097152 | tf_op jit(solution)/shard_map/local/pallas_call | solution.py:766
  103.9 1.6 %step.9 = (f32[1,128,128]{2,1,0:T(8,128)S(1)}, f32[1,128,128]{2,1,0:T(8,128)S(1)}, f32[1,128,128]{2,1,0:T(8,128)S(1)}, f32[1,128,128]{2,1,0:T(8,128)S(1)}) custom-call(s32[3]{0:T(128)S(1)} %pad_add_fusion.info_ref, f32[8,128,128]{2,1,0:T(8,128)S(1)} %local.7.local_ref, f32[96,128]{1,0:T(8,128)S(1)} %get-tuple-element.73.refs_0_, ...), custom_call_target="tpu_custom_call" | custom-call | tf_op jit(solution)/shard_map/step/pallas_call | solution.py:825
  107.3 1.7 %collective-permute-start.25 = (f32[1,128,128]{2,1,0:T(8,128)S(1)}, f32[1,128,128]{2,1,0:T(8,128)S(1)}, u32[]{:S(2)}, u32[]{:S(2)}) collective-permute-start(f32[1,128,128]{2,1,0:T(8,128)S(1)} %get-tuple-element.84), channel_id=1, source_target_pairs={{0,25},{1,24},{8,17},{9,16},{16,9},{17,8},{24,1},{25,0},{2,27},{3,... | collective-permute-start | bytes 196616 | tf_op jit(solution)/shard_map/ppermute | solution.py:851
  113.1 1.6 %collective-permute-start.21 = (f32[1,128,128]{2,1,0:T(8,128)S(1)}, f32[1,128,128]{2,1,0:T(8,128)S(1)}, u32[]{:S(2)}, u32[]{:S(2)}) collective-permute-start(f32[1,128,128]{2,1,0:T(8,128)S(1)} %get-tuple-element.80), channel_id=1, source_target_pairs={{0,17},{1,16},{8,25},{9,24},{16,1},{17,0},{24,9},{25,8},{2,19},{3,... | collective-permute-start | bytes 196616 | tf_op jit(solution)/shard_map/ppermute | solution.py:851
  115.8 2.4 %collective-permute-done.21.refs_3_ = f32[1,128,128]{2,1,0:T(8,128)S(1)} collective-permute-done((f32[1,128,128]{2,1,0:T(8,128)S(1)}, f32[1,128,128]{2,1,0:T(8,128)S(1)}, u32[]{:S(2)}, u32[]{:S(2)}) %collective-permute-start.21) | collective-permute-done | bytes 65568 | tf_op jit(solution)/shard_map/ppermute | solution.py:851
  118.8 17.7 %place.1 = f32[8,128,128]{2,1,0:T(8,128)} custom-call(s32[3]{0:T(128)} %copy-done.3, f32[1,128,128]{2,1,0:T(8,128)} %copy-done.4, f32[1,128,128]{2,1,0:T(8,128)} %copy-done.10, f32[1,128,128]{2,1,0:T(8,128)} %copy-done.11, f32[1,128,128]{2,1,0:T(8,128)} %copy-done.12, f32[1,128,128]{2,1,0:T(8,128)} %copy-done.6, f32[1,128,128]{2,1,0:T(8,128)} %copy-done.7, ...), custom_call_target="tpu_custom_call" | custom-call | tf_op jit(solution)/shard_map/place/pallas_call | solution.py:852
  (94 shorter events, 37.3 us)
Async XLA Ops:
  2.1 10.8 %collective-permute-start = (f32[1,512,128]{2,1,0:T(8,128)S(1)}, f32[1,512,128]{2,1,0:T(8,128)S(1)}, u32[]{:S(2)}, u32[]{:S(2)}) collective-permute-start(f32[1,512,128]{2,1,0:T(8,128)S(1)} %get-tuple-element.45.part_a_ref), channel_id=1, source_target_pairs={{0,1},{1,0},{2,3},{3,2},{4,5},{5,4},{6,7},{7,6},{8,9},{9,8},{10,11... | collective-permute-start | bytes 786440 | tf_op jit(solution)/shard_map/ppermute | solution.py:580
  5.1 8.5 %collective-permute-start.1 = (f32[1,576,128]{2,1,0:T(8,128)S(1)}, f32[1,576,128]{2,1,0:T(8,128)S(1)}, u32[]{:S(2)}, u32[]{:S(2)}) collective-permute-start(f32[1,576,128]{2,1,0:T(8,128)S(1)} %get-tuple-element.46.part_b_ref), channel_id=1, source_target_pairs={{0,16},{8,24},{16,0},{24,8},{1,17},{9,25},{17,1},{25,9},{2,18},{10... | collective-permute-start | bytes 884744 | tf_op jit(solution)/shard_map/ppermute | solution.py:580
  13.6 13.9 %all-to-all-start = ((f32[8,152,128]{2,1,0:T(8,128)}), f32[8,152,128]{2,1,0:T(8,128)S(1)}, u32[]{:S(2)}, u32[]{:S(2)}) async-start(f32[8,152,128]{2,1,0:T(8,128)} %own_tiles.1), calls=%async_computation | async-start | bytes 1245184 | tf_op jit(solution)/shard_map/all_to_all | solution.py:672
  17.9 21.8 %collective-permute-start.3 = (f32[2,576,128]{2,1,0:T(8,128)}, f32[2,576,128]{2,1,0:T(8,128)}, u32[]{:S(2)}, u32[]{:S(2)}) collective-permute-start(f32[2,576,128]{2,1,0:T(8,128)} %constant_dynamic-update-slice_fusion), channel_id=1, source_target_pairs={{0,1},{1,0},{2,3},{3,2},{4,5},{5,4},{6,7},{7,6},{8,9},{9,8},{10,11... | collective-permute-start | bytes 1769480 | tf_op jit(solution)/shard_map/ppermute | solution.py:580
  20.7 17.7 %collective-permute-start.2 = (f32[2,512,128]{2,1,0:T(8,128)}, f32[2,512,128]{2,1,0:T(8,128)}, u32[]{:S(2)}, u32[]{:S(2)}) collective-permute-start(f32[2,512,128]{2,1,0:T(8,128)} %pad_maximum_fusion.1), channel_id=1, source_target_pairs={{0,16},{8,24},{16,0},{24,8},{1,17},{9,25},{17,1},{25,9},{2,18},{10... | collective-permute-start | bytes 1572872 | tf_op jit(solution)/shard_map/ppermute | solution.py:580
  42.1 14.8 %collective-permute-start.9 = (f32[4,576,128]{2,1,0:T(8,128)}, f32[4,576,128]{2,1,0:T(8,128)}, u32[]{:S(2)}, u32[]{:S(2)}) collective-permute-start(f32[4,576,128]{2,1,0:T(8,128)} %bitcast.12.refs_7_), channel_id=1, source_target_pairs={{0,8},{8,0},{16,24},{24,16},{1,9},{9,1},{17,25},{25,17},{2,10},{10... | collective-permute-start | bytes 3538952 | tf_op jit(solution)/shard_map/ppermute | solution.py:580
  43.2 13.7 %collective-permute-start.8 = (f32[4,512,128]{2,1,0:T(8,128)S(1)}, f32[4,512,128]{2,1,0:T(8,128)}, u32[]{:S(2)}, u32[]{:S(2)}) collective-permute-start(f32[4,512,128]{2,1,0:T(8,128)S(1)} %constant_dynamic-update-slice_fusion.2.refs_6_), channel_id=1, source_target_pairs={{0,8},{8,0},{16,24},{24,16},{1,9},{9,1},{17,25},{25,17},{2,10},{10... | collective-permute-start | bytes 3145736 | tf_op jit(solution)/shard_map/ppermute | solution.py:580
  46.7 9.4 %collective-permute-start.7 = (f32[16,128]{1,0:T(8,128)S(1)}, f32[16,128]{1,0:T(8,128)S(1)}, u32[]{:S(2)}, u32[]{:S(2)}) collective-permute-start(f32[16,128]{1,0:T(8,128)S(1)} %slice.9.refs_0_), channel_id=1, source_target_pairs={{0,6},{2,4},{4,2},{6,0},{1,7},{3,5},{5,3},{7,1},{8,14},{10,12},{12... | collective-permute-start | bytes 24584 | tf_op jit(solution)/shard_map/ppermute | solution.py:757
  48.1 8.8 %collective-permute-start.5 = (f32[320,128]{1,0:T(8,128)S(1)}, f32[320,128]{1,0:T(8,128)S(1)}, u32[]{:S(2)}, u32[]{:S(2)}) collective-permute-start(f32[320,128]{1,0:T(8,128)S(1)} %get-tuple-element.54), channel_id=1, source_target_pairs={{2,4},{4,2},{3,5},{5,3},{10,12},{12,10},{11,13},{13,11},{18,20},{2... | collective-permute-start | bytes 491528 | tf_op jit(solution)/shard_map/ppermute | solution.py:736
  49.0 7.0 %collective-permute-start.4 = (f32[336,128]{1,0:T(8,128)S(1)}, f32[336,128]{1,0:T(8,128)S(1)}, u32[]{:S(2)}, u32[]{:S(2)}) collective-permute-start(f32[336,128]{1,0:T(8,128)S(1)} %get-tuple-element.53), channel_id=1, source_target_pairs={{0,2},{4,6},{2,0},{6,4},{1,3},{5,7},{3,1},{7,5},{8,10},{12,14},{10... | collective-permute-start | bytes 516104 | tf_op jit(solution)/shard_map/ppermute | solution.py:736
  65.4 8.8 %collective-permute-start.10 = (f32[320,128]{1,0:T(8,128)S(1)}, f32[320,128]{1,0:T(8,128)S(1)}, u32[]{:S(2)}, u32[]{:S(2)}) collective-permute-start(f32[320,128]{1,0:T(8,128)S(1)} %get-tuple-element.63), channel_id=1, source_target_pairs={{0,2},{4,6},{2,0},{6,4},{1,3},{5,7},{3,1},{7,5},{8,10},{12,14},{10... | collective-permute-start | bytes 491528 | tf_op jit(solution)/shard_map/ppermute | solution.py:736
  67.1 7.1 %collective-permute-start.11 = (f32[320,128]{1,0:T(8,128)S(1)}, f32[320,128]{1,0:T(8,128)S(1)}, u32[]{:S(2)}, u32[]{:S(2)}) collective-permute-start(f32[320,128]{1,0:T(8,128)S(1)} %get-tuple-element.64), channel_id=1, source_target_pairs={{2,4},{4,2},{3,5},{5,3},{10,12},{12,10},{11,13},{13,11},{18,20},{2... | collective-permute-start | bytes 491528 | tf_op jit(solution)/shard_map/ppermute | solution.py:736
  67.8 6.4 %collective-permute-start.12 = (f32[32,128]{1,0:T(8,128)S(1)}, f32[32,128]{1,0:T(8,128)S(1)}, u32[]{:S(2)}, u32[]{:S(2)}) collective-permute-start(f32[32,128]{1,0:T(8,128)S(1)} %get-tuple-element.65), channel_id=1, source_target_pairs={{0,4},{2,6},{4,0},{6,2},{1,5},{3,7},{5,1},{7,3},{8,12},{10,14},{12... | collective-permute-start | bytes 49160 | tf_op jit(solution)/shard_map/ppermute | solution.py:736
  80.0 8.9 %collective-permute-start.13 = (f32[320,128]{1,0:T(8,128)S(1)}, f32[320,128]{1,0:T(8,128)S(1)}, u32[]{:S(2)}, u32[]{:S(2)}) collective-permute-start(f32[320,128]{1,0:T(8,128)S(1)} %get-tuple-element.69), channel_id=1, source_target_pairs={{0,2},{4,6},{2,0},{6,4},{1,3},{5,7},{3,1},{7,5},{8,10},{12,14},{10... | collective-permute-start | bytes 491528 | tf_op jit(solution)/shard_map/ppermute | solution.py:736
  80.9 8.0 %collective-permute-start.14 = (f32[320,128]{1,0:T(8,128)S(1)}, f32[320,128]{1,0:T(8,128)S(1)}, u32[]{:S(2)}, u32[]{:S(2)}) collective-permute-start(f32[320,128]{1,0:T(8,128)S(1)} %get-tuple-element.70), channel_id=1, source_target_pairs={{2,4},{4,2},{3,5},{5,3},{10,12},{12,10},{11,13},{13,11},{18,20},{2... | collective-permute-start | bytes 491528 | tf_op jit(solution)/shard_map/ppermute | solution.py:736
  81.8 7.1 %collective-permute-start.15 = (f32[32,128]{1,0:T(8,128)S(1)}, f32[32,128]{1,0:T(8,128)S(1)}, u32[]{:S(2)}, u32[]{:S(2)}) collective-permute-start(f32[32,128]{1,0:T(8,128)S(1)} %get-tuple-element.71), channel_id=1, source_target_pairs={{0,4},{2,6},{4,0},{6,2},{1,5},{3,7},{5,1},{7,3},{8,12},{10,14},{12... | collective-permute-start | bytes 49160 | tf_op jit(solution)/shard_map/ppermute | solution.py:736
  95.0 8.9 %collective-permute-start.16 = (f32[320,128]{1,0:T(8,128)S(1)}, f32[320,128]{1,0:T(8,128)S(1)}, u32[]{:S(2)}, u32[]{:S(2)}) collective-permute-start(f32[320,128]{1,0:T(8,128)S(1)} %get-tuple-element.74), channel_id=1, source_target_pairs={{0,2},{4,6},{2,0},{6,4},{1,3},{5,7},{3,1},{7,5},{8,10},{12,14},{10... | collective-permute-start | bytes 491528 | tf_op jit(solution)/shard_map/ppermute | solution.py:736
  96.1 7.8 %collective-permute-start.17 = (f32[320,128]{1,0:T(8,128)S(1)}, f32[320,128]{1,0:T(8,128)S(1)}, u32[]{:S(2)}, u32[]{:S(2)}) collective-permute-start(f32[320,128]{1,0:T(8,128)S(1)} %get-tuple-element.75), channel_id=1, source_target_pairs={{2,4},{4,2},{3,5},{5,3},{10,12},{12,10},{11,13},{13,11},{18,20},{2... | collective-permute-start | bytes 491528 | tf_op jit(solution)/shard_map/ppermute | solution.py:736
  96.8 7.1 %collective-permute-start.18 = (f32[32,128]{1,0:T(8,128)S(1)}, f32[32,128]{1,0:T(8,128)S(1)}, u32[]{:S(2)}, u32[]{:S(2)}) collective-permute-start(f32[32,128]{1,0:T(8,128)S(1)} %get-tuple-element.76), channel_id=1, source_target_pairs={{0,4},{2,6},{4,0},{6,2},{1,5},{3,7},{5,1},{7,3},{8,12},{10,14},{12... | collective-permute-start | bytes 49160 | tf_op jit(solution)/shard_map/ppermute | solution.py:736
  105.5 6.0 %collective-permute-start.22 = (f32[1,128,128]{2,1,0:T(8,128)S(1)}, f32[1,128,128]{2,1,0:T(8,128)S(1)}, u32[]{:S(2)}, u32[]{:S(2)}) collective-permute-start(f32[1,128,128]{2,1,0:T(8,128)S(1)} %get-tuple-element.81), channel_id=1, source_target_pairs={{0,8},{1,9},{8,0},{9,1},{16,24},{17,25},{24,16},{25,17},{2,10},{3,... | collective-permute-start | bytes 196616 | tf_op jit(solution)/shard_map/ppermute | solution.py:851
  105.6 7.5 %collective-permute-start.23 = (f32[1,128,128]{2,1,0:T(8,128)S(1)}, f32[1,128,128]{2,1,0:T(8,128)S(1)}, u32[]{:S(2)}, u32[]{:S(2)}) collective-permute-start(f32[1,128,128]{2,1,0:T(8,128)S(1)} %get-tuple-element.82), channel_id=1, source_target_pairs={{0,9},{1,8},{8,1},{9,0},{16,25},{17,24},{24,17},{25,16},{2,11},{3,... | collective-permute-start | bytes 196616 | tf_op jit(solution)/shard_map/ppermute | solution.py:851
  106.1 8.6 %collective-permute-start.24 = (f32[1,128,128]{2,1,0:T(8,128)S(1)}, f32[1,128,128]{2,1,0:T(8,128)S(1)}, u32[]{:S(2)}, u32[]{:S(2)}) collective-permute-start(f32[1,128,128]{2,1,0:T(8,128)S(1)} %get-tuple-element.83), channel_id=1, source_target_pairs={{0,24},{1,25},{8,16},{9,17},{16,8},{17,9},{24,0},{25,1},{2,26},{3,... | collective-permute-start | bytes 196616 | tf_op jit(solution)/shard_map/ppermute | solution.py:851
  107.3 7.4 %collective-permute-start.25 = (f32[1,128,128]{2,1,0:T(8,128)S(1)}, f32[1,128,128]{2,1,0:T(8,128)S(1)}, u32[]{:S(2)}, u32[]{:S(2)}) collective-permute-start(f32[1,128,128]{2,1,0:T(8,128)S(1)} %get-tuple-element.84), channel_id=1, source_target_pairs={{0,25},{1,24},{8,17},{9,16},{16,9},{17,8},{24,1},{25,0},{2,27},{3,... | collective-permute-start | bytes 196616 | tf_op jit(solution)/shard_map/ppermute | solution.py:851
  113.1 5.2 %collective-permute-start.21 = (f32[1,128,128]{2,1,0:T(8,128)S(1)}, f32[1,128,128]{2,1,0:T(8,128)S(1)}, u32[]{:S(2)}, u32[]{:S(2)}) collective-permute-start(f32[1,128,128]{2,1,0:T(8,128)S(1)} %get-tuple-element.80), channel_id=1, source_target_pairs={{0,17},{1,16},{8,25},{9,24},{16,1},{17,0},{24,9},{25,8},{2,19},{3,... | collective-permute-start | bytes 196616 | tf_op jit(solution)/shard_map/ppermute | solution.py:851
  (17 other events, 145.3 us)

commit v5 on v4

--- a/solution.py
+++ b/solution.py
@@ -326,28 +326,42 @@
     return jnp.concatenate([low] + middle + [high], axis=1).reshape(lines * cy, cx)
 
 
-def pack_kernel(plan, tile_ref, potential_ref, part_a_ref, part_b_ref):
-    half = plan.projs // 2
+def pack_kernel(plan, tile_ref, potential_ref, out_ref):
     slots = plan.slots
-    for p in range(half):
-        part_a_ref[0, p * slots : (p + 1) * slots, :] = tile_ref[:, p, :]
-        part_b_ref[0, p * slots : (p + 1) * slots, :] = tile_ref[:, half + p, :]
-    part_b_ref[0, half * slots :, :] = potential_ref[...]
-
-
-def fill_stack(plan, stack_ref, first_rows, second_rows):
-    rows = first_rows.shape[0]
-    for start, value in ((0, first_rows), (rows, second_rows)):
-        hi, lo = hi_lo(value)
-        stack_ref[start : start + rows, : plan.cx] = hi
-        stack_ref[start : start + rows, plan.cx :] = lo
-
-
-def own_tiles_kernel(plan, part_a_ref, part_b_ref, meta_ref, y_ref, out_ref, stack_ref):
+    for p in range(plan.projs):
+        out_ref[p * slots : (p + 1) * slots, :] = tile_ref[:, p, :]
+    out_ref[plan.projs * slots :, :] = potential_ref[...]
+
+
+def own_tiles_kernel(
+    plan, info_ref, payload_ref, atom_ref, column_ref, coupling_ref, y_ref,
+    out_ref, info_out_ref, stack_ref, meta_ref,
+):
+    count = plan.slots // LANE
+
     @pl.when(pl.program_id(0) == 0)
     def _():
-        rows = part_a_ref.shape[1]
-        fill_stack(plan, stack_ref, part_a_ref[0], part_b_ref[0, :rows, :])
+        fill_stack(plan, stack_ref, payload_ref[: plan.projs * plan.slots, :])
+        for i in range(info_out_ref.shape[0]):
+            info_out_ref[i] = info_ref[i]
+        atom, column = atom_ref[...], column_ref[...]
+        owner = lax.shift_right_logical(atom, log2(plan.owned))
+        owner_z = owner & (plan.gz - 1)
+        owner_y = lax.shift_right_logical(owner, log2(plan.gz)) & (plan.gy - 1)
+        owner_x = lax.shift_right_logical(owner, log2(plan.gz) + log2(plan.gy))
+        key = (owner_y - info_ref[3] + 1) * (plan.blocks * plan.owned)
+        key = key + (owner_x * plan.gz + owner_z) * plan.owned + (atom & (plan.owned - 1))
+        lane = lax.broadcasted_iota(jnp.int32, column.shape, 1)
+        column = jnp.where(lane < info_ref[4], column, -1)
+        meta_ref[...] = jnp.zeros_like(meta_ref)
+        for row, line in enumerate((key, column)):
+            line = line.astype(jnp.float32)
+            for i in range(count):
+                at = row * count + i
+                meta_ref[at : at + 1, :] = line[:, i * LANE : (i + 1) * LANE]
+        for p in range(plan.projs):
+            at = 2 * count + p
+            meta_ref[at : at + 1, : plan.owned] = coupling_ref[p : p + 1, :]
 
     meta = meta_ref[...]
     columns = meta_line(plan, meta, 1).astype(jnp.int32)
@@ -356,10 +370,16 @@
     partials = tile_sums(plan, y_blocks, [stack_ref[...]] * plan.per, [columns] * plan.per)
     for part, (y_block, partial) in enumerate(zip(y_blocks, partials)):
         out_ref[part, :y_rows, :] = y_block
-        for j in range(plan.slots // LANE):
+        for j in range(count):
             row = y_rows + j * f
             out_ref[part, row : row + f, :] = partial[:, j * LANE : (j + 1) * LANE]
         out_ref[part, plan.meta_at :, :] = meta
+
+
+def fill_stack(plan, stack_ref, value):
+    hi, lo = hi_lo(value)
+    stack_ref[:, : plan.cx] = hi
+    stack_ref[:, plan.cx :] = lo
 
 
 def meta_line(plan, meta, which):
@@ -452,7 +472,7 @@
         mask = within_index == within_ref[0:1, lanes]
         lines = []
         for p in range(plan.projs):
-            piece = jnp.where(mask, rows[p * owned : (p + 1) * owned], 0.0)
+            piece = jnp.where(mask, rows[p * LANE : p * LANE + owned], 0.0)
             lines += [jnp.sum(piece, axis=0, keepdims=True)] * plan.on
         out_ref[j * plan.features : (j + 1) * plan.features, :] = jnp.concatenate(lines, axis=0)
 
@@ -461,8 +481,7 @@
     received, refs = refs[:5], refs[5:]
     own_in, even_in, odd_in, far_in, scale_ref = received
     if first:
-        y_ref, near_a_ref, near_b_ref, far_a_ref, far_b_ref = refs[:5]
-        refs = refs[5:]
+        y_ref, piece_refs, refs = refs[0], refs[1:11], refs[11:]
     else:
         stack_ref, refs = refs[0], refs[1:]
     hot_ref, place_ref = refs[:2]
@@ -490,21 +509,33 @@
         high_ref[...] = jnp.zeros_like(high_ref)
 
     if first:
-        def unpack(part_a_ref, part_b_ref):
-            tiles = part_a_ref.shape[1]
-            for part in range(plan.per):
-                fill_stack(
-                    plan, stack_ref.at[part], part_a_ref[part], part_b_ref[part, :tiles, :]
-                )
-                potential_ref[part] = part_b_ref[part, tiles:, :]
-
-        @pl.when(step * plan.per < plan.blocks // 2)
+        held_ref, sem = refs[-2:]
+        cut = piece_refs[3].shape[0]
+        copies = []
+        for index, piece in enumerate(piece_refs):
+            side, which = index // 5, index % 5
+            there = held_ref.at[side * (plan.blocks // 2) + min(which, 3)]
+            if which >= 3:
+                there = there.at[pl.ds((which - 3) * cut, cut)]
+            copies.append(pltpu.make_async_copy(piece, there, sem.at[index]))
+
+        @pl.when(step == 0)
         def _():
-            unpack(near_a_ref, near_b_ref)
-
-        @pl.when(step * plan.per >= plan.blocks // 2)
+            for copy in copies:
+                copy.start()
+            for copy in copies[:5]:
+                copy.wait()
+
+        @pl.when(step == 1)
         def _():
-            unpack(far_a_ref, far_b_ref)
+            for copy in copies[5:]:
+                copy.wait()
+
+        tiles = plan.projs * plan.slots
+        for part in range(plan.per):
+            slot = step * plan.per + part
+            fill_stack(plan, stack_ref.at[part], held_ref[slot, :tiles, :])
+            potential_ref[part] = held_ref[slot, tiles:, :]
 
     rows = plan.on * plan.cz * REACH
     parts = range(plan.per)
@@ -553,20 +584,6 @@
         emit_sums(plan, total_ref[...], odd, upper, own_ref, even_ref, odd_ref, far_ref)
 
 
-def place_kernel(plan, info_ref, *refs):
-    pieces, out_ref, sem = refs[: plan.blocks], refs[plan.blocks], refs[plan.blocks + 1]
-    copies = []
-    for slot in range(plan.blocks):
-        where = plan.block_of(slot, info_ref[0])
-        copies.append(
-            pltpu.make_async_copy(pieces[slot], out_ref.at[pl.ds(where, 1)], sem.at[slot])
-        )
-    for copy in copies:
-        copy.start()
-    for copy in copies:
-        copy.wait()
-
-
 class Plan:
     pass
 
@@ -601,7 +618,9 @@
     plan.third = plan.groups // 3 * plan.features
     plan.halo_rows = blocks * on * cz * REACH
     plan.y_rows = on * points
-    plan.coupling_rows = owned * projs // LANE
+    plan.coupling_rows = projs
+    plan.gy = gy
+    meta_rows = -(-(2 * slots // LANE + projs) // SUB) * SUB
     plan.meta_at = plan.y_rows + plan.features * slots // LANE
     rounds = [("gz", 1 << b) for b in range(log2(gz))]
     rounds += [("gx", 1 << b) for b in reversed(range(log2(gx)))]
@@ -612,25 +631,9 @@
         return moved ^ me
 
     plan.block_of = block_of
-    plan.per = 4
+    plan.per = blocks // 2
     plan.factor = lambda first: (1.0 if first else 2.0) / HALF_WIDTH
     plan.weight = lambda first, k: -0.5 * plan.factor(first) * stencil_weights[k]
-
-    live = jnp.arange(slots, dtype=jnp.int32) < tile_count[0]
-    column = jnp.where(live, tile_column, -1)
-    owner = tile_atom // owned
-    owner_x = owner // (gy * gz)
-    owner_y = owner // gz % gy
-    owner_z = owner % gz
-    key = (
-        (owner_y - iy + 1) * (blocks * owned)
-        + (owner_x * gz + owner_z) * owned
-        + tile_atom % owned
-    )
-    lanes = lambda value: value.astype(jnp.float32).reshape(-1, LANE)
-    meta = jnp.concatenate([lanes(key), lanes(column), lanes(coupling.T)], axis=0)
-    meta_rows = -(-meta.shape[0] // SUB) * SUB
-    meta = jnp.pad(meta, ((0, meta_rows - meta.shape[0]), (0, 0)))
 
     f32 = jnp.float32
     per = plan.per
@@ -639,42 +642,58 @@
     full = lambda *shape: pl.BlockSpec(shape, lambda *_: (0,) * len(shape))
     each = lambda count, *shape: pl.BlockSpec((count,) + shape, lambda i, *_: (i, 0, 0))
     params = pltpu.CompilerParams(vmem_limit_bytes=48 * 1024 * 1024)
-    half_rows = tile_rows // 2
-    part_a, part_b = pl.pallas_call(
+    rows = tile_rows + points
+    payload = pl.pallas_call(
         functools.partial(pack_kernel, plan),
-        out_shape=[
-            jax.ShapeDtypeStruct((1, half_rows, cx), f32),
-            jax.ShapeDtypeStruct((1, half_rows + points, cx), f32),
-        ],
+        out_shape=jax.ShapeDtypeStruct((rows, cx), f32),
         compiler_params=params,
         name="pack",
     )(tile_proj, potential.reshape(points, cx))
-
-    messages = pl.pallas_call(
+    me = ix * gz + iz
+    info = jnp.stack([me, iy & 1, (iy >> 1) & 1, iy, tile_count[0]]).astype(jnp.int32)
+
+    from_z = exchange(payload, *rounds[0])
+    from_x = exchange(payload, *rounds[1])
+    from_c = exchange(payload, *rounds[2])
+
+    smem = pl.BlockSpec(memory_space=pltpu.SMEM)
+    messages, late_info = pl.pallas_call(
         functools.partial(own_tiles_kernel, plan),
-        out_shape=jax.ShapeDtypeStruct((blocks, plan.meta_at + meta_rows, cx), f32),
+        out_shape=[
+            jax.ShapeDtypeStruct((blocks, plan.meta_at + meta_rows, cx), f32),
+            jax.ShapeDtypeStruct(info.shape, jnp.int32),
+        ],
         grid=(blocks // per,),
         in_specs=[
-            full(1, half_rows, cx),
-            full(1, half_rows + points, cx),
-            full(meta_rows, LANE),
+            smem,
+            full(rows, cx),
+            full(1, slots),
+            full(1, slots),
+            full(projs, owned),
             each(per, y_rows, cx),
         ],
-        out_specs=each(per, plan.meta_at + meta_rows, cx),
-        scratch_shapes=[pltpu.VMEM((tile_rows, 2 * cx), jnp.bfloat16)],
+        out_specs=[each(per, plan.meta_at + meta_rows, cx), smem],
+        scratch_shapes=[
+            pltpu.VMEM((tile_rows, 2 * cx), jnp.bfloat16),
+            pltpu.VMEM((meta_rows, LANE), f32),
+        ],
         compiler_params=params,
         name="own_tiles",
-    )(part_a, part_b, meta, orbitals.reshape(blocks, y_rows, cx))
-
-    far_a = exchange(part_a, *rounds[0])
-    far_b = exchange(part_b, *rounds[1])
-    far_a, far_b, messages = lax.optimization_barrier((far_a, far_b, messages))
+    )(
+        info,
+        payload,
+        tile_atom.reshape(1, slots),
+        tile_column.reshape(1, slots),
+        coupling.T,
+        orbitals.reshape(blocks, y_rows, cx),
+    )
     arrived = lax.all_to_all(messages, ("gx", "gz"), 0, 0, tiled=True)
-    part_a = jnp.concatenate([part_a, far_a], axis=0)
-    part_b = jnp.concatenate([part_b, far_b], axis=0)
-    far_a = exchange(part_a, *rounds[1])
-    far_b = exchange(part_b, *rounds[0])
-    me = ix * gz + iz
+
+    from_z, from_x, late_info = lax.optimization_barrier((from_z, from_x, late_info))
+    cut = rows // 2
+    from_xz = [exchange(from_z[:cut], *rounds[1]), exchange(from_x[cut:], *rounds[0])]
+    from_core = [from_c, exchange(from_z, *rounds[2]), exchange(from_x, *rounds[2])]
+
     home = atom_home.reshape(gx, gy, gz, owned).transpose(1, 0, 2, 3).reshape(gy, blocks * owned)
     home = jnp.pad(home, ((1, 1), (0, 0)))
     home = lax.dynamic_slice_in_dim(home, iy, 3, axis=0).reshape(1, plan.keys)
@@ -686,7 +705,6 @@
     home_device = (home_y ^ iy) * blocks + place
     home_within = home % owned
 
-    info = jnp.stack([me, iy & 1, (iy >> 1) & 1]).astype(jnp.int32)
     table_rows = plan.coupling_rows * blocks
     message_rows = plan.halo_rows + 2 * plan.third
     half = blocks // 2
@@ -720,15 +738,6 @@
         name="first_sums",
     )(info, arrived)
 
-    far_a, far_b, sends[0] = lax.optimization_barrier((far_a, far_b, sends[0]))
-    part_a = jnp.concatenate([part_a, far_a], axis=0)
-    part_b = jnp.stack([part_b, far_b], axis=1).reshape((4,) + part_b.shape[1:])
-    for axis, bit in rounds[2:-1]:
-        part_a = jnp.concatenate([part_a, exchange(part_a, axis, bit)], axis=0)
-        part_b = jnp.concatenate([part_b, exchange(part_b, axis, bit)], axis=0)
-    far_a = exchange(part_a, *rounds[-1])
-    far_b = exchange(part_b, *rounds[-1])
-
     def pairwise(value, pairs):
         pairs = [(a, b) for a, b in pairs if b < gy]
         if not pairs:
@@ -744,7 +753,7 @@
             pairwise(distant, [(i, i + 2) for i in range(gy) if i & 2 == 0]),
         )
 
-    previous, pieces = None, []
+    previous, blocks_out = None, []
     for repeat in range(DEGREE):
         first, last = repeat == 0, repeat == DEGREE - 1
         received = swap(sends)
@@ -784,6 +793,10 @@
             ),
             name="local",
         )(info, current, *([] if first else [previous, plane_potential]))
+        if first:
+            *from_xz, local = lax.optimization_barrier((*from_xz, local))
+            pieces = [payload, from_z, from_x, *from_xz]
+            pieces += from_core + [exchange(part, *rounds[2]) for part in from_xz]
         lines = on * cz
         scratch = [
             pltpu.VMEM((6 * plan.third, LANE), jnp.bfloat16),
@@ -796,13 +809,9 @@
             in_specs = [each(per, y_rows, cx)] + send_specs(extra) + [full(3 * plan.third, LANE)]
             arrays = [local, *received, scale]
             if first:
-                arrays += [current, part_a, part_b, far_a, far_b]
+                arrays += [current, *pieces]
                 in_specs.append(each(per, y_rows, cx))
-                near_index = lambda i, m: (jnp.minimum(i, half // per - 1), 0, 0)
-                far_index = lambda i, m: (jnp.maximum(i - half // per, 0), 0, 0)
-                for index in (near_index, far_index):
-                    for array in (part_a, part_b):
-                        in_specs.append(pl.BlockSpec((per,) + array.shape[1:], index))
+                in_specs += [pl.BlockSpec(memory_space=pl.ANY)] * len(pieces)
             else:
                 arrays.append(stack)
                 in_specs.append(each(per, tile_rows, 2 * cx))
@@ -822,6 +831,10 @@
             if not last:
                 out_shapes += send_shapes(0)
                 out_specs += send_specs(0)
+            held = []
+            if first:
+                held = [pltpu.VMEM((blocks, rows, cx), f32)]
+                held.append(pltpu.SemaphoreType.DMA((len(pieces),)))
             result = pl.pallas_call(
                 functools.partial(step_kernel, plan, first, last, base),
                 out_shape=out_shapes,
@@ -830,13 +843,13 @@
                     grid=((half if last else blocks) // per,),
                     in_specs=in_specs,
                     out_specs=out_specs,
-                    scratch_shapes=scratch + ([] if last else [sums_scratch]),
+                    scratch_shapes=scratch + ([] if last else [sums_scratch]) + held,
                 ),
                 compiler_params=params,
                 name="step",
-            )(info, *arrays)
+            )(late_info, *arrays)
             if last:
-                pieces = list(result) + pieces
+                blocks_out = list(result) + blocks_out
         if last:
             break
         previous, current = current, result[0]
@@ -845,19 +858,12 @@
             stack, plane_potential, *result = result
         sends = result
 
-    for slot in range(1, blocks):
-        moved = block_of(slot, 0)
-        pairs = [(i, i ^ moved) for i in range(blocks)]
-        pieces[slot] = lax.ppermute(pieces[slot], ("gx", "gz"), pairs)
-    turned = pl.pallas_call(
-        functools.partial(place_kernel, plan),
-        out_shape=y_shape,
-        in_specs=[pl.BlockSpec(memory_space=pltpu.SMEM)]
-        + [pl.BlockSpec(memory_space=pl.ANY)] * blocks,
-        out_specs=pl.BlockSpec(memory_space=pl.ANY),
-        scratch_shapes=[pltpu.SemaphoreType.DMA((blocks,))],
-        name="place",
-    )(info, *pieces)
+    turned = jnp.zeros((blocks, y_rows, cx), f32)
+    for slot, block in enumerate(blocks_out):
+        if slot:
+            moved = block_of(slot, 0)
+            block = lax.ppermute(block, ("gx", "gz"), [(i, i ^ moved) for i in range(blocks)])
+        turned = lax.dynamic_update_slice(turned, block, (block_of(slot, me), 0, 0))
     return turned.reshape(norb, cz, cy, cx)
 
 
@@ -875,10 +881,10 @@
     turned = all(power_of_two(size) for size in (gx, gy, gz)) and gx > 1 and gz > 1 and gy <= 4
     turned = turned and norb % blocks == 0 and cx == LANE and slots % LANE == 0
     if turned:
-        turned = (norb // blocks * projs) % SUB == 0 and (owned * projs) % LANE == 0
-        turned = turned and owned % SUB == 0 and blocks % SUB == 0
+        turned = (norb // blocks * projs) % SUB == 0 and power_of_two(owned) and owned <= LANE
+        turned = turned and owned % SUB == 0 and blocks == 2 * 2 * 2
         turned = turned and (blocks * owned) % LANE == 0 and cy % SUB == 0 and cy >= 2 * SUB
-        turned = turned and cz % 2 == 0 and projs % 2 == 0 and blocks % 4 == 0
+        turned = turned and cz % 2 == 0 and (projs * slots + cz * cy) % (2 * SUB) == 0
     return turned_path(*arguments) if turned else general_path(*arguments)
 
 

time: 137 us -> 109 us (0.80)
  Pallas kernels: 54.9 us -> 34.6 us
  waiting for transfers between devices: 25.2 us -> 18.5 us
  local copies, waits for them, and re-layouts: 8.76 us -> 13.9 us
  other arithmetic: 3.15 us -> 0.16 us
  starting transfers between devices: 43.6 us -> 40.7 us
    pallas_call x3 -> x2, Pallas kernels: 20.4 us -> 3.19 us  [the longest x1 2.92 us: turned_path(): pl.pallas_call(functools.partial(own_tiles_kernel, plan), out_shape=[jax....]
    ppermute x6 -> x9, waiting for transfers between devices: 11.6 us -> 2.32 us  [exchange(): return lax.ppermute(value, axis, [(i, i ^ bit) for i in range(count)])]
    unnamed x33 -> x24, local copies, waits for them, and re-layouts: 4.88 us -> 8.9 us
    pallas_call x5 -> x4, Pallas kernels: 23.5 us -> 19.8 us  [turned_path(): pl.pallas_call(functools.partial(step_kernel, plan, first, last, base), o...]
    pallas_call x0 -> x1, local copies, waits for them, and re-layouts: none -> 3.14 us  [turned_path(): pl.pallas_call(functools.partial(step_kernel, plan, first, last, base), o...]
    ppermute x7, waiting for transfers between devices: 3.53 us -> 5.62 us  [turned_path(): lax.ppermute(block, ('gx', 'gz'), [(i, i ^ moved) for i in range(blocks)])]
    concatenate x2 -> x0, local copies, waits for them, and re-layouts: 1.82 us -> none  [the longest x1 1.08 us: turned_path(): part_a = jnp.concatenate([part_a, far_a], axis=0)]
    slice x0 -> x2, local copies, waits for them, and re-layouts: none -> 1.45 us  [the longest x1 0.73 us: turned_path(): from_z[:cut]]
  transfers between devices with their start and end apart: 27 -> 30, of which waited for: 12 -> 12; matrix products, arithmetic and copies ran while one was open for 4% -> 2% of each run, Pallas kernels for 11% -> 15%
where the time goes in v5:
time: 109 us
  starting transfers between devices  40.7 us (37%)
  Pallas kernels  34.6 us (32%)
  waiting for transfers between devices  18.5 us (17%)
  local copies, waits for them, and re-layouts  13.9 us (13%)
    ppermute x12, starting transfers between devices, pairwise(): return lax.ppermute(value, 'gy', pairs + [(b, a) for a, b in pairs])  23.2 us
    pallas_call x4, Pallas kernels, turned_path(): pl.pallas_call(functools.partial(step_kernel, plan, first, last, base), o...  19.8 us
    unnamed x24, local copies, waits for them, and re-layouts  8.9 us
    pallas_call x4, Pallas kernels, turned_path(): pl.pallas_call(functools.partial(local_kernel, plan, first), out_shape=y_...  8.86 us
    ppermute x9, starting transfers between devices, exchange(): return lax.ppermute(value, axis, [(i, i ^ bit) for i in range(count)])  7.11 us
    ppermute x7, waiting for transfers between devices, turned_path(): lax.ppermute(block, ('gx', 'gz'), [(i, i ^ moved) for i in range(blocks)])  5.62 us
    ppermute x7, starting transfers between devices, turned_path(): lax.ppermute(block, ('gx', 'gz'), [(i, i ^ moved) for i in range(blocks)])  5.52 us
    ppermute x12, waiting for transfers between devices, pairwise(): return lax.ppermute(value, 'gy', pairs + [(b, a) for a, b in pairs])  4.91 us
  transfers between devices with their start and end apart: 30, of which 12 were waited for; matrix products, arithmetic and copies ran while one was open for 2% of the time, Pallas kernels for 15%

profile of v5, /device:TPU:0, one launch (start us, length us, event | category | flops | bytes accessed | tf_op | source)
XLA Modules:
  0.0 108.8 jit_solution(4078227608961492099)
XLA Ops:
  2.1 3.0 %collective-permute-start = (f32[1088,128]{1,0:T(8,128)S(1)}, f32[1088,128]{1,0:T(8,128)S(1)}, u32[]{:S(2)}, u32[]{:S(2)}) collective-permute-start(f32[1088,128]{1,0:T(8,128)S(1)} %pack.1.payload_ref.refs_6_), channel_id=1, source_target_pairs={{0,1},{1,0},{2,3},{3,2},{4,5},{5,4},{6,7},{7,6},{8,9},{9,8},{10,11... | collective-permute-start | bytes 1671176 | tf_op jit(solution)/shard_map/ppermute | solution.py:597
  10.4 2.9 %own_tiles.1 = (f32[8,152,128]{2,1,0:T(8,128)}, s32[5]{0:T(128)S(1)}) custom-call(s32[5]{0:T(128)S(1)} %stack.19.info_ref, f32[1088,128]{1,0:T(8,128)S(1)} %pack.1.payload_ref.refs_6_, s32[1,256]{1,0:T(1,128)S(1)} %bitcast.18, s32[1,256]{1,0:T(1,128)S(1)} %bitcast.19, f32[4,64]{1,0:T(4,128)S(1)} %bitcast.17, f32[8,128,128]{2,1,0:T(8,128)S(1)} %bitcast.15), custom_call_target="tpu_custom_call" | custom-call | tf_op jit(solution)/shard_map/own_tiles/pallas_call | solution.py:660
  13.4 3.5 %all-to-all-start = ((f32[8,152,128]{2,1,0:T(8,128)}), f32[8,152,128]{2,1,0:T(8,128)S(1)}, u32[]{:S(2)}, u32[]{:S(2)}) async-start(f32[8,152,128]{2,1,0:T(8,128)} %get-tuple-element.49), calls=%async_computation | async-start | bytes 1245184 | tf_op jit(solution)/shard_map/all_to_all | solution.py:690
  19.9 1.7 %collective-permute-start.2 = (f32[544,128]{1,0:T(8,128)}, f32[544,128]{1,0:T(8,128)S(1)}, u32[]{:S(2)}, u32[]{:S(2)}) collective-permute-start(f32[544,128]{1,0:T(8,128)} %slice.15), channel_id=1, source_target_pairs={{0,16},{8,24},{16,0},{24,8},{1,17},{9,25},{17,1},{25,9},{2,18},{10... | collective-permute-start | bytes 835592 | tf_op jit(solution)/shard_map/ppermute | solution.py:597
  22.9 4.4 %all-to-all-done.in_ref = f32[8,152,128]{2,1,0:T(8,128)S(1)} async-done(((f32[8,152,128]{2,1,0:T(8,128)}), f32[8,152,128]{2,1,0:T(8,128)S(1)}, u32[]{:S(2)}, u32[]{:S(2)}) %all-to-all-start) | async-done | bytes 622624 | tf_op jit(solution)/shard_map/all_to_all | solution.py:690
  28.5 2.7 %collective-permute-start.6 = (f32[64,128]{1,0:T(8,128)S(1)}, f32[64,128]{1,0:T(8,128)S(1)}, u32[]{:S(2)}, u32[]{:S(2)}) collective-permute-start(f32[64,128]{1,0:T(8,128)S(1)} %get-tuple-element.55), channel_id=1, source_target_pairs={{0,4},{2,6},{4,0},{6,2},{1,5},{3,7},{5,1},{7,3},{8,12},{10,14},{12... | collective-permute-start | bytes 98312 | tf_op jit(solution)/shard_map/ppermute | solution.py:745
  33.4 2.2 %local.4.local_ref = f32[8,128,128]{2,1,0:T(8,128)S(1)} custom-call(s32[5]{0:T(128)S(1)} %stack.19.info_ref, f32[8,128,128]{2,1,0:T(8,128)S(1)} %get-tuple-element.50.y_ref.refs_5_.refs_0_), custom_call_target="tpu_custom_call" | custom-call | flops 7864320 | bytes 2097152 | tf_op jit(solution)/shard_map/local/pallas_call | solution.py:775
  41.6 6.8 %step.5 = (f32[8,128,128]{2,1,0:T(8,128)S(1)}, bf16[8,1024,256]{2,1,0:T(8,128)(2,1)}, f32[8,64,128]{2,1,0:T(8,128)S(1)}, f32[96,128]{1,0:T(8,128)S(1)}, f32[320,...) custom-call(s32[5]{0:T(128)S(1)} %get-tuple-element.46.info_ref, ...), custom_call_target="tpu_custom_call" | custom-call | tf_op jit(solution)/shard_map/step/pallas_call | solution.py:838
  48.4 5.0 %collective-permute-start.13 = (f32[320,128]{1,0:T(8,128)S(1)}, f32[320,128]{1,0:T(8,128)S(1)}, u32[]{:S(2)}, u32[]{:S(2)}) collective-permute-start(f32[320,128]{1,0:T(8,128)S(1)} %get-tuple-element.63), channel_id=1, source_target_pairs={{0,2},{4,6},{2,0},{6,4},{1,3},{5,7},{3,1},{7,5},{8,10},{12,14},{10... | collective-permute-start | bytes 491528 | tf_op jit(solution)/shard_map/ppermute | solution.py:745
  54.0 2.8 %collective-permute-start.15 = (f32[32,128]{1,0:T(8,128)S(1)}, f32[32,128]{1,0:T(8,128)S(1)}, u32[]{:S(2)}, u32[]{:S(2)}) collective-permute-start(f32[32,128]{1,0:T(8,128)S(1)} %get-tuple-element.65), channel_id=1, source_target_pairs={{0,4},{2,6},{4,0},{6,2},{1,5},{3,7},{5,1},{7,3},{8,12},{10,14},{12... | collective-permute-start | bytes 49160 | tf_op jit(solution)/shard_map/ppermute | solution.py:745
  56.8 2.2 %local.5.local_ref = f32[8,128,128]{2,1,0:T(8,128)S(1)} custom-call(s32[5]{0:T(128)S(1)} %stack.19.info_ref, f32[8,128,128]{2,1,0:T(8,128)S(1)} %get-tuple-element.60.y_ref.refs_0_, f32[8,128,128]{2,1,0:T(8,128)S(1)} %get-tuple-element.50.y_ref.refs_5_.refs_0_, f32[8,64,128]{2,1,0:T(8,128)S(1)} %get-tuple-element.61.refs_1_), custom_call_target="tpu_custom_call" | custom-call | flops 7864320 | bytes 2097152 | tf_op jit(solution)/shard_map/local/pallas_call | solution.py:775
  60.5 5.7 %step.6 = (f32[8,128,128]{2,1,0:T(8,128)S(1)}, f32[96,128]{1,0:T(8,128)S(1)}, f32[320,128]{1,0:T(8,128)S(1)}, f32[320,128]{1,0:T(8,128)S(1)}, f32[32,128]{1,0:T(8,128)S(1)}) custom-call(s32[5]{0:T(128)S(1)} %get-tuple-element.46.info_ref, f32[8,128,128]{2,1,0:T(8,128)S(1)} %local.5.local_ref, f32[96,128]{1,0:T(8,128)S(1)} %get-tuple-element.62.refs_0_, ...), custom_call_target="tpu_custom_call" | custom-call | tf_op jit(solution)/shard_map/step/pallas_call | solution.py:838
  68.2 3.8 %collective-permute-start.18 = (f32[32,128]{1,0:T(8,128)S(1)}, f32[32,128]{1,0:T(8,128)S(1)}, u32[]{:S(2)}, u32[]{:S(2)}) collective-permute-start(f32[32,128]{1,0:T(8,128)S(1)} %get-tuple-element.71), channel_id=1, source_target_pairs={{0,4},{2,6},{4,0},{6,2},{1,5},{3,7},{5,1},{7,3},{8,12},{10,14},{12... | collective-permute-start | bytes 49160 | tf_op jit(solution)/shard_map/ppermute | solution.py:745
  72.0 2.2 %local.6.local_ref = f32[8,128,128]{2,1,0:T(8,128)S(1)} custom-call(s32[5]{0:T(128)S(1)} %stack.19.info_ref, f32[8,128,128]{2,1,0:T(8,128)S(1)} %get-tuple-element.67.y_ref.refs_0_, f32[8,128,128]{2,1,0:T(8,128)S(1)} %get-tuple-element.60.y_ref.refs_0_, f32[8,64,128]{2,1,0:T(8,128)S(1)} %get-tuple-element.61.refs_1_), custom_call_target="tpu_custom_call" | custom-call | flops 7864320 | bytes 2097152 | tf_op jit(solution)/shard_map/local/pallas_call | solution.py:775
  75.2 5.7 %step.7 = (f32[8,128,128]{2,1,0:T(8,128)S(1)}, f32[96,128]{1,0:T(8,128)S(1)}, f32[320,128]{1,0:T(8,128)S(1)}, f32[320,128]{1,0:T(8,128)S(1)}, f32[32,128]{1,0:T(8,128)S(1)}) custom-call(s32[5]{0:T(128)S(1)} %get-tuple-element.46.info_ref, f32[8,128,128]{2,1,0:T(8,128)S(1)} %local.6.local_ref, f32[96,128]{1,0:T(8,128)S(1)} %get-tuple-element.68.refs_0_, ...), custom_call_target="tpu_custom_call" | custom-call | tf_op jit(solution)/shard_map/step/pallas_call | solution.py:838
  80.9 1.8 %collective-permute-start.19 = (f32[320,128]{1,0:T(8,128)S(1)}, f32[320,128]{1,0:T(8,128)S(1)}, u32[]{:S(2)}, u32[]{:S(2)}) collective-permute-start(f32[320,128]{1,0:T(8,128)S(1)} %get-tuple-element.74), channel_id=1, source_target_pairs={{0,2},{4,6},{2,0},{6,4},{1,3},{5,7},{3,1},{7,5},{8,10},{12,14},{10... | collective-permute-start | bytes 491528 | tf_op jit(solution)/shard_map/ppermute | solution.py:745
  83.4 3.1 %collective-permute-start.21 = (f32[32,128]{1,0:T(8,128)S(1)}, f32[32,128]{1,0:T(8,128)S(1)}, u32[]{:S(2)}, u32[]{:S(2)}) collective-permute-start(f32[32,128]{1,0:T(8,128)S(1)} %get-tuple-element.76), channel_id=1, source_target_pairs={{0,4},{2,6},{4,0},{6,2},{1,5},{3,7},{5,1},{7,3},{8,12},{10,14},{12... | collective-permute-start | bytes 49160 | tf_op jit(solution)/shard_map/ppermute | solution.py:745
  86.4 2.2 %local.7.local_ref = f32[8,128,128]{2,1,0:T(8,128)S(1)} custom-call(s32[5]{0:T(128)S(1)} %stack.19.info_ref, f32[8,128,128]{2,1,0:T(8,128)S(1)} %get-tuple-element.72.y_ref, f32[8,128,128]{2,1,0:T(8,128)S(1)} %get-tuple-element.67.y_ref.refs_0_, f32[8,64,128]{2,1,0:T(8,128)S(1)} %get-tuple-element.61.refs_1_), custom_call_target="tpu_custom_call" | custom-call | flops 7864320 | bytes 2097152 | tf_op jit(solution)/shard_map/local/pallas_call | solution.py:775
  89.9 3.1 %step.9 = (f32[8,128,128]{2,1,0:T(8,128)S(1)}, f32[1,128,128]{2,1,0:T(8,128)S(1)}, f32[1,128,128]{2,1,0:T(8,128)S(1)}, f32[1,128,128]{2,1,0:T(8,128)S(1)}) fusion(f32[8,128,128]{2,1,0:T(8,128)S(1)} %broadcast_in_dim.3, s32[]{:T(128)S(6)} %select_n.100, s32[5]{0:T(128)S(1)} %get-tuple-element.46.info_ref, f32[8,128,128]{2,1,0:T(8,128)S(1)} %local.7.local_ref, ...), kind=kCustom, calls=%fused_computation.29 | custom fusion | bytes 6013444 | tf_op jit(solution)/shard_map/step/pallas_call | solution.py:838
  93.0 1.5 %collective-permute-start.22 = (f32[1,128,128]{2,1,0:T(8,128)S(1)}, f32[1,128,128]{2,1,0:T(8,128)S(1)}, u32[]{:S(2)}, u32[]{:S(2)}) collective-permute-start(f32[1,128,128]{2,1,0:T(8,128)S(1)} %get-tuple-element.88), channel_id=1, source_target_pairs={{0,1},{1,0},{8,9},{9,8},{16,17},{17,16},{24,25},{25,24},{2,3},{3,2... | collective-permute-start | bytes 196616 | tf_op jit(solution)/shard_map/ppermute | solution.py:865
  94.5 2.2 %copy-done = bf16[8,1024,256]{2,1,0:T(8,128)(2,1)S(1)} copy-done((bf16[8,1024,256]{2,1,0:T(8,128)(2,1)S(1)}, bf16[8,1024,256]{2,1,0:T(8,128)(2,1)}, u32[]{:S(2)}) %copy-start) | copy-done | bytes 4194328
  96.7 1.6 %step.8 = (f32[1,128,128]{2,1,0:T(8,128)S(1)}, f32[1,128,128]{2,1,0:T(8,128)S(1)}, f32[1,128,128]{2,1,0:T(8,128)S(1)}, f32[1,128,128]{2,1,0:T(8,128)S(1)}) custom-call(s32[5]{0:T(128)S(1)} %get-tuple-element.46.info_ref, f32[8,128,128]{2,1,0:T(8,128)S(1)} %local.7.local_ref, f32[96,128]{1,0:T(8,128)S(1)} %get-tuple-element.73.refs_0_, ...), custom_call_target="tpu_custom_call" | custom-call | tf_op jit(solution)/shard_map/step/pallas_call | solution.py:838
  98.9 1.5 %collective-permute-start.24 = (f32[1,128,128]{2,1,0:T(8,128)S(1)}, f32[1,128,128]{2,1,0:T(8,128)S(1)}, u32[]{:S(2)}, u32[]{:S(2)}) collective-permute-start(f32[1,128,128]{2,1,0:T(8,128)S(1)} %get-tuple-element.92), channel_id=1, source_target_pairs={{0,17},{1,16},{8,25},{9,24},{16,1},{17,0},{24,9},{25,8},{2,19},{3,... | collective-permute-start | bytes 196616 | tf_op jit(solution)/shard_map/ppermute | solution.py:865
  105.7 2.3 %collective-permute-done.28 = f32[1,128,128]{2,1,0:T(8,128)S(1)} collective-permute-done((f32[1,128,128]{2,1,0:T(8,128)S(1)}, f32[1,128,128]{2,1,0:T(8,128)S(1)}, u32[]{:S(2)}, u32[]{:S(2)}) %collective-permute-start.28) | collective-permute-done | bytes 65568 | tf_op jit(solution)/shard_map/ppermute | solution.py:865
  (92 shorter events, 33.9 us)
Async XLA Ops:
  2.1 15.7 %collective-permute-start = (f32[1088,128]{1,0:T(8,128)S(1)}, f32[1088,128]{1,0:T(8,128)S(1)}, u32[]{:S(2)}, u32[]{:S(2)}) collective-permute-start(f32[1088,128]{1,0:T(8,128)S(1)} %pack.1.payload_ref.refs_6_), channel_id=1, source_target_pairs={{0,1},{1,0},{2,3},{3,2},{4,5},{5,4},{6,7},{7,6},{8,9},{9,8},{10,11... | collective-permute-start | bytes 1671176 | tf_op jit(solution)/shard_map/ppermute | solution.py:597
  5.1 14.1 %collective-permute-start.1 = (f32[1088,128]{1,0:T(8,128)S(1)}, f32[1088,128]{1,0:T(8,128)S(1)}, u32[]{:S(2)}, u32[]{:S(2)}) collective-permute-start(f32[1088,128]{1,0:T(8,128)S(1)} %pack.1.payload_ref.refs_6_), channel_id=1, source_target_pairs={{0,16},{8,24},{16,0},{24,8},{1,17},{9,25},{17,1},{25,9},{2,18},{10... | collective-permute-start | bytes 1671176 | tf_op jit(solution)/shard_map/ppermute | solution.py:597
  6.6 25.9 %collective-permute-start.8 = (f32[1088,128]{1,0:T(8,128)S(1)}, f32[1088,128]{1,0:T(8,128)}, u32[]{:S(2)}, u32[]{:S(2)}) collective-permute-start(f32[1088,128]{1,0:T(8,128)S(1)} %pack.1.payload_ref.refs_6_), channel_id=1, source_target_pairs={{0,8},{8,0},{16,24},{24,16},{1,9},{9,1},{17,25},{25,17},{2,10},{10... | collective-permute-start | bytes 1671176 | tf_op jit(solution)/shard_map/ppermute | solution.py:597
  13.4 13.9 %all-to-all-start = ((f32[8,152,128]{2,1,0:T(8,128)}), f32[8,152,128]{2,1,0:T(8,128)S(1)}, u32[]{:S(2)}, u32[]{:S(2)}) async-start(f32[8,152,128]{2,1,0:T(8,128)} %get-tuple-element.49), calls=%async_computation | async-start | bytes 1245184 | tf_op jit(solution)/shard_map/all_to_all | solution.py:690
  19.9 12.9 %collective-permute-start.2 = (f32[544,128]{1,0:T(8,128)}, f32[544,128]{1,0:T(8,128)S(1)}, u32[]{:S(2)}, u32[]{:S(2)}) collective-permute-start(f32[544,128]{1,0:T(8,128)} %slice.15), channel_id=1, source_target_pairs={{0,16},{8,24},{16,0},{24,8},{1,17},{9,25},{17,1},{25,9},{2,18},{10... | collective-permute-start | bytes 835592 | tf_op jit(solution)/shard_map/ppermute | solution.py:597
  22.4 10.5 %collective-permute-start.3 = (f32[544,128]{1,0:T(8,128)}, f32[544,128]{1,0:T(8,128)S(1)}, u32[]{:S(2)}, u32[]{:S(2)}) collective-permute-start(f32[544,128]{1,0:T(8,128)} %slice.16), channel_id=1, source_target_pairs={{0,1},{1,0},{2,3},{3,2},{4,5},{5,4},{6,7},{7,6},{8,9},{9,8},{10,11... | collective-permute-start | bytes 835592 | tf_op jit(solution)/shard_map/ppermute | solution.py:597
  28.5 9.0 %collective-permute-start.6 = (f32[64,128]{1,0:T(8,128)S(1)}, f32[64,128]{1,0:T(8,128)S(1)}, u32[]{:S(2)}, u32[]{:S(2)}) collective-permute-start(f32[64,128]{1,0:T(8,128)S(1)} %get-tuple-element.55), channel_id=1, source_target_pairs={{0,4},{2,6},{4,0},{6,2},{1,5},{3,7},{5,1},{7,3},{8,12},{10,14},{12... | collective-permute-start | bytes 98312 | tf_op jit(solution)/shard_map/ppermute | solution.py:745
  31.2 5.7 %collective-permute-start.7 = (f32[32,128]{1,0:T(8,128)S(1)}, f32[32,128]{1,0:T(8,128)S(1)}, u32[]{:S(2)}, u32[]{:S(2)}) collective-permute-start(f32[32,128]{1,0:T(8,128)S(1)} %slice.17.refs_0_), channel_id=1, source_target_pairs={{0,6},{2,4},{4,2},{6,0},{1,7},{3,5},{5,3},{7,1},{8,14},{10,12},{12... | collective-permute-start | bytes 49160 | tf_op jit(solution)/shard_map/ppermute | solution.py:766
  32.5 6.3 %collective-permute-start.4 = (f32[352,128]{1,0:T(8,128)S(1)}, f32[352,128]{1,0:T(8,128)S(1)}, u32[]{:S(2)}, u32[]{:S(2)}) collective-permute-start(f32[352,128]{1,0:T(8,128)S(1)} %get-tuple-element.53), channel_id=1, source_target_pairs={{0,2},{4,6},{2,0},{6,4},{1,3},{5,7},{3,1},{7,5},{8,10},{12,14},{10... | collective-permute-start | bytes 540680 | tf_op jit(solution)/shard_map/ppermute | solution.py:745
  32.8 7.7 %collective-permute-start.10 = (f32[1088,128]{1,0:T(8,128)S(1)}, f32[1088,128]{1,0:T(8,128)S(1)}, u32[]{:S(2)}, u32[]{:S(2)}) collective-permute-start(f32[1088,128]{1,0:T(8,128)S(1)} %collective-permute-done.1.refs_8_), channel_id=1, source_target_pairs={{0,8},{8,0},{16,24},{24,16},{1,9},{9,1},{17,25},{25,17},{2,10},{10... | collective-permute-start | bytes 1671176 | tf_op jit(solution)/shard_map/ppermute | solution.py:597
  32.8 7.7 %collective-permute-start.9 = (f32[1088,128]{1,0:T(8,128)S(1)}, f32[1088,128]{1,0:T(8,128)S(1)}, u32[]{:S(2)}, u32[]{:S(2)}) collective-permute-start(f32[1088,128]{1,0:T(8,128)S(1)} %collective-permute-done.refs_7_), channel_id=1, source_target_pairs={{0,8},{8,0},{16,24},{24,16},{1,9},{9,1},{17,25},{25,17},{2,10},{10... | collective-permute-start | bytes 1671176 | tf_op jit(solution)/shard_map/ppermute | solution.py:597
  48.4 12.2 %collective-permute-start.13 = (f32[320,128]{1,0:T(8,128)S(1)}, f32[320,128]{1,0:T(8,128)S(1)}, u32[]{:S(2)}, u32[]{:S(2)}) collective-permute-start(f32[320,128]{1,0:T(8,128)S(1)} %get-tuple-element.63), channel_id=1, source_target_pairs={{0,2},{4,6},{2,0},{6,4},{1,3},{5,7},{3,1},{7,5},{8,10},{12,14},{10... | collective-permute-start | bytes 491528 | tf_op jit(solution)/shard_map/ppermute | solution.py:745
  53.3 7.2 %collective-permute-start.14 = (f32[320,128]{1,0:T(8,128)S(1)}, f32[320,128]{1,0:T(8,128)S(1)}, u32[]{:S(2)}, u32[]{:S(2)}) collective-permute-start(f32[320,128]{1,0:T(8,128)S(1)} %get-tuple-element.64), channel_id=1, source_target_pairs={{2,4},{4,2},{3,5},{5,3},{10,12},{12,10},{11,13},{13,11},{18,20},{2... | collective-permute-start | bytes 491528 | tf_op jit(solution)/shard_map/ppermute | solution.py:745
  54.0 6.5 %collective-permute-start.15 = (f32[32,128]{1,0:T(8,128)S(1)}, f32[32,128]{1,0:T(8,128)S(1)}, u32[]{:S(2)}, u32[]{:S(2)}) collective-permute-start(f32[32,128]{1,0:T(8,128)S(1)} %get-tuple-element.65), channel_id=1, source_target_pairs={{0,4},{2,6},{4,0},{6,2},{1,5},{3,7},{5,1},{7,3},{8,12},{10,14},{12... | collective-permute-start | bytes 49160 | tf_op jit(solution)/shard_map/ppermute | solution.py:745
  66.3 8.9 %collective-permute-start.16 = (f32[320,128]{1,0:T(8,128)S(1)}, f32[320,128]{1,0:T(8,128)S(1)}, u32[]{:S(2)}, u32[]{:S(2)}) collective-permute-start(f32[320,128]{1,0:T(8,128)S(1)} %get-tuple-element.69), channel_id=1, source_target_pairs={{0,2},{4,6},{2,0},{6,4},{1,3},{5,7},{3,1},{7,5},{8,10},{12,14},{10... | collective-permute-start | bytes 491528 | tf_op jit(solution)/shard_map/ppermute | solution.py:745
  67.3 7.8 %collective-permute-start.17 = (f32[320,128]{1,0:T(8,128)S(1)}, f32[320,128]{1,0:T(8,128)S(1)}, u32[]{:S(2)}, u32[]{:S(2)}) collective-permute-start(f32[320,128]{1,0:T(8,128)S(1)} %get-tuple-element.70), channel_id=1, source_target_pairs={{2,4},{4,2},{3,5},{5,3},{10,12},{12,10},{11,13},{13,11},{18,20},{2... | collective-permute-start | bytes 491528 | tf_op jit(solution)/shard_map/ppermute | solution.py:745
  68.2 7.0 %collective-permute-start.18 = (f32[32,128]{1,0:T(8,128)S(1)}, f32[32,128]{1,0:T(8,128)S(1)}, u32[]{:S(2)}, u32[]{:S(2)}) collective-permute-start(f32[32,128]{1,0:T(8,128)S(1)} %get-tuple-element.71), channel_id=1, source_target_pairs={{0,4},{2,6},{4,0},{6,2},{1,5},{3,7},{5,1},{7,3},{8,12},{10,14},{12... | collective-permute-start | bytes 49160 | tf_op jit(solution)/shard_map/ppermute | solution.py:745
  80.9 8.9 %collective-permute-start.19 = (f32[320,128]{1,0:T(8,128)S(1)}, f32[320,128]{1,0:T(8,128)S(1)}, u32[]{:S(2)}, u32[]{:S(2)}) collective-permute-start(f32[320,128]{1,0:T(8,128)S(1)} %get-tuple-element.74), channel_id=1, source_target_pairs={{0,2},{4,6},{2,0},{6,4},{1,3},{5,7},{3,1},{7,5},{8,10},{12,14},{10... | collective-permute-start | bytes 491528 | tf_op jit(solution)/shard_map/ppermute | solution.py:745
  82.7 7.1 %collective-permute-start.20 = (f32[320,128]{1,0:T(8,128)S(1)}, f32[320,128]{1,0:T(8,128)S(1)}, u32[]{:S(2)}, u32[]{:S(2)}) collective-permute-start(f32[320,128]{1,0:T(8,128)S(1)} %get-tuple-element.75), channel_id=1, source_target_pairs={{2,4},{4,2},{3,5},{5,3},{10,12},{12,10},{11,13},{13,11},{18,20},{2... | collective-permute-start | bytes 491528 | tf_op jit(solution)/shard_map/ppermute | solution.py:745
  83.4 6.4 %collective-permute-start.21 = (f32[32,128]{1,0:T(8,128)S(1)}, f32[32,128]{1,0:T(8,128)S(1)}, u32[]{:S(2)}, u32[]{:S(2)}) collective-permute-start(f32[32,128]{1,0:T(8,128)S(1)} %get-tuple-element.76), channel_id=1, source_target_pairs={{0,4},{2,6},{4,0},{6,2},{1,5},{3,7},{5,1},{7,3},{8,12},{10,14},{12... | collective-permute-start | bytes 49160 | tf_op jit(solution)/shard_map/ppermute | solution.py:745
  93.0 8.4 %collective-permute-start.22 = (f32[1,128,128]{2,1,0:T(8,128)S(1)}, f32[1,128,128]{2,1,0:T(8,128)S(1)}, u32[]{:S(2)}, u32[]{:S(2)}) collective-permute-start(f32[1,128,128]{2,1,0:T(8,128)S(1)} %get-tuple-element.88), channel_id=1, source_target_pairs={{0,1},{1,0},{8,9},{9,8},{16,17},{17,16},{24,25},{25,24},{2,3},{3,2... | collective-permute-start | bytes 196616 | tf_op jit(solution)/shard_map/ppermute | solution.py:865
  98.3 6.1 %collective-permute-start.25 = (f32[1,128,128]{2,1,0:T(8,128)S(1)}, f32[1,128,128]{2,1,0:T(8,128)S(1)}, u32[]{:S(2)}, u32[]{:S(2)}) collective-permute-start(f32[1,128,128]{2,1,0:T(8,128)S(1)} %get-tuple-element.81), channel_id=1, source_target_pairs={{0,8},{1,9},{8,0},{9,1},{16,24},{17,25},{24,16},{25,17},{2,10},{3,... | collective-permute-start | bytes 196616 | tf_op jit(solution)/shard_map/ppermute | solution.py:865
  98.9 5.4 %collective-permute-start.24 = (f32[1,128,128]{2,1,0:T(8,128)S(1)}, f32[1,128,128]{2,1,0:T(8,128)S(1)}, u32[]{:S(2)}, u32[]{:S(2)}) collective-permute-start(f32[1,128,128]{2,1,0:T(8,128)S(1)} %get-tuple-element.92), channel_id=1, source_target_pairs={{0,17},{1,16},{8,25},{9,24},{16,1},{17,0},{24,9},{25,8},{2,19},{3,... | collective-permute-start | bytes 196616 | tf_op jit(solution)/shard_map/ppermute | solution.py:865
  100.5 5.2 %collective-permute-start.26 = (f32[1,128,128]{2,1,0:T(8,128)S(1)}, f32[1,128,128]{2,1,0:T(8,128)S(1)}, u32[]{:S(2)}, u32[]{:S(2)}) collective-permute-start(f32[1,128,128]{2,1,0:T(8,128)S(1)} %get-tuple-element.82), channel_id=1, source_target_pairs={{0,9},{1,8},{8,1},{9,0},{16,25},{17,24},{24,17},{25,16},{2,11},{3,... | collective-permute-start | bytes 196616 | tf_op jit(solution)/shard_map/ppermute | solution.py:865
  (17 other events, 52.7 us)

commit v6 on v5

--- a/solution.py
+++ b/solution.py
@@ -145,12 +145,12 @@
     on, points, slots, projs = plan.on, plan.points, plan.slots, plan.projs
     rows = on * points
     boths = []
-    for y_block, stack in zip(y_blocks, stacks):
+    for y_block, stack_of in zip(y_blocks, stacks):
         hi, lo = hi_lo(y_block)
         left = jnp.concatenate(
             [jnp.concatenate([hi, hi], axis=1), jnp.concatenate([lo, lo], axis=1)], axis=0
         )
-        boths.append(dot_nt(left, stack))
+        boths.append(dot_nt(left, stack_of()))
     partials = []
     for both, column in zip(boths, columns):
         mask = column == lax.broadcasted_iota(jnp.int32, (points, slots), 0)
@@ -202,7 +202,7 @@
             bands.append(jnp.concatenate(pieces, axis=1))
         hi, lo = hi_lo(jnp.concatenate(bands, axis=0))
         splits.append(jnp.concatenate([hi, lo], axis=0))
-    fours = [dot_nn(split, stack) for split, stack in zip(splits, stacks)]
+    fours = [dot_nn(split, ready()) for split, ready in zip(splits, stacks)]
     rows, cx = on * points, plan.cx
     return [
         (four[:rows, :cx] + four[rows:, cx:]) + (four[:rows, cx:] + four[rows:, :cx])
@@ -326,48 +326,57 @@
     return jnp.concatenate([low] + middle + [high], axis=1).reshape(lines * cy, cx)
 
 
-def pack_kernel(plan, tile_ref, potential_ref, out_ref):
+def pack_kernel(plan, tile_ref, potential_ref, out_ref, held_ref, sem):
     slots = plan.slots
+    tiles = pltpu.make_async_copy(tile_ref, held_ref, sem.at[0])
+    tail = out_ref.at[pl.ds(plan.projs * slots, plan.points)]
+    tail_copy = pltpu.make_async_copy(potential_ref, tail, sem.at[1])
+    tiles.start()
+    tail_copy.start()
+    tiles.wait()
     for p in range(plan.projs):
-        out_ref[p * slots : (p + 1) * slots, :] = tile_ref[:, p, :]
-    out_ref[plan.projs * slots :, :] = potential_ref[...]
+        out_ref[p * slots : (p + 1) * slots, :] = held_ref[:, p, :]
+    tail_copy.wait()
 
 
 def own_tiles_kernel(
-    plan, info_ref, payload_ref, atom_ref, column_ref, coupling_ref, y_ref,
-    out_ref, info_out_ref, stack_ref, meta_ref,
+    plan, info_ref, payload_ref, atom_in, column_in, coupling_in, y_in,
+    out_ref, info_out_ref, stack_ref, meta_ref, atom_ref, column_ref, coupling_ref, y_ref, sem,
 ):
     count = plan.slots // LANE
-
-    @pl.when(pl.program_id(0) == 0)
-    def _():
-        fill_stack(plan, stack_ref, payload_ref[: plan.projs * plan.slots, :])
-        for i in range(info_out_ref.shape[0]):
-            info_out_ref[i] = info_ref[i]
-        atom, column = atom_ref[...], column_ref[...]
-        owner = lax.shift_right_logical(atom, log2(plan.owned))
-        owner_z = owner & (plan.gz - 1)
-        owner_y = lax.shift_right_logical(owner, log2(plan.gz)) & (plan.gy - 1)
-        owner_x = lax.shift_right_logical(owner, log2(plan.gz) + log2(plan.gy))
-        key = (owner_y - info_ref[3] + 1) * (plan.blocks * plan.owned)
-        key = key + (owner_x * plan.gz + owner_z) * plan.owned + (atom & (plan.owned - 1))
-        lane = lax.broadcasted_iota(jnp.int32, column.shape, 1)
-        column = jnp.where(lane < info_ref[4], column, -1)
-        meta_ref[...] = jnp.zeros_like(meta_ref)
-        for row, line in enumerate((key, column)):
-            line = line.astype(jnp.float32)
-            for i in range(count):
-                at = row * count + i
-                meta_ref[at : at + 1, :] = line[:, i * LANE : (i + 1) * LANE]
-        for p in range(plan.projs):
-            at = 2 * count + p
-            meta_ref[at : at + 1, : plan.owned] = coupling_ref[p : p + 1, :]
-
+    pairs = ((atom_in, atom_ref), (column_in, column_ref), (coupling_in, coupling_ref), (y_in, y_ref))
+    copies = [pltpu.make_async_copy(a, b, sem.at[i]) for i, (a, b) in enumerate(pairs)]
+    for copy in copies:
+        copy.start()
+    fill_stack(plan, stack_ref, payload_ref[: plan.projs * plan.slots, :])
+    for i in range(info_out_ref.shape[0]):
+        info_out_ref[i] = info_ref[i]
+    for copy in copies[:3]:
+        copy.wait()
+    atom, column = atom_ref[...], column_ref[...]
+    owner = lax.shift_right_logical(atom, log2(plan.owned))
+    owner_z = owner & (plan.gz - 1)
+    owner_y = lax.shift_right_logical(owner, log2(plan.gz)) & (plan.gy - 1)
+    owner_x = lax.shift_right_logical(owner, log2(plan.gz) + log2(plan.gy))
+    key = (owner_y - info_ref[3] + 1) * (plan.blocks * plan.owned)
+    key = key + (owner_x * plan.gz + owner_z) * plan.owned + (atom & (plan.owned - 1))
+    lane = lax.broadcasted_iota(jnp.int32, column.shape, 1)
+    column = jnp.where(lane < info_ref[4], column, -1)
+    meta_ref[...] = jnp.zeros_like(meta_ref)
+    for row, line in enumerate((key, column)):
+        line = line.astype(jnp.float32)
+        for i in range(count):
+            at = row * count + i
+            meta_ref[at : at + 1, :] = line[:, i * LANE : (i + 1) * LANE]
+    for p in range(plan.projs):
+        at = 2 * count + p
+        meta_ref[at : at + 1, : plan.owned] = coupling_ref[p : p + 1, :]
     meta = meta_ref[...]
-    columns = meta_line(plan, meta, 1).astype(jnp.int32)
-    y_rows, f = plan.y_rows, plan.features
-    y_blocks = [y_ref[part] for part in range(plan.per)]
-    partials = tile_sums(plan, y_blocks, [stack_ref[...]] * plan.per, [columns] * plan.per)
+    copies[3].wait()
+    y_rows, f, blocks = plan.y_rows, plan.features, plan.blocks
+    y_blocks = [y_ref[part] for part in range(blocks)]
+    load = lambda: stack_ref[...]
+    partials = tile_sums(plan, y_blocks, [load] * blocks, [column] * blocks)
     for part, (y_block, partial) in enumerate(zip(y_blocks, partials)):
         out_ref[part, :y_rows, :] = y_block
         for j in range(count):
@@ -478,76 +487,78 @@
 
 
 def step_kernel(plan, first, last, base, info_ref, local_ref, *refs):
-    received, refs = refs[:5], refs[5:]
-    own_in, even_in, odd_in, far_in, scale_ref = received
+    own_in, even_in, odd_in, far_in, scale_ref = refs[:5]
+    refs = refs[5:]
     if first:
         y_ref, piece_refs, refs = refs[0], refs[1:11], refs[11:]
     else:
-        stack_ref, refs = refs[0], refs[1:]
-    hot_ref, place_ref = refs[:2]
-    count = plan.blocks // 2 if last else 1
-    out_refs, refs = refs[2 : 2 + count], refs[2 + count :]
+        stack_in, refs = refs[0], refs[1:]
+    hot_ref, place_ref, refs = refs[0], refs[1], refs[2:]
+    count = plan.blocks // 2 if last else plan.blocks
+    out_refs, refs = (refs[:count], refs[count:]) if last else (refs[:1], refs[1:])
     if first:
-        stack_ref, potential_ref = refs[:2]
-        refs = refs[2:]
+        stack_out, potential_ref, refs = refs[0], refs[1], refs[2:]
     if not last:
         own_ref, even_ref, odd_ref, far_ref = refs[:4]
         refs = refs[4:]
-    coef_ref, low_ref, high_ref = refs[:3]
-    step = pl.program_id(0)
+    low_ref, high_ref, stack_ref, sem = refs[:4]
     odd, upper = info_ref[1] == 1, info_ref[2] == 1
     factor = plan.factor(first)
-
-    @pl.when(step == 0)
-    def _():
-        coefs = factor * load_coefs(
-            plan, odd, upper, own_in, even_in, odd_in, far_in, scale_ref
-        )
-        hi, lo = hi_lo(coefs)
-        coef_ref[...] = jnp.concatenate([hi, lo], axis=0)
-        low_ref[...] = jnp.zeros_like(low_ref)
-        high_ref[...] = jnp.zeros_like(high_ref)
-
+    parts = range(count)
+
+    stores = []
     if first:
-        held_ref, sem = refs[-2:]
+        held_ref, held_sem = refs[4:6]
         cut = piece_refs[3].shape[0]
         copies = []
         for index, piece in enumerate(piece_refs):
             side, which = index // 5, index % 5
-            there = held_ref.at[side * (plan.blocks // 2) + min(which, 3)]
+            there = held_ref.at[side * (count // 2) + min(which, 3)]
             if which >= 3:
                 there = there.at[pl.ds((which - 3) * cut, cut)]
-            copies.append(pltpu.make_async_copy(piece, there, sem.at[index]))
-
-        @pl.when(step == 0)
-        def _():
-            for copy in copies:
-                copy.start()
-            for copy in copies[:5]:
+            copies.append(pltpu.make_async_copy(piece, there, held_sem.at[index]))
+        tiles = plan.projs * plan.slots
+
+        def ready(part):
+            side, which = part // (count // 2), part % (count // 2)
+            for copy in copies[5 * side + which : 5 * side + (which + 1 if which < 3 else 5)]:
                 copy.wait()
-
-        @pl.when(step == 1)
-        def _():
-            for copy in copies[5:]:
-                copy.wait()
-
-        tiles = plan.projs * plan.slots
-        for part in range(plan.per):
-            slot = step * plan.per + part
-            fill_stack(plan, stack_ref.at[part], held_ref[slot, :tiles, :])
-            potential_ref[part] = held_ref[slot, tiles:, :]
+            fill_stack(plan, stack_ref.at[part], held_ref[part, :tiles, :])
+            potential_ref[part] = held_ref[part, tiles:, :]
+            store = pltpu.make_async_copy(stack_ref.at[part], stack_out.at[part], sem.at[part])
+            store.start()
+            stores.append(store)
+            return stack_ref[part]
+
+    else:
+        copies = [
+            pltpu.make_async_copy(stack_in.at[base + part], stack_ref.at[part], sem.at[part])
+            for part in parts
+        ]
+
+        def ready(part):
+            copies[part].wait()
+            return stack_ref[part]
+
+    for copy in copies:
+        copy.start()
+
+    coefs = factor * load_coefs(plan, odd, upper, own_in, even_in, odd_in, far_in, scale_ref)
+    hi, lo = hi_lo(coefs)
+    coef_split = jnp.concatenate([hi, lo], axis=0)
+    low_ref[...] = jnp.zeros_like(low_ref)
+    high_ref[...] = jnp.zeros_like(high_ref)
 
     rows = plan.on * plan.cz * REACH
-    parts = range(plan.per)
     columns = [place_ref[part, 0:1, :] for part in parts]
     groups = [place_ref[part, 1:2, :] for part in parts]
     hots = [hot_ref[part] for part in parts]
-    stacks = [stack_ref[part] for part in parts]
-    projected = backward_blocks(plan, coef_ref[...], stacks, hots, groups, columns)
+    fetch = [functools.partial(ready, part) for part in parts]
+    projected = backward_blocks(plan, coef_split, fetch, hots, groups, columns)
     y_blocks = []
     for part in parts:
-        slot = (base + step) * plan.per + part
-        where = pl.ds(pl.multiple_of(slot * rows, SUB), rows)
+        slot = base + part
+        where = slice(slot * rows, (slot + 1) * rows)
         from_even, from_odd = even_in[where, :], odd_in[where, :]
         low_rows = jnp.where(odd, from_even, from_odd)
         high_rows = jnp.where(odd, from_odd, from_even)
@@ -558,30 +569,19 @@
             y_new = y_new + jnp.concatenate([potential] * plan.on, axis=0) * y_ref[part]
         y_blocks.append(y_new)
         if last:
-            for other in range(len(out_refs) // plan.per):
-                @pl.when(step == other)
-                def _(other=other, y_new=y_new, part=part):
-                    out_refs[other * plan.per + part][0] = y_new
+            out_refs[part][0] = y_new
         else:
             out_refs[0][part] = y_new
             emit_halo(plan, y_new, slot, odd, even_ref, odd_ref)
     if last:
         return
-    partials = tile_sums(plan, y_blocks, stacks, columns)
+    again = [lambda part=part: stack_ref[part] for part in parts]
+    partials = tile_sums(plan, y_blocks, again, columns)
+    hots = [hot_ref[part] for part in parts]
     sums = key_sums(plan, partials, hots, groups)
-    total_ref = refs[3]
-
-    @pl.when(step == 0)
-    def _():
-        total_ref[...] = sums
-
-    @pl.when(step > 0)
-    def _():
-        total_ref[...] += sums
-
-    @pl.when(step == plan.blocks // plan.per - 1)
-    def _():
-        emit_sums(plan, total_ref[...], odd, upper, own_ref, even_ref, odd_ref, far_ref)
+    emit_sums(plan, sums, odd, upper, own_ref, even_ref, odd_ref, far_ref)
+    for store in stores:
+        store.wait()
 
 
 class Plan:
@@ -642,11 +642,16 @@
     full = lambda *shape: pl.BlockSpec(shape, lambda *_: (0,) * len(shape))
     each = lambda count, *shape: pl.BlockSpec((count,) + shape, lambda i, *_: (i, 0, 0))
     params = pltpu.CompilerParams(vmem_limit_bytes=48 * 1024 * 1024)
+    alone = pltpu.CompilerParams(vmem_limit_bytes=62 * 1024 * 1024)
     rows = tile_rows + points
+    in_hbm = pl.BlockSpec(memory_space=pltpu.HBM)
+    anywhere = pl.BlockSpec(memory_space=pl.ANY)
     payload = pl.pallas_call(
         functools.partial(pack_kernel, plan),
         out_shape=jax.ShapeDtypeStruct((rows, cx), f32),
-        compiler_params=params,
+        in_specs=[in_hbm, in_hbm],
+        scratch_shapes=[pltpu.VMEM(tile_proj.shape, f32), pltpu.SemaphoreType.DMA((2,))],
+        compiler_params=alone,
         name="pack",
     )(tile_proj, potential.reshape(points, cx))
     me = ix * gz + iz
@@ -663,21 +668,18 @@
             jax.ShapeDtypeStruct((blocks, plan.meta_at + meta_rows, cx), f32),
             jax.ShapeDtypeStruct(info.shape, jnp.int32),
         ],
-        grid=(blocks // per,),
-        in_specs=[
-            smem,
-            full(rows, cx),
-            full(1, slots),
-            full(1, slots),
-            full(projs, owned),
-            each(per, y_rows, cx),
-        ],
-        out_specs=[each(per, plan.meta_at + meta_rows, cx), smem],
+        in_specs=[smem, full(rows, cx), in_hbm, in_hbm, in_hbm, in_hbm],
+        out_specs=[full(blocks, plan.meta_at + meta_rows, cx), smem],
         scratch_shapes=[
             pltpu.VMEM((tile_rows, 2 * cx), jnp.bfloat16),
             pltpu.VMEM((meta_rows, LANE), f32),
+            pltpu.VMEM((1, slots), jnp.int32),
+            pltpu.VMEM((1, slots), jnp.int32),
+            pltpu.VMEM((projs, owned), f32),
+            pltpu.VMEM((blocks, y_rows, cx), f32),
+            pltpu.SemaphoreType.DMA((4,)),
         ],
-        compiler_params=params,
+        compiler_params=alone,
         name="own_tiles",
     )(
         info,
@@ -689,10 +691,14 @@
     )
     arrived = lax.all_to_all(messages, ("gx", "gz"), 0, 0, tiled=True)
 
-    from_z, from_x, late_info = lax.optimization_barrier((from_z, from_x, late_info))
+    from_z, from_x, from_c, late_info = lax.optimization_barrier(
+        (from_z, from_x, from_c, late_info)
+    )
     cut = rows // 2
     from_xz = [exchange(from_z[:cut], *rounds[1]), exchange(from_x[cut:], *rounds[0])]
-    from_core = [from_c, exchange(from_z, *rounds[2]), exchange(from_x, *rounds[2])]
+    from_core = [exchange(from_z, *rounds[2]), exchange(from_x, *rounds[2])]
+    *from_core, arrived = lax.optimization_barrier((*from_core, arrived))
+    from_core = [from_c, *from_core]
 
     home = atom_home.reshape(gx, gy, gz, owned).transpose(1, 0, 2, 3).reshape(gy, blocks * owned)
     home = jnp.pad(home, ((1, 1), (0, 0)))
@@ -798,52 +804,53 @@
             pieces = [payload, from_z, from_x, *from_xz]
             pieces += from_core + [exchange(part, *rounds[2]) for part in from_xz]
         lines = on * cz
-        scratch = [
-            pltpu.VMEM((6 * plan.third, LANE), jnp.bfloat16),
-            pltpu.VMEM((per, lines, 2 * SUB, cx), f32),
-            pltpu.VMEM((per, lines, 2 * SUB, cx), f32),
-        ]
-        for base in (half // per, 0) if last else (0,):
-            slots_at = lambda i, *_, base=base: (i + base, 0, 0)
-            each = lambda count, *shape: pl.BlockSpec((count,) + shape, slots_at)
-            in_specs = [each(per, y_rows, cx)] + send_specs(extra) + [full(3 * plan.third, LANE)]
+        count = half if last else blocks
+        for base in (half, 0) if last else (0,):
+            at = base // count
+            part_of = lambda *shape, at=at: pl.BlockSpec(
+                (count,) + shape, lambda i, m, at=at: (at, 0, 0)
+            )
+            in_specs = [part_of(y_rows, cx)] + send_specs(extra) + [full(3 * plan.third, LANE)]
             arrays = [local, *received, scale]
             if first:
                 arrays += [current, *pieces]
-                in_specs.append(each(per, y_rows, cx))
-                in_specs += [pl.BlockSpec(memory_space=pl.ANY)] * len(pieces)
+                in_specs += [part_of(y_rows, cx)] + [anywhere] * len(pieces)
             else:
                 arrays.append(stack)
-                in_specs.append(each(per, tile_rows, 2 * cx))
+                in_specs.append(in_hbm)
             arrays += [hot, places]
-            in_specs += [each(per, LANE, slots), each(per, SUB, slots)]
+            in_specs += [part_of(LANE, slots), part_of(SUB, slots)]
             if last:
                 out_shapes = [jax.ShapeDtypeStruct((1, y_rows, cx), f32)] * half
                 out_specs = [full(1, y_rows, cx)] * half
             else:
-                out_shapes, out_specs = [y_shape], [each(per, y_rows, cx)]
+                out_shapes, out_specs = [y_shape], [full(blocks, y_rows, cx)]
+            scratch = [
+                pltpu.VMEM((count, lines, 2 * SUB, cx), f32),
+                pltpu.VMEM((count, lines, 2 * SUB, cx), f32),
+                pltpu.VMEM((count, tile_rows, 2 * cx), jnp.bfloat16),
+                pltpu.SemaphoreType.DMA((count,)),
+            ]
             if first:
                 out_shapes += [
                     jax.ShapeDtypeStruct((blocks, tile_rows, 2 * cx), jnp.bfloat16),
                     jax.ShapeDtypeStruct((blocks, points, cx), f32),
                 ]
-                out_specs += [each(per, tile_rows, 2 * cx), each(per, points, cx)]
+                out_specs += [in_hbm, full(blocks, points, cx)]
+                scratch.append(pltpu.VMEM((blocks, rows, cx), f32))
+                scratch.append(pltpu.SemaphoreType.DMA((len(pieces),)))
             if not last:
                 out_shapes += send_shapes(0)
                 out_specs += send_specs(0)
-            held = []
-            if first:
-                held = [pltpu.VMEM((blocks, rows, cx), f32)]
-                held.append(pltpu.SemaphoreType.DMA((len(pieces),)))
             result = pl.pallas_call(
                 functools.partial(step_kernel, plan, first, last, base),
                 out_shape=out_shapes,
                 grid_spec=pltpu.PrefetchScalarGridSpec(
                     num_scalar_prefetch=1,
-                    grid=((half if last else blocks) // per,),
+                    grid=(1,),
                     in_specs=in_specs,
                     out_specs=out_specs,
-                    scratch_shapes=scratch + ([] if last else [sums_scratch]) + held,
+                    scratch_shapes=scratch,
                 ),
                 compiler_params=params,
                 name="step",

time: 109 us -> 118 us (1.083)
  Pallas kernels: 34.6 us -> 41.6 us
  local copies, waits for them, and re-layouts: 13.9 us -> 11 us
  waiting for transfers between devices: 18.5 us -> 21.1 us
  starting transfers between devices: 40.7 us -> 42.9 us
    unnamed x24 -> x18, local copies, waits for them, and re-layouts: 8.9 us -> 3.6 us
    ppermute x9, waiting for transfers between devices: 2.32 us -> 7.34 us  [exchange(): return lax.ppermute(value, axis, [(i, i ^ bit) for i in range(count)])]
    pallas_call x4, Pallas kernels: 19.8 us -> 22.7 us  [turned_path(): pl.pallas_call(functools.partial(step_kernel, plan, first, last, base), o...]
    ppermute x9, starting transfers between devices: 7.11 us -> 9.01 us  [exchange(): return lax.ppermute(value, axis, [(i, i ^ bit) for i in range(count)])]
    pallas_call x1, Pallas kernels: 0.28 us -> 2.15 us  [turned_path(): pl.pallas_call(functools.partial(pack_kernel, plan), out_shape=jax.ShapeD...]
    ppermute x12, starting transfers between devices: 23.2 us -> 24.8 us  [pairwise(): return lax.ppermute(value, 'gy', pairs + [(b, a) for a, b in pairs])]
    pallas_call x1, Pallas kernels: 2.92 us -> 4.32 us  [turned_path(): pl.pallas_call(functools.partial(own_tiles_kernel, plan), out_shape=[jax....]
  transfers between devices with their start and end apart: 30 -> 30, of which waited for: 12 -> 12; matrix products, arithmetic and copies ran while one was open for 2% -> 3% of each run, Pallas kernels for 15% -> 17%
where the time goes in v6:
time: 118 us
  starting transfers between devices  42.9 us (36%)
  Pallas kernels  41.6 us (35%)
  waiting for transfers between devices  21.1 us (18%)
  local copies, waits for them, and re-layouts  11 us (9%)
    ppermute x12, starting transfers between devices, pairwise(): return lax.ppermute(value, 'gy', pairs + [(b, a) for a, b in pairs])  24.8 us
    pallas_call x4, Pallas kernels, turned_path(): pl.pallas_call(functools.partial(step_kernel, plan, first, last, base), o...  22.7 us
    pallas_call x4, Pallas kernels, turned_path(): pl.pallas_call(functools.partial(local_kernel, plan, first), out_shape=y_...  9.64 us
    ppermute x9, starting transfers between devices, exchange(): return lax.ppermute(value, axis, [(i, i ^ bit) for i in range(count)])  9.01 us
    ppermute x9, waiting for transfers between devices, exchange(): return lax.ppermute(value, axis, [(i, i ^ bit) for i in range(count)])  7.34 us
    ppermute x7, waiting for transfers between devices, turned_path(): lax.ppermute(block, ('gx', 'gz'), [(i, i ^ moved) for i in range(blocks)])  5.77 us
    ppermute x7, starting transfers between devices, turned_path(): lax.ppermute(block, ('gx', 'gz'), [(i, i ^ moved) for i in range(blocks)])  5.37 us
    pallas_call x1, Pallas kernels, turned_path(): pl.pallas_call(functools.partial(own_tiles_kernel, plan), out_shape=[jax....  4.32 us
  transfers between devices with their start and end apart: 30, of which 12 were waited for; matrix products, arithmetic and copies ran while one was open for 3% of the time, Pallas kernels for 17%

profile of v6, /device:TPU:0, one launch (start us, length us, event | category | flops | bytes accessed | tf_op | source)
XLA Modules:
  0.0 117.9 jit_solution(14394389470302075747)
XLA Ops:
  0.0 2.1 %pack.1.payload_ref.refs_6_ = f32[1088,128]{1,0:T(8,128)} custom-call(f32[256,4,128]{2,1,0:T(4,128)} %tile_ref.1, f32[64,128]{1,0:T(8,128)} %bitcast.19), custom_call_target="tpu_custom_call" | custom-call | tf_op jit(solution)/shard_map/pack/pallas_call | solution.py:649
  2.2 3.0 %collective-permute-start = (f32[1088,128]{1,0:T(8,128)}, f32[1088,128]{1,0:T(8,128)S(1)}, u32[]{:S(2)}, u32[]{:S(2)}) collective-permute-start(f32[1088,128]{1,0:T(8,128)} %pack.1.payload_ref.refs_6_), channel_id=1, source_target_pairs={{0,1},{1,0},{2,3},{3,2},{4,5},{5,4},{6,7},{7,6},{8,9},{9,8},{10,11... | collective-permute-start | bytes 1671176 | tf_op jit(solution)/shard_map/ppermute | solution.py:597
  7.9 4.3 %own_tiles.1 = (f32[8,152,128]{2,1,0:T(8,128)}, s32[5]{0:T(128)}) custom-call(s32[5]{0:T(128)} %stack.19.info_ref, f32[1088,128]{1,0:T(8,128)} %pack.1.payload_ref.refs_6_, s32[1,256]{1,0:T(1,128)} %bitcast.21, s32[1,256]{1,0:T(1,128)} %bitcast.22, f32[4,64]{1,0:T(4,128)} %bitcast.20, f32[8,128,128]{2,1,0:T(8,128)} %bitcast.15), custom_call_target="tpu_custom_call" | custom-call | tf_op jit(solution)/shard_map/own_tiles/pallas_call | solution.py:665
  12.3 5.8 %collective-permute-done.refs_7_ = f32[1088,128]{1,0:T(8,128)S(1)} collective-permute-done((f32[1088,128]{1,0:T(8,128)}, f32[1088,128]{1,0:T(8,128)S(1)}, u32[]{:S(2)}, u32[]{:S(2)}) %collective-permute-start) | collective-permute-done | bytes 557088 | tf_op jit(solution)/shard_map/ppermute | solution.py:597
  20.1 3.5 %all-to-all-start = ((f32[8,152,128]{2,1,0:T(8,128)}), f32[8,152,128]{2,1,0:T(8,128)S(1)}, u32[]{:S(2)}, u32[]{:S(2)}) async-start(f32[8,152,128]{2,1,0:T(8,128)} %get-tuple-element.53), calls=%async_computation | async-start | bytes 1245184 | tf_op jit(solution)/shard_map/all_to_all | solution.py:692
  25.3 1.7 %slice.16 = f32[544,128]{1,0:T(8,128)} slice(f32[1088,128]{1,0:T(8,128)} %collective-permute-done.1.refs_8_), slice={[544:1088], [0:128]} | slice | bytes 557056 | tf_op jit(solution)/shard_map/slice | solution.py:698
  27.0 1.9 %collective-permute-start.3 = (f32[544,128]{1,0:T(8,128)}, f32[544,128]{1,0:T(8,128)S(1)}, u32[]{:S(2)}, u32[]{:S(2)}) collective-permute-start(f32[544,128]{1,0:T(8,128)} %slice.15), channel_id=1, source_target_pairs={{0,16},{8,24},{16,0},{24,8},{1,17},{9,25},{17,1},{25,9},{2,18},{10... | collective-permute-start | bytes 835592 | tf_op jit(solution)/shard_map/ppermute | solution.py:597
  30.4 3.6 %all-to-all-done.in_ref = f32[8,152,128]{2,1,0:T(8,128)S(1)} async-done(((f32[8,152,128]{2,1,0:T(8,128)}), f32[8,152,128]{2,1,0:T(8,128)S(1)}, u32[]{:S(2)}, u32[]{:S(2)}) %all-to-all-start) | async-done | bytes 622624 | tf_op jit(solution)/shard_map/all_to_all | solution.py:692
  35.9 2.7 %collective-permute-start.9 = (f32[64,128]{1,0:T(8,128)S(1)}, f32[64,128]{1,0:T(8,128)S(1)}, u32[]{:S(2)}, u32[]{:S(2)}) collective-permute-start(f32[64,128]{1,0:T(8,128)S(1)} %get-tuple-element.60), channel_id=1, source_target_pairs={{0,4},{2,6},{4,0},{6,2},{1,5},{3,7},{5,1},{7,3},{8,12},{10,14},{12... | collective-permute-start | bytes 98312 | tf_op jit(solution)/shard_map/ppermute | solution.py:751
  40.5 2.4 %local.4.local_ref = f32[8,128,128]{2,1,0:T(8,128)S(1)} custom-call(s32[5]{0:T(128)S(1)} %copy-done.2, f32[8,128,128]{2,1,0:T(8,128)S(1)} %get-tuple-element.55.y_ref.refs_5_.refs_0_), custom_call_target="tpu_custom_call" | custom-call | flops 7864320 | bytes 2097152 | tf_op jit(solution)/shard_map/local/pallas_call | solution.py:781
  47.3 7.0 %step.5 = (f32[8,128,128]{2,1,0:T(8,128)S(1)}, bf16[8,1024,256]{2,1,0:T(8,128)(2,1)}, f32[8,64,128]{2,1,0:T(8,128)S(1)}, f32[96,128]{1,0:T(8,128)S(1)}, f32[320,...) custom-call(s32[5]{0:T(128)S(1)} %copy-done.4, f32[8,128,128]{2,1,0:T(8,128)S(1)} %local.4.local_ref, ...), custom_call_target="tpu_custom_call" | custom-call | tf_op jit(solution)/shard_map/step/pallas_call | solution.py:845
  54.3 5.0 %collective-permute-start.13 = (f32[320,128]{1,0:T(8,128)S(1)}, f32[320,128]{1,0:T(8,128)S(1)}, u32[]{:S(2)}, u32[]{:S(2)}) collective-permute-start(f32[320,128]{1,0:T(8,128)S(1)} %get-tuple-element.71), channel_id=1, source_target_pairs={{0,2},{4,6},{2,0},{6,4},{1,3},{5,7},{3,1},{7,5},{8,10},{12,14},{10... | collective-permute-start | bytes 491528 | tf_op jit(solution)/shard_map/ppermute | solution.py:751
  60.1 2.8 %collective-permute-start.15 = (f32[32,128]{1,0:T(8,128)S(1)}, f32[32,128]{1,0:T(8,128)S(1)}, u32[]{:S(2)}, u32[]{:S(2)}) collective-permute-start(f32[32,128]{1,0:T(8,128)S(1)} %get-tuple-element.73), channel_id=1, source_target_pairs={{0,4},{2,6},{4,0},{6,2},{1,5},{3,7},{5,1},{7,3},{8,12},{10,14},{12... | collective-permute-start | bytes 49160 | tf_op jit(solution)/shard_map/ppermute | solution.py:751
  62.9 2.4 %local.5.local_ref = f32[8,128,128]{2,1,0:T(8,128)S(1)} custom-call(s32[5]{0:T(128)S(1)} %copy-done.2, f32[8,128,128]{2,1,0:T(8,128)S(1)} %get-tuple-element.68.y_ref.refs_0_, f32[8,128,128]{2,1,0:T(8,128)S(1)} %get-tuple-element.55.y_ref.refs_5_.refs_0_, f32[8,64,128]{2,1,0:T(8,128)S(1)} %get-tuple-element.69.refs_1_), custom_call_target="tpu_custom_call" | custom-call | flops 7864320 | bytes 2097152 | tf_op jit(solution)/shard_map/local/pallas_call | solution.py:781
  66.5 6.4 %step.6 = (f32[8,128,128]{2,1,0:T(8,128)S(1)}, f32[96,128]{1,0:T(8,128)S(1)}, f32[320,128]{1,0:T(8,128)S(1)}, f32[320,128]{1,0:T(8,128)S(1)}, f32[32,128]{1,0:T(8,128)S(1)}) custom-call(s32[5]{0:T(128)S(1)} %copy-done.4, f32[8,128,128]{2,1,0:T(8,128)S(1)} %local.5.local_ref, f32[96,128]{1,0:T(8,128)S(1)} %get-tuple-element.70.refs_0_, ...), custom_call_target="tpu_custom_call" | custom-call | tf_op jit(solution)/shard_map/step/pallas_call | solution.py:845
  74.8 3.6 %collective-permute-start.18 = (f32[32,128]{1,0:T(8,128)S(1)}, f32[32,128]{1,0:T(8,128)S(1)}, u32[]{:S(2)}, u32[]{:S(2)}) collective-permute-start(f32[32,128]{1,0:T(8,128)S(1)} %get-tuple-element.79), channel_id=1, source_target_pairs={{0,4},{2,6},{4,0},{6,2},{1,5},{3,7},{5,1},{7,3},{8,12},{10,14},{12... | collective-permute-start | bytes 49160 | tf_op jit(solution)/shard_map/ppermute | solution.py:751
  78.4 2.4 %local.6.local_ref = f32[8,128,128]{2,1,0:T(8,128)S(1)} custom-call(s32[5]{0:T(128)S(1)} %copy-done.3, f32[8,128,128]{2,1,0:T(8,128)S(1)} %get-tuple-element.75.y_ref.refs_0_, f32[8,128,128]{2,1,0:T(8,128)S(1)} %get-tuple-element.68.y_ref.refs_0_, f32[8,64,128]{2,1,0:T(8,128)S(1)} %get-tuple-element.69.refs_1_), custom_call_target="tpu_custom_call" | custom-call | flops 7864320 | bytes 2097152 | tf_op jit(solution)/shard_map/local/pallas_call | solution.py:781
  81.8 6.4 %step.7 = (f32[8,128,128]{2,1,0:T(8,128)S(1)}, f32[96,128]{1,0:T(8,128)S(1)}, f32[320,128]{1,0:T(8,128)S(1)}, f32[320,128]{1,0:T(8,128)S(1)}, f32[32,128]{1,0:T(8,128)S(1)}) custom-call(s32[5]{0:T(128)S(1)} %copy-done.4, f32[8,128,128]{2,1,0:T(8,128)S(1)} %local.6.local_ref, f32[96,128]{1,0:T(8,128)S(1)} %get-tuple-element.76.refs_0_, ...), custom_call_target="tpu_custom_call" | custom-call | tf_op jit(solution)/shard_map/step/pallas_call | solution.py:845
  90.6 3.2 %collective-permute-start.21 = (f32[32,128]{1,0:T(8,128)S(1)}, f32[32,128]{1,0:T(8,128)S(1)}, u32[]{:S(2)}, u32[]{:S(2)}) collective-permute-start(f32[32,128]{1,0:T(8,128)S(1)} %get-tuple-element.84), channel_id=1, source_target_pairs={{0,4},{2,6},{4,0},{6,2},{1,5},{3,7},{5,1},{7,3},{8,12},{10,14},{12... | collective-permute-start | bytes 49160 | tf_op jit(solution)/shard_map/ppermute | solution.py:751
  93.9 2.4 %local.7.local_ref = f32[8,128,128]{2,1,0:T(8,128)S(1)} custom-call(s32[5]{0:T(128)S(1)} %copy-done.3, f32[8,128,128]{2,1,0:T(8,128)S(1)} %get-tuple-element.80.y_ref, f32[8,128,128]{2,1,0:T(8,128)S(1)} %get-tuple-element.75.y_ref.refs_0_, f32[8,64,128]{2,1,0:T(8,128)S(1)} %get-tuple-element.69.refs_1_), custom_call_target="tpu_custom_call" | custom-call | flops 7864320 | bytes 2097152 | tf_op jit(solution)/shard_map/local/pallas_call | solution.py:781
  97.1 3.5 %step.9 = (f32[8,128,128]{2,1,0:T(8,128)S(1)}, f32[1,128,128]{2,1,0:T(8,128)S(1)}, f32[1,128,128]{2,1,0:T(8,128)S(1)}, f32[1,128,128]{2,1,0:T(8,128)S(1)}) fusion(f32[8,128,128]{2,1,0:T(8,128)S(1)} %broadcast_in_dim.3, s32[]{:T(128)S(6)} %select_n.100, s32[5]{0:T(128)S(1)} %copy-done.4, f32[8,128,128]{2,1,0:T(8,128)S(1)} %local.7.local_ref, ...), kind=kCustom, calls=%fused_computation.29 | custom fusion | bytes 6013444 | tf_op jit(solution)/shard_map/step/pallas_call | solution.py:845
  102.1 2.2 %copy-done = bf16[8,1024,256]{2,1,0:T(8,128)(2,1)S(1)} copy-done((bf16[8,1024,256]{2,1,0:T(8,128)(2,1)S(1)}, bf16[8,1024,256]{2,1,0:T(8,128)(2,1)}, u32[]{:S(2)}) %copy-start) | copy-done | bytes 4194328
  104.3 3.1 %step.8 = (f32[1,128,128]{2,1,0:T(8,128)S(1)}, f32[1,128,128]{2,1,0:T(8,128)S(1)}, f32[1,128,128]{2,1,0:T(8,128)S(1)}, f32[1,128,128]{2,1,0:T(8,128)S(1)}) custom-call(s32[5]{0:T(128)S(1)} %copy-done.4, f32[8,128,128]{2,1,0:T(8,128)S(1)} %local.7.local_ref, f32[96,128]{1,0:T(8,128)S(1)} %get-tuple-element.81.refs_0_, ...), custom_call_target="tpu_custom_call" | custom-call | tf_op jit(solution)/shard_map/step/pallas_call | solution.py:845
  114.8 2.3 %collective-permute-done.28 = f32[1,128,128]{2,1,0:T(8,128)S(1)} collective-permute-done((f32[1,128,128]{2,1,0:T(8,128)S(1)}, f32[1,128,128]{2,1,0:T(8,128)S(1)}, u32[]{:S(2)}, u32[]{:S(2)}) %collective-permute-start.28) | collective-permute-done | bytes 65568 | tf_op jit(solution)/shard_map/ppermute | solution.py:872
  (86 shorter events, 33.2 us)
Async XLA Ops:
  2.2 15.9 %collective-permute-start = (f32[1088,128]{1,0:T(8,128)}, f32[1088,128]{1,0:T(8,128)S(1)}, u32[]{:S(2)}, u32[]{:S(2)}) collective-permute-start(f32[1088,128]{1,0:T(8,128)} %pack.1.payload_ref.refs_6_), channel_id=1, source_target_pairs={{0,1},{1,0},{2,3},{3,2},{4,5},{5,4},{6,7},{7,6},{8,9},{9,8},{10,11... | collective-permute-start | bytes 1671176 | tf_op jit(solution)/shard_map/ppermute | solution.py:597
  5.2 14.4 %collective-permute-start.1 = (f32[1088,128]{1,0:T(8,128)}, f32[1088,128]{1,0:T(8,128)}, u32[]{:S(2)}, u32[]{:S(2)}) collective-permute-start(f32[1088,128]{1,0:T(8,128)} %pack.1.payload_ref.refs_6_), channel_id=1, source_target_pairs={{0,16},{8,24},{16,0},{24,8},{1,17},{9,25},{17,1},{25,9},{2,18},{10... | collective-permute-start | bytes 1671176 | tf_op jit(solution)/shard_map/ppermute | solution.py:597
  6.7 12.9 %collective-permute-start.2 = (f32[1088,128]{1,0:T(8,128)}, f32[1088,128]{1,0:T(8,128)S(1)}, u32[]{:S(2)}, u32[]{:S(2)}) collective-permute-start(f32[1088,128]{1,0:T(8,128)} %pack.1.payload_ref.refs_6_), channel_id=1, source_target_pairs={{0,8},{8,0},{16,24},{24,16},{1,9},{9,1},{17,25},{25,17},{2,10},{10... | collective-permute-start | bytes 1671176 | tf_op jit(solution)/shard_map/ppermute | solution.py:597
  19.6 14.4 %collective-permute-start.5 = (f32[1088,128]{1,0:T(8,128)S(1)}, f32[1088,128]{1,0:T(8,128)S(1)}, u32[]{:S(2)}, u32[]{:S(2)}) collective-permute-start(f32[1088,128]{1,0:T(8,128)S(1)} %collective-permute-done.refs_7_), channel_id=1, source_target_pairs={{0,8},{8,0},{16,24},{24,16},{1,9},{9,1},{17,25},{25,17},{2,10},{10... | collective-permute-start | bytes 1671176 | tf_op jit(solution)/shard_map/ppermute | solution.py:597
  19.6 14.4 %collective-permute-start.6 = (f32[1088,128]{1,0:T(8,128)}, f32[1088,128]{1,0:T(8,128)}, u32[]{:S(2)}, u32[]{:S(2)}) collective-permute-start(f32[1088,128]{1,0:T(8,128)} %collective-permute-done.1.refs_8_), channel_id=1, source_target_pairs={{0,8},{8,0},{16,24},{24,16},{1,9},{9,1},{17,25},{25,17},{2,10},{10... | collective-permute-start | bytes 1671176 | tf_op jit(solution)/shard_map/ppermute | solution.py:597
  20.1 13.9 %all-to-all-start = ((f32[8,152,128]{2,1,0:T(8,128)}), f32[8,152,128]{2,1,0:T(8,128)S(1)}, u32[]{:S(2)}, u32[]{:S(2)}) async-start(f32[8,152,128]{2,1,0:T(8,128)} %get-tuple-element.53), calls=%async_computation | async-start | bytes 1245184 | tf_op jit(solution)/shard_map/all_to_all | solution.py:692
  27.0 15.9 %collective-permute-start.3 = (f32[544,128]{1,0:T(8,128)}, f32[544,128]{1,0:T(8,128)S(1)}, u32[]{:S(2)}, u32[]{:S(2)}) collective-permute-start(f32[544,128]{1,0:T(8,128)} %slice.15), channel_id=1, source_target_pairs={{0,16},{8,24},{16,0},{24,8},{1,17},{9,25},{17,1},{25,9},{2,18},{10... | collective-permute-start | bytes 835592 | tf_op jit(solution)/shard_map/ppermute | solution.py:597
  28.9 13.9 %collective-permute-start.4 = (f32[544,128]{1,0:T(8,128)}, f32[544,128]{1,0:T(8,128)}, u32[]{:S(2)}, u32[]{:S(2)}) collective-permute-start(f32[544,128]{1,0:T(8,128)} %slice.16), channel_id=1, source_target_pairs={{0,1},{1,0},{2,3},{3,2},{4,5},{5,4},{6,7},{7,6},{8,9},{9,8},{10,11... | collective-permute-start | bytes 835592 | tf_op jit(solution)/shard_map/ppermute | solution.py:597
  35.9 7.5 %collective-permute-start.9 = (f32[64,128]{1,0:T(8,128)S(1)}, f32[64,128]{1,0:T(8,128)S(1)}, u32[]{:S(2)}, u32[]{:S(2)}) collective-permute-start(f32[64,128]{1,0:T(8,128)S(1)} %get-tuple-element.60), channel_id=1, source_target_pairs={{0,4},{2,6},{4,0},{6,2},{1,5},{3,7},{5,1},{7,3},{8,12},{10,14},{12... | collective-permute-start | bytes 98312 | tf_op jit(solution)/shard_map/ppermute | solution.py:751
  38.6 6.6 %collective-permute-start.7 = (f32[352,128]{1,0:T(8,128)S(1)}, f32[352,128]{1,0:T(8,128)S(1)}, u32[]{:S(2)}, u32[]{:S(2)}) collective-permute-start(f32[352,128]{1,0:T(8,128)S(1)} %get-tuple-element.58), channel_id=1, source_target_pairs={{0,2},{4,6},{2,0},{6,4},{1,3},{5,7},{3,1},{7,5},{8,10},{12,14},{10... | collective-permute-start | bytes 540680 | tf_op jit(solution)/shard_map/ppermute | solution.py:751
  40.2 5.5 %collective-permute-start.10 = (f32[32,128]{1,0:T(8,128)S(1)}, f32[32,128]{1,0:T(8,128)S(1)}, u32[]{:S(2)}, u32[]{:S(2)}) collective-permute-start(f32[32,128]{1,0:T(8,128)S(1)} %slice.17.refs_0_), channel_id=1, source_target_pairs={{0,6},{2,4},{4,2},{6,0},{1,7},{3,5},{5,3},{7,1},{8,14},{10,12},{12... | collective-permute-start | bytes 49160 | tf_op jit(solution)/shard_map/ppermute | solution.py:772
  54.3 12.2 %collective-permute-start.13 = (f32[320,128]{1,0:T(8,128)S(1)}, f32[320,128]{1,0:T(8,128)S(1)}, u32[]{:S(2)}, u32[]{:S(2)}) collective-permute-start(f32[320,128]{1,0:T(8,128)S(1)} %get-tuple-element.71), channel_id=1, source_target_pairs={{0,2},{4,6},{2,0},{6,4},{1,3},{5,7},{3,1},{7,5},{8,10},{12,14},{10... | collective-permute-start | bytes 491528 | tf_op jit(solution)/shard_map/ppermute | solution.py:751
  59.3 7.2 %collective-permute-start.14 = (f32[320,128]{1,0:T(8,128)S(1)}, f32[320,128]{1,0:T(8,128)S(1)}, u32[]{:S(2)}, u32[]{:S(2)}) collective-permute-start(f32[320,128]{1,0:T(8,128)S(1)} %get-tuple-element.72), channel_id=1, source_target_pairs={{2,4},{4,2},{3,5},{5,3},{10,12},{12,10},{11,13},{13,11},{18,20},{2... | collective-permute-start | bytes 491528 | tf_op jit(solution)/shard_map/ppermute | solution.py:751
  60.1 6.4 %collective-permute-start.15 = (f32[32,128]{1,0:T(8,128)S(1)}, f32[32,128]{1,0:T(8,128)S(1)}, u32[]{:S(2)}, u32[]{:S(2)}) collective-permute-start(f32[32,128]{1,0:T(8,128)S(1)} %get-tuple-element.73), channel_id=1, source_target_pairs={{0,4},{2,6},{4,0},{6,2},{1,5},{3,7},{5,1},{7,3},{8,12},{10,14},{12... | collective-permute-start | bytes 49160 | tf_op jit(solution)/shard_map/ppermute | solution.py:751
  72.9 8.9 %collective-permute-start.16 = (f32[320,128]{1,0:T(8,128)S(1)}, f32[320,128]{1,0:T(8,128)S(1)}, u32[]{:S(2)}, u32[]{:S(2)}) collective-permute-start(f32[320,128]{1,0:T(8,128)S(1)} %get-tuple-element.77), channel_id=1, source_target_pairs={{0,2},{4,6},{2,0},{6,4},{1,3},{5,7},{3,1},{7,5},{8,10},{12,14},{10... | collective-permute-start | bytes 491528 | tf_op jit(solution)/shard_map/ppermute | solution.py:751
  74.1 7.7 %collective-permute-start.17 = (f32[320,128]{1,0:T(8,128)S(1)}, f32[320,128]{1,0:T(8,128)S(1)}, u32[]{:S(2)}, u32[]{:S(2)}) collective-permute-start(f32[320,128]{1,0:T(8,128)S(1)} %get-tuple-element.78), channel_id=1, source_target_pairs={{2,4},{4,2},{3,5},{5,3},{10,12},{12,10},{11,13},{13,11},{18,20},{2... | collective-permute-start | bytes 491528 | tf_op jit(solution)/shard_map/ppermute | solution.py:751
  74.8 7.0 %collective-permute-start.18 = (f32[32,128]{1,0:T(8,128)S(1)}, f32[32,128]{1,0:T(8,128)S(1)}, u32[]{:S(2)}, u32[]{:S(2)}) collective-permute-start(f32[32,128]{1,0:T(8,128)S(1)} %get-tuple-element.79), channel_id=1, source_target_pairs={{0,4},{2,6},{4,0},{6,2},{1,5},{3,7},{5,1},{7,3},{8,12},{10,14},{12... | collective-permute-start | bytes 49160 | tf_op jit(solution)/shard_map/ppermute | solution.py:751
  88.1 8.9 %collective-permute-start.19 = (f32[320,128]{1,0:T(8,128)S(1)}, f32[320,128]{1,0:T(8,128)S(1)}, u32[]{:S(2)}, u32[]{:S(2)}) collective-permute-start(f32[320,128]{1,0:T(8,128)S(1)} %get-tuple-element.82), channel_id=1, source_target_pairs={{0,2},{4,6},{2,0},{6,4},{1,3},{5,7},{3,1},{7,5},{8,10},{12,14},{10... | collective-permute-start | bytes 491528 | tf_op jit(solution)/shard_map/ppermute | solution.py:751
  89.7 7.3 %collective-permute-start.20 = (f32[320,128]{1,0:T(8,128)S(1)}, f32[320,128]{1,0:T(8,128)S(1)}, u32[]{:S(2)}, u32[]{:S(2)}) collective-permute-start(f32[320,128]{1,0:T(8,128)S(1)} %get-tuple-element.83), channel_id=1, source_target_pairs={{2,4},{4,2},{3,5},{5,3},{10,12},{12,10},{11,13},{13,11},{18,20},{2... | collective-permute-start | bytes 491528 | tf_op jit(solution)/shard_map/ppermute | solution.py:751
  90.6 6.4 %collective-permute-start.21 = (f32[32,128]{1,0:T(8,128)S(1)}, f32[32,128]{1,0:T(8,128)S(1)}, u32[]{:S(2)}, u32[]{:S(2)}) collective-permute-start(f32[32,128]{1,0:T(8,128)S(1)} %get-tuple-element.84), channel_id=1, source_target_pairs={{0,4},{2,6},{4,0},{6,2},{1,5},{3,7},{5,1},{7,3},{8,12},{10,14},{12... | collective-permute-start | bytes 49160 | tf_op jit(solution)/shard_map/ppermute | solution.py:751
  100.6 9.9 %collective-permute-start.22 = (f32[1,128,128]{2,1,0:T(8,128)S(1)}, f32[1,128,128]{2,1,0:T(8,128)S(1)}, u32[]{:S(2)}, u32[]{:S(2)}) collective-permute-start(f32[1,128,128]{2,1,0:T(8,128)S(1)} %get-tuple-element.96), channel_id=1, source_target_pairs={{0,1},{1,0},{8,9},{9,8},{16,17},{17,16},{24,25},{25,24},{2,3},{3,2... | collective-permute-start | bytes 196616 | tf_op jit(solution)/shard_map/ppermute | solution.py:872
  107.3 6.1 %collective-permute-start.25 = (f32[1,128,128]{2,1,0:T(8,128)S(1)}, f32[1,128,128]{2,1,0:T(8,128)S(1)}, u32[]{:S(2)}, u32[]{:S(2)}) collective-permute-start(f32[1,128,128]{2,1,0:T(8,128)S(1)} %get-tuple-element.89), channel_id=1, source_target_pairs={{0,8},{1,9},{8,0},{9,1},{16,24},{17,25},{24,16},{25,17},{2,10},{3,... | collective-permute-start | bytes 196616 | tf_op jit(solution)/shard_map/ppermute | solution.py:872
  108.0 5.4 %collective-permute-start.24 = (f32[1,128,128]{2,1,0:T(8,128)S(1)}, f32[1,128,128]{2,1,0:T(8,128)S(1)}, u32[]{:S(2)}, u32[]{:S(2)}) collective-permute-start(f32[1,128,128]{2,1,0:T(8,128)S(1)} %get-tuple-element.100), channel_id=1, source_target_pairs={{0,17},{1,16},{8,25},{9,24},{16,1},{17,0},{24,9},{25,8},{2,19},{3,... | collective-permute-start | bytes 196616 | tf_op jit(solution)/shard_map/ppermute | solution.py:872
  109.5 5.2 %collective-permute-start.26 = (f32[1,128,128]{2,1,0:T(8,128)S(1)}, f32[1,128,128]{2,1,0:T(8,128)S(1)}, u32[]{:S(2)}, u32[]{:S(2)}) collective-permute-start(f32[1,128,128]{2,1,0:T(8,128)S(1)} %get-tuple-element.90), channel_id=1, source_target_pairs={{0,9},{1,8},{8,1},{9,0},{16,25},{17,24},{24,17},{25,16},{2,11},{3,... | collective-permute-start | bytes 196616 | tf_op jit(solution)/shard_map/ppermute | solution.py:872
  (14 other events, 162.0 us)

commit v7 on v5

--- a/solution.py
+++ b/solution.py
@@ -145,12 +145,12 @@
     on, points, slots, projs = plan.on, plan.points, plan.slots, plan.projs
     rows = on * points
     boths = []
-    for y_block, stack in zip(y_blocks, stacks):
+    for y_block, stack_of in zip(y_blocks, stacks):
         hi, lo = hi_lo(y_block)
         left = jnp.concatenate(
             [jnp.concatenate([hi, hi], axis=1), jnp.concatenate([lo, lo], axis=1)], axis=0
         )
-        boths.append(dot_nt(left, stack))
+        boths.append(dot_nt(left, stack_of()))
     partials = []
     for both, column in zip(boths, columns):
         mask = column == lax.broadcasted_iota(jnp.int32, (points, slots), 0)
@@ -202,7 +202,7 @@
             bands.append(jnp.concatenate(pieces, axis=1))
         hi, lo = hi_lo(jnp.concatenate(bands, axis=0))
         splits.append(jnp.concatenate([hi, lo], axis=0))
-    fours = [dot_nn(split, stack) for split, stack in zip(splits, stacks)]
+    fours = [dot_nn(split, stack_of()) for split, stack_of in zip(splits, stacks)]
     rows, cx = on * points, plan.cx
     return [
         (four[:rows, :cx] + four[rows:, cx:]) + (four[:rows, cx:] + four[rows:, :cx])
@@ -334,40 +334,43 @@
 
 
 def own_tiles_kernel(
-    plan, info_ref, payload_ref, atom_ref, column_ref, coupling_ref, y_ref,
-    out_ref, info_out_ref, stack_ref, meta_ref,
+    plan, info_ref, payload_ref, atom_in, column_in, coupling_in, y_in,
+    out_ref, info_out_ref, stack_ref, meta_ref, atom_ref, column_ref, coupling_ref, y_ref, sem,
 ):
     count = plan.slots // LANE
-
-    @pl.when(pl.program_id(0) == 0)
-    def _():
-        fill_stack(plan, stack_ref, payload_ref[: plan.projs * plan.slots, :])
-        for i in range(info_out_ref.shape[0]):
-            info_out_ref[i] = info_ref[i]
-        atom, column = atom_ref[...], column_ref[...]
-        owner = lax.shift_right_logical(atom, log2(plan.owned))
-        owner_z = owner & (plan.gz - 1)
-        owner_y = lax.shift_right_logical(owner, log2(plan.gz)) & (plan.gy - 1)
-        owner_x = lax.shift_right_logical(owner, log2(plan.gz) + log2(plan.gy))
-        key = (owner_y - info_ref[3] + 1) * (plan.blocks * plan.owned)
-        key = key + (owner_x * plan.gz + owner_z) * plan.owned + (atom & (plan.owned - 1))
-        lane = lax.broadcasted_iota(jnp.int32, column.shape, 1)
-        column = jnp.where(lane < info_ref[4], column, -1)
-        meta_ref[...] = jnp.zeros_like(meta_ref)
-        for row, line in enumerate((key, column)):
-            line = line.astype(jnp.float32)
-            for i in range(count):
-                at = row * count + i
-                meta_ref[at : at + 1, :] = line[:, i * LANE : (i + 1) * LANE]
-        for p in range(plan.projs):
-            at = 2 * count + p
-            meta_ref[at : at + 1, : plan.owned] = coupling_ref[p : p + 1, :]
-
+    pairs = ((atom_in, atom_ref), (column_in, column_ref), (coupling_in, coupling_ref), (y_in, y_ref))
+    copies = [pltpu.make_async_copy(a, b, sem.at[i]) for i, (a, b) in enumerate(pairs)]
+    for copy in copies:
+        copy.start()
+    fill_stack(plan, stack_ref, payload_ref[: plan.projs * plan.slots, :])
+    for i in range(info_out_ref.shape[0]):
+        info_out_ref[i] = info_ref[i]
+    for copy in copies[:3]:
+        copy.wait()
+    atom, column = atom_ref[...], column_ref[...]
+    owner = lax.shift_right_logical(atom, log2(plan.owned))
+    owner_z = owner & (plan.gz - 1)
+    owner_y = lax.shift_right_logical(owner, log2(plan.gz)) & (plan.gy - 1)
+    owner_x = lax.shift_right_logical(owner, log2(plan.gz) + log2(plan.gy))
+    key = (owner_y - info_ref[3] + 1) * (plan.blocks * plan.owned)
+    key = key + (owner_x * plan.gz + owner_z) * plan.owned + (atom & (plan.owned - 1))
+    lane = lax.broadcasted_iota(jnp.int32, column.shape, 1)
+    column = jnp.where(lane < info_ref[4], column, -1)
+    meta_ref[...] = jnp.zeros_like(meta_ref)
+    for row, line in enumerate((key, column)):
+        line = line.astype(jnp.float32)
+        for i in range(count):
+            at = row * count + i
+            meta_ref[at : at + 1, :] = line[:, i * LANE : (i + 1) * LANE]
+    for p in range(plan.projs):
+        at = 2 * count + p
+        meta_ref[at : at + 1, : plan.owned] = coupling_ref[p : p + 1, :]
     meta = meta_ref[...]
-    columns = meta_line(plan, meta, 1).astype(jnp.int32)
-    y_rows, f = plan.y_rows, plan.features
-    y_blocks = [y_ref[part] for part in range(plan.per)]
-    partials = tile_sums(plan, y_blocks, [stack_ref[...]] * plan.per, [columns] * plan.per)
+    copies[3].wait()
+    y_rows, f, blocks = plan.y_rows, plan.features, plan.blocks
+    y_blocks = [y_ref[part] for part in range(blocks)]
+    load = lambda: stack_ref[...]
+    partials = tile_sums(plan, y_blocks, [load] * blocks, [column] * blocks)
     for part, (y_block, partial) in enumerate(zip(y_blocks, partials)):
         out_ref[part, :y_rows, :] = y_block
         for j in range(count):
@@ -542,7 +545,7 @@
     columns = [place_ref[part, 0:1, :] for part in parts]
     groups = [place_ref[part, 1:2, :] for part in parts]
     hots = [hot_ref[part] for part in parts]
-    stacks = [stack_ref[part] for part in parts]
+    stacks = [lambda part=part: stack_ref[part] for part in parts]
     projected = backward_blocks(plan, coef_ref[...], stacks, hots, groups, columns)
     y_blocks = []
     for part in parts:
@@ -641,8 +644,10 @@
     y_rows = plan.y_rows
     full = lambda *shape: pl.BlockSpec(shape, lambda *_: (0,) * len(shape))
     each = lambda count, *shape: pl.BlockSpec((count,) + shape, lambda i, *_: (i, 0, 0))
-    params = pltpu.CompilerParams(vmem_limit_bytes=48 * 1024 * 1024)
+    params = pltpu.CompilerParams(vmem_limit_bytes=28 * 1024 * 1024)
     rows = tile_rows + points
+    in_hbm = pl.BlockSpec(memory_space=pltpu.HBM)
+    alone = pltpu.CompilerParams(vmem_limit_bytes=61 * 1024 * 1024)
     payload = pl.pallas_call(
         functools.partial(pack_kernel, plan),
         out_shape=jax.ShapeDtypeStruct((rows, cx), f32),
@@ -663,21 +668,18 @@
             jax.ShapeDtypeStruct((blocks, plan.meta_at + meta_rows, cx), f32),
             jax.ShapeDtypeStruct(info.shape, jnp.int32),
         ],
-        grid=(blocks // per,),
-        in_specs=[
-            smem,
-            full(rows, cx),
-            full(1, slots),
-            full(1, slots),
-            full(projs, owned),
-            each(per, y_rows, cx),
-        ],
-        out_specs=[each(per, plan.meta_at + meta_rows, cx), smem],
+        in_specs=[smem, full(rows, cx), in_hbm, in_hbm, in_hbm, in_hbm],
+        out_specs=[full(blocks, plan.meta_at + meta_rows, cx), smem],
         scratch_shapes=[
             pltpu.VMEM((tile_rows, 2 * cx), jnp.bfloat16),
             pltpu.VMEM((meta_rows, LANE), f32),
+            pltpu.VMEM((1, slots), jnp.int32),
+            pltpu.VMEM((1, slots), jnp.int32),
+            pltpu.VMEM((projs, owned), f32),
+            pltpu.VMEM((blocks, y_rows, cx), f32),
+            pltpu.SemaphoreType.DMA((4,)),
         ],
-        compiler_params=params,
+        compiler_params=alone,
         name="own_tiles",
     )(
         info,
@@ -689,7 +691,9 @@
     )
     arrived = lax.all_to_all(messages, ("gx", "gz"), 0, 0, tiled=True)
 
-    from_z, from_x, late_info = lax.optimization_barrier((from_z, from_x, late_info))
+    from_z, from_x, from_c, late_info = lax.optimization_barrier(
+        (from_z, from_x, from_c, late_info)
+    )
     cut = rows // 2
     from_xz = [exchange(from_z[:cut], *rounds[1]), exchange(from_x[cut:], *rounds[0])]
     from_core = [from_c, exchange(from_z, *rounds[2]), exchange(from_x, *rounds[2])]

time: 109 us -> 106 us (0.972)
  starting transfers between devices: 40.7 us -> 43.8 us
  local copies, waits for them, and re-layouts: 13.9 us -> 11.3 us
  waiting for transfers between devices: 18.5 us -> 16.1 us
  Pallas kernels: 34.6 us -> 33.4 us
    pallas_call x4, Pallas kernels: 19.8 us -> 16.3 us  [turned_path(): pl.pallas_call(functools.partial(step_kernel, plan, first, last, base), o...]
    ppermute x7, waiting for transfers between devices: 5.62 us -> 2.95 us  [turned_path(): lax.ppermute(block, ('gx', 'gz'), [(i, i ^ moved) for i in range(blocks)])]
    unnamed x24, local copies, waits for them, and re-layouts: 8.9 us -> 6.45 us
    ppermute x7, starting transfers between devices: 5.52 us -> 7.73 us  [turned_path(): lax.ppermute(block, ('gx', 'gz'), [(i, i ^ moved) for i in range(blocks)])]
    ppermute x9, waiting for transfers between devices: 2.32 us -> 4.38 us  [exchange(): return lax.ppermute(value, axis, [(i, i ^ bit) for i in range(count)])]
    pallas_call x1, Pallas kernels: 2.92 us -> 4.32 us  [turned_path(): pl.pallas_call(functools.partial(own_tiles_kernel, plan), out_shape=[jax....]
    all_to_all x1, waiting for transfers between devices: 4.37 us -> 3.25 us  [turned_path(): arrived = lax.all_to_all(messages, ('gx', 'gz'), 0, 0, tiled=True)]
  transfers between devices with their start and end apart: 30 -> 30, of which waited for: 12 -> 12; matrix products, arithmetic and copies ran while one was open for 2% -> 2% of each run, Pallas kernels for 15% -> 17%
where the time goes in v7:
time: 106 us
  starting transfers between devices  43.8 us (41%)
  Pallas kernels  33.4 us (32%)
  waiting for transfers between devices  16.1 us (15%)
  local copies, waits for them, and re-layouts  11.3 us (11%)
    ppermute x12, starting transfers between devices, pairwise(): return lax.ppermute(value, 'gy', pairs + [(b, a) for a, b in pairs])  23.7 us
    pallas_call x4, Pallas kernels, turned_path(): pl.pallas_call(functools.partial(step_kernel, plan, first, last, base), o...  16.3 us
    pallas_call x4, Pallas kernels, turned_path(): pl.pallas_call(functools.partial(local_kernel, plan, first), out_shape=y_...  8.96 us
    ppermute x7, starting transfers between devices, turned_path(): lax.ppermute(block, ('gx', 'gz'), [(i, i ^ moved) for i in range(blocks)])  7.73 us
    ppermute x9, starting transfers between devices, exchange(): return lax.ppermute(value, axis, [(i, i ^ bit) for i in range(count)])  7.49 us
    unnamed x24, local copies, waits for them, and re-layouts  6.45 us
    ppermute x9, waiting for transfers between devices, exchange(): return lax.ppermute(value, axis, [(i, i ^ bit) for i in range(count)])  4.38 us
    pallas_call x1, Pallas kernels, turned_path(): pl.pallas_call(functools.partial(own_tiles_kernel, plan), out_shape=[jax....  4.32 us
  transfers between devices with their start and end apart: 30, of which 12 were waited for; matrix products, arithmetic and copies ran while one was open for 2% of the time, Pallas kernels for 17%

profile of v7, /device:TPU:0, one launch (start us, length us, event | category | flops | bytes accessed | tf_op | source)
XLA Modules:
  0.0 105.8 jit_solution(12366896420160409743)
XLA Ops:
  2.9 3.0 %collective-permute-start = (f32[1088,128]{1,0:T(8,128)}, f32[1088,128]{1,0:T(8,128)S(1)}, u32[]{:S(2)}, u32[]{:S(2)}) collective-permute-start(f32[1088,128]{1,0:T(8,128)} %pack.1.payload_ref.refs_6_), channel_id=1, source_target_pairs={{0,1},{1,0},{2,3},{3,2},{4,5},{5,4},{6,7},{7,6},{8,9},{9,8},{10,11... | collective-permute-start | bytes 1671176 | tf_op jit(solution)/shard_map/ppermute | solution.py:600
  8.6 4.3 %own_tiles.1 = (f32[8,152,128]{2,1,0:T(8,128)}, s32[5]{0:T(128)}) custom-call(s32[5]{0:T(128)} %stack.19.info_ref, f32[1088,128]{1,0:T(8,128)} %pack.1.payload_ref.refs_6_, s32[1,256]{1,0:T(1,128)} %bitcast.21, s32[1,256]{1,0:T(1,128)} %bitcast.22, f32[4,64]{1,0:T(4,128)} %bitcast.20, f32[8,128,128]{2,1,0:T(8,128)} %bitcast.16), custom_call_target="tpu_custom_call" | custom-call | tf_op jit(solution)/shard_map/own_tiles/pallas_call | solution.py:665
  12.9 3.6 %all-to-all-start = ((f32[8,152,128]{2,1,0:T(8,128)}), f32[8,152,128]{2,1,0:T(8,128)S(1)}, u32[]{:S(2)}, u32[]{:S(2)}) async-start(f32[8,152,128]{2,1,0:T(8,128)} %get-tuple-element.50), calls=%async_computation | async-start | bytes 1245184 | tf_op jit(solution)/shard_map/all_to_all | solution.py:692
  16.5 2.2 %collective-permute-done.refs_7_ = f32[1088,128]{1,0:T(8,128)S(1)} collective-permute-done((f32[1088,128]{1,0:T(8,128)}, f32[1088,128]{1,0:T(8,128)S(1)}, u32[]{:S(2)}, u32[]{:S(2)}) %collective-permute-start) | collective-permute-done | bytes 557088 | tf_op jit(solution)/shard_map/ppermute | solution.py:600
  18.7 2.0 %collective-permute-done.1.refs_8_ = f32[1088,128]{1,0:T(8,128)S(1)} collective-permute-done((f32[1088,128]{1,0:T(8,128)}, f32[1088,128]{1,0:T(8,128)S(1)}, u32[]{:S(2)}, u32[]{:S(2)}) %collective-permute-start.1) | collective-permute-done | bytes 557088 | tf_op jit(solution)/shard_map/ppermute | solution.py:600
  21.5 2.4 %collective-permute-start.3 = (f32[544,128]{1,0:T(8,128)}, f32[544,128]{1,0:T(8,128)S(1)}, u32[]{:S(2)}, u32[]{:S(2)}) collective-permute-start(f32[544,128]{1,0:T(8,128)} %slice.15), channel_id=1, source_target_pairs={{0,16},{8,24},{16,0},{24,8},{1,17},{9,25},{17,1},{25,9},{2,18},{10... | collective-permute-start | bytes 835592 | tf_op jit(solution)/shard_map/ppermute | solution.py:600
  24.2 3.2 %all-to-all-done.in_ref = f32[8,152,128]{2,1,0:T(8,128)S(1)} async-done(((f32[8,152,128]{2,1,0:T(8,128)}), f32[8,152,128]{2,1,0:T(8,128)S(1)}, u32[]{:S(2)}, u32[]{:S(2)}) %all-to-all-start) | async-done | bytes 622624 | tf_op jit(solution)/shard_map/all_to_all | solution.py:692
  29.3 2.7 %collective-permute-start.7 = (f32[64,128]{1,0:T(8,128)S(1)}, f32[64,128]{1,0:T(8,128)S(1)}, u32[]{:S(2)}, u32[]{:S(2)}) collective-permute-start(f32[64,128]{1,0:T(8,128)S(1)} %get-tuple-element.56), channel_id=1, source_target_pairs={{0,4},{2,6},{4,0},{6,2},{1,5},{3,7},{5,1},{7,3},{8,12},{10,14},{12... | collective-permute-start | bytes 98312 | tf_op jit(solution)/shard_map/ppermute | solution.py:749
  34.1 2.2 %local.4.local_ref = f32[8,128,128]{2,1,0:T(8,128)S(1)} custom-call(s32[5]{0:T(128)S(1)} %copy-done.6, f32[8,128,128]{2,1,0:T(8,128)S(1)} %get-tuple-element.51.y_ref.refs_5_.refs_0_), custom_call_target="tpu_custom_call" | custom-call | flops 7864320 | bytes 2097152 | tf_op jit(solution)/shard_map/local/pallas_call | solution.py:779
  41.9 6.1 %step.5 = (f32[8,128,128]{2,1,0:T(8,128)S(1)}, bf16[8,1024,256]{2,1,0:T(8,128)(2,1)S(1)}, f32[8,64,128]{2,1,0:T(8,128)S(1)}, f32[96,128]{1,0:T(8,128)S(1)}, f32[...) custom-call(s32[5]{0:T(128)S(1)} %copy-done.8, f32[8,128,128]{2,1,0:T(8,128)S(1)} %local.4.local_ref, ...), custom_call_target="tpu_custom_call" | custom-call | tf_op jit(solution)/shard_map/step/pallas_call | solution.py:842
  48.0 5.5 %collective-permute-start.13 = (f32[320,128]{1,0:T(8,128)S(1)}, f32[320,128]{1,0:T(8,128)S(1)}, u32[]{:S(2)}, u32[]{:S(2)}) collective-permute-start(f32[320,128]{1,0:T(8,128)S(1)} %get-tuple-element.65), channel_id=1, source_target_pairs={{0,2},{4,6},{2,0},{6,4},{1,3},{5,7},{3,1},{7,5},{8,10},{12,14},{10... | collective-permute-start | bytes 491528 | tf_op jit(solution)/shard_map/ppermute | solution.py:749
  54.2 2.8 %collective-permute-start.15 = (f32[32,128]{1,0:T(8,128)S(1)}, f32[32,128]{1,0:T(8,128)S(1)}, u32[]{:S(2)}, u32[]{:S(2)}) collective-permute-start(f32[32,128]{1,0:T(8,128)S(1)} %get-tuple-element.67), channel_id=1, source_target_pairs={{0,4},{2,6},{4,0},{6,2},{1,5},{3,7},{5,1},{7,3},{8,12},{10,14},{12... | collective-permute-start | bytes 49160 | tf_op jit(solution)/shard_map/ppermute | solution.py:749
  57.0 2.2 %local.5.local_ref = f32[8,128,128]{2,1,0:T(8,128)S(1)} custom-call(s32[5]{0:T(128)S(1)} %copy-done.6, f32[8,128,128]{2,1,0:T(8,128)S(1)} %get-tuple-element.62.y_ref.refs_0_, f32[8,128,128]{2,1,0:T(8,128)S(1)} %get-tuple-element.51.y_ref.refs_5_.refs_0_, f32[8,64,128]{2,1,0:T(8,128)S(1)} %get-tuple-element.63.refs_1_), custom_call_target="tpu_custom_call" | custom-call | flops 7864320 | bytes 2097152 | tf_op jit(solution)/shard_map/local/pallas_call | solution.py:779
  60.7 4.3 %step.6 = (f32[8,128,128]{2,1,0:T(8,128)S(1)}, f32[96,128]{1,0:T(8,128)S(1)}, f32[320,128]{1,0:T(8,128)S(1)}, f32[320,128]{1,0:T(8,128)S(1)}, f32[32,128]{1,0:T(8,128)S(1)}) custom-call(s32[5]{0:T(128)S(1)} %copy-done.8, f32[8,128,128]{2,1,0:T(8,128)S(1)} %local.5.local_ref, f32[96,128]{1,0:T(8,128)S(1)} %get-tuple-element.64.refs_0_, ...), custom_call_target="tpu_custom_call" | custom-call | tf_op jit(solution)/shard_map/step/pallas_call | solution.py:842
  67.0 3.8 %collective-permute-start.18 = (f32[32,128]{1,0:T(8,128)S(1)}, f32[32,128]{1,0:T(8,128)S(1)}, u32[]{:S(2)}, u32[]{:S(2)}) collective-permute-start(f32[32,128]{1,0:T(8,128)S(1)} %get-tuple-element.73), channel_id=1, source_target_pairs={{0,4},{2,6},{4,0},{6,2},{1,5},{3,7},{5,1},{7,3},{8,12},{10,14},{12... | collective-permute-start | bytes 49160 | tf_op jit(solution)/shard_map/ppermute | solution.py:749
  70.7 2.2 %local.6.local_ref = f32[8,128,128]{2,1,0:T(8,128)S(1)} custom-call(s32[5]{0:T(128)S(1)} %copy-done.6, f32[8,128,128]{2,1,0:T(8,128)S(1)} %get-tuple-element.69.y_ref.refs_0_, f32[8,128,128]{2,1,0:T(8,128)S(1)} %get-tuple-element.62.y_ref.refs_0_, f32[8,64,128]{2,1,0:T(8,128)S(1)} %get-tuple-element.63.refs_1_), custom_call_target="tpu_custom_call" | custom-call | flops 7864320 | bytes 2097152 | tf_op jit(solution)/shard_map/local/pallas_call | solution.py:779
  74.0 4.3 %step.7 = (f32[8,128,128]{2,1,0:T(8,128)S(1)}, f32[96,128]{1,0:T(8,128)S(1)}, f32[320,128]{1,0:T(8,128)S(1)}, f32[320,128]{1,0:T(8,128)S(1)}, f32[32,128]{1,0:T(8,128)S(1)}) custom-call(s32[5]{0:T(128)S(1)} %copy-done.8, f32[8,128,128]{2,1,0:T(8,128)S(1)} %local.6.local_ref, f32[96,128]{1,0:T(8,128)S(1)} %get-tuple-element.70.refs_0_, ...), custom_call_target="tpu_custom_call" | custom-call | tf_op jit(solution)/shard_map/step/pallas_call | solution.py:842
  78.3 1.8 %collective-permute-start.19 = (f32[320,128]{1,0:T(8,128)S(1)}, f32[320,128]{1,0:T(8,128)S(1)}, u32[]{:S(2)}, u32[]{:S(2)}) collective-permute-start(f32[320,128]{1,0:T(8,128)S(1)} %get-tuple-element.76), channel_id=1, source_target_pairs={{0,2},{4,6},{2,0},{6,4},{1,3},{5,7},{3,1},{7,5},{8,10},{12,14},{10... | collective-permute-start | bytes 491528 | tf_op jit(solution)/shard_map/ppermute | solution.py:749
  80.7 3.1 %collective-permute-start.21 = (f32[32,128]{1,0:T(8,128)S(1)}, f32[32,128]{1,0:T(8,128)S(1)}, u32[]{:S(2)}, u32[]{:S(2)}) collective-permute-start(f32[32,128]{1,0:T(8,128)S(1)} %get-tuple-element.78), channel_id=1, source_target_pairs={{0,4},{2,6},{4,0},{6,2},{1,5},{3,7},{5,1},{7,3},{8,12},{10,14},{12... | collective-permute-start | bytes 49160 | tf_op jit(solution)/shard_map/ppermute | solution.py:749
  83.8 2.2 %local.7.local_ref = f32[8,128,128]{2,1,0:T(8,128)S(1)} custom-call(s32[5]{0:T(128)S(1)} %copy-done.7, f32[8,128,128]{2,1,0:T(8,128)S(1)} %get-tuple-element.74.y_ref, f32[8,128,128]{2,1,0:T(8,128)S(1)} %get-tuple-element.69.y_ref.refs_0_, f32[8,64,128]{2,1,0:T(8,128)S(1)} %get-tuple-element.63.refs_1_), custom_call_target="tpu_custom_call" | custom-call | flops 7864320 | bytes 2097152 | tf_op jit(solution)/shard_map/local/pallas_call | solution.py:779
  87.2 3.2 %step.9 = (f32[8,128,128]{2,1,0:T(8,128)S(1)}, f32[1,128,128]{2,1,0:T(8,128)S(1)}, f32[1,128,128]{2,1,0:T(8,128)S(1)}, f32[1,128,128]{2,1,0:T(8,128)S(1)}) fusion(f32[8,128,128]{2,1,0:T(8,128)S(1)} %broadcast_in_dim.3, s32[]{:T(128)S(6)} %select_n.100, s32[5]{0:T(128)S(1)} %copy-done.8, f32[8,128,128]{2,1,0:T(8,128)S(1)} %local.7.local_ref, ...), kind=kCustom, calls=%fused_computation.29 | custom fusion | bytes 6013444 | tf_op jit(solution)/shard_map/step/pallas_call | solution.py:842
  91.3 2.2 %copy-done.1 = bf16[8,1024,256]{2,1,0:T(8,128)(2,1)S(1)} copy-done((bf16[8,1024,256]{2,1,0:T(8,128)(2,1)S(1)}, bf16[8,1024,256]{2,1,0:T(8,128)(2,1)}, u32[]{:S(2)}) %copy-start.1) | copy-done | bytes 4194328
  95.2 1.7 %collective-permute-start.23 = (f32[1,128,128]{2,1,0:T(8,128)S(1)}, f32[1,128,128]{2,1,0:T(8,128)S(1)}, u32[]{:S(2)}, u32[]{:S(2)}) collective-permute-start(f32[1,128,128]{2,1,0:T(8,128)S(1)} %get-tuple-element.92), channel_id=1, source_target_pairs={{0,16},{1,17},{8,24},{9,25},{16,0},{17,1},{24,8},{25,9},{2,18},{3,... | collective-permute-start | bytes 196616 | tf_op jit(solution)/shard_map/ppermute | solution.py:869
  100.1 1.9 %collective-permute-start.28 = (f32[1,128,128]{2,1,0:T(8,128)S(1)}, f32[1,128,128]{2,1,0:T(8,128)S(1)}, u32[]{:S(2)}, u32[]{:S(2)}) collective-permute-start(f32[1,128,128]{2,1,0:T(8,128)S(1)} %get-tuple-element.86), channel_id=1, source_target_pairs={{0,25},{1,24},{8,17},{9,16},{16,9},{17,8},{24,1},{25,0},{2,27},{3,... | collective-permute-start | bytes 196616 | tf_op jit(solution)/shard_map/ppermute | solution.py:869
  (92 shorter events, 31.9 us)
Async XLA Ops:
  2.9 15.8 %collective-permute-start = (f32[1088,128]{1,0:T(8,128)}, f32[1088,128]{1,0:T(8,128)S(1)}, u32[]{:S(2)}, u32[]{:S(2)}) collective-permute-start(f32[1088,128]{1,0:T(8,128)} %pack.1.payload_ref.refs_6_), channel_id=1, source_target_pairs={{0,1},{1,0},{2,3},{3,2},{4,5},{5,4},{6,7},{7,6},{8,9},{9,8},{10,11... | collective-permute-start | bytes 1671176 | tf_op jit(solution)/shard_map/ppermute | solution.py:600
  5.9 14.9 %collective-permute-start.1 = (f32[1088,128]{1,0:T(8,128)}, f32[1088,128]{1,0:T(8,128)S(1)}, u32[]{:S(2)}, u32[]{:S(2)}) collective-permute-start(f32[1088,128]{1,0:T(8,128)} %pack.1.payload_ref.refs_6_), channel_id=1, source_target_pairs={{0,16},{8,24},{16,0},{24,8},{1,17},{9,25},{17,1},{25,9},{2,18},{10... | collective-permute-start | bytes 1671176 | tf_op jit(solution)/shard_map/ppermute | solution.py:600
  7.4 13.4 %collective-permute-start.2 = (f32[1088,128]{1,0:T(8,128)}, f32[1088,128]{1,0:T(8,128)S(1)}, u32[]{:S(2)}, u32[]{:S(2)}) collective-permute-start(f32[1088,128]{1,0:T(8,128)} %pack.1.payload_ref.refs_6_), channel_id=1, source_target_pairs={{0,8},{8,0},{16,24},{24,16},{1,9},{9,1},{17,25},{25,17},{2,10},{10... | collective-permute-start | bytes 1671176 | tf_op jit(solution)/shard_map/ppermute | solution.py:600
  12.9 14.5 %all-to-all-start = ((f32[8,152,128]{2,1,0:T(8,128)}), f32[8,152,128]{2,1,0:T(8,128)S(1)}, u32[]{:S(2)}, u32[]{:S(2)}) async-start(f32[8,152,128]{2,1,0:T(8,128)} %get-tuple-element.50), calls=%async_computation | async-start | bytes 1245184 | tf_op jit(solution)/shard_map/all_to_all | solution.py:692
  21.5 12.1 %collective-permute-start.3 = (f32[544,128]{1,0:T(8,128)}, f32[544,128]{1,0:T(8,128)S(1)}, u32[]{:S(2)}, u32[]{:S(2)}) collective-permute-start(f32[544,128]{1,0:T(8,128)} %slice.15), channel_id=1, source_target_pairs={{0,16},{8,24},{16,0},{24,8},{1,17},{9,25},{17,1},{25,9},{2,18},{10... | collective-permute-start | bytes 835592 | tf_op jit(solution)/shard_map/ppermute | solution.py:600
  23.9 9.7 %collective-permute-start.4 = (f32[544,128]{1,0:T(8,128)S(1)}, f32[544,128]{1,0:T(8,128)}, u32[]{:S(2)}, u32[]{:S(2)}) collective-permute-start(f32[544,128]{1,0:T(8,128)S(1)} %slice.16), channel_id=1, source_target_pairs={{0,1},{1,0},{2,3},{3,2},{4,5},{5,4},{6,7},{7,6},{8,9},{9,8},{10,11... | collective-permute-start | bytes 835592 | tf_op jit(solution)/shard_map/ppermute | solution.py:600
  29.3 9.1 %collective-permute-start.7 = (f32[64,128]{1,0:T(8,128)S(1)}, f32[64,128]{1,0:T(8,128)S(1)}, u32[]{:S(2)}, u32[]{:S(2)}) collective-permute-start(f32[64,128]{1,0:T(8,128)S(1)} %get-tuple-element.56), channel_id=1, source_target_pairs={{0,4},{2,6},{4,0},{6,2},{1,5},{3,7},{5,1},{7,3},{8,12},{10,14},{12... | collective-permute-start | bytes 98312 | tf_op jit(solution)/shard_map/ppermute | solution.py:749
  32.0 5.8 %collective-permute-start.8 = (f32[32,128]{1,0:T(8,128)S(1)}, f32[32,128]{1,0:T(8,128)S(1)}, u32[]{:S(2)}, u32[]{:S(2)}) collective-permute-start(f32[32,128]{1,0:T(8,128)S(1)} %slice.17.refs_0_), channel_id=1, source_target_pairs={{0,6},{2,4},{4,2},{6,0},{1,7},{3,5},{5,3},{7,1},{8,14},{10,12},{12... | collective-permute-start | bytes 49160 | tf_op jit(solution)/shard_map/ppermute | solution.py:770
  33.3 5.7 %collective-permute-start.5 = (f32[352,128]{1,0:T(8,128)S(1)}, f32[352,128]{1,0:T(8,128)S(1)}, u32[]{:S(2)}, u32[]{:S(2)}) collective-permute-start(f32[352,128]{1,0:T(8,128)S(1)} %get-tuple-element.54), channel_id=1, source_target_pairs={{0,2},{4,6},{2,0},{6,4},{1,3},{5,7},{3,1},{7,5},{8,10},{12,14},{10... | collective-permute-start | bytes 540680 | tf_op jit(solution)/shard_map/ppermute | solution.py:749
  33.6 7.2 %collective-permute-start.10 = (f32[1088,128]{1,0:T(8,128)S(1)}, f32[1088,128]{1,0:T(8,128)S(1)}, u32[]{:S(2)}, u32[]{:S(2)}) collective-permute-start(f32[1088,128]{1,0:T(8,128)S(1)} %collective-permute-done.1.refs_8_), channel_id=1, source_target_pairs={{0,8},{8,0},{16,24},{24,16},{1,9},{9,1},{17,25},{25,17},{2,10},{10... | collective-permute-start | bytes 1671176 | tf_op jit(solution)/shard_map/ppermute | solution.py:600
  33.6 7.2 %collective-permute-start.9 = (f32[1088,128]{1,0:T(8,128)S(1)}, f32[1088,128]{1,0:T(8,128)S(1)}, u32[]{:S(2)}, u32[]{:S(2)}) collective-permute-start(f32[1088,128]{1,0:T(8,128)S(1)} %collective-permute-done.refs_7_), channel_id=1, source_target_pairs={{0,8},{8,0},{16,24},{24,16},{1,9},{9,1},{17,25},{25,17},{2,10},{10... | collective-permute-start | bytes 1671176 | tf_op jit(solution)/shard_map/ppermute | solution.py:600
  48.0 12.7 %collective-permute-start.13 = (f32[320,128]{1,0:T(8,128)S(1)}, f32[320,128]{1,0:T(8,128)S(1)}, u32[]{:S(2)}, u32[]{:S(2)}) collective-permute-start(f32[320,128]{1,0:T(8,128)S(1)} %get-tuple-element.65), channel_id=1, source_target_pairs={{0,2},{4,6},{2,0},{6,4},{1,3},{5,7},{3,1},{7,5},{8,10},{12,14},{10... | collective-permute-start | bytes 491528 | tf_op jit(solution)/shard_map/ppermute | solution.py:749
  53.5 7.2 %collective-permute-start.14 = (f32[320,128]{1,0:T(8,128)S(1)}, f32[320,128]{1,0:T(8,128)S(1)}, u32[]{:S(2)}, u32[]{:S(2)}) collective-permute-start(f32[320,128]{1,0:T(8,128)S(1)} %get-tuple-element.66), channel_id=1, source_target_pairs={{2,4},{4,2},{3,5},{5,3},{10,12},{12,10},{11,13},{13,11},{18,20},{2... | collective-permute-start | bytes 491528 | tf_op jit(solution)/shard_map/ppermute | solution.py:749
  54.2 6.5 %collective-permute-start.15 = (f32[32,128]{1,0:T(8,128)S(1)}, f32[32,128]{1,0:T(8,128)S(1)}, u32[]{:S(2)}, u32[]{:S(2)}) collective-permute-start(f32[32,128]{1,0:T(8,128)S(1)} %get-tuple-element.67), channel_id=1, source_target_pairs={{0,4},{2,6},{4,0},{6,2},{1,5},{3,7},{5,1},{7,3},{8,12},{10,14},{12... | collective-permute-start | bytes 49160 | tf_op jit(solution)/shard_map/ppermute | solution.py:749
  65.0 8.9 %collective-permute-start.16 = (f32[320,128]{1,0:T(8,128)S(1)}, f32[320,128]{1,0:T(8,128)S(1)}, u32[]{:S(2)}, u32[]{:S(2)}) collective-permute-start(f32[320,128]{1,0:T(8,128)S(1)} %get-tuple-element.71), channel_id=1, source_target_pairs={{0,2},{4,6},{2,0},{6,4},{1,3},{5,7},{3,1},{7,5},{8,10},{12,14},{10... | collective-permute-start | bytes 491528 | tf_op jit(solution)/shard_map/ppermute | solution.py:749
  66.1 7.8 %collective-permute-start.17 = (f32[320,128]{1,0:T(8,128)S(1)}, f32[320,128]{1,0:T(8,128)S(1)}, u32[]{:S(2)}, u32[]{:S(2)}) collective-permute-start(f32[320,128]{1,0:T(8,128)S(1)} %get-tuple-element.72), channel_id=1, source_target_pairs={{2,4},{4,2},{3,5},{5,3},{10,12},{12,10},{11,13},{13,11},{18,20},{2... | collective-permute-start | bytes 491528 | tf_op jit(solution)/shard_map/ppermute | solution.py:749
  67.0 7.0 %collective-permute-start.18 = (f32[32,128]{1,0:T(8,128)S(1)}, f32[32,128]{1,0:T(8,128)S(1)}, u32[]{:S(2)}, u32[]{:S(2)}) collective-permute-start(f32[32,128]{1,0:T(8,128)S(1)} %get-tuple-element.73), channel_id=1, source_target_pairs={{0,4},{2,6},{4,0},{6,2},{1,5},{3,7},{5,1},{7,3},{8,12},{10,14},{12... | collective-permute-start | bytes 49160 | tf_op jit(solution)/shard_map/ppermute | solution.py:749
  78.3 8.9 %collective-permute-start.19 = (f32[320,128]{1,0:T(8,128)S(1)}, f32[320,128]{1,0:T(8,128)S(1)}, u32[]{:S(2)}, u32[]{:S(2)}) collective-permute-start(f32[320,128]{1,0:T(8,128)S(1)} %get-tuple-element.76), channel_id=1, source_target_pairs={{0,2},{4,6},{2,0},{6,4},{1,3},{5,7},{3,1},{7,5},{8,10},{12,14},{10... | collective-permute-start | bytes 491528 | tf_op jit(solution)/shard_map/ppermute | solution.py:749
  80.1 7.1 %collective-permute-start.20 = (f32[320,128]{1,0:T(8,128)S(1)}, f32[320,128]{1,0:T(8,128)S(1)}, u32[]{:S(2)}, u32[]{:S(2)}) collective-permute-start(f32[320,128]{1,0:T(8,128)S(1)} %get-tuple-element.77), channel_id=1, source_target_pairs={{2,4},{4,2},{3,5},{5,3},{10,12},{12,10},{11,13},{13,11},{18,20},{2... | collective-permute-start | bytes 491528 | tf_op jit(solution)/shard_map/ppermute | solution.py:749
  80.7 6.4 %collective-permute-start.21 = (f32[32,128]{1,0:T(8,128)S(1)}, f32[32,128]{1,0:T(8,128)S(1)}, u32[]{:S(2)}, u32[]{:S(2)}) collective-permute-start(f32[32,128]{1,0:T(8,128)S(1)} %get-tuple-element.78), channel_id=1, source_target_pairs={{0,4},{2,6},{4,0},{6,2},{1,5},{3,7},{5,1},{7,3},{8,12},{10,14},{12... | collective-permute-start | bytes 49160 | tf_op jit(solution)/shard_map/ppermute | solution.py:749
  90.4 8.2 %collective-permute-start.22 = (f32[1,128,128]{2,1,0:T(8,128)S(1)}, f32[1,128,128]{2,1,0:T(8,128)S(1)}, u32[]{:S(2)}, u32[]{:S(2)}) collective-permute-start(f32[1,128,128]{2,1,0:T(8,128)S(1)} %get-tuple-element.90), channel_id=1, source_target_pairs={{0,1},{1,0},{8,9},{9,8},{16,17},{17,16},{24,25},{25,24},{2,3},{3,2... | collective-permute-start | bytes 196616 | tf_op jit(solution)/shard_map/ppermute | solution.py:869
  95.1 7.4 %collective-permute-start.25 = (f32[1,128,128]{2,1,0:T(8,128)S(1)}, f32[1,128,128]{2,1,0:T(8,128)S(1)}, u32[]{:S(2)}, u32[]{:S(2)}) collective-permute-start(f32[1,128,128]{2,1,0:T(8,128)S(1)} %get-tuple-element.83), channel_id=1, source_target_pairs={{0,8},{1,9},{8,0},{9,1},{16,24},{17,25},{24,16},{25,17},{2,10},{3,... | collective-permute-start | bytes 196616 | tf_op jit(solution)/shard_map/ppermute | solution.py:869
  96.8 5.6 %collective-permute-start.24 = (f32[1,128,128]{2,1,0:T(8,128)S(1)}, f32[1,128,128]{2,1,0:T(8,128)S(1)}, u32[]{:S(2)}, u32[]{:S(2)}) collective-permute-start(f32[1,128,128]{2,1,0:T(8,128)S(1)} %get-tuple-element.94), channel_id=1, source_target_pairs={{0,17},{1,16},{8,25},{9,24},{16,1},{17,0},{24,9},{25,8},{2,19},{3,... | collective-permute-start | bytes 196616 | tf_op jit(solution)/shard_map/ppermute | solution.py:869
  98.3 5.4 %collective-permute-start.26 = (f32[1,128,128]{2,1,0:T(8,128)S(1)}, f32[1,128,128]{2,1,0:T(8,128)S(1)}, u32[]{:S(2)}, u32[]{:S(2)}) collective-permute-start(f32[1,128,128]{2,1,0:T(8,128)S(1)} %get-tuple-element.84), channel_id=1, source_target_pairs={{0,9},{1,8},{8,1},{9,0},{16,25},{17,24},{24,17},{25,16},{2,11},{3,... | collective-permute-start | bytes 196616 | tf_op jit(solution)/shard_map/ppermute | solution.py:869
  (17 other events, 143.2 us)

commit v8 on v7

--- a/solution.py
+++ b/solution.py
@@ -251,14 +251,14 @@
     return jnp.concatenate([first, second, last], axis=0) * scale_ref[...]
 
 
-def local_kernel(plan, first, info_ref, y_ref, *refs):
+def local_kernel(plan, first, y_ref, *refs):
     if first:
         out_ref, pad_ref = refs
     else:
         previous_ref, potential_ref, out_ref, pad_ref = refs
     on, cz, cy, cx, gx, gz = plan.on, plan.cz, plan.cy, plan.cx, plan.gx, plan.gz
     step = pl.program_id(0)
-    me = info_ref[0]
+    me = lax.axis_index("gx") * plan.gz + lax.axis_index("gz")
     own = slice(SUB, SUB + cy)
     depth = cz * gz
 
@@ -393,10 +393,12 @@
 
 
 def sums_kernel(
-    plan, info_ref, in_ref, hot_ref, place_ref, y_ref, own_ref, even_ref, odd_ref, far_ref, total_ref
+    plan, in_ref, hot_ref, place_ref, y_ref, own_ref, even_ref, odd_ref, far_ref, total_ref
 ):
     step = pl.program_id(0)
-    me, odd, upper = info_ref[0], info_ref[1] == 1, info_ref[2] == 1
+    me = lax.axis_index("gx") * plan.gz + lax.axis_index("gz")
+    iy = lax.axis_index("gy")
+    odd, upper = (iy & 1) == 1, (lax.shift_right_logical(iy, 1) & 1) == 1
     f, y_rows = plan.features, plan.y_rows
     count = plan.slots // LANE
     index = lax.broadcasted_iota(jnp.int32, (LANE, plan.slots), 0)
@@ -488,7 +490,7 @@
     else:
         stack_ref, refs = refs[0], refs[1:]
     hot_ref, place_ref = refs[:2]
-    count = plan.blocks // 2 if last else 1
+    count = plan.blocks if last else 1
     out_refs, refs = refs[2 : 2 + count], refs[2 + count :]
     if first:
         stack_ref, potential_ref = refs[:2]
@@ -644,7 +646,7 @@
     y_rows = plan.y_rows
     full = lambda *shape: pl.BlockSpec(shape, lambda *_: (0,) * len(shape))
     each = lambda count, *shape: pl.BlockSpec((count,) + shape, lambda i, *_: (i, 0, 0))
-    params = pltpu.CompilerParams(vmem_limit_bytes=28 * 1024 * 1024)
+    params = pltpu.CompilerParams(vmem_limit_bytes=20 * 1024 * 1024)
     rows = tile_rows + points
     in_hbm = pl.BlockSpec(memory_space=pltpu.HBM)
     alone = pltpu.CompilerParams(vmem_limit_bytes=61 * 1024 * 1024)
@@ -731,7 +733,7 @@
         ]
         + send_shapes(table_rows),
         grid_spec=pltpu.PrefetchScalarGridSpec(
-            num_scalar_prefetch=1,
+            num_scalar_prefetch=0,
             grid=(blocks // per,),
             in_specs=[full(*arrived.shape)],
             out_specs=[each(per, LANE, slots), each(per, SUB, slots), each(per, y_rows, cx)]
@@ -740,7 +742,11 @@
         ),
         compiler_params=params,
         name="first_sums",
-    )(info, arrived)
+    )(arrived)
+
+    from_xz[0], from_xz[1], from_core[1], from_core[2], *sends[1:] = lax.optimization_barrier(
+        (*from_xz, *from_core[1:], *sends[1:])
+    )
 
     def pairwise(value, pairs):
         pairs = [(a, b) for a, b in pairs if b < gy]
@@ -760,8 +766,9 @@
     previous, blocks_out = None, []
     for repeat in range(DEGREE):
         first, last = repeat == 0, repeat == DEGREE - 1
-        received = swap(sends)
+        received = list(swap(sends))
         if first:
+            current, received[3] = lax.optimization_barrier((current, received[3]))
             own_table = sends[3][plan.third :]
             across = [own_table] * (gy > 1) + [received[1][message_rows:]] * (gy > 1)
             across += [received[3][plan.third :]] * (gy > 2)
@@ -780,7 +787,7 @@
             functools.partial(local_kernel, plan, first),
             out_shape=y_shape,
             grid_spec=pltpu.PrefetchScalarGridSpec(
-                num_scalar_prefetch=1,
+                num_scalar_prefetch=0,
                 grid=(blocks // per,),
                 in_specs=[full(blocks, y_rows, cx)]
                 + ([] if first else [each(per, y_rows, cx), each(per, points, cx)]),
@@ -796,7 +803,7 @@
                 transcendentals=0,
             ),
             name="local",
-        )(info, current, *([] if first else [previous, plane_potential]))
+        )(current, *([] if first else [previous, plane_potential]))
         if first:
             *from_xz, local = lax.optimization_barrier((*from_xz, local))
             pieces = [payload, from_z, from_x, *from_xz]
@@ -807,7 +814,7 @@
             pltpu.VMEM((per, lines, 2 * SUB, cx), f32),
             pltpu.VMEM((per, lines, 2 * SUB, cx), f32),
         ]
-        for base in (half // per, 0) if last else (0,):
+        for base in (0,):
             slots_at = lambda i, *_, base=base: (i + base, 0, 0)
             each = lambda count, *shape: pl.BlockSpec((count,) + shape, slots_at)
             in_specs = [each(per, y_rows, cx)] + send_specs(extra) + [full(3 * plan.third, LANE)]
@@ -822,8 +829,8 @@
             arrays += [hot, places]
             in_specs += [each(per, LANE, slots), each(per, SUB, slots)]
             if last:
-                out_shapes = [jax.ShapeDtypeStruct((1, y_rows, cx), f32)] * half
-                out_specs = [full(1, y_rows, cx)] * half
+                out_shapes = [jax.ShapeDtypeStruct((1, y_rows, cx), f32)] * blocks
+                out_specs = [full(1, y_rows, cx)] * blocks
             else:
                 out_shapes, out_specs = [y_shape], [each(per, y_rows, cx)]
             if first:
@@ -844,7 +851,7 @@
                 out_shape=out_shapes,
                 grid_spec=pltpu.PrefetchScalarGridSpec(
                     num_scalar_prefetch=1,
-                    grid=((half if last else blocks) // per,),
+                    grid=(blocks // per,),
                     in_specs=in_specs,
                     out_specs=out_specs,
                     scratch_shapes=scratch + ([] if last else [sums_scratch]) + held,

time: 106 us -> 110 us (1.038)
  waiting for transfers between devices: 16.1 us -> 28.6 us
  Pallas kernels: 33.4 us -> 29.9 us
  starting transfers between devices: 43.8 us -> 40.9 us
  local copies, waits for them, and re-layouts: 11.3 us -> 9.4 us
    ppermute x9, waiting for transfers between devices: 4.38 us -> 12 us  [exchange(): return lax.ppermute(value, axis, [(i, i ^ bit) for i in range(count)])]
    unnamed x24 -> x14, local copies, waits for them, and re-layouts: 6.45 us -> 2.62 us
    ppermute x12, starting transfers between devices: 23.7 us -> 21.7 us  [pairwise(): return lax.ppermute(value, 'gy', pairs + [(b, a) for a, b in pairs])]
    all_to_all x1, waiting for transfers between devices: 3.25 us -> 5.25 us  [turned_path(): arrived = lax.all_to_all(messages, ('gx', 'gz'), 0, 0, tiled=True)]
    ppermute x12, waiting for transfers between devices: 4.09 us -> 6.08 us  [pairwise(): return lax.ppermute(value, 'gy', pairs + [(b, a) for a, b in pairs])]
    pallas_call x4, Pallas kernels: 8.96 us -> 7.43 us  [turned_path(): pl.pallas_call(functools.partial(local_kernel, plan, first), out_shape=y_...]
    pallas_call x4 -> x3, Pallas kernels: 16.3 us -> 14.8 us  [turned_path(): pl.pallas_call(functools.partial(step_kernel, plan, first, last, base), o...]
    ppermute x9, starting transfers between devices: 7.49 us -> 8.95 us  [exchange(): return lax.ppermute(value, axis, [(i, i ^ bit) for i in range(count)])]
  transfers between devices with their start and end apart: 30 -> 30, of which waited for: 12 -> 14; matrix products, arithmetic and copies ran while one was open for 2% -> 2% of each run, Pallas kernels for 17% -> 13%
where the time goes in v8:
time: 110 us
  starting transfers between devices  40.9 us (37%)
  Pallas kernels  29.9 us (27%)
  waiting for transfers between devices  28.6 us (26%)
  local copies, waits for them, and re-layouts  9.4 us (9%)
    ppermute x12, starting transfers between devices, pairwise(): return lax.ppermute(value, 'gy', pairs + [(b, a) for a, b in pairs])  21.7 us
    pallas_call x3, Pallas kernels, turned_path(): pl.pallas_call(functools.partial(step_kernel, plan, first, last, base), o...  14.8 us
    ppermute x9, waiting for transfers between devices, exchange(): return lax.ppermute(value, axis, [(i, i ^ bit) for i in range(count)])  12 us
    ppermute x9, starting transfers between devices, exchange(): return lax.ppermute(value, axis, [(i, i ^ bit) for i in range(count)])  8.95 us
    pallas_call x4, Pallas kernels, turned_path(): pl.pallas_call(functools.partial(local_kernel, plan, first), out_shape=y_...  7.43 us
    ppermute x7, starting transfers between devices, turned_path(): lax.ppermute(block, ('gx', 'gz'), [(i, i ^ moved) for i in range(blocks)])  6.5 us
    ppermute x12, waiting for transfers between devices, pairwise(): return lax.ppermute(value, 'gy', pairs + [(b, a) for a, b in pairs])  6.08 us
    all_to_all x1, waiting for transfers between devices, turned_path(): arrived = lax.all_to_all(messages, ('gx', 'gz'), 0, 0, tiled=True)  5.25 us
  transfers between devices with their start and end apart: 30, of which 14 were waited for; matrix products, arithmetic and copies ran while one was open for 2% of the time, Pallas kernels for 13%

profile of v8, /device:TPU:0, one launch (start us, length us, event | category | flops | bytes accessed | tf_op | source)
XLA Modules:
  0.0 109.9 jit_solution(16640506744538843649)
XLA Ops:
  2.9 3.0 %collective-permute-start = (f32[1088,128]{1,0:T(8,128)}, f32[1088,128]{1,0:T(8,128)S(1)}, u32[]{:S(2)}, u32[]{:S(2)}) collective-permute-start(f32[1088,128]{1,0:T(8,128)} %pack.1.payload_ref.refs_6_), channel_id=1, source_target_pairs={{0,1},{1,0},{2,3},{3,2},{4,5},{5,4},{6,7},{7,6},{8,9},{9,8},{10,11... | collective-permute-start | bytes 1671176 | tf_op jit(solution)/shard_map/ppermute | solution.py:602
  8.7 4.3 %own_tiles.1 = (f32[8,152,128]{2,1,0:T(8,128)}, s32[5]{0:T(128)}) custom-call(s32[5]{0:T(128)} %stack.19.info_ref, f32[1088,128]{1,0:T(8,128)} %pack.1.payload_ref.refs_6_, s32[1,256]{1,0:T(1,128)} %bitcast.21, s32[1,256]{1,0:T(1,128)} %bitcast.22, f32[4,64]{1,0:T(4,128)} %bitcast.20, f32[8,128,128]{2,1,0:T(8,128)} %bitcast.16), custom_call_target="tpu_custom_call" | custom-call | tf_op jit(solution)/shard_map/own_tiles/pallas_call | solution.py:667
  13.0 5.7 %collective-permute-done.refs_7_ = f32[1088,128]{1,0:T(8,128)S(1)} collective-permute-done((f32[1088,128]{1,0:T(8,128)}, f32[1088,128]{1,0:T(8,128)S(1)}, u32[]{:S(2)}, u32[]{:S(2)}) %collective-permute-start) | collective-permute-done | bytes 557088 | tf_op jit(solution)/shard_map/ppermute | solution.py:602
  20.7 3.5 %all-to-all-start = ((f32[8,152,128]{2,1,0:T(8,128)}), f32[8,152,128]{2,1,0:T(8,128)S(1)}, u32[]{:S(2)}, u32[]{:S(2)}) async-start(f32[8,152,128]{2,1,0:T(8,128)} %get-tuple-element.59), calls=%async_computation | async-start | bytes 1245184 | tf_op jit(solution)/shard_map/all_to_all | solution.py:694
  25.7 1.9 %collective-permute-start.3 = (f32[544,128]{1,0:T(8,128)}, f32[544,128]{1,0:T(8,128)}, u32[]{:S(2)}, u32[]{:S(2)}) collective-permute-start(f32[544,128]{1,0:T(8,128)} %slice.15), channel_id=1, source_target_pairs={{0,16},{8,24},{16,0},{24,8},{1,17},{9,25},{17,1},{25,9},{2,18},{10... | collective-permute-start | bytes 835592 | tf_op jit(solution)/shard_map/ppermute | solution.py:602
  29.3 5.2 %all-to-all-done.in_ref = f32[8,152,128]{2,1,0:T(8,128)S(1)} async-done(((f32[8,152,128]{2,1,0:T(8,128)}), f32[8,152,128]{2,1,0:T(8,128)S(1)}, u32[]{:S(2)}, u32[]{:S(2)}) %all-to-all-start) | async-done | bytes 622624 | tf_op jit(solution)/shard_map/all_to_all | solution.py:694
  35.3 4.9 %collective-permute-done.3.refs_9_ = f32[544,128]{1,0:T(8,128)} collective-permute-done((f32[544,128]{1,0:T(8,128)}, f32[544,128]{1,0:T(8,128)}, u32[]{:S(2)}, u32[]{:S(2)}) %collective-permute-start.3) | collective-permute-done | bytes 278560 | tf_op jit(solution)/shard_map/ppermute | solution.py:602
  40.2 2.7 %collective-permute-start.7 = (f32[64,128]{1,0:T(8,128)S(1)}, f32[64,128]{1,0:T(8,128)S(1)}, u32[]{:S(2)}, u32[]{:S(2)}) collective-permute-start(f32[64,128]{1,0:T(8,128)S(1)} %get-tuple-element.66), channel_id=1, source_target_pairs={{0,4},{2,6},{4,0},{6,2},{1,5},{3,7},{5,1},{7,3},{8,12},{10,14},{12... | collective-permute-start | bytes 98312 | tf_op jit(solution)/shard_map/ppermute | solution.py:755
  42.9 1.6 %collective-permute-start.8 = (f32[352,128]{1,0:T(8,128)S(1)}, f32[352,128]{1,0:T(8,128)S(1)}, u32[]{:S(2)}, u32[]{:S(2)}) collective-permute-start(f32[352,128]{1,0:T(8,128)S(1)} %get-tuple-element.70), channel_id=1, source_target_pairs={{0,2},{4,6},{2,0},{6,4},{1,3},{5,7},{3,1},{7,5},{8,10},{12,14},{10... | collective-permute-start | bytes 540680 | tf_op jit(solution)/shard_map/ppermute | solution.py:755
  45.4 1.8 %local.4.local_ref = f32[8,128,128]{2,1,0:T(8,128)S(1)} custom-call(f32[8,128,128]{2,1,0:T(8,128)S(1)} %get-tuple-element.67.y_ref.refs_5_.refs_0_), custom_call_target="tpu_custom_call" | custom-call | flops 7864320 | bytes 2097152 | tf_op jit(solution)/shard_map/local/pallas_call | solution.py:786
  51.7 6.1 %step.4 = (f32[8,128,128]{2,1,0:T(8,128)S(1)}, bf16[8,1024,256]{2,1,0:T(8,128)(2,1)S(1)}, f32[8,64,128]{2,1,0:T(8,128)S(1)}, f32[96,128]{1,0:T(8,128)S(1)}, f32[...) custom-call(s32[5]{0:T(128)S(1)} %copy-done.3, f32[8,128,128]{2,1,0:T(8,128)S(1)} %local.4.local_ref, ...), custom_call_target="tpu_custom_call" | custom-call | tf_op jit(solution)/shard_map/step/pallas_call | solution.py:849
  59.9 3.4 %collective-permute-start.15 = (f32[32,128]{1,0:T(8,128)S(1)}, f32[32,128]{1,0:T(8,128)S(1)}, u32[]{:S(2)}, u32[]{:S(2)}) collective-permute-start(f32[32,128]{1,0:T(8,128)S(1)} %get-tuple-element.85), channel_id=1, source_target_pairs={{0,4},{2,6},{4,0},{6,2},{1,5},{3,7},{5,1},{7,3},{8,12},{10,14},{12... | collective-permute-start | bytes 49160 | tf_op jit(solution)/shard_map/ppermute | solution.py:755
  63.4 1.9 %local.5.local_ref = f32[8,128,128]{2,1,0:T(8,128)S(1)} custom-call(f32[8,128,128]{2,1,0:T(8,128)S(1)} %get-tuple-element.80.y_ref.refs_0_, f32[8,128,128]{2,1,0:T(8,128)S(1)} %get-tuple-element.67.y_ref.refs_5_.refs_0_, f32[8,64,128]{2,1,0:T(8,128)S(1)} %get-tuple-element.81.refs_1_), custom_call_target="tpu_custom_call" | custom-call | flops 7864320 | bytes 2097152 | tf_op jit(solution)/shard_map/local/pallas_call | solution.py:786
  65.2 2.1 %collective-permute-done.15.refs_3_ = f32[32,128]{1,0:T(8,128)S(1)} collective-permute-done((f32[32,128]{1,0:T(8,128)S(1)}, f32[32,128]{1,0:T(8,128)S(1)}, u32[]{:S(2)}, u32[]{:S(2)}) %collective-permute-start.15) | collective-permute-done | bytes 16416 | tf_op jit(solution)/shard_map/ppermute | solution.py:755
  67.3 4.3 %step.5 = (f32[8,128,128]{2,1,0:T(8,128)S(1)}, f32[96,128]{1,0:T(8,128)S(1)}, f32[320,128]{1,0:T(8,128)S(1)}, f32[320,128]{1,0:T(8,128)S(1)}, f32[32,128]{1,0:T(8,128)S(1)}) custom-call(s32[5]{0:T(128)S(1)} %copy-done.3, f32[8,128,128]{2,1,0:T(8,128)S(1)} %local.5.local_ref, f32[96,128]{1,0:T(8,128)S(1)} %get-tuple-element.82.refs_0_, ...), custom_call_target="tpu_custom_call" | custom-call | tf_op jit(solution)/shard_map/step/pallas_call | solution.py:849
  73.5 3.9 %collective-permute-start.18 = (f32[32,128]{1,0:T(8,128)S(1)}, f32[32,128]{1,0:T(8,128)S(1)}, u32[]{:S(2)}, u32[]{:S(2)}) collective-permute-start(f32[32,128]{1,0:T(8,128)S(1)} %get-tuple-element.91), channel_id=1, source_target_pairs={{0,4},{2,6},{4,0},{6,2},{1,5},{3,7},{5,1},{7,3},{8,12},{10,14},{12... | collective-permute-start | bytes 49160 | tf_op jit(solution)/shard_map/ppermute | solution.py:755
  77.4 1.9 %local.6.local_ref = f32[8,128,128]{2,1,0:T(8,128)S(1)} custom-call(f32[8,128,128]{2,1,0:T(8,128)S(1)} %get-tuple-element.87.y_ref.refs_0_, f32[8,128,128]{2,1,0:T(8,128)S(1)} %get-tuple-element.80.y_ref.refs_0_, f32[8,64,128]{2,1,0:T(8,128)S(1)} %get-tuple-element.81.refs_1_), custom_call_target="tpu_custom_call" | custom-call | flops 7864320 | bytes 2097152 | tf_op jit(solution)/shard_map/local/pallas_call | solution.py:786
  80.6 4.3 %step.6 = (f32[8,128,128]{2,1,0:T(8,128)S(1)}, f32[96,128]{1,0:T(8,128)S(1)}, f32[320,128]{1,0:T(8,128)S(1)}, f32[320,128]{1,0:T(8,128)S(1)}, f32[32,128]{1,0:T(8,128)S(1)}) custom-call(s32[5]{0:T(128)S(1)} %copy-done.3, f32[8,128,128]{2,1,0:T(8,128)S(1)} %local.6.local_ref, f32[96,128]{1,0:T(8,128)S(1)} %get-tuple-element.88.refs_0_, ...), custom_call_target="tpu_custom_call" | custom-call | tf_op jit(solution)/shard_map/step/pallas_call | solution.py:849
  86.9 3.5 %collective-permute-start.21 = (f32[32,128]{1,0:T(8,128)S(1)}, f32[32,128]{1,0:T(8,128)S(1)}, u32[]{:S(2)}, u32[]{:S(2)}) collective-permute-start(f32[32,128]{1,0:T(8,128)S(1)} %get-tuple-element.96), channel_id=1, source_target_pairs={{0,4},{2,6},{4,0},{6,2},{1,5},{3,7},{5,1},{7,3},{8,12},{10,14},{12... | collective-permute-start | bytes 49160 | tf_op jit(solution)/shard_map/ppermute | solution.py:755
  90.4 1.9 %local.7 = f32[8,128,128]{2,1,0:T(8,128)S(1)} custom-call(f32[8,128,128]{2,1,0:T(8,128)S(1)} %get-tuple-element.92.y_ref, f32[8,128,128]{2,1,0:T(8,128)S(1)} %get-tuple-element.87.y_ref.refs_0_, f32[8,64,128]{2,1,0:T(8,128)S(1)} %get-tuple-element.81.refs_1_), custom_call_target="tpu_custom_call" | custom-call | flops 7864320 | bytes 2097152 | tf_op jit(solution)/shard_map/local/pallas_call | solution.py:786
  93.9 4.4 %step.7 = (f32[8,128,128]{2,1,0:T(8,128)S(1)}, f32[1,128,128]{2,1,0:T(8,128)S(1)}, f32[1,128,128]{2,1,0:T(8,128)S(1)}, f32[1,128,128]{2,1,0:T(8,128)S(1)}, f32[1...) fusion(f32[8,128,128]{2,1,0:T(8,128)S(1)} %broadcast_in_dim.3, ...), kind=kCustom, calls=%fused_computation.29 | custom fusion | bytes 6275588 | tf_op jit(solution)/shard_map/step/pallas_call | solution.py:849
  98.2 1.5 %collective-permute-start.22 = (f32[1,128,128]{2,1,0:T(8,128)S(1)}, f32[1,128,128]{2,1,0:T(8,128)S(1)}, u32[]{:S(2)}, u32[]{:S(2)}) collective-permute-start(f32[1,128,128]{2,1,0:T(8,128)S(1)} %get-tuple-element.108), channel_id=1, source_target_pairs={{0,1},{1,0},{8,9},{9,8},{16,17},{17,16},{24,25},{25,24},{2,3},{3,2... | collective-permute-start | bytes 196616 | tf_op jit(solution)/shard_map/ppermute | solution.py:876
  100.3 1.5 %collective-permute-start.24 = (f32[1,128,128]{2,1,0:T(8,128)S(1)}, f32[1,128,128]{2,1,0:T(8,128)S(1)}, u32[]{:S(2)}, u32[]{:S(2)}) collective-permute-start(f32[1,128,128]{2,1,0:T(8,128)S(1)} %get-tuple-element.112), channel_id=1, source_target_pairs={{0,17},{1,16},{8,25},{9,24},{16,1},{17,0},{24,9},{25,8},{2,19},{3,... | collective-permute-start | bytes 196616 | tf_op jit(solution)/shard_map/ppermute | solution.py:876
  101.8 1.6 %collective-permute-start.26 = (f32[1,128,128]{2,1,0:T(8,128)S(1)}, f32[1,128,128]{2,1,0:T(8,128)S(1)}, u32[]{:S(2)}, u32[]{:S(2)}) collective-permute-start(f32[1,128,128]{2,1,0:T(8,128)S(1)} %get-tuple-element.116), channel_id=1, source_target_pairs={{0,9},{1,8},{8,1},{9,0},{16,25},{17,24},{24,17},{25,16},{2,11},{3,... | collective-permute-start | bytes 196616 | tf_op jit(solution)/shard_map/ppermute | solution.py:876
  (81 shorter events, 31.9 us)
Async XLA Ops:
  2.9 15.8 %collective-permute-start = (f32[1088,128]{1,0:T(8,128)}, f32[1088,128]{1,0:T(8,128)S(1)}, u32[]{:S(2)}, u32[]{:S(2)}) collective-permute-start(f32[1088,128]{1,0:T(8,128)} %pack.1.payload_ref.refs_6_), channel_id=1, source_target_pairs={{0,1},{1,0},{2,3},{3,2},{4,5},{5,4},{6,7},{7,6},{8,9},{9,8},{10,11... | collective-permute-start | bytes 1671176 | tf_op jit(solution)/shard_map/ppermute | solution.py:602
  5.9 14.3 %collective-permute-start.1 = (f32[1088,128]{1,0:T(8,128)}, f32[1088,128]{1,0:T(8,128)S(1)}, u32[]{:S(2)}, u32[]{:S(2)}) collective-permute-start(f32[1088,128]{1,0:T(8,128)} %pack.1.payload_ref.refs_6_), channel_id=1, source_target_pairs={{0,16},{8,24},{16,0},{24,8},{1,17},{9,25},{17,1},{25,9},{2,18},{10... | collective-permute-start | bytes 1671176 | tf_op jit(solution)/shard_map/ppermute | solution.py:602
  7.4 12.8 %collective-permute-start.2 = (f32[1088,128]{1,0:T(8,128)}, f32[1088,128]{1,0:T(8,128)S(1)}, u32[]{:S(2)}, u32[]{:S(2)}) collective-permute-start(f32[1088,128]{1,0:T(8,128)} %pack.1.payload_ref.refs_6_), channel_id=1, source_target_pairs={{0,8},{8,0},{16,24},{24,16},{1,9},{9,1},{17,25},{25,17},{2,10},{10... | collective-permute-start | bytes 1671176 | tf_op jit(solution)/shard_map/ppermute | solution.py:602
  20.2 20.0 %collective-permute-start.5 = (f32[1088,128]{1,0:T(8,128)S(1)}, f32[1088,128]{1,0:T(8,128)S(1)}, u32[]{:S(2)}, u32[]{:S(2)}) collective-permute-start(f32[1088,128]{1,0:T(8,128)S(1)} %collective-permute-done.refs_7_), channel_id=1, source_target_pairs={{0,8},{8,0},{16,24},{24,16},{1,9},{9,1},{17,25},{25,17},{2,10},{10... | collective-permute-start | bytes 1671176 | tf_op jit(solution)/shard_map/ppermute | solution.py:602
  20.2 20.0 %collective-permute-start.6 = (f32[1088,128]{1,0:T(8,128)S(1)}, f32[1088,128]{1,0:T(8,128)}, u32[]{:S(2)}, u32[]{:S(2)}) collective-permute-start(f32[1088,128]{1,0:T(8,128)S(1)} %collective-permute-done.1.refs_8_), channel_id=1, source_target_pairs={{0,8},{8,0},{16,24},{24,16},{1,9},{9,1},{17,25},{25,17},{2,10},{10... | collective-permute-start | bytes 1671176 | tf_op jit(solution)/shard_map/ppermute | solution.py:602
  20.7 13.9 %all-to-all-start = ((f32[8,152,128]{2,1,0:T(8,128)}), f32[8,152,128]{2,1,0:T(8,128)S(1)}, u32[]{:S(2)}, u32[]{:S(2)}) async-start(f32[8,152,128]{2,1,0:T(8,128)} %get-tuple-element.59), calls=%async_computation | async-start | bytes 1245184 | tf_op jit(solution)/shard_map/all_to_all | solution.py:694
  25.7 14.5 %collective-permute-start.3 = (f32[544,128]{1,0:T(8,128)}, f32[544,128]{1,0:T(8,128)}, u32[]{:S(2)}, u32[]{:S(2)}) collective-permute-start(f32[544,128]{1,0:T(8,128)} %slice.15), channel_id=1, source_target_pairs={{0,16},{8,24},{16,0},{24,8},{1,17},{9,25},{17,1},{25,9},{2,18},{10... | collective-permute-start | bytes 835592 | tf_op jit(solution)/shard_map/ppermute | solution.py:602
  27.6 12.5 %collective-permute-start.4 = (f32[544,128]{1,0:T(8,128)}, f32[544,128]{1,0:T(8,128)}, u32[]{:S(2)}, u32[]{:S(2)}) collective-permute-start(f32[544,128]{1,0:T(8,128)} %slice.16), channel_id=1, source_target_pairs={{0,1},{1,0},{2,3},{3,2},{4,5},{5,4},{6,7},{7,6},{8,9},{9,8},{10,11... | collective-permute-start | bytes 835592 | tf_op jit(solution)/shard_map/ppermute | solution.py:602
  40.2 5.2 %collective-permute-start.7 = (f32[64,128]{1,0:T(8,128)S(1)}, f32[64,128]{1,0:T(8,128)S(1)}, u32[]{:S(2)}, u32[]{:S(2)}) collective-permute-start(f32[64,128]{1,0:T(8,128)S(1)} %get-tuple-element.66), channel_id=1, source_target_pairs={{0,4},{2,6},{4,0},{6,2},{1,5},{3,7},{5,1},{7,3},{8,12},{10,14},{12... | collective-permute-start | bytes 98312 | tf_op jit(solution)/shard_map/ppermute | solution.py:755
  42.9 6.3 %collective-permute-start.8 = (f32[352,128]{1,0:T(8,128)S(1)}, f32[352,128]{1,0:T(8,128)S(1)}, u32[]{:S(2)}, u32[]{:S(2)}) collective-permute-start(f32[352,128]{1,0:T(8,128)S(1)} %get-tuple-element.70), channel_id=1, source_target_pairs={{0,2},{4,6},{2,0},{6,4},{1,3},{5,7},{3,1},{7,5},{8,10},{12,14},{10... | collective-permute-start | bytes 540680 | tf_op jit(solution)/shard_map/ppermute | solution.py:755
  44.5 5.6 %collective-permute-start.10 = (f32[32,128]{1,0:T(8,128)S(1)}, f32[32,128]{1,0:T(8,128)S(1)}, u32[]{:S(2)}, u32[]{:S(2)}) collective-permute-start(f32[32,128]{1,0:T(8,128)S(1)} %slice.17.refs_0_), channel_id=1, source_target_pairs={{0,6},{2,4},{4,2},{6,0},{1,7},{3,5},{5,3},{7,1},{8,14},{10,12},{12... | collective-permute-start | bytes 49160 | tf_op jit(solution)/shard_map/ppermute | solution.py:777
  44.7 6.9 %collective-permute-start.9 = (f32[320,128]{1,0:T(8,128)S(1)}, f32[320,128]{1,0:T(8,128)S(1)}, u32[]{:S(2)}, u32[]{:S(2)}) collective-permute-start(f32[320,128]{1,0:T(8,128)S(1)} %get-tuple-element.71), channel_id=1, source_target_pairs={{2,4},{4,2},{3,5},{5,3},{10,12},{12,10},{11,13},{13,11},{18,20},{2... | collective-permute-start | bytes 491528 | tf_op jit(solution)/shard_map/ppermute | solution.py:755
  57.8 9.5 %collective-permute-start.13 = (f32[320,128]{1,0:T(8,128)S(1)}, f32[320,128]{1,0:T(8,128)S(1)}, u32[]{:S(2)}, u32[]{:S(2)}) collective-permute-start(f32[320,128]{1,0:T(8,128)S(1)} %get-tuple-element.83), channel_id=1, source_target_pairs={{0,2},{4,6},{2,0},{6,4},{1,3},{5,7},{3,1},{7,5},{8,10},{12,14},{10... | collective-permute-start | bytes 491528 | tf_op jit(solution)/shard_map/ppermute | solution.py:755
  59.2 8.1 %collective-permute-start.14 = (f32[320,128]{1,0:T(8,128)S(1)}, f32[320,128]{1,0:T(8,128)S(1)}, u32[]{:S(2)}, u32[]{:S(2)}) collective-permute-start(f32[320,128]{1,0:T(8,128)S(1)} %get-tuple-element.84), channel_id=1, source_target_pairs={{2,4},{4,2},{3,5},{5,3},{10,12},{12,10},{11,13},{13,11},{18,20},{2... | collective-permute-start | bytes 491528 | tf_op jit(solution)/shard_map/ppermute | solution.py:755
  59.9 7.4 %collective-permute-start.15 = (f32[32,128]{1,0:T(8,128)S(1)}, f32[32,128]{1,0:T(8,128)S(1)}, u32[]{:S(2)}, u32[]{:S(2)}) collective-permute-start(f32[32,128]{1,0:T(8,128)S(1)} %get-tuple-element.85), channel_id=1, source_target_pairs={{0,4},{2,6},{4,0},{6,2},{1,5},{3,7},{5,1},{7,3},{8,12},{10,14},{12... | collective-permute-start | bytes 49160 | tf_op jit(solution)/shard_map/ppermute | solution.py:755
  71.6 8.9 %collective-permute-start.16 = (f32[320,128]{1,0:T(8,128)S(1)}, f32[320,128]{1,0:T(8,128)S(1)}, u32[]{:S(2)}, u32[]{:S(2)}) collective-permute-start(f32[320,128]{1,0:T(8,128)S(1)} %get-tuple-element.89), channel_id=1, source_target_pairs={{0,2},{4,6},{2,0},{6,4},{1,3},{5,7},{3,1},{7,5},{8,10},{12,14},{10... | collective-permute-start | bytes 491528 | tf_op jit(solution)/shard_map/ppermute | solution.py:755
  72.6 7.9 %collective-permute-start.17 = (f32[320,128]{1,0:T(8,128)S(1)}, f32[320,128]{1,0:T(8,128)S(1)}, u32[]{:S(2)}, u32[]{:S(2)}) collective-permute-start(f32[320,128]{1,0:T(8,128)S(1)} %get-tuple-element.90), channel_id=1, source_target_pairs={{2,4},{4,2},{3,5},{5,3},{10,12},{12,10},{11,13},{13,11},{18,20},{2... | collective-permute-start | bytes 491528 | tf_op jit(solution)/shard_map/ppermute | solution.py:755
  73.5 7.1 %collective-permute-start.18 = (f32[32,128]{1,0:T(8,128)S(1)}, f32[32,128]{1,0:T(8,128)S(1)}, u32[]{:S(2)}, u32[]{:S(2)}) collective-permute-start(f32[32,128]{1,0:T(8,128)S(1)} %get-tuple-element.91), channel_id=1, source_target_pairs={{0,4},{2,6},{4,0},{6,2},{1,5},{3,7},{5,1},{7,3},{8,12},{10,14},{12... | collective-permute-start | bytes 49160 | tf_op jit(solution)/shard_map/ppermute | solution.py:755
  84.9 8.9 %collective-permute-start.19 = (f32[320,128]{1,0:T(8,128)S(1)}, f32[320,128]{1,0:T(8,128)S(1)}, u32[]{:S(2)}, u32[]{:S(2)}) collective-permute-start(f32[320,128]{1,0:T(8,128)S(1)} %get-tuple-element.94), channel_id=1, source_target_pairs={{0,2},{4,6},{2,0},{6,4},{1,3},{5,7},{3,1},{7,5},{8,10},{12,14},{10... | collective-permute-start | bytes 491528 | tf_op jit(solution)/shard_map/ppermute | solution.py:755
  86.3 7.6 %collective-permute-start.20 = (f32[320,128]{1,0:T(8,128)S(1)}, f32[320,128]{1,0:T(8,128)S(1)}, u32[]{:S(2)}, u32[]{:S(2)}) collective-permute-start(f32[320,128]{1,0:T(8,128)S(1)} %get-tuple-element.95), channel_id=1, source_target_pairs={{2,4},{4,2},{3,5},{5,3},{10,12},{12,10},{11,13},{13,11},{18,20},{2... | collective-permute-start | bytes 491528 | tf_op jit(solution)/shard_map/ppermute | solution.py:755
  86.9 6.9 %collective-permute-start.21 = (f32[32,128]{1,0:T(8,128)S(1)}, f32[32,128]{1,0:T(8,128)S(1)}, u32[]{:S(2)}, u32[]{:S(2)}) collective-permute-start(f32[32,128]{1,0:T(8,128)S(1)} %get-tuple-element.96), channel_id=1, source_target_pairs={{0,4},{2,6},{4,0},{6,2},{1,5},{3,7},{5,1},{7,3},{8,12},{10,14},{12... | collective-permute-start | bytes 49160 | tf_op jit(solution)/shard_map/ppermute | solution.py:755
  98.2 5.1 %collective-permute-start.22 = (f32[1,128,128]{2,1,0:T(8,128)S(1)}, f32[1,128,128]{2,1,0:T(8,128)S(1)}, u32[]{:S(2)}, u32[]{:S(2)}) collective-permute-start(f32[1,128,128]{2,1,0:T(8,128)S(1)} %get-tuple-element.108), channel_id=1, source_target_pairs={{0,1},{1,0},{8,9},{9,8},{16,17},{17,16},{24,25},{25,24},{2,3},{3,2... | collective-permute-start | bytes 196616 | tf_op jit(solution)/shard_map/ppermute | solution.py:876
  100.3 5.2 %collective-permute-start.24 = (f32[1,128,128]{2,1,0:T(8,128)S(1)}, f32[1,128,128]{2,1,0:T(8,128)S(1)}, u32[]{:S(2)}, u32[]{:S(2)}) collective-permute-start(f32[1,128,128]{2,1,0:T(8,128)S(1)} %get-tuple-element.112), channel_id=1, source_target_pairs={{0,17},{1,16},{8,25},{9,24},{16,1},{17,0},{24,9},{25,8},{2,19},{3,... | collective-permute-start | bytes 196616 | tf_op jit(solution)/shard_map/ppermute | solution.py:876
  104.0 5.0 %collective-permute-start.28 = (f32[1,128,128]{2,1,0:T(8,128)S(1)}, f32[1,128,128]{2,1,0:T(8,128)S(1)}, u32[]{:S(2)}, u32[]{:S(2)}) collective-permute-start(f32[1,128,128]{2,1,0:T(8,128)S(1)} %get-tuple-element.120), channel_id=1, source_target_pairs={{0,25},{1,24},{8,17},{9,16},{16,9},{17,8},{24,1},{25,0},{2,27},{3,... | collective-permute-start | bytes 196616 | tf_op jit(solution)/shard_map/ppermute | solution.py:876
  (12 other events, 117.1 us)

commit v9 on v8

--- a/solution.py
+++ b/solution.py
@@ -352,10 +352,10 @@
     owner_z = owner & (plan.gz - 1)
     owner_y = lax.shift_right_logical(owner, log2(plan.gz)) & (plan.gy - 1)
     owner_x = lax.shift_right_logical(owner, log2(plan.gz) + log2(plan.gy))
-    key = (owner_y - info_ref[3] + 1) * (plan.blocks * plan.owned)
+    key = (owner_y - lax.axis_index("gy") + 1) * (plan.blocks * plan.owned)
     key = key + (owner_x * plan.gz + owner_z) * plan.owned + (atom & (plan.owned - 1))
     lane = lax.broadcasted_iota(jnp.int32, column.shape, 1)
-    column = jnp.where(lane < info_ref[4], column, -1)
+    column = jnp.where(lane < info_ref[0], column, -1)
     meta_ref[...] = jnp.zeros_like(meta_ref)
     for row, line in enumerate((key, column)):
         line = line.astype(jnp.float32)
@@ -445,7 +445,7 @@
         emit_sums(plan, total_ref[...], odd, upper, own_ref, even_ref, odd_ref, far_ref)
 
 
-def scale_kernel(plan, device_ref, within_ref, *refs):
+def scale_kernel(plan, device_ref, within_ref, _, *refs):
     table_refs, out_ref = refs[:-1], refs[-1]
     blocks, owned = plan.blocks, plan.owned
     tables = []
@@ -482,7 +482,7 @@
         out_ref[j * plan.features : (j + 1) * plan.features, :] = jnp.concatenate(lines, axis=0)
 
 
-def step_kernel(plan, first, last, base, info_ref, local_ref, *refs):
+def step_kernel(plan, first, last, base, local_ref, *refs):
     received, refs = refs[:5], refs[5:]
     own_in, even_in, odd_in, far_in, scale_ref = received
     if first:
@@ -500,7 +500,8 @@
         refs = refs[4:]
     coef_ref, low_ref, high_ref = refs[:3]
     step = pl.program_id(0)
-    odd, upper = info_ref[1] == 1, info_ref[2] == 1
+    iy = lax.axis_index("gy")
+    odd, upper = (iy & 1) == 1, (lax.shift_right_logical(iy, 1) & 1) == 1
     factor = plan.factor(first)
 
     @pl.when(step == 0)
@@ -657,7 +658,6 @@
         name="pack",
     )(tile_proj, potential.reshape(points, cx))
     me = ix * gz + iz
-    info = jnp.stack([me, iy & 1, (iy >> 1) & 1, iy, tile_count[0]]).astype(jnp.int32)
 
     from_z = exchange(payload, *rounds[0])
     from_x = exchange(payload, *rounds[1])
@@ -668,7 +668,7 @@
         functools.partial(own_tiles_kernel, plan),
         out_shape=[
             jax.ShapeDtypeStruct((blocks, plan.meta_at + meta_rows, cx), f32),
-            jax.ShapeDtypeStruct(info.shape, jnp.int32),
+            jax.ShapeDtypeStruct(tile_count.shape, jnp.int32),
         ],
         in_specs=[smem, full(rows, cx), in_hbm, in_hbm, in_hbm, in_hbm],
         out_specs=[full(blocks, plan.meta_at + meta_rows, cx), smem],
@@ -684,7 +684,7 @@
         compiler_params=alone,
         name="own_tiles",
     )(
-        info,
+        tile_count,
         payload,
         tile_atom.reshape(1, slots),
         tile_column.reshape(1, slots),
@@ -698,7 +698,6 @@
     )
     cut = rows // 2
     from_xz = [exchange(from_z[:cut], *rounds[1]), exchange(from_x[cut:], *rounds[0])]
-    from_core = [from_c, exchange(from_z, *rounds[2]), exchange(from_x, *rounds[2])]
 
     home = atom_home.reshape(gx, gy, gz, owned).transpose(1, 0, 2, 3).reshape(gy, blocks * owned)
     home = jnp.pad(home, ((1, 1), (0, 0)))
@@ -744,10 +743,6 @@
         name="first_sums",
     )(arrived)
 
-    from_xz[0], from_xz[1], from_core[1], from_core[2], *sends[1:] = lax.optimization_barrier(
-        (*from_xz, *from_core[1:], *sends[1:])
-    )
-
     def pairwise(value, pairs):
         pairs = [(a, b) for a, b in pairs if b < gy]
         if not pairs:
@@ -779,9 +774,11 @@
             scale = pl.pallas_call(
                 functools.partial(scale_kernel, plan),
                 out_shape=jax.ShapeDtypeStruct((3 * plan.third, LANE), f32),
+                in_specs=[full(1, plan.keys), full(1, plan.keys), pl.BlockSpec(memory_space=pl.ANY)]
+                + [full(*table.shape) for table in across],
                 compiler_params=params,
                 name="scale",
-            )(home_device, home_within, *across)
+            )(home_device, home_within, late_info, *across)
         extra = table_rows if first else 0
         local = pl.pallas_call(
             functools.partial(local_kernel, plan, first),
@@ -805,9 +802,9 @@
             name="local",
         )(current, *([] if first else [previous, plane_potential]))
         if first:
-            *from_xz, local = lax.optimization_barrier((*from_xz, local))
-            pieces = [payload, from_z, from_x, *from_xz]
-            pieces += from_core + [exchange(part, *rounds[2]) for part in from_xz]
+            others = [from_z, from_x, *from_xz]
+            *others, local = lax.optimization_barrier((*others, local))
+            pieces = [payload, *others, from_c] + [exchange(part, *rounds[2]) for part in others]
         lines = on * cz
         scratch = [
             pltpu.VMEM((6 * plan.third, LANE), jnp.bfloat16),
@@ -850,7 +847,7 @@
                 functools.partial(step_kernel, plan, first, last, base),
                 out_shape=out_shapes,
                 grid_spec=pltpu.PrefetchScalarGridSpec(
-                    num_scalar_prefetch=1,
+                    num_scalar_prefetch=0,
                     grid=(blocks // per,),
                     in_specs=in_specs,
                     out_specs=out_specs,
@@ -858,7 +855,7 @@
                 ),
                 compiler_params=params,
                 name="step",
-            )(late_info, *arrays)
+            )(*arrays)
             if last:
                 blocks_out = list(result) + blocks_out
         if last:

time: 110 us -> 102 us (0.927)
  waiting for transfers between devices: 28.6 us -> 19.3 us
  Pallas kernels: 29.9 us -> 28.1 us
  starting transfers between devices: 40.9 us -> 42.5 us
    ppermute x9, waiting for transfers between devices: 12 us -> 5.36 us  [exchange(): return lax.ppermute(value, axis, [(i, i ^ bit) for i in range(count)])]
    all_to_all x1, waiting for transfers between devices: 5.25 us -> 2.62 us  [turned_path(): arrived = lax.all_to_all(messages, ('gx', 'gz'), 0, 0, tiled=True)]
    pallas_call x3, Pallas kernels: 14.8 us -> 12.5 us  [turned_path(): pl.pallas_call(functools.partial(step_kernel, plan, first, last, base), o...]
    unnamed x14 -> x22, local copies, waits for them, and re-layouts: 2.62 us -> 4.47 us
    ppermute x12, starting transfers between devices: 21.7 us -> 23.4 us  [pairwise(): return lax.ppermute(value, 'gy', pairs + [(b, a) for a, b in pairs])]
    ppermute x9, starting transfers between devices: 8.95 us -> 7.39 us  [exchange(): return lax.ppermute(value, axis, [(i, i ^ bit) for i in range(count)])]
    ppermute x12, waiting for transfers between devices: 6.08 us -> 7.48 us  [pairwise(): return lax.ppermute(value, 'gy', pairs + [(b, a) for a, b in pairs])]
    ppermute x1, starting transfers between devices: 0.22 us -> 1.41 us  [turned_path(): across.append(lax.ppermute(own_table, 'gy', pairs))]
  transfers between devices with their start and end apart: 30 -> 30, of which waited for: 14 -> 14; matrix products, arithmetic and copies ran while one was open for 2% -> 2% of each run, Pallas kernels for 13% -> 14%
where the time goes in v9:
time: 102 us; the launch traced here: 101 us
  starting transfers between devices  42.5 us (42%)
  Pallas kernels  28.1 us (28%)
  waiting for transfers between devices  19.3 us (19%)
  local copies, waits for them, and re-layouts  10.1 us (10%)
    ppermute x12, starting transfers between devices, pairwise(): return lax.ppermute(value, 'gy', pairs + [(b, a) for a, b in pairs])  23.4 us
    pallas_call x3, Pallas kernels, turned_path(): pl.pallas_call(functools.partial(step_kernel, plan, first, last, base), o...  12.5 us
    ppermute x12, waiting for transfers between devices, pairwise(): return lax.ppermute(value, 'gy', pairs + [(b, a) for a, b in pairs])  7.48 us
    ppermute x9, starting transfers between devices, exchange(): return lax.ppermute(value, axis, [(i, i ^ bit) for i in range(count)])  7.39 us
    ppermute x7, starting transfers between devices, turned_path(): lax.ppermute(block, ('gx', 'gz'), [(i, i ^ moved) for i in range(blocks)])  6.72 us
    pallas_call x4, Pallas kernels, turned_path(): pl.pallas_call(functools.partial(local_kernel, plan, first), out_shape=y_...  6.66 us
    ppermute x9, waiting for transfers between devices, exchange(): return lax.ppermute(value, axis, [(i, i ^ bit) for i in range(count)])  5.36 us
    unnamed x22, local copies, waits for them, and re-layouts  4.47 us
  transfers between devices with their start and end apart: 30, of which 14 were waited for; matrix products, arithmetic and copies ran while one was open for 2% of the time, Pallas kernels for 14%

profile of v9, /device:TPU:0, one launch (start us, length us, event | category | flops | bytes accessed | tf_op | source)
XLA Modules:
  0.0 101.1 jit_solution(6732509030087309601)
XLA Ops:
  2.9 3.0 %collective-permute-start = (f32[1088,128]{1,0:T(8,128)}, f32[1088,128]{1,0:T(8,128)S(1)}, u32[]{:S(2)}, u32[]{:S(2)}) collective-permute-start(f32[1088,128]{1,0:T(8,128)} %pack.1.payload_ref.refs_6_), channel_id=1, source_target_pairs={{0,1},{1,0},{2,3},{3,2},{4,5},{5,4},{6,7},{7,6},{8,9},{9,8},{10,11... | collective-permute-start | bytes 1671176 | tf_op jit(solution)/shard_map/ppermute | solution.py:603
  8.0 4.3 %own_tiles.1 = (f32[8,152,128]{2,1,0:T(8,128)}, s32[1]{0:T(128)}) custom-call(s32[1]{0:T(128)S(6)} %copy.19.info_ref, f32[1088,128]{1,0:T(8,128)} %pack.1.payload_ref.refs_6_, s32[1,256]{1,0:T(1,128)} %bitcast.17, s32[1,256]{1,0:T(1,128)} %bitcast.18, f32[4,64]{1,0:T(4,128)} %bitcast.16, f32[8,128,128]{2,1,0:T(8,128)} %bitcast.12), custom_call_target="tpu_custom_call" | custom-call | tf_op jit(solution)/shard_map/own_tiles/pallas_call | solution.py:667
  12.3 3.6 %all-to-all-start = ((f32[8,152,128]{2,1,0:T(8,128)}), f32[8,152,128]{2,1,0:T(8,128)S(1)}, u32[]{:S(2)}, u32[]{:S(2)}) async-start(f32[8,152,128]{2,1,0:T(8,128)} %get-tuple-element.53), calls=%async_computation | async-start | bytes 1245184 | tf_op jit(solution)/shard_map/all_to_all | solution.py:694
  15.9 3.6 %collective-permute-done.refs_7_ = f32[1088,128]{1,0:T(8,128)S(1)} collective-permute-done((f32[1088,128]{1,0:T(8,128)}, f32[1088,128]{1,0:T(8,128)S(1)}, u32[]{:S(2)}, u32[]{:S(2)}) %collective-permute-start) | collective-permute-done | bytes 557088 | tf_op jit(solution)/shard_map/ppermute | solution.py:603
  19.4 1.8 %collective-permute-done.1.refs_8_ = f32[1088,128]{1,0:T(8,128)S(1)} collective-permute-done((f32[1088,128]{1,0:T(8,128)}, f32[1088,128]{1,0:T(8,128)S(1)}, u32[]{:S(2)}, u32[]{:S(2)}) %collective-permute-start.1) | collective-permute-done | bytes 557088 | tf_op jit(solution)/shard_map/ppermute | solution.py:603
  22.0 1.9 %collective-permute-start.3 = (f32[544,128]{1,0:T(8,128)}, f32[544,128]{1,0:T(8,128)S(1)}, u32[]{:S(2)}, u32[]{:S(2)}) collective-permute-start(f32[544,128]{1,0:T(8,128)} %slice.15), channel_id=1, source_target_pairs={{0,16},{8,24},{16,0},{24,8},{1,17},{9,25},{17,1},{25,9},{2,18},{10... | collective-permute-start | bytes 835592 | tf_op jit(solution)/shard_map/ppermute | solution.py:603
  25.3 2.6 %all-to-all-done.in_ref = f32[8,152,128]{2,1,0:T(8,128)S(1)} async-done(((f32[8,152,128]{2,1,0:T(8,128)}), f32[8,152,128]{2,1,0:T(8,128)S(1)}, u32[]{:S(2)}, u32[]{:S(2)}) %all-to-all-start) | async-done | bytes 622624 | tf_op jit(solution)/shard_map/all_to_all | solution.py:694
  29.3 2.6 %collective-permute-start.5 = (f32[64,128]{1,0:T(8,128)S(1)}, f32[64,128]{1,0:T(8,128)S(1)}, u32[]{:S(2)}, u32[]{:S(2)}) collective-permute-start(f32[64,128]{1,0:T(8,128)S(1)} %get-tuple-element.55), channel_id=1, source_target_pairs={{0,4},{2,6},{4,0},{6,2},{1,5},{3,7},{5,1},{7,3},{8,12},{10,14},{12... | collective-permute-start | bytes 98312 | tf_op jit(solution)/shard_map/ppermute | solution.py:750
  39.4 2.1 %scale.1.refs_4_ = f32[96,128]{1,0:T(8,128)S(1)} custom-call(s32[1,1536]{1,0:T(1,128)S(1)} %fusion.4.device_ref, s32[1,1536]{1,0:T(1,128)S(1)} %get-tuple-element.111.within_ref, s32[1]{0:T(128)} %get-tuple-element.62._, f32[32,128]{1,0:T(8,128)S(1)} %slice.17.refs_0_, f32[32,128]{1,0:T(8,128)S(1)} %slice.20.refs_1_, f32[32,128]{1,0:T(8,128)S(1)} %slice.19.refs_2_, ...), custom_call_target="tpu_custom_call" | custom-call | tf_op jit(solution)/shard_map/scale/pallas_call | solution.py:774
  43.4 5.3 %step.4 = (f32[8,128,128]{2,1,0:T(8,128)S(1)}, bf16[8,1024,256]{2,1,0:T(8,128)(2,1)S(1)}, f32[8,64,128]{2,1,0:T(8,128)S(1)}, f32[96,128]{1,0:T(8,128)S(1)}, f32[...) custom-call(f32[8,128,128]{2,1,0:T(8,128)S(1)} %local.4.local_ref, f32[96,128]{1,0:T(8,128)S(1)} %copy-done.5, ...), custom_call_target="tpu_custom_call" | custom-call | tf_op jit(solution)/shard_map/step/pallas_call | solution.py:846
  48.8 5.2 %collective-permute-start.13 = (f32[320,128]{1,0:T(8,128)S(1)}, f32[320,128]{1,0:T(8,128)S(1)}, u32[]{:S(2)}, u32[]{:S(2)}) collective-permute-start(f32[320,128]{1,0:T(8,128)S(1)} %get-tuple-element.73), channel_id=1, source_target_pairs={{0,2},{4,6},{2,0},{6,4},{1,3},{5,7},{3,1},{7,5},{8,10},{12,14},{10... | collective-permute-start | bytes 491528 | tf_op jit(solution)/shard_map/ppermute | solution.py:750
  54.6 2.8 %collective-permute-start.15 = (f32[32,128]{1,0:T(8,128)S(1)}, f32[32,128]{1,0:T(8,128)S(1)}, u32[]{:S(2)}, u32[]{:S(2)}) collective-permute-start(f32[32,128]{1,0:T(8,128)S(1)} %get-tuple-element.75), channel_id=1, source_target_pairs={{0,4},{2,6},{4,0},{6,2},{1,5},{3,7},{5,1},{7,3},{8,12},{10,14},{12... | collective-permute-start | bytes 49160 | tf_op jit(solution)/shard_map/ppermute | solution.py:750
  57.4 1.7 %local.5.local_ref = f32[8,128,128]{2,1,0:T(8,128)S(1)} custom-call(f32[8,128,128]{2,1,0:T(8,128)S(1)} %get-tuple-element.70.y_ref.refs_0_, f32[8,128,128]{2,1,0:T(8,128)S(1)} %get-tuple-element.56.y_ref.refs_5_.refs_0_, f32[8,64,128]{2,1,0:T(8,128)S(1)} %get-tuple-element.71.refs_1_), custom_call_target="tpu_custom_call" | custom-call | flops 7864320 | bytes 2097152 | tf_op jit(solution)/shard_map/local/pallas_call | solution.py:783
  59.0 2.1 %collective-permute-done.15.refs_3_ = f32[32,128]{1,0:T(8,128)S(1)} collective-permute-done((f32[32,128]{1,0:T(8,128)S(1)}, f32[32,128]{1,0:T(8,128)S(1)}, u32[]{:S(2)}, u32[]{:S(2)}) %collective-permute-start.15) | collective-permute-done | bytes 16416 | tf_op jit(solution)/shard_map/ppermute | solution.py:750
  61.1 3.6 %step.5 = (f32[8,128,128]{2,1,0:T(8,128)S(1)}, f32[96,128]{1,0:T(8,128)S(1)}, f32[320,128]{1,0:T(8,128)S(1)}, f32[320,128]{1,0:T(8,128)S(1)}, f32[32,128]{1,0:T(8,128)S(1)}) custom-call(f32[8,128,128]{2,1,0:T(8,128)S(1)} %local.5.local_ref, f32[96,128]{1,0:T(8,128)S(1)} %get-tuple-element.72.refs_0_, f32[320,128]{1,0:T(8,128)S(1)} %collective-permute-done.13.refs_1_, ...), custom_call_target="tpu_custom_call" | custom-call | tf_op jit(solution)/shard_map/step/pallas_call | solution.py:846
  66.7 3.7 %collective-permute-start.18 = (f32[32,128]{1,0:T(8,128)S(1)}, f32[32,128]{1,0:T(8,128)S(1)}, u32[]{:S(2)}, u32[]{:S(2)}) collective-permute-start(f32[32,128]{1,0:T(8,128)S(1)} %get-tuple-element.81), channel_id=1, source_target_pairs={{0,4},{2,6},{4,0},{6,2},{1,5},{3,7},{5,1},{7,3},{8,12},{10,14},{12... | collective-permute-start | bytes 49160 | tf_op jit(solution)/shard_map/ppermute | solution.py:750
  70.4 1.7 %local.6.local_ref = f32[8,128,128]{2,1,0:T(8,128)S(1)} custom-call(f32[8,128,128]{2,1,0:T(8,128)S(1)} %get-tuple-element.77.y_ref.refs_0_, f32[8,128,128]{2,1,0:T(8,128)S(1)} %get-tuple-element.70.y_ref.refs_0_, f32[8,64,128]{2,1,0:T(8,128)S(1)} %get-tuple-element.71.refs_1_), custom_call_target="tpu_custom_call" | custom-call | flops 7864320 | bytes 2097152 | tf_op jit(solution)/shard_map/local/pallas_call | solution.py:783
  73.6 3.6 %step.6 = (f32[8,128,128]{2,1,0:T(8,128)S(1)}, f32[96,128]{1,0:T(8,128)S(1)}, f32[320,128]{1,0:T(8,128)S(1)}, f32[320,128]{1,0:T(8,128)S(1)}, f32[32,128]{1,0:T(8,128)S(1)}) custom-call(f32[8,128,128]{2,1,0:T(8,128)S(1)} %local.6.local_ref, f32[96,128]{1,0:T(8,128)S(1)} %get-tuple-element.78.refs_0_, f32[320,128]{1,0:T(8,128)S(1)} %collective-permute-done.16.refs_1_, ...), custom_call_target="tpu_custom_call" | custom-call | tf_op jit(solution)/shard_map/step/pallas_call | solution.py:846
  77.3 1.8 %collective-permute-start.19 = (f32[320,128]{1,0:T(8,128)S(1)}, f32[320,128]{1,0:T(8,128)S(1)}, u32[]{:S(2)}, u32[]{:S(2)}) collective-permute-start(f32[320,128]{1,0:T(8,128)S(1)} %get-tuple-element.84), channel_id=1, source_target_pairs={{0,2},{4,6},{2,0},{6,4},{1,3},{5,7},{3,1},{7,5},{8,10},{12,14},{10... | collective-permute-start | bytes 491528 | tf_op jit(solution)/shard_map/ppermute | solution.py:750
  79.8 3.0 %collective-permute-start.21 = (f32[32,128]{1,0:T(8,128)S(1)}, f32[32,128]{1,0:T(8,128)S(1)}, u32[]{:S(2)}, u32[]{:S(2)}) collective-permute-start(f32[32,128]{1,0:T(8,128)S(1)} %get-tuple-element.86), channel_id=1, source_target_pairs={{0,4},{2,6},{4,0},{6,2},{1,5},{3,7},{5,1},{7,3},{8,12},{10,14},{12... | collective-permute-start | bytes 49160 | tf_op jit(solution)/shard_map/ppermute | solution.py:750
  82.8 1.7 %local.7 = f32[8,128,128]{2,1,0:T(8,128)S(1)} custom-call(f32[8,128,128]{2,1,0:T(8,128)S(1)} %get-tuple-element.82.y_ref, f32[8,128,128]{2,1,0:T(8,128)S(1)} %get-tuple-element.77.y_ref.refs_0_, f32[8,64,128]{2,1,0:T(8,128)S(1)} %get-tuple-element.71.refs_1_), custom_call_target="tpu_custom_call" | custom-call | flops 7864320 | bytes 2097152 | tf_op jit(solution)/shard_map/local/pallas_call | solution.py:783
  84.5 1.7 %collective-permute-done.21 = f32[32,128]{1,0:T(8,128)S(1)} collective-permute-done((f32[32,128]{1,0:T(8,128)S(1)}, f32[32,128]{1,0:T(8,128)S(1)}, u32[]{:S(2)}, u32[]{:S(2)}) %collective-permute-start.21) | collective-permute-done | bytes 16416 | tf_op jit(solution)/shard_map/ppermute | solution.py:750
  86.2 3.8 %step.7 = (f32[8,128,128]{2,1,0:T(8,128)S(1)}, f32[1,128,128]{2,1,0:T(8,128)S(1)}, f32[1,128,128]{2,1,0:T(8,128)S(1)}, f32[1,128,128]{2,1,0:T(8,128)S(1)}, f32[1...) fusion(f32[8,128,128]{2,1,0:T(8,128)S(1)} %broadcast_in_dim.3, ...), kind=kCustom, calls=%fused_computation.29 | custom fusion | bytes 6275076 | tf_op jit(solution)/shard_map/step/pallas_call | solution.py:846
  90.4 1.7 %collective-permute-start.23 = (f32[1,128,128]{2,1,0:T(8,128)S(1)}, f32[1,128,128]{2,1,0:T(8,128)S(1)}, u32[]{:S(2)}, u32[]{:S(2)}) collective-permute-start(f32[1,128,128]{2,1,0:T(8,128)S(1)} %get-tuple-element.100), channel_id=1, source_target_pairs={{0,16},{1,17},{8,24},{9,25},{16,0},{17,1},{24,8},{25,9},{2,18},{3,... | collective-permute-start | bytes 196616 | tf_op jit(solution)/shard_map/ppermute | solution.py:873
  (88 shorter events, 31.3 us)
Async XLA Ops:
  2.9 16.6 %collective-permute-start = (f32[1088,128]{1,0:T(8,128)}, f32[1088,128]{1,0:T(8,128)S(1)}, u32[]{:S(2)}, u32[]{:S(2)}) collective-permute-start(f32[1088,128]{1,0:T(8,128)} %pack.1.payload_ref.refs_6_), channel_id=1, source_target_pairs={{0,1},{1,0},{2,3},{3,2},{4,5},{5,4},{6,7},{7,6},{8,9},{9,8},{10,11... | collective-permute-start | bytes 1671176 | tf_op jit(solution)/shard_map/ppermute | solution.py:603
  5.9 15.4 %collective-permute-start.1 = (f32[1088,128]{1,0:T(8,128)}, f32[1088,128]{1,0:T(8,128)S(1)}, u32[]{:S(2)}, u32[]{:S(2)}) collective-permute-start(f32[1088,128]{1,0:T(8,128)} %pack.1.payload_ref.refs_6_), channel_id=1, source_target_pairs={{0,16},{8,24},{16,0},{24,8},{1,17},{9,25},{17,1},{25,9},{2,18},{10... | collective-permute-start | bytes 1671176 | tf_op jit(solution)/shard_map/ppermute | solution.py:603
  7.4 13.9 %collective-permute-start.2 = (f32[1088,128]{1,0:T(8,128)}, f32[1088,128]{1,0:T(8,128)S(1)}, u32[]{:S(2)}, u32[]{:S(2)}) collective-permute-start(f32[1088,128]{1,0:T(8,128)} %pack.1.payload_ref.refs_6_), channel_id=1, source_target_pairs={{0,8},{8,0},{16,24},{24,16},{1,9},{9,1},{17,25},{25,17},{2,10},{10... | collective-permute-start | bytes 1671176 | tf_op jit(solution)/shard_map/ppermute | solution.py:603
  12.3 15.6 %all-to-all-start = ((f32[8,152,128]{2,1,0:T(8,128)}), f32[8,152,128]{2,1,0:T(8,128)S(1)}, u32[]{:S(2)}, u32[]{:S(2)}) async-start(f32[8,152,128]{2,1,0:T(8,128)} %get-tuple-element.53), calls=%async_computation | async-start | bytes 1245184 | tf_op jit(solution)/shard_map/all_to_all | solution.py:694
  22.0 13.9 %collective-permute-start.3 = (f32[544,128]{1,0:T(8,128)}, f32[544,128]{1,0:T(8,128)S(1)}, u32[]{:S(2)}, u32[]{:S(2)}) collective-permute-start(f32[544,128]{1,0:T(8,128)} %slice.15), channel_id=1, source_target_pairs={{0,16},{8,24},{16,0},{24,8},{1,17},{9,25},{17,1},{25,9},{2,18},{10... | collective-permute-start | bytes 835592 | tf_op jit(solution)/shard_map/ppermute | solution.py:603
  24.6 11.3 %collective-permute-start.4 = (f32[544,128]{1,0:T(8,128)}, f32[544,128]{1,0:T(8,128)}, u32[]{:S(2)}, u32[]{:S(2)}) collective-permute-start(f32[544,128]{1,0:T(8,128)} %slice.16), channel_id=1, source_target_pairs={{0,1},{1,0},{2,3},{3,2},{4,5},{5,4},{6,7},{7,6},{8,9},{9,8},{10,11... | collective-permute-start | bytes 835592 | tf_op jit(solution)/shard_map/ppermute | solution.py:603
  29.3 4.9 %collective-permute-start.5 = (f32[64,128]{1,0:T(8,128)S(1)}, f32[64,128]{1,0:T(8,128)S(1)}, u32[]{:S(2)}, u32[]{:S(2)}) collective-permute-start(f32[64,128]{1,0:T(8,128)S(1)} %get-tuple-element.55), channel_id=1, source_target_pairs={{0,4},{2,6},{4,0},{6,2},{1,5},{3,7},{5,1},{7,3},{8,12},{10,14},{12... | collective-permute-start | bytes 98312 | tf_op jit(solution)/shard_map/ppermute | solution.py:750
  31.9 5.7 %collective-permute-start.8 = (f32[32,128]{1,0:T(8,128)S(1)}, f32[32,128]{1,0:T(8,128)S(1)}, u32[]{:S(2)}, u32[]{:S(2)}) collective-permute-start(f32[32,128]{1,0:T(8,128)S(1)} %slice.17.refs_0_), channel_id=1, source_target_pairs={{0,6},{2,4},{4,2},{6,0},{1,7},{3,5},{5,3},{7,1},{8,14},{10,12},{12... | collective-permute-start | bytes 49160 | tf_op jit(solution)/shard_map/ppermute | solution.py:772
  33.3 5.9 %collective-permute-start.6 = (f32[352,128]{1,0:T(8,128)}, f32[352,128]{1,0:T(8,128)S(1)}, u32[]{:S(2)}, u32[]{:S(2)}) collective-permute-start(f32[352,128]{1,0:T(8,128)} %get-tuple-element.59), channel_id=1, source_target_pairs={{0,2},{4,6},{2,0},{6,4},{1,3},{5,7},{3,1},{7,5},{8,10},{12,14},{10... | collective-permute-start | bytes 540680 | tf_op jit(solution)/shard_map/ppermute | solution.py:750
  35.9 5.6 %collective-permute-start.10 = (f32[1088,128]{1,0:T(8,128)S(1)}, f32[1088,128]{1,0:T(8,128)}, u32[]{:S(2)}, u32[]{:S(2)}) collective-permute-start(f32[1088,128]{1,0:T(8,128)S(1)} %collective-permute-done.1.refs_8_), channel_id=1, source_target_pairs={{0,8},{8,0},{16,24},{24,16},{1,9},{9,1},{17,25},{25,17},{2,10},{10... | collective-permute-start | bytes 1671176 | tf_op jit(solution)/shard_map/ppermute | solution.py:603
  36.0 5.6 %collective-permute-start.9 = (f32[1088,128]{1,0:T(8,128)S(1)}, f32[1088,128]{1,0:T(8,128)}, u32[]{:S(2)}, u32[]{:S(2)}) collective-permute-start(f32[1088,128]{1,0:T(8,128)S(1)} %collective-permute-done.refs_7_), channel_id=1, source_target_pairs={{0,8},{8,0},{16,24},{24,16},{1,9},{9,1},{17,25},{25,17},{2,10},{10... | collective-permute-start | bytes 1671176 | tf_op jit(solution)/shard_map/ppermute | solution.py:603
  36.5 5.0 %collective-permute-start.7 = (f32[320,128]{1,0:T(8,128)}, f32[320,128]{1,0:T(8,128)S(1)}, u32[]{:S(2)}, u32[]{:S(2)}) collective-permute-start(f32[320,128]{1,0:T(8,128)} %copy-done.7), channel_id=1, source_target_pairs={{2,4},{4,2},{3,5},{5,3},{10,12},{12,10},{11,13},{13,11},{18,20},{2... | collective-permute-start | bytes 491528 | tf_op jit(solution)/shard_map/ppermute | solution.py:750
  48.8 12.4 %collective-permute-start.13 = (f32[320,128]{1,0:T(8,128)S(1)}, f32[320,128]{1,0:T(8,128)S(1)}, u32[]{:S(2)}, u32[]{:S(2)}) collective-permute-start(f32[320,128]{1,0:T(8,128)S(1)} %get-tuple-element.73), channel_id=1, source_target_pairs={{0,2},{4,6},{2,0},{6,4},{1,3},{5,7},{3,1},{7,5},{8,10},{12,14},{10... | collective-permute-start | bytes 491528 | tf_op jit(solution)/shard_map/ppermute | solution.py:750
  53.9 7.2 %collective-permute-start.14 = (f32[320,128]{1,0:T(8,128)S(1)}, f32[320,128]{1,0:T(8,128)S(1)}, u32[]{:S(2)}, u32[]{:S(2)}) collective-permute-start(f32[320,128]{1,0:T(8,128)S(1)} %get-tuple-element.74), channel_id=1, source_target_pairs={{2,4},{4,2},{3,5},{5,3},{10,12},{12,10},{11,13},{13,11},{18,20},{2... | collective-permute-start | bytes 491528 | tf_op jit(solution)/shard_map/ppermute | solution.py:750
  54.6 6.5 %collective-permute-start.15 = (f32[32,128]{1,0:T(8,128)S(1)}, f32[32,128]{1,0:T(8,128)S(1)}, u32[]{:S(2)}, u32[]{:S(2)}) collective-permute-start(f32[32,128]{1,0:T(8,128)S(1)} %get-tuple-element.75), channel_id=1, source_target_pairs={{0,4},{2,6},{4,0},{6,2},{1,5},{3,7},{5,1},{7,3},{8,12},{10,14},{12... | collective-permute-start | bytes 49160 | tf_op jit(solution)/shard_map/ppermute | solution.py:750
  64.7 8.9 %collective-permute-start.16 = (f32[320,128]{1,0:T(8,128)S(1)}, f32[320,128]{1,0:T(8,128)S(1)}, u32[]{:S(2)}, u32[]{:S(2)}) collective-permute-start(f32[320,128]{1,0:T(8,128)S(1)} %get-tuple-element.79), channel_id=1, source_target_pairs={{0,2},{4,6},{2,0},{6,4},{1,3},{5,7},{3,1},{7,5},{8,10},{12,14},{10... | collective-permute-start | bytes 491528 | tf_op jit(solution)/shard_map/ppermute | solution.py:750
  65.8 7.8 %collective-permute-start.17 = (f32[320,128]{1,0:T(8,128)S(1)}, f32[320,128]{1,0:T(8,128)S(1)}, u32[]{:S(2)}, u32[]{:S(2)}) collective-permute-start(f32[320,128]{1,0:T(8,128)S(1)} %get-tuple-element.80), channel_id=1, source_target_pairs={{2,4},{4,2},{3,5},{5,3},{10,12},{12,10},{11,13},{13,11},{18,20},{2... | collective-permute-start | bytes 491528 | tf_op jit(solution)/shard_map/ppermute | solution.py:750
  66.7 6.9 %collective-permute-start.18 = (f32[32,128]{1,0:T(8,128)S(1)}, f32[32,128]{1,0:T(8,128)S(1)}, u32[]{:S(2)}, u32[]{:S(2)}) collective-permute-start(f32[32,128]{1,0:T(8,128)S(1)} %get-tuple-element.81), channel_id=1, source_target_pairs={{0,4},{2,6},{4,0},{6,2},{1,5},{3,7},{5,1},{7,3},{8,12},{10,14},{12... | collective-permute-start | bytes 49160 | tf_op jit(solution)/shard_map/ppermute | solution.py:750
  77.3 8.9 %collective-permute-start.19 = (f32[320,128]{1,0:T(8,128)S(1)}, f32[320,128]{1,0:T(8,128)S(1)}, u32[]{:S(2)}, u32[]{:S(2)}) collective-permute-start(f32[320,128]{1,0:T(8,128)S(1)} %get-tuple-element.84), channel_id=1, source_target_pairs={{0,2},{4,6},{2,0},{6,4},{1,3},{5,7},{3,1},{7,5},{8,10},{12,14},{10... | collective-permute-start | bytes 491528 | tf_op jit(solution)/shard_map/ppermute | solution.py:750
  79.1 7.1 %collective-permute-start.20 = (f32[320,128]{1,0:T(8,128)S(1)}, f32[320,128]{1,0:T(8,128)S(1)}, u32[]{:S(2)}, u32[]{:S(2)}) collective-permute-start(f32[320,128]{1,0:T(8,128)S(1)} %get-tuple-element.85), channel_id=1, source_target_pairs={{2,4},{4,2},{3,5},{5,3},{10,12},{12,10},{11,13},{13,11},{18,20},{2... | collective-permute-start | bytes 491528 | tf_op jit(solution)/shard_map/ppermute | solution.py:750
  79.8 6.4 %collective-permute-start.21 = (f32[32,128]{1,0:T(8,128)S(1)}, f32[32,128]{1,0:T(8,128)S(1)}, u32[]{:S(2)}, u32[]{:S(2)}) collective-permute-start(f32[32,128]{1,0:T(8,128)S(1)} %get-tuple-element.86), channel_id=1, source_target_pairs={{0,4},{2,6},{4,0},{6,2},{1,5},{3,7},{5,1},{7,3},{8,12},{10,14},{12... | collective-permute-start | bytes 49160 | tf_op jit(solution)/shard_map/ppermute | solution.py:750
  90.4 5.2 %collective-permute-start.23 = (f32[1,128,128]{2,1,0:T(8,128)S(1)}, f32[1,128,128]{2,1,0:T(8,128)S(1)}, u32[]{:S(2)}, u32[]{:S(2)}) collective-permute-start(f32[1,128,128]{2,1,0:T(8,128)S(1)} %get-tuple-element.100), channel_id=1, source_target_pairs={{0,16},{1,17},{8,24},{9,25},{16,0},{17,1},{24,8},{25,9},{2,18},{3,... | collective-permute-start | bytes 196616 | tf_op jit(solution)/shard_map/ppermute | solution.py:873
  92.1 5.2 %collective-permute-start.24 = (f32[1,128,128]{2,1,0:T(8,128)S(1)}, f32[1,128,128]{2,1,0:T(8,128)S(1)}, u32[]{:S(2)}, u32[]{:S(2)}) collective-permute-start(f32[1,128,128]{2,1,0:T(8,128)S(1)} %get-tuple-element.102), channel_id=1, source_target_pairs={{0,17},{1,16},{8,25},{9,24},{16,1},{17,0},{24,9},{25,8},{2,19},{3,... | collective-permute-start | bytes 196616 | tf_op jit(solution)/shard_map/ppermute | solution.py:873
  93.6 5.0 %collective-permute-start.26 = (f32[1,128,128]{2,1,0:T(8,128)S(1)}, f32[1,128,128]{2,1,0:T(8,128)S(1)}, u32[]{:S(2)}, u32[]{:S(2)}) collective-permute-start(f32[1,128,128]{2,1,0:T(8,128)S(1)} %get-tuple-element.106), channel_id=1, source_target_pairs={{0,9},{1,8},{8,1},{9,0},{16,25},{17,24},{24,17},{25,16},{2,11},{3,... | collective-permute-start | bytes 196616 | tf_op jit(solution)/shard_map/ppermute | solution.py:873
  (16 other events, 97.3 us)

commit v10 on v9

--- a/solution.py
+++ b/solution.py
@@ -326,11 +326,17 @@
     return jnp.concatenate([low] + middle + [high], axis=1).reshape(lines * cy, cx)
 
 
-def pack_kernel(plan, tile_ref, potential_ref, out_ref):
+def pack_kernel(plan, tile_ref, potential_ref, out_ref, held_ref, sem):
     slots = plan.slots
+    tiles = pltpu.make_async_copy(tile_ref, held_ref, sem.at[0])
+    tail = out_ref.at[pl.ds(plan.projs * slots, plan.points)]
+    tail_copy = pltpu.make_async_copy(potential_ref, tail, sem.at[1])
+    tiles.start()
+    tail_copy.start()
+    tiles.wait()
     for p in range(plan.projs):
-        out_ref[p * slots : (p + 1) * slots, :] = tile_ref[:, p, :]
-    out_ref[plan.projs * slots :, :] = potential_ref[...]
+        out_ref[p * slots : (p + 1) * slots, :] = held_ref[:, p, :]
+    tail_copy.wait()
 
 
 def own_tiles_kernel(
@@ -650,11 +656,14 @@
     params = pltpu.CompilerParams(vmem_limit_bytes=20 * 1024 * 1024)
     rows = tile_rows + points
     in_hbm = pl.BlockSpec(memory_space=pltpu.HBM)
+    in_vmem = pl.BlockSpec(memory_space=pltpu.VMEM)
     alone = pltpu.CompilerParams(vmem_limit_bytes=61 * 1024 * 1024)
     payload = pl.pallas_call(
         functools.partial(pack_kernel, plan),
         out_shape=jax.ShapeDtypeStruct((rows, cx), f32),
-        compiler_params=params,
+        in_specs=[in_hbm, in_hbm],
+        scratch_shapes=[pltpu.VMEM(tile_proj.shape, f32), pltpu.SemaphoreType.DMA((2,))],
+        compiler_params=alone,
         name="pack",
     )(tile_proj, potential.reshape(points, cx))
     me = ix * gz + iz
@@ -764,21 +773,6 @@
         received = list(swap(sends))
         if first:
             current, received[3] = lax.optimization_barrier((current, received[3]))
-            own_table = sends[3][plan.third :]
-            across = [own_table] * (gy > 1) + [received[1][message_rows:]] * (gy > 1)
-            across += [received[3][plan.third :]] * (gy > 2)
-            if gy > 2:
-                pairs = [(i, i ^ 3) for i in range(gy)]
-                across.append(lax.ppermute(own_table, "gy", pairs))
-            across = across or [own_table]
-            scale = pl.pallas_call(
-                functools.partial(scale_kernel, plan),
-                out_shape=jax.ShapeDtypeStruct((3 * plan.third, LANE), f32),
-                in_specs=[full(1, plan.keys), full(1, plan.keys), pl.BlockSpec(memory_space=pl.ANY)]
-                + [full(*table.shape) for table in across],
-                compiler_params=params,
-                name="scale",
-            )(home_device, home_within, late_info, *across)
         extra = table_rows if first else 0
         local = pl.pallas_call(
             functools.partial(local_kernel, plan, first),
@@ -803,7 +797,22 @@
         )(current, *([] if first else [previous, plane_potential]))
         if first:
             others = [from_z, from_x, *from_xz]
-            *others, local = lax.optimization_barrier((*others, local))
+            *others, local, received[1] = lax.optimization_barrier((*others, local, received[1]))
+            own_table = sends[3][plan.third :]
+            across = [own_table] * (gy > 1) + [received[1][message_rows:]] * (gy > 1)
+            across += [received[3][plan.third :]] * (gy > 2)
+            if gy > 2:
+                pairs = [(i, i ^ 3) for i in range(gy)]
+                across.append(lax.ppermute(own_table, "gy", pairs))
+            across = across or [own_table]
+            scale = pl.pallas_call(
+                functools.partial(scale_kernel, plan),
+                out_shape=jax.ShapeDtypeStruct((3 * plan.third, LANE), f32),
+                in_specs=[in_vmem, in_vmem, pl.BlockSpec(memory_space=pl.ANY)]
+                + [in_vmem] * len(across),
+                compiler_params=params,
+                name="scale",
+            )(home_device, home_within, late_info, *across)
             pieces = [payload, *others, from_c] + [exchange(part, *rounds[2]) for part in others]
         lines = on * cz
         scratch = [

time: 102 us -> 103 us (level)
  starting transfers between devices: 42.5 us -> 44.4 us
  Pallas kernels: 28.1 us -> 29.3 us
  waiting for transfers between devices: 19.3 us -> 18.1 us
    ppermute x12, starting transfers between devices: 23.4 us -> 25.7 us  [pairwise(): return lax.ppermute(value, 'gy', pairs + [(b, a) for a, b in pairs])]
    unnamed x22 -> x16, local copies, waits for them, and re-layouts: 4.47 us -> 3.13 us
    ppermute x1, starting transfers between devices: 1.41 us -> 0.29 us  [turned_path(): across.append(lax.ppermute(own_table, 'gy', pairs))]
    pallas_call x1, Pallas kernels: 1.09 us -> 2.18 us  [turned_path(): pl.pallas_call(functools.partial(pack_kernel, plan), out_shape=jax.ShapeD...]
  transfers between devices with their start and end apart: 30 -> 30, of which waited for: 14 -> 11; matrix products, arithmetic and copies ran while one was open for 2% -> 3% of each run, Pallas kernels for 14% -> 14%
where the time goes in v10:
time: 103 us
  starting transfers between devices  44.4 us (43%)
  Pallas kernels  29.3 us (28%)
  waiting for transfers between devices  18.1 us (18%)
  local copies, waits for them, and re-layouts  9.65 us (9%)
    ppermute x12, starting transfers between devices, pairwise(): return lax.ppermute(value, 'gy', pairs + [(b, a) for a, b in pairs])  25.7 us
    pallas_call x3, Pallas kernels, turned_path(): pl.pallas_call(functools.partial(step_kernel, plan, first, last, base), o...  12.6 us
    ppermute x9, starting transfers between devices, exchange(): return lax.ppermute(value, axis, [(i, i ^ bit) for i in range(count)])  7.92 us
    ppermute x12, waiting for transfers between devices, pairwise(): return lax.ppermute(value, 'gy', pairs + [(b, a) for a, b in pairs])  7.53 us
    ppermute x7, starting transfers between devices, turned_path(): lax.ppermute(block, ('gx', 'gz'), [(i, i ^ moved) for i in range(blocks)])  6.94 us
    pallas_call x4, Pallas kernels, turned_path(): pl.pallas_call(functools.partial(local_kernel, plan, first), out_shape=y_...  6.66 us
    ppermute x9, waiting for transfers between devices, exchange(): return lax.ppermute(value, axis, [(i, i ^ bit) for i in range(count)])  5.44 us
    pallas_call x1, Pallas kernels, turned_path(): pl.pallas_call(functools.partial(own_tiles_kernel, plan), out_shape=[jax....  4.32 us
  transfers between devices with their start and end apart: 30, of which 11 were waited for; matrix products, arithmetic and copies ran while one was open for 3% of the time, Pallas kernels for 14%

profile of v10, /device:TPU:0, one launch (start us, length us, event | category | flops | bytes accessed | tf_op | source)
XLA Modules:
  0.0 102.7 jit_solution(15467370607919844238)
XLA Ops:
  0.0 2.2 %pack.1.payload_ref.refs_6_ = f32[1088,128]{1,0:T(8,128)} custom-call(f32[256,4,128]{2,1,0:T(4,128)} %tile_ref.1, f32[64,128]{1,0:T(8,128)} %bitcast.15), custom_call_target="tpu_custom_call" | custom-call | tf_op jit(solution)/shard_map/pack/pallas_call | solution.py:661
  2.2 3.0 %collective-permute-start = (f32[1088,128]{1,0:T(8,128)}, f32[1088,128]{1,0:T(8,128)S(1)}, u32[]{:S(2)}, u32[]{:S(2)}) collective-permute-start(f32[1088,128]{1,0:T(8,128)} %pack.1.payload_ref.refs_6_), channel_id=1, source_target_pairs={{0,1},{1,0},{2,3},{3,2},{4,5},{5,4},{6,7},{7,6},{8,9},{9,8},{10,11... | collective-permute-start | bytes 1671176 | tf_op jit(solution)/shard_map/ppermute | solution.py:609
  7.4 4.3 %own_tiles.1 = (f32[8,152,128]{2,1,0:T(8,128)}, s32[1]{0:T(128)}) custom-call(s32[1]{0:T(128)S(6)} %copy.19.info_ref, f32[1088,128]{1,0:T(8,128)} %pack.1.payload_ref.refs_6_, s32[1,256]{1,0:T(1,128)} %bitcast.17, s32[1,256]{1,0:T(1,128)} %bitcast.18, f32[4,64]{1,0:T(4,128)} %bitcast.16, f32[8,128,128]{2,1,0:T(8,128)} %bitcast.11), custom_call_target="tpu_custom_call" | custom-call | tf_op jit(solution)/shard_map/own_tiles/pallas_call | solution.py:676
  11.7 3.6 %all-to-all-start = ((f32[8,152,128]{2,1,0:T(8,128)}), f32[8,152,128]{2,1,0:T(8,128)S(1)}, u32[]{:S(2)}, u32[]{:S(2)}) async-start(f32[8,152,128]{2,1,0:T(8,128)} %get-tuple-element.54), calls=%async_computation | async-start | bytes 1245184 | tf_op jit(solution)/shard_map/all_to_all | solution.py:703
  15.3 3.5 %collective-permute-done.refs_7_ = f32[1088,128]{1,0:T(8,128)S(1)} collective-permute-done((f32[1088,128]{1,0:T(8,128)}, f32[1088,128]{1,0:T(8,128)S(1)}, u32[]{:S(2)}, u32[]{:S(2)}) %collective-permute-start) | collective-permute-done | bytes 557088 | tf_op jit(solution)/shard_map/ppermute | solution.py:609
  18.8 1.9 %collective-permute-done.1.refs_8_ = f32[1088,128]{1,0:T(8,128)} collective-permute-done((f32[1088,128]{1,0:T(8,128)}, f32[1088,128]{1,0:T(8,128)}, u32[]{:S(2)}, u32[]{:S(2)}) %collective-permute-start.1) | collective-permute-done | bytes 557088 | tf_op jit(solution)/shard_map/ppermute | solution.py:609
  21.4 1.9 %collective-permute-start.3 = (f32[544,128]{1,0:T(8,128)}, f32[544,128]{1,0:T(8,128)S(1)}, u32[]{:S(2)}, u32[]{:S(2)}) collective-permute-start(f32[544,128]{1,0:T(8,128)} %slice.15), channel_id=1, source_target_pairs={{0,16},{8,24},{16,0},{24,8},{1,17},{9,25},{17,1},{25,9},{2,18},{10... | collective-permute-start | bytes 835592 | tf_op jit(solution)/shard_map/ppermute | solution.py:609
  23.3 1.7 %slice.16 = f32[544,128]{1,0:T(8,128)} slice(f32[1088,128]{1,0:T(8,128)} %collective-permute-done.1.refs_8_), slice={[544:1088], [0:128]} | slice | bytes 557056 | tf_op jit(solution)/shard_map/slice | solution.py:709
  25.4 1.9 %all-to-all-done.in_ref = f32[8,152,128]{2,1,0:T(8,128)S(1)} async-done(((f32[8,152,128]{2,1,0:T(8,128)}), f32[8,152,128]{2,1,0:T(8,128)S(1)}, u32[]{:S(2)}, u32[]{:S(2)}) %all-to-all-start) | async-done | bytes 622624 | tf_op jit(solution)/shard_map/all_to_all | solution.py:703
  31.1 2.6 %collective-permute-start.5 = (f32[64,128]{1,0:T(8,128)S(1)}, f32[64,128]{1,0:T(8,128)S(1)}, u32[]{:S(2)}, u32[]{:S(2)}) collective-permute-start(f32[64,128]{1,0:T(8,128)S(1)} %get-tuple-element.56), channel_id=1, source_target_pairs={{0,4},{2,6},{4,0},{6,2},{1,5},{3,7},{5,1},{7,3},{8,12},{10,14},{12... | collective-permute-start | bytes 98312 | tf_op jit(solution)/shard_map/ppermute | solution.py:759
  34.0 2.0 %collective-permute-done.5.refs_3_ = f32[64,128]{1,0:T(8,128)S(1)} collective-permute-done((f32[64,128]{1,0:T(8,128)S(1)}, f32[64,128]{1,0:T(8,128)S(1)}, u32[]{:S(2)}, u32[]{:S(2)}) %collective-permute-start.5) | collective-permute-done | bytes 32800 | tf_op jit(solution)/shard_map/ppermute | solution.py:759
  40.4 2.1 %scale.1.refs_4_ = f32[96,128]{1,0:T(8,128)S(1)} custom-call(s32[1,1536]{1,0:T(1,128)S(1)} %fusion.4.device_ref, s32[1,1536]{1,0:T(1,128)S(1)} %get-tuple-element.113.within_ref, s32[1]{0:T(128)} %get-tuple-element.64._, f32[32,128]{1,0:T(8,128)S(1)} %slice.17.refs_0_, f32[32,128]{1,0:T(8,128)S(1)} %slice.18.refs_1_, f32[32,128]{1,0:T(8,128)S(1)} %slice.19.refs_2_, ...), custom_call_target="tpu_custom_call" | custom-call | tf_op jit(solution)/shard_map/scale/pallas_call | solution.py:808
  43.6 5.4 %step.4 = (f32[8,128,128]{2,1,0:T(8,128)S(1)}, bf16[8,1024,256]{2,1,0:T(8,128)(2,1)S(1)}, f32[8,64,128]{2,1,0:T(8,128)S(1)}, f32[96,128]{1,0:T(8,128)S(1)}, f32[...) custom-call(f32[8,128,128]{2,1,0:T(8,128)S(1)} %local.4.local_ref, ...), custom_call_target="tpu_custom_call" | custom-call | tf_op jit(solution)/shard_map/step/pallas_call | solution.py:855
  49.0 6.2 %collective-permute-start.13 = (f32[320,128]{1,0:T(8,128)S(1)}, f32[320,128]{1,0:T(8,128)S(1)}, u32[]{:S(2)}, u32[]{:S(2)}) collective-permute-start(f32[320,128]{1,0:T(8,128)S(1)} %get-tuple-element.75), channel_id=1, source_target_pairs={{0,2},{4,6},{2,0},{6,4},{1,3},{5,7},{3,1},{7,5},{8,10},{12,14},{10... | collective-permute-start | bytes 491528 | tf_op jit(solution)/shard_map/ppermute | solution.py:759
  55.9 2.8 %collective-permute-start.15 = (f32[32,128]{1,0:T(8,128)S(1)}, f32[32,128]{1,0:T(8,128)S(1)}, u32[]{:S(2)}, u32[]{:S(2)}) collective-permute-start(f32[32,128]{1,0:T(8,128)S(1)} %get-tuple-element.77), channel_id=1, source_target_pairs={{0,4},{2,6},{4,0},{6,2},{1,5},{3,7},{5,1},{7,3},{8,12},{10,14},{12... | collective-permute-start | bytes 49160 | tf_op jit(solution)/shard_map/ppermute | solution.py:759
  58.7 1.7 %local.5.local_ref = f32[8,128,128]{2,1,0:T(8,128)S(1)} custom-call(f32[8,128,128]{2,1,0:T(8,128)S(1)} %get-tuple-element.72.y_ref.refs_0_, f32[8,128,128]{2,1,0:T(8,128)S(1)} %get-tuple-element.57.y_ref.refs_5_.refs_0_, f32[8,64,128]{2,1,0:T(8,128)S(1)} %get-tuple-element.73.refs_1_), custom_call_target="tpu_custom_call" | custom-call | flops 7864320 | bytes 2097152 | tf_op jit(solution)/shard_map/local/pallas_call | solution.py:777
  60.4 2.3 %collective-permute-done.15.refs_3_ = f32[32,128]{1,0:T(8,128)S(1)} collective-permute-done((f32[32,128]{1,0:T(8,128)S(1)}, f32[32,128]{1,0:T(8,128)S(1)}, u32[]{:S(2)}, u32[]{:S(2)}) %collective-permute-start.15) | collective-permute-done | bytes 16416 | tf_op jit(solution)/shard_map/ppermute | solution.py:759
  62.6 3.6 %step.5 = (f32[8,128,128]{2,1,0:T(8,128)S(1)}, f32[96,128]{1,0:T(8,128)S(1)}, f32[320,128]{1,0:T(8,128)S(1)}, f32[320,128]{1,0:T(8,128)S(1)}, f32[32,128]{1,0:T(8,128)S(1)}) custom-call(f32[8,128,128]{2,1,0:T(8,128)S(1)} %local.5.local_ref, f32[96,128]{1,0:T(8,128)S(1)} %get-tuple-element.74.refs_0_, f32[320,128]{1,0:T(8,128)S(1)} %collective-permute-done.13.refs_1_, ...), custom_call_target="tpu_custom_call" | custom-call | tf_op jit(solution)/shard_map/step/pallas_call | solution.py:855
  67.5 4.4 %collective-permute-start.18 = (f32[32,128]{1,0:T(8,128)S(1)}, f32[32,128]{1,0:T(8,128)S(1)}, u32[]{:S(2)}, u32[]{:S(2)}) collective-permute-start(f32[32,128]{1,0:T(8,128)S(1)} %get-tuple-element.83), channel_id=1, source_target_pairs={{0,4},{2,6},{4,0},{6,2},{1,5},{3,7},{5,1},{7,3},{8,12},{10,14},{12... | collective-permute-start | bytes 49160 | tf_op jit(solution)/shard_map/ppermute | solution.py:759
  71.9 1.7 %local.6.local_ref = f32[8,128,128]{2,1,0:T(8,128)S(1)} custom-call(f32[8,128,128]{2,1,0:T(8,128)S(1)} %get-tuple-element.79.y_ref.refs_0_, f32[8,128,128]{2,1,0:T(8,128)S(1)} %get-tuple-element.72.y_ref.refs_0_, f32[8,64,128]{2,1,0:T(8,128)S(1)} %get-tuple-element.73.refs_1_), custom_call_target="tpu_custom_call" | custom-call | flops 7864320 | bytes 2097152 | tf_op jit(solution)/shard_map/local/pallas_call | solution.py:777
  75.1 3.6 %step.6 = (f32[8,128,128]{2,1,0:T(8,128)S(1)}, f32[96,128]{1,0:T(8,128)S(1)}, f32[320,128]{1,0:T(8,128)S(1)}, f32[320,128]{1,0:T(8,128)S(1)}, f32[32,128]{1,0:T(8,128)S(1)}) custom-call(f32[8,128,128]{2,1,0:T(8,128)S(1)} %local.6.local_ref, f32[96,128]{1,0:T(8,128)S(1)} %get-tuple-element.80.refs_0_, f32[320,128]{1,0:T(8,128)S(1)} %collective-permute-done.16.refs_1_, ...), custom_call_target="tpu_custom_call" | custom-call | tf_op jit(solution)/shard_map/step/pallas_call | solution.py:855
  80.4 3.9 %collective-permute-start.21 = (f32[32,128]{1,0:T(8,128)S(1)}, f32[32,128]{1,0:T(8,128)S(1)}, u32[]{:S(2)}, u32[]{:S(2)}) collective-permute-start(f32[32,128]{1,0:T(8,128)S(1)} %get-tuple-element.88), channel_id=1, source_target_pairs={{0,4},{2,6},{4,0},{6,2},{1,5},{3,7},{5,1},{7,3},{8,12},{10,14},{12... | collective-permute-start | bytes 49160 | tf_op jit(solution)/shard_map/ppermute | solution.py:759
  86.0 1.7 %collective-permute-done.21 = f32[32,128]{1,0:T(8,128)S(1)} collective-permute-done((f32[32,128]{1,0:T(8,128)S(1)}, f32[32,128]{1,0:T(8,128)S(1)}, u32[]{:S(2)}, u32[]{:S(2)}) %collective-permute-start.21) | collective-permute-done | bytes 16416 | tf_op jit(solution)/shard_map/ppermute | solution.py:759
  87.7 3.8 %step.7 = (f32[8,128,128]{2,1,0:T(8,128)S(1)}, f32[1,128,128]{2,1,0:T(8,128)S(1)}, f32[1,128,128]{2,1,0:T(8,128)S(1)}, f32[1,128,128]{2,1,0:T(8,128)S(1)}, f32[1...) fusion(f32[8,128,128]{2,1,0:T(8,128)S(1)} %broadcast_in_dim.3, ...), kind=kCustom, calls=%fused_computation.29 | custom fusion | bytes 6275076 | tf_op jit(solution)/shard_map/step/pallas_call | solution.py:855
  (82 shorter events, 29.8 us)
Async XLA Ops:
  2.2 16.6 %collective-permute-start = (f32[1088,128]{1,0:T(8,128)}, f32[1088,128]{1,0:T(8,128)S(1)}, u32[]{:S(2)}, u32[]{:S(2)}) collective-permute-start(f32[1088,128]{1,0:T(8,128)} %pack.1.payload_ref.refs_6_), channel_id=1, source_target_pairs={{0,1},{1,0},{2,3},{3,2},{4,5},{5,4},{6,7},{7,6},{8,9},{9,8},{10,11... | collective-permute-start | bytes 1671176 | tf_op jit(solution)/shard_map/ppermute | solution.py:609
  5.2 15.5 %collective-permute-start.1 = (f32[1088,128]{1,0:T(8,128)}, f32[1088,128]{1,0:T(8,128)}, u32[]{:S(2)}, u32[]{:S(2)}) collective-permute-start(f32[1088,128]{1,0:T(8,128)} %pack.1.payload_ref.refs_6_), channel_id=1, source_target_pairs={{0,16},{8,24},{16,0},{24,8},{1,17},{9,25},{17,1},{25,9},{2,18},{10... | collective-permute-start | bytes 1671176 | tf_op jit(solution)/shard_map/ppermute | solution.py:609
  6.7 14.0 %collective-permute-start.2 = (f32[1088,128]{1,0:T(8,128)}, f32[1088,128]{1,0:T(8,128)}, u32[]{:S(2)}, u32[]{:S(2)}) collective-permute-start(f32[1088,128]{1,0:T(8,128)} %pack.1.payload_ref.refs_6_), channel_id=1, source_target_pairs={{0,8},{8,0},{16,24},{24,16},{1,9},{9,1},{17,25},{25,17},{2,10},{10... | collective-permute-start | bytes 1671176 | tf_op jit(solution)/shard_map/ppermute | solution.py:609
  11.7 15.5 %all-to-all-start = ((f32[8,152,128]{2,1,0:T(8,128)}), f32[8,152,128]{2,1,0:T(8,128)S(1)}, u32[]{:S(2)}, u32[]{:S(2)}) async-start(f32[8,152,128]{2,1,0:T(8,128)} %get-tuple-element.54), calls=%async_computation | async-start | bytes 1245184 | tf_op jit(solution)/shard_map/all_to_all | solution.py:703
  21.4 16.3 %collective-permute-start.3 = (f32[544,128]{1,0:T(8,128)}, f32[544,128]{1,0:T(8,128)S(1)}, u32[]{:S(2)}, u32[]{:S(2)}) collective-permute-start(f32[544,128]{1,0:T(8,128)} %slice.15), channel_id=1, source_target_pairs={{0,16},{8,24},{16,0},{24,8},{1,17},{9,25},{17,1},{25,9},{2,18},{10... | collective-permute-start | bytes 835592 | tf_op jit(solution)/shard_map/ppermute | solution.py:609
  25.0 12.7 %collective-permute-start.4 = (f32[544,128]{1,0:T(8,128)}, f32[544,128]{1,0:T(8,128)}, u32[]{:S(2)}, u32[]{:S(2)}) collective-permute-start(f32[544,128]{1,0:T(8,128)} %slice.16), channel_id=1, source_target_pairs={{0,1},{1,0},{2,3},{3,2},{4,5},{5,4},{6,7},{7,6},{8,9},{9,8},{10,11... | collective-permute-start | bytes 835592 | tf_op jit(solution)/shard_map/ppermute | solution.py:609
  29.3 8.4 %collective-permute-start.6 = (f32[352,128]{1,0:T(8,128)}, f32[352,128]{1,0:T(8,128)S(1)}, u32[]{:S(2)}, u32[]{:S(2)}) collective-permute-start(f32[352,128]{1,0:T(8,128)} %get-tuple-element.58), channel_id=1, source_target_pairs={{0,2},{4,6},{2,0},{6,4},{1,3},{5,7},{3,1},{7,5},{8,10},{12,14},{10... | collective-permute-start | bytes 540680 | tf_op jit(solution)/shard_map/ppermute | solution.py:759
  31.1 4.9 %collective-permute-start.5 = (f32[64,128]{1,0:T(8,128)S(1)}, f32[64,128]{1,0:T(8,128)S(1)}, u32[]{:S(2)}, u32[]{:S(2)}) collective-permute-start(f32[64,128]{1,0:T(8,128)S(1)} %get-tuple-element.56), channel_id=1, source_target_pairs={{0,4},{2,6},{4,0},{6,2},{1,5},{3,7},{5,1},{7,3},{8,12},{10,14},{12... | collective-permute-start | bytes 98312 | tf_op jit(solution)/shard_map/ppermute | solution.py:759
  33.7 6.1 %collective-permute-start.8 = (f32[32,128]{1,0:T(8,128)S(1)}, f32[32,128]{1,0:T(8,128)S(1)}, u32[]{:S(2)}, u32[]{:S(2)}) collective-permute-start(f32[32,128]{1,0:T(8,128)S(1)} %slice.17.refs_0_), channel_id=1, source_target_pairs={{0,6},{2,4},{4,2},{6,0},{1,7},{3,5},{5,3},{7,1},{8,14},{10,12},{12... | collective-permute-start | bytes 49160 | tf_op jit(solution)/shard_map/ppermute | solution.py:806
  37.7 4.9 %collective-permute-start.10 = (f32[1088,128]{1,0:T(8,128)}, f32[1088,128]{1,0:T(8,128)}, u32[]{:S(2)}, u32[]{:S(2)}) collective-permute-start(f32[1088,128]{1,0:T(8,128)} %collective-permute-done.1.refs_8_), channel_id=1, source_target_pairs={{0,8},{8,0},{16,24},{24,16},{1,9},{9,1},{17,25},{25,17},{2,10},{10... | collective-permute-start | bytes 1671176 | tf_op jit(solution)/shard_map/ppermute | solution.py:609
  37.8 4.8 %collective-permute-start.9 = (f32[1088,128]{1,0:T(8,128)S(1)}, f32[1088,128]{1,0:T(8,128)}, u32[]{:S(2)}, u32[]{:S(2)}) collective-permute-start(f32[1088,128]{1,0:T(8,128)S(1)} %collective-permute-done.refs_7_), channel_id=1, source_target_pairs={{0,8},{8,0},{16,24},{24,16},{1,9},{9,1},{17,25},{25,17},{2,10},{10... | collective-permute-start | bytes 1671176 | tf_op jit(solution)/shard_map/ppermute | solution.py:609
  49.0 13.6 %collective-permute-start.13 = (f32[320,128]{1,0:T(8,128)S(1)}, f32[320,128]{1,0:T(8,128)S(1)}, u32[]{:S(2)}, u32[]{:S(2)}) collective-permute-start(f32[320,128]{1,0:T(8,128)S(1)} %get-tuple-element.75), channel_id=1, source_target_pairs={{0,2},{4,6},{2,0},{6,4},{1,3},{5,7},{3,1},{7,5},{8,10},{12,14},{10... | collective-permute-start | bytes 491528 | tf_op jit(solution)/shard_map/ppermute | solution.py:759
  55.2 7.4 %collective-permute-start.14 = (f32[320,128]{1,0:T(8,128)S(1)}, f32[320,128]{1,0:T(8,128)S(1)}, u32[]{:S(2)}, u32[]{:S(2)}) collective-permute-start(f32[320,128]{1,0:T(8,128)S(1)} %get-tuple-element.76), channel_id=1, source_target_pairs={{2,4},{4,2},{3,5},{5,3},{10,12},{12,10},{11,13},{13,11},{18,20},{2... | collective-permute-start | bytes 491528 | tf_op jit(solution)/shard_map/ppermute | solution.py:759
  55.9 6.7 %collective-permute-start.15 = (f32[32,128]{1,0:T(8,128)S(1)}, f32[32,128]{1,0:T(8,128)S(1)}, u32[]{:S(2)}, u32[]{:S(2)}) collective-permute-start(f32[32,128]{1,0:T(8,128)S(1)} %get-tuple-element.77), channel_id=1, source_target_pairs={{0,4},{2,6},{4,0},{6,2},{1,5},{3,7},{5,1},{7,3},{8,12},{10,14},{12... | collective-permute-start | bytes 49160 | tf_op jit(solution)/shard_map/ppermute | solution.py:759
  66.2 8.9 %collective-permute-start.16 = (f32[320,128]{1,0:T(8,128)S(1)}, f32[320,128]{1,0:T(8,128)S(1)}, u32[]{:S(2)}, u32[]{:S(2)}) collective-permute-start(f32[320,128]{1,0:T(8,128)S(1)} %get-tuple-element.81), channel_id=1, source_target_pairs={{0,2},{4,6},{2,0},{6,4},{1,3},{5,7},{3,1},{7,5},{8,10},{12,14},{10... | collective-permute-start | bytes 491528 | tf_op jit(solution)/shard_map/ppermute | solution.py:759
  66.7 8.5 %collective-permute-start.17 = (f32[320,128]{1,0:T(8,128)S(1)}, f32[320,128]{1,0:T(8,128)S(1)}, u32[]{:S(2)}, u32[]{:S(2)}) collective-permute-start(f32[320,128]{1,0:T(8,128)S(1)} %get-tuple-element.82), channel_id=1, source_target_pairs={{2,4},{4,2},{3,5},{5,3},{10,12},{12,10},{11,13},{13,11},{18,20},{2... | collective-permute-start | bytes 491528 | tf_op jit(solution)/shard_map/ppermute | solution.py:759
  67.5 7.6 %collective-permute-start.18 = (f32[32,128]{1,0:T(8,128)S(1)}, f32[32,128]{1,0:T(8,128)S(1)}, u32[]{:S(2)}, u32[]{:S(2)}) collective-permute-start(f32[32,128]{1,0:T(8,128)S(1)} %get-tuple-element.83), channel_id=1, source_target_pairs={{0,4},{2,6},{4,0},{6,2},{1,5},{3,7},{5,1},{7,3},{8,12},{10,14},{12... | collective-permute-start | bytes 49160 | tf_op jit(solution)/shard_map/ppermute | solution.py:759
  78.8 8.9 %collective-permute-start.19 = (f32[320,128]{1,0:T(8,128)S(1)}, f32[320,128]{1,0:T(8,128)S(1)}, u32[]{:S(2)}, u32[]{:S(2)}) collective-permute-start(f32[320,128]{1,0:T(8,128)S(1)} %get-tuple-element.86), channel_id=1, source_target_pairs={{0,2},{4,6},{2,0},{6,4},{1,3},{5,7},{3,1},{7,5},{8,10},{12,14},{10... | collective-permute-start | bytes 491528 | tf_op jit(solution)/shard_map/ppermute | solution.py:759
  79.7 8.0 %collective-permute-start.20 = (f32[320,128]{1,0:T(8,128)S(1)}, f32[320,128]{1,0:T(8,128)S(1)}, u32[]{:S(2)}, u32[]{:S(2)}) collective-permute-start(f32[320,128]{1,0:T(8,128)S(1)} %get-tuple-element.87), channel_id=1, source_target_pairs={{2,4},{4,2},{3,5},{5,3},{10,12},{12,10},{11,13},{13,11},{18,20},{2... | collective-permute-start | bytes 491528 | tf_op jit(solution)/shard_map/ppermute | solution.py:759
  80.4 7.3 %collective-permute-start.21 = (f32[32,128]{1,0:T(8,128)S(1)}, f32[32,128]{1,0:T(8,128)S(1)}, u32[]{:S(2)}, u32[]{:S(2)}) collective-permute-start(f32[32,128]{1,0:T(8,128)S(1)} %get-tuple-element.88), channel_id=1, source_target_pairs={{0,4},{2,6},{4,0},{6,2},{1,5},{3,7},{5,1},{7,3},{8,12},{10,14},{12... | collective-permute-start | bytes 49160 | tf_op jit(solution)/shard_map/ppermute | solution.py:759
  91.6 4.6 %collective-permute-start.22 = (f32[1,128,128]{2,1,0:T(8,128)S(1)}, f32[1,128,128]{2,1,0:T(8,128)S(1)}, u32[]{:S(2)}, u32[]{:S(2)}) collective-permute-start(f32[1,128,128]{2,1,0:T(8,128)S(1)} %get-tuple-element.100), channel_id=1, source_target_pairs={{0,1},{1,0},{8,9},{9,8},{16,17},{17,16},{24,25},{25,24},{2,3},{3,2... | collective-permute-start | bytes 196616 | tf_op jit(solution)/shard_map/ppermute | solution.py:882
  93.7 5.3 %collective-permute-start.24 = (f32[1,128,128]{2,1,0:T(8,128)S(1)}, f32[1,128,128]{2,1,0:T(8,128)S(1)}, u32[]{:S(2)}, u32[]{:S(2)}) collective-permute-start(f32[1,128,128]{2,1,0:T(8,128)S(1)} %get-tuple-element.104), channel_id=1, source_target_pairs={{0,17},{1,16},{8,25},{9,24},{16,1},{17,0},{24,9},{25,8},{2,19},{3,... | collective-permute-start | bytes 196616 | tf_op jit(solution)/shard_map/ppermute | solution.py:882
  95.1 4.9 %collective-permute-start.26 = (f32[1,128,128]{2,1,0:T(8,128)S(1)}, f32[1,128,128]{2,1,0:T(8,128)S(1)}, u32[]{:S(2)}, u32[]{:S(2)}) collective-permute-start(f32[1,128,128]{2,1,0:T(8,128)S(1)} %get-tuple-element.108), channel_id=1, source_target_pairs={{0,9},{1,8},{8,1},{9,0},{16,25},{17,24},{24,17},{25,16},{2,11},{3,... | collective-permute-start | bytes 196616 | tf_op jit(solution)/shard_map/ppermute | solution.py:882
  97.2 4.7 %collective-permute-start.28 = (f32[1,128,128]{2,1,0:T(8,128)S(1)}, f32[1,128,128]{2,1,0:T(8,128)S(1)}, u32[]{:S(2)}, u32[]{:S(2)}) collective-permute-start(f32[1,128,128]{2,1,0:T(8,128)S(1)} %get-tuple-element.112), channel_id=1, source_target_pairs={{0,25},{1,24},{8,17},{9,16},{16,9},{17,8},{24,1},{25,0},{2,27},{3,... | collective-permute-start | bytes 196616 | tf_op jit(solution)/shard_map/ppermute | solution.py:882
  (13 other events, 124.0 us)

commit v11 on v9

--- a/solution.py
+++ b/solution.py
@@ -445,7 +445,7 @@
         emit_sums(plan, total_ref[...], odd, upper, own_ref, even_ref, odd_ref, far_ref)
 
 
-def scale_kernel(plan, device_ref, within_ref, _, *refs):
+def scale_kernel(plan, device_ref, within_ref, _, __, *refs):
     table_refs, out_ref = refs[:-1], refs[-1]
     blocks, owned = plan.blocks, plan.owned
     tables = []
@@ -650,6 +650,7 @@
     params = pltpu.CompilerParams(vmem_limit_bytes=20 * 1024 * 1024)
     rows = tile_rows + points
     in_hbm = pl.BlockSpec(memory_space=pltpu.HBM)
+    in_vmem = pl.BlockSpec(memory_space=pltpu.VMEM)
     alone = pltpu.CompilerParams(vmem_limit_bytes=61 * 1024 * 1024)
     payload = pl.pallas_call(
         functools.partial(pack_kernel, plan),
@@ -774,11 +775,12 @@
             scale = pl.pallas_call(
                 functools.partial(scale_kernel, plan),
                 out_shape=jax.ShapeDtypeStruct((3 * plan.third, LANE), f32),
-                in_specs=[full(1, plan.keys), full(1, plan.keys), pl.BlockSpec(memory_space=pl.ANY)]
-                + [full(*table.shape) for table in across],
+                in_specs=[in_vmem, in_vmem]
+                + [pl.BlockSpec(memory_space=pl.ANY)] * 2
+                + [in_vmem] * len(across),
                 compiler_params=params,
                 name="scale",
-            )(home_device, home_within, late_info, *across)
+            )(home_device, home_within, late_info, received[2], *across)
         extra = table_rows if first else 0
         local = pl.pallas_call(
             functools.partial(local_kernel, plan, first),

time: 102 us -> 104 us (1.020)
  starting transfers between devices: 42.5 us -> 44.6 us
    ppermute x12, starting transfers between devices: 23.4 us -> 25.5 us  [pairwise(): return lax.ppermute(value, 'gy', pairs + [(b, a) for a, b in pairs])]
where the time goes in v11:
time: 104 us; the launch traced here: 103 us
  starting transfers between devices  44.6 us (43%)
  Pallas kernels  28.1 us (27%)
  waiting for transfers between devices  19.3 us (19%)
  local copies, waits for them, and re-layouts  10.1 us (10%)
    ppermute x12, starting transfers between devices, pairwise(): return lax.ppermute(value, 'gy', pairs + [(b, a) for a, b in pairs])  25.5 us
    pallas_call x3, Pallas kernels, turned_path(): pl.pallas_call(functools.partial(step_kernel, plan, first, last, base), o...  12.5 us
    ppermute x12, waiting for transfers between devices, pairwise(): return lax.ppermute(value, 'gy', pairs + [(b, a) for a, b in pairs])  7.49 us
    ppermute x9, starting transfers between devices, exchange(): return lax.ppermute(value, axis, [(i, i ^ bit) for i in range(count)])  7.39 us
    ppermute x7, starting transfers between devices, turned_path(): lax.ppermute(block, ('gx', 'gz'), [(i, i ^ moved) for i in range(blocks)])  6.72 us
    pallas_call x4, Pallas kernels, turned_path(): pl.pallas_call(functools.partial(local_kernel, plan, first), out_shape=y_...  6.66 us
    ppermute x9, waiting for transfers between devices, exchange(): return lax.ppermute(value, axis, [(i, i ^ bit) for i in range(count)])  5.36 us
    unnamed x22, local copies, waits for them, and re-layouts  4.47 us
  transfers between devices with their start and end apart: 30, of which 14 were waited for; matrix products, arithmetic and copies ran while one was open for 2% of the time, Pallas kernels for 14%

profile of v11, /device:TPU:0, one launch (start us, length us, event | category | flops | bytes accessed | tf_op | source)
XLA Modules:
  0.0 103.2 jit_solution(9087196158475902304)
XLA Ops:
  2.9 3.0 %collective-permute-start = (f32[1088,128]{1,0:T(8,128)}, f32[1088,128]{1,0:T(8,128)S(1)}, u32[]{:S(2)}, u32[]{:S(2)}) collective-permute-start(f32[1088,128]{1,0:T(8,128)} %pack.1.payload_ref.refs_6_), channel_id=1, source_target_pairs={{0,1},{1,0},{2,3},{3,2},{4,5},{5,4},{6,7},{7,6},{8,9},{9,8},{10,11... | collective-permute-start | bytes 1671176 | tf_op jit(solution)/shard_map/ppermute | solution.py:603
  8.0 4.3 %own_tiles.1 = (f32[8,152,128]{2,1,0:T(8,128)}, s32[1]{0:T(128)}) custom-call(s32[1]{0:T(128)S(6)} %copy.19.info_ref, f32[1088,128]{1,0:T(8,128)} %pack.1.payload_ref.refs_6_, s32[1,256]{1,0:T(1,128)} %bitcast.17, s32[1,256]{1,0:T(1,128)} %bitcast.18, f32[4,64]{1,0:T(4,128)} %bitcast.16, f32[8,128,128]{2,1,0:T(8,128)} %bitcast.12), custom_call_target="tpu_custom_call" | custom-call | tf_op jit(solution)/shard_map/own_tiles/pallas_call | solution.py:668
  12.3 3.6 %all-to-all-start = ((f32[8,152,128]{2,1,0:T(8,128)}), f32[8,152,128]{2,1,0:T(8,128)S(1)}, u32[]{:S(2)}, u32[]{:S(2)}) async-start(f32[8,152,128]{2,1,0:T(8,128)} %get-tuple-element.53), calls=%async_computation | async-start | bytes 1245184 | tf_op jit(solution)/shard_map/all_to_all | solution.py:695
  15.9 3.6 %collective-permute-done.refs_7_ = f32[1088,128]{1,0:T(8,128)S(1)} collective-permute-done((f32[1088,128]{1,0:T(8,128)}, f32[1088,128]{1,0:T(8,128)S(1)}, u32[]{:S(2)}, u32[]{:S(2)}) %collective-permute-start) | collective-permute-done | bytes 557088 | tf_op jit(solution)/shard_map/ppermute | solution.py:603
  19.4 1.8 %collective-permute-done.1.refs_8_ = f32[1088,128]{1,0:T(8,128)S(1)} collective-permute-done((f32[1088,128]{1,0:T(8,128)}, f32[1088,128]{1,0:T(8,128)S(1)}, u32[]{:S(2)}, u32[]{:S(2)}) %collective-permute-start.1) | collective-permute-done | bytes 557088 | tf_op jit(solution)/shard_map/ppermute | solution.py:603
  22.0 1.9 %collective-permute-start.3 = (f32[544,128]{1,0:T(8,128)}, f32[544,128]{1,0:T(8,128)S(1)}, u32[]{:S(2)}, u32[]{:S(2)}) collective-permute-start(f32[544,128]{1,0:T(8,128)} %slice.15), channel_id=1, source_target_pairs={{0,16},{8,24},{16,0},{24,8},{1,17},{9,25},{17,1},{25,9},{2,18},{10... | collective-permute-start | bytes 835592 | tf_op jit(solution)/shard_map/ppermute | solution.py:603
  25.3 2.6 %all-to-all-done.in_ref = f32[8,152,128]{2,1,0:T(8,128)S(1)} async-done(((f32[8,152,128]{2,1,0:T(8,128)}), f32[8,152,128]{2,1,0:T(8,128)S(1)}, u32[]{:S(2)}, u32[]{:S(2)}) %all-to-all-start) | async-done | bytes 622624 | tf_op jit(solution)/shard_map/all_to_all | solution.py:695
  29.3 2.6 %collective-permute-start.5 = (f32[64,128]{1,0:T(8,128)S(1)}, f32[64,128]{1,0:T(8,128)S(1)}, u32[]{:S(2)}, u32[]{:S(2)}) collective-permute-start(f32[64,128]{1,0:T(8,128)S(1)} %get-tuple-element.55), channel_id=1, source_target_pairs={{0,4},{2,6},{4,0},{6,2},{1,5},{3,7},{5,1},{7,3},{8,12},{10,14},{12... | collective-permute-start | bytes 98312 | tf_op jit(solution)/shard_map/ppermute | solution.py:751
  39.4 2.1 %scale.1.refs_4_ = f32[96,128]{1,0:T(8,128)S(1)} custom-call(s32[1,1536]{1,0:T(1,128)S(1)} %fusion.4.device_ref, s32[1,1536]{1,0:T(1,128)S(1)} %get-tuple-element.111.within_ref, s32[1]{0:T(128)} %get-tuple-element.62._, f32[320,128]{1,0:T(8,128)S(1)} %collective-permute-done.7.__.refs_2_, f32[32,128]{1,0:T(8,128)S(1)} %slice.17.refs_0_, ...), custom_call_target="tpu_custom_call" | custom-call | tf_op jit(solution)/shard_map/scale/pallas_call | solution.py:775
  43.4 5.3 %step.4 = (f32[8,128,128]{2,1,0:T(8,128)S(1)}, bf16[8,1024,256]{2,1,0:T(8,128)(2,1)S(1)}, f32[8,64,128]{2,1,0:T(8,128)S(1)}, f32[96,128]{1,0:T(8,128)S(1)}, f32[...) custom-call(f32[8,128,128]{2,1,0:T(8,128)S(1)} %local.4.local_ref, f32[96,128]{1,0:T(8,128)S(1)} %copy-done.5, ...), custom_call_target="tpu_custom_call" | custom-call | tf_op jit(solution)/shard_map/step/pallas_call | solution.py:848
  48.7 7.3 %collective-permute-start.13 = (f32[320,128]{1,0:T(8,128)S(1)}, f32[320,128]{1,0:T(8,128)S(1)}, u32[]{:S(2)}, u32[]{:S(2)}) collective-permute-start(f32[320,128]{1,0:T(8,128)S(1)} %get-tuple-element.73), channel_id=1, source_target_pairs={{0,2},{4,6},{2,0},{6,4},{1,3},{5,7},{3,1},{7,5},{8,10},{12,14},{10... | collective-permute-start | bytes 491528 | tf_op jit(solution)/shard_map/ppermute | solution.py:751
  56.7 2.8 %collective-permute-start.15 = (f32[32,128]{1,0:T(8,128)S(1)}, f32[32,128]{1,0:T(8,128)S(1)}, u32[]{:S(2)}, u32[]{:S(2)}) collective-permute-start(f32[32,128]{1,0:T(8,128)S(1)} %get-tuple-element.75), channel_id=1, source_target_pairs={{0,4},{2,6},{4,0},{6,2},{1,5},{3,7},{5,1},{7,3},{8,12},{10,14},{12... | collective-permute-start | bytes 49160 | tf_op jit(solution)/shard_map/ppermute | solution.py:751
  59.5 1.7 %local.5.local_ref = f32[8,128,128]{2,1,0:T(8,128)S(1)} custom-call(f32[8,128,128]{2,1,0:T(8,128)S(1)} %get-tuple-element.70.y_ref.refs_0_, f32[8,128,128]{2,1,0:T(8,128)S(1)} %get-tuple-element.56.y_ref.refs_5_.refs_0_, f32[8,64,128]{2,1,0:T(8,128)S(1)} %get-tuple-element.71.refs_1_), custom_call_target="tpu_custom_call" | custom-call | flops 7864320 | bytes 2097152 | tf_op jit(solution)/shard_map/local/pallas_call | solution.py:785
  61.2 2.1 %collective-permute-done.15.refs_3_ = f32[32,128]{1,0:T(8,128)S(1)} collective-permute-done((f32[32,128]{1,0:T(8,128)S(1)}, f32[32,128]{1,0:T(8,128)S(1)}, u32[]{:S(2)}, u32[]{:S(2)}) %collective-permute-start.15) | collective-permute-done | bytes 16416 | tf_op jit(solution)/shard_map/ppermute | solution.py:751
  63.3 3.6 %step.5 = (f32[8,128,128]{2,1,0:T(8,128)S(1)}, f32[96,128]{1,0:T(8,128)S(1)}, f32[320,128]{1,0:T(8,128)S(1)}, f32[320,128]{1,0:T(8,128)S(1)}, f32[32,128]{1,0:T(8,128)S(1)}) custom-call(f32[8,128,128]{2,1,0:T(8,128)S(1)} %local.5.local_ref, f32[96,128]{1,0:T(8,128)S(1)} %get-tuple-element.72.refs_0_, f32[320,128]{1,0:T(8,128)S(1)} %collective-permute-done.13.refs_1_, ...), custom_call_target="tpu_custom_call" | custom-call | tf_op jit(solution)/shard_map/step/pallas_call | solution.py:848
  68.8 3.7 %collective-permute-start.18 = (f32[32,128]{1,0:T(8,128)S(1)}, f32[32,128]{1,0:T(8,128)S(1)}, u32[]{:S(2)}, u32[]{:S(2)}) collective-permute-start(f32[32,128]{1,0:T(8,128)S(1)} %get-tuple-element.81), channel_id=1, source_target_pairs={{0,4},{2,6},{4,0},{6,2},{1,5},{3,7},{5,1},{7,3},{8,12},{10,14},{12... | collective-permute-start | bytes 49160 | tf_op jit(solution)/shard_map/ppermute | solution.py:751
  72.6 1.7 %local.6.local_ref = f32[8,128,128]{2,1,0:T(8,128)S(1)} custom-call(f32[8,128,128]{2,1,0:T(8,128)S(1)} %get-tuple-element.77.y_ref.refs_0_, f32[8,128,128]{2,1,0:T(8,128)S(1)} %get-tuple-element.70.y_ref.refs_0_, f32[8,64,128]{2,1,0:T(8,128)S(1)} %get-tuple-element.71.refs_1_), custom_call_target="tpu_custom_call" | custom-call | flops 7864320 | bytes 2097152 | tf_op jit(solution)/shard_map/local/pallas_call | solution.py:785
  75.8 3.6 %step.6 = (f32[8,128,128]{2,1,0:T(8,128)S(1)}, f32[96,128]{1,0:T(8,128)S(1)}, f32[320,128]{1,0:T(8,128)S(1)}, f32[320,128]{1,0:T(8,128)S(1)}, f32[32,128]{1,0:T(8,128)S(1)}) custom-call(f32[8,128,128]{2,1,0:T(8,128)S(1)} %local.6.local_ref, f32[96,128]{1,0:T(8,128)S(1)} %get-tuple-element.78.refs_0_, f32[320,128]{1,0:T(8,128)S(1)} %collective-permute-done.16.refs_1_, ...), custom_call_target="tpu_custom_call" | custom-call | tf_op jit(solution)/shard_map/step/pallas_call | solution.py:848
  79.4 1.8 %collective-permute-start.19 = (f32[320,128]{1,0:T(8,128)S(1)}, f32[320,128]{1,0:T(8,128)S(1)}, u32[]{:S(2)}, u32[]{:S(2)}) collective-permute-start(f32[320,128]{1,0:T(8,128)S(1)} %get-tuple-element.84), channel_id=1, source_target_pairs={{0,2},{4,6},{2,0},{6,4},{1,3},{5,7},{3,1},{7,5},{8,10},{12,14},{10... | collective-permute-start | bytes 491528 | tf_op jit(solution)/shard_map/ppermute | solution.py:751
  81.9 3.0 %collective-permute-start.21 = (f32[32,128]{1,0:T(8,128)S(1)}, f32[32,128]{1,0:T(8,128)S(1)}, u32[]{:S(2)}, u32[]{:S(2)}) collective-permute-start(f32[32,128]{1,0:T(8,128)S(1)} %get-tuple-element.86), channel_id=1, source_target_pairs={{0,4},{2,6},{4,0},{6,2},{1,5},{3,7},{5,1},{7,3},{8,12},{10,14},{12... | collective-permute-start | bytes 49160 | tf_op jit(solution)/shard_map/ppermute | solution.py:751
  84.9 1.7 %local.7 = f32[8,128,128]{2,1,0:T(8,128)S(1)} custom-call(f32[8,128,128]{2,1,0:T(8,128)S(1)} %get-tuple-element.82.y_ref, f32[8,128,128]{2,1,0:T(8,128)S(1)} %get-tuple-element.77.y_ref.refs_0_, f32[8,64,128]{2,1,0:T(8,128)S(1)} %get-tuple-element.71.refs_1_), custom_call_target="tpu_custom_call" | custom-call | flops 7864320 | bytes 2097152 | tf_op jit(solution)/shard_map/local/pallas_call | solution.py:785
  86.6 1.7 %collective-permute-done.21 = f32[32,128]{1,0:T(8,128)S(1)} collective-permute-done((f32[32,128]{1,0:T(8,128)S(1)}, f32[32,128]{1,0:T(8,128)S(1)}, u32[]{:S(2)}, u32[]{:S(2)}) %collective-permute-start.21) | collective-permute-done | bytes 16416 | tf_op jit(solution)/shard_map/ppermute | solution.py:751
  88.3 3.8 %step.7 = (f32[8,128,128]{2,1,0:T(8,128)S(1)}, f32[1,128,128]{2,1,0:T(8,128)S(1)}, f32[1,128,128]{2,1,0:T(8,128)S(1)}, f32[1,128,128]{2,1,0:T(8,128)S(1)}, f32[1...) fusion(f32[8,128,128]{2,1,0:T(8,128)S(1)} %broadcast_in_dim.3, ...), kind=kCustom, calls=%fused_computation.29 | custom fusion | bytes 6275076 | tf_op jit(solution)/shard_map/step/pallas_call | solution.py:848
  92.5 1.7 %collective-permute-start.23 = (f32[1,128,128]{2,1,0:T(8,128)S(1)}, f32[1,128,128]{2,1,0:T(8,128)S(1)}, u32[]{:S(2)}, u32[]{:S(2)}) collective-permute-start(f32[1,128,128]{2,1,0:T(8,128)S(1)} %get-tuple-element.100), channel_id=1, source_target_pairs={{0,16},{1,17},{8,24},{9,25},{16,0},{17,1},{24,8},{25,9},{2,18},{3,... | collective-permute-start | bytes 196616 | tf_op jit(solution)/shard_map/ppermute | solution.py:875
  (88 shorter events, 31.3 us)
Async XLA Ops:
  2.9 16.6 %collective-permute-start = (f32[1088,128]{1,0:T(8,128)}, f32[1088,128]{1,0:T(8,128)S(1)}, u32[]{:S(2)}, u32[]{:S(2)}) collective-permute-start(f32[1088,128]{1,0:T(8,128)} %pack.1.payload_ref.refs_6_), channel_id=1, source_target_pairs={{0,1},{1,0},{2,3},{3,2},{4,5},{5,4},{6,7},{7,6},{8,9},{9,8},{10,11... | collective-permute-start | bytes 1671176 | tf_op jit(solution)/shard_map/ppermute | solution.py:603
  5.9 15.4 %collective-permute-start.1 = (f32[1088,128]{1,0:T(8,128)}, f32[1088,128]{1,0:T(8,128)S(1)}, u32[]{:S(2)}, u32[]{:S(2)}) collective-permute-start(f32[1088,128]{1,0:T(8,128)} %pack.1.payload_ref.refs_6_), channel_id=1, source_target_pairs={{0,16},{8,24},{16,0},{24,8},{1,17},{9,25},{17,1},{25,9},{2,18},{10... | collective-permute-start | bytes 1671176 | tf_op jit(solution)/shard_map/ppermute | solution.py:603
  7.4 13.9 %collective-permute-start.2 = (f32[1088,128]{1,0:T(8,128)}, f32[1088,128]{1,0:T(8,128)S(1)}, u32[]{:S(2)}, u32[]{:S(2)}) collective-permute-start(f32[1088,128]{1,0:T(8,128)} %pack.1.payload_ref.refs_6_), channel_id=1, source_target_pairs={{0,8},{8,0},{16,24},{24,16},{1,9},{9,1},{17,25},{25,17},{2,10},{10... | collective-permute-start | bytes 1671176 | tf_op jit(solution)/shard_map/ppermute | solution.py:603
  12.3 15.6 %all-to-all-start = ((f32[8,152,128]{2,1,0:T(8,128)}), f32[8,152,128]{2,1,0:T(8,128)S(1)}, u32[]{:S(2)}, u32[]{:S(2)}) async-start(f32[8,152,128]{2,1,0:T(8,128)} %get-tuple-element.53), calls=%async_computation | async-start | bytes 1245184 | tf_op jit(solution)/shard_map/all_to_all | solution.py:695
  22.0 13.9 %collective-permute-start.3 = (f32[544,128]{1,0:T(8,128)}, f32[544,128]{1,0:T(8,128)S(1)}, u32[]{:S(2)}, u32[]{:S(2)}) collective-permute-start(f32[544,128]{1,0:T(8,128)} %slice.15), channel_id=1, source_target_pairs={{0,16},{8,24},{16,0},{24,8},{1,17},{9,25},{17,1},{25,9},{2,18},{10... | collective-permute-start | bytes 835592 | tf_op jit(solution)/shard_map/ppermute | solution.py:603
  24.6 11.3 %collective-permute-start.4 = (f32[544,128]{1,0:T(8,128)}, f32[544,128]{1,0:T(8,128)}, u32[]{:S(2)}, u32[]{:S(2)}) collective-permute-start(f32[544,128]{1,0:T(8,128)} %slice.16), channel_id=1, source_target_pairs={{0,1},{1,0},{2,3},{3,2},{4,5},{5,4},{6,7},{7,6},{8,9},{9,8},{10,11... | collective-permute-start | bytes 835592 | tf_op jit(solution)/shard_map/ppermute | solution.py:603
  29.3 4.9 %collective-permute-start.5 = (f32[64,128]{1,0:T(8,128)S(1)}, f32[64,128]{1,0:T(8,128)S(1)}, u32[]{:S(2)}, u32[]{:S(2)}) collective-permute-start(f32[64,128]{1,0:T(8,128)S(1)} %get-tuple-element.55), channel_id=1, source_target_pairs={{0,4},{2,6},{4,0},{6,2},{1,5},{3,7},{5,1},{7,3},{8,12},{10,14},{12... | collective-permute-start | bytes 98312 | tf_op jit(solution)/shard_map/ppermute | solution.py:751
  31.9 5.7 %collective-permute-start.8 = (f32[32,128]{1,0:T(8,128)S(1)}, f32[32,128]{1,0:T(8,128)S(1)}, u32[]{:S(2)}, u32[]{:S(2)}) collective-permute-start(f32[32,128]{1,0:T(8,128)S(1)} %slice.17.refs_0_), channel_id=1, source_target_pairs={{0,6},{2,4},{4,2},{6,0},{1,7},{3,5},{5,3},{7,1},{8,14},{10,12},{12... | collective-permute-start | bytes 49160 | tf_op jit(solution)/shard_map/ppermute | solution.py:773
  33.3 5.9 %collective-permute-start.6 = (f32[352,128]{1,0:T(8,128)}, f32[352,128]{1,0:T(8,128)S(1)}, u32[]{:S(2)}, u32[]{:S(2)}) collective-permute-start(f32[352,128]{1,0:T(8,128)} %get-tuple-element.59), channel_id=1, source_target_pairs={{0,2},{4,6},{2,0},{6,4},{1,3},{5,7},{3,1},{7,5},{8,10},{12,14},{10... | collective-permute-start | bytes 540680 | tf_op jit(solution)/shard_map/ppermute | solution.py:751
  35.9 5.6 %collective-permute-start.10 = (f32[1088,128]{1,0:T(8,128)S(1)}, f32[1088,128]{1,0:T(8,128)}, u32[]{:S(2)}, u32[]{:S(2)}) collective-permute-start(f32[1088,128]{1,0:T(8,128)S(1)} %collective-permute-done.1.refs_8_), channel_id=1, source_target_pairs={{0,8},{8,0},{16,24},{24,16},{1,9},{9,1},{17,25},{25,17},{2,10},{10... | collective-permute-start | bytes 1671176 | tf_op jit(solution)/shard_map/ppermute | solution.py:603
  36.0 5.6 %collective-permute-start.9 = (f32[1088,128]{1,0:T(8,128)S(1)}, f32[1088,128]{1,0:T(8,128)}, u32[]{:S(2)}, u32[]{:S(2)}) collective-permute-start(f32[1088,128]{1,0:T(8,128)S(1)} %collective-permute-done.refs_7_), channel_id=1, source_target_pairs={{0,8},{8,0},{16,24},{24,16},{1,9},{9,1},{17,25},{25,17},{2,10},{10... | collective-permute-start | bytes 1671176 | tf_op jit(solution)/shard_map/ppermute | solution.py:603
  48.7 14.5 %collective-permute-start.13 = (f32[320,128]{1,0:T(8,128)S(1)}, f32[320,128]{1,0:T(8,128)S(1)}, u32[]{:S(2)}, u32[]{:S(2)}) collective-permute-start(f32[320,128]{1,0:T(8,128)S(1)} %get-tuple-element.73), channel_id=1, source_target_pairs={{0,2},{4,6},{2,0},{6,4},{1,3},{5,7},{3,1},{7,5},{8,10},{12,14},{10... | collective-permute-start | bytes 491528 | tf_op jit(solution)/shard_map/ppermute | solution.py:751
  56.0 7.2 %collective-permute-start.14 = (f32[320,128]{1,0:T(8,128)S(1)}, f32[320,128]{1,0:T(8,128)S(1)}, u32[]{:S(2)}, u32[]{:S(2)}) collective-permute-start(f32[320,128]{1,0:T(8,128)S(1)} %get-tuple-element.74), channel_id=1, source_target_pairs={{2,4},{4,2},{3,5},{5,3},{10,12},{12,10},{11,13},{13,11},{18,20},{2... | collective-permute-start | bytes 491528 | tf_op jit(solution)/shard_map/ppermute | solution.py:751
  56.7 6.5 %collective-permute-start.15 = (f32[32,128]{1,0:T(8,128)S(1)}, f32[32,128]{1,0:T(8,128)S(1)}, u32[]{:S(2)}, u32[]{:S(2)}) collective-permute-start(f32[32,128]{1,0:T(8,128)S(1)} %get-tuple-element.75), channel_id=1, source_target_pairs={{0,4},{2,6},{4,0},{6,2},{1,5},{3,7},{5,1},{7,3},{8,12},{10,14},{12... | collective-permute-start | bytes 49160 | tf_op jit(solution)/shard_map/ppermute | solution.py:751
  66.8 8.9 %collective-permute-start.16 = (f32[320,128]{1,0:T(8,128)S(1)}, f32[320,128]{1,0:T(8,128)S(1)}, u32[]{:S(2)}, u32[]{:S(2)}) collective-permute-start(f32[320,128]{1,0:T(8,128)S(1)} %get-tuple-element.79), channel_id=1, source_target_pairs={{0,2},{4,6},{2,0},{6,4},{1,3},{5,7},{3,1},{7,5},{8,10},{12,14},{10... | collective-permute-start | bytes 491528 | tf_op jit(solution)/shard_map/ppermute | solution.py:751
  68.0 7.8 %collective-permute-start.17 = (f32[320,128]{1,0:T(8,128)S(1)}, f32[320,128]{1,0:T(8,128)S(1)}, u32[]{:S(2)}, u32[]{:S(2)}) collective-permute-start(f32[320,128]{1,0:T(8,128)S(1)} %get-tuple-element.80), channel_id=1, source_target_pairs={{2,4},{4,2},{3,5},{5,3},{10,12},{12,10},{11,13},{13,11},{18,20},{2... | collective-permute-start | bytes 491528 | tf_op jit(solution)/shard_map/ppermute | solution.py:751
  68.8 6.9 %collective-permute-start.18 = (f32[32,128]{1,0:T(8,128)S(1)}, f32[32,128]{1,0:T(8,128)S(1)}, u32[]{:S(2)}, u32[]{:S(2)}) collective-permute-start(f32[32,128]{1,0:T(8,128)S(1)} %get-tuple-element.81), channel_id=1, source_target_pairs={{0,4},{2,6},{4,0},{6,2},{1,5},{3,7},{5,1},{7,3},{8,12},{10,14},{12... | collective-permute-start | bytes 49160 | tf_op jit(solution)/shard_map/ppermute | solution.py:751
  79.4 8.9 %collective-permute-start.19 = (f32[320,128]{1,0:T(8,128)S(1)}, f32[320,128]{1,0:T(8,128)S(1)}, u32[]{:S(2)}, u32[]{:S(2)}) collective-permute-start(f32[320,128]{1,0:T(8,128)S(1)} %get-tuple-element.84), channel_id=1, source_target_pairs={{0,2},{4,6},{2,0},{6,4},{1,3},{5,7},{3,1},{7,5},{8,10},{12,14},{10... | collective-permute-start | bytes 491528 | tf_op jit(solution)/shard_map/ppermute | solution.py:751
  81.2 7.1 %collective-permute-start.20 = (f32[320,128]{1,0:T(8,128)S(1)}, f32[320,128]{1,0:T(8,128)S(1)}, u32[]{:S(2)}, u32[]{:S(2)}) collective-permute-start(f32[320,128]{1,0:T(8,128)S(1)} %get-tuple-element.85), channel_id=1, source_target_pairs={{2,4},{4,2},{3,5},{5,3},{10,12},{12,10},{11,13},{13,11},{18,20},{2... | collective-permute-start | bytes 491528 | tf_op jit(solution)/shard_map/ppermute | solution.py:751
  81.9 6.4 %collective-permute-start.21 = (f32[32,128]{1,0:T(8,128)S(1)}, f32[32,128]{1,0:T(8,128)S(1)}, u32[]{:S(2)}, u32[]{:S(2)}) collective-permute-start(f32[32,128]{1,0:T(8,128)S(1)} %get-tuple-element.86), channel_id=1, source_target_pairs={{0,4},{2,6},{4,0},{6,2},{1,5},{3,7},{5,1},{7,3},{8,12},{10,14},{12... | collective-permute-start | bytes 49160 | tf_op jit(solution)/shard_map/ppermute | solution.py:751
  92.5 5.2 %collective-permute-start.23 = (f32[1,128,128]{2,1,0:T(8,128)S(1)}, f32[1,128,128]{2,1,0:T(8,128)S(1)}, u32[]{:S(2)}, u32[]{:S(2)}) collective-permute-start(f32[1,128,128]{2,1,0:T(8,128)S(1)} %get-tuple-element.100), channel_id=1, source_target_pairs={{0,16},{1,17},{8,24},{9,25},{16,0},{17,1},{24,8},{25,9},{2,18},{3,... | collective-permute-start | bytes 196616 | tf_op jit(solution)/shard_map/ppermute | solution.py:875
  94.2 5.2 %collective-permute-start.24 = (f32[1,128,128]{2,1,0:T(8,128)S(1)}, f32[1,128,128]{2,1,0:T(8,128)S(1)}, u32[]{:S(2)}, u32[]{:S(2)}) collective-permute-start(f32[1,128,128]{2,1,0:T(8,128)S(1)} %get-tuple-element.102), channel_id=1, source_target_pairs={{0,17},{1,16},{8,25},{9,24},{16,1},{17,0},{24,9},{25,8},{2,19},{3,... | collective-permute-start | bytes 196616 | tf_op jit(solution)/shard_map/ppermute | solution.py:875
  95.7 5.0 %collective-permute-start.26 = (f32[1,128,128]{2,1,0:T(8,128)S(1)}, f32[1,128,128]{2,1,0:T(8,128)S(1)}, u32[]{:S(2)}, u32[]{:S(2)}) collective-permute-start(f32[1,128,128]{2,1,0:T(8,128)S(1)} %get-tuple-element.106), channel_id=1, source_target_pairs={{0,9},{1,8},{8,1},{9,0},{16,25},{17,24},{24,17},{25,16},{2,11},{3,... | collective-permute-start | bytes 196616 | tf_op jit(solution)/shard_map/ppermute | solution.py:875
  97.8 4.7 %collective-permute-start.28 = (f32[1,128,128]{2,1,0:T(8,128)S(1)}, f32[1,128,128]{2,1,0:T(8,128)S(1)}, u32[]{:S(2)}, u32[]{:S(2)}) collective-permute-start(f32[1,128,128]{2,1,0:T(8,128)S(1)} %get-tuple-element.110), channel_id=1, source_target_pairs={{0,25},{1,24},{8,17},{9,16},{16,9},{17,8},{24,1},{25,0},{2,27},{3,... | collective-permute-start | bytes 196616 | tf_op jit(solution)/shard_map/ppermute | solution.py:875
  (16 other events, 97.6 us)

commit v12 on v9

--- a/solution.py
+++ b/solution.py
@@ -255,7 +255,7 @@
     if first:
         out_ref, pad_ref = refs
     else:
-        previous_ref, potential_ref, out_ref, pad_ref = refs
+        previous_ref, potential_ref, out_ref, pad_ref = refs[-4:]
     on, cz, cy, cx, gx, gz = plan.on, plan.cz, plan.cy, plan.cx, plan.gx, plan.gz
     step = pl.program_id(0)
     me = lax.axis_index("gx") * plan.gz + lax.axis_index("gz")
@@ -445,7 +445,7 @@
         emit_sums(plan, total_ref[...], odd, upper, own_ref, even_ref, odd_ref, far_ref)
 
 
-def scale_kernel(plan, device_ref, within_ref, _, *refs):
+def scale_kernel(plan, device_ref, within_ref, *refs):
     table_refs, out_ref = refs[:-1], refs[-1]
     blocks, owned = plan.blocks, plan.owned
     tables = []
@@ -763,22 +763,22 @@
         first, last = repeat == 0, repeat == DEGREE - 1
         received = list(swap(sends))
         if first:
-            current, received[3] = lax.optimization_barrier((current, received[3]))
             own_table = sends[3][plan.third :]
+            pairs = [(i, i ^ 3) for i in range(gy)]
+            last_table = [lax.ppermute(own_table, "gy", pairs)] if gy > 2 else []
+            current, received[3], *last_table = lax.optimization_barrier(
+                (current, received[3], *last_table)
+            )
             across = [own_table] * (gy > 1) + [received[1][message_rows:]] * (gy > 1)
             across += [received[3][plan.third :]] * (gy > 2)
-            if gy > 2:
-                pairs = [(i, i ^ 3) for i in range(gy)]
-                across.append(lax.ppermute(own_table, "gy", pairs))
+            across += last_table
             across = across or [own_table]
             scale = pl.pallas_call(
                 functools.partial(scale_kernel, plan),
                 out_shape=jax.ShapeDtypeStruct((3 * plan.third, LANE), f32),
-                in_specs=[full(1, plan.keys), full(1, plan.keys), pl.BlockSpec(memory_space=pl.ANY)]
-                + [full(*table.shape) for table in across],
                 compiler_params=params,
                 name="scale",
-            )(home_device, home_within, late_info, *across)
+            )(home_device, home_within, *across)
         extra = table_rows if first else 0
         local = pl.pallas_call(
             functools.partial(local_kernel, plan, first),
@@ -787,6 +787,7 @@
                 num_scalar_prefetch=0,
                 grid=(blocks // per,),
                 in_specs=[full(blocks, y_rows, cx)]
+                + [pl.BlockSpec(memory_space=pl.ANY)] * (repeat == 1)
                 + ([] if first else [each(per, y_rows, cx), each(per, points, cx)]),
                 out_specs=each(per, y_rows, cx),
                 scratch_shapes=[
@@ -800,7 +801,7 @@
                 transcendentals=0,
             ),
             name="local",
-        )(current, *([] if first else [previous, plane_potential]))
+        )(current, *[late_info] * (repeat == 1), *([] if first else [previous, plane_potential]))
         if first:
             others = [from_z, from_x, *from_xz]
             *others, local = lax.optimization_barrier((*others, local))

time: 102 us -> 104 us (1.020)
  waiting for transfers between devices: 19.3 us -> 20.9 us
    ppermute x1, waiting for transfers between devices: 0.43 us -> 3.97 us  [turned_path(): last_table = [lax.ppermute(own_table, 'gy', pairs)] if gy > 2 else []]
    ppermute x12, waiting for transfers between devices: 7.48 us -> 5.23 us  [pairwise(): return lax.ppermute(value, 'gy', pairs + [(b, a) for a, b in pairs])]
where the time goes in v12:
time: 104 us; the launch traced here: 103 us
  starting transfers between devices  42.6 us (41%)
  Pallas kernels  28.1 us (27%)
  waiting for transfers between devices  20.9 us (20%)
  local copies, waits for them, and re-layouts  10.1 us (10%)
    ppermute x12, starting transfers between devices, pairwise(): return lax.ppermute(value, 'gy', pairs + [(b, a) for a, b in pairs])  23 us
    pallas_call x3, Pallas kernels, turned_path(): pl.pallas_call(functools.partial(step_kernel, plan, first, last, base), o...  12.5 us
    ppermute x9, starting transfers between devices, exchange(): return lax.ppermute(value, axis, [(i, i ^ bit) for i in range(count)])  7.96 us
    pallas_call x4, Pallas kernels, turned_path(): pl.pallas_call(functools.partial(local_kernel, plan, first), out_shape=y_...  7.29 us
    ppermute x7, starting transfers between devices, turned_path(): lax.ppermute(block, ('gx', 'gz'), [(i, i ^ moved) for i in range(blocks)])  6.74 us
    ppermute x9, waiting for transfers between devices, exchange(): return lax.ppermute(value, axis, [(i, i ^ bit) for i in range(count)])  5.66 us
    ppermute x12, waiting for transfers between devices, pairwise(): return lax.ppermute(value, 'gy', pairs + [(b, a) for a, b in pairs])  5.23 us
    unnamed x22, local copies, waits for them, and re-layouts  4.48 us
  transfers between devices with their start and end apart: 30, of which 14 were waited for; matrix products, arithmetic and copies ran while one was open for 2% of the time, Pallas kernels for 14%

profile of v12, /device:TPU:0, one launch (start us, length us, event | category | flops | bytes accessed | tf_op | source)
XLA Modules:
  0.0 102.8 jit_solution(14040243041913864287)
XLA Ops:
  2.9 3.0 %collective-permute-start = (f32[1088,128]{1,0:T(8,128)}, f32[1088,128]{1,0:T(8,128)S(1)}, u32[]{:S(2)}, u32[]{:S(2)}) collective-permute-start(f32[1088,128]{1,0:T(8,128)} %pack.1.payload_ref.refs_6_), channel_id=1, source_target_pairs={{0,1},{1,0},{2,3},{3,2},{4,5},{5,4},{6,7},{7,6},{8,9},{9,8},{10,11... | collective-permute-start | bytes 1671176 | tf_op jit(solution)/shard_map/ppermute | solution.py:603
  8.0 4.3 %own_tiles.1 = (f32[8,152,128]{2,1,0:T(8,128)}, s32[1]{0:T(128)}) custom-call(s32[1]{0:T(128)S(6)} %copy.19.info_ref, f32[1088,128]{1,0:T(8,128)} %pack.1.payload_ref.refs_6_, s32[1,256]{1,0:T(1,128)} %bitcast.17, s32[1,256]{1,0:T(1,128)} %bitcast.18, f32[4,64]{1,0:T(4,128)} %bitcast.16, f32[8,128,128]{2,1,0:T(8,128)} %bitcast.12), custom_call_target="tpu_custom_call" | custom-call | tf_op jit(solution)/shard_map/own_tiles/pallas_call | solution.py:667
  12.3 3.6 %all-to-all-start = ((f32[8,152,128]{2,1,0:T(8,128)}), f32[8,152,128]{2,1,0:T(8,128)S(1)}, u32[]{:S(2)}, u32[]{:S(2)}) async-start(f32[8,152,128]{2,1,0:T(8,128)} %get-tuple-element.54), calls=%async_computation | async-start | bytes 1245184 | tf_op jit(solution)/shard_map/all_to_all | solution.py:694
  15.9 3.6 %collective-permute-done.refs_7_ = f32[1088,128]{1,0:T(8,128)S(1)} collective-permute-done((f32[1088,128]{1,0:T(8,128)}, f32[1088,128]{1,0:T(8,128)S(1)}, u32[]{:S(2)}, u32[]{:S(2)}) %collective-permute-start) | collective-permute-done | bytes 557088 | tf_op jit(solution)/shard_map/ppermute | solution.py:603
  19.4 1.8 %collective-permute-done.1.refs_8_ = f32[1088,128]{1,0:T(8,128)S(1)} collective-permute-done((f32[1088,128]{1,0:T(8,128)}, f32[1088,128]{1,0:T(8,128)S(1)}, u32[]{:S(2)}, u32[]{:S(2)}) %collective-permute-start.1) | collective-permute-done | bytes 557088 | tf_op jit(solution)/shard_map/ppermute | solution.py:603
  22.0 1.9 %collective-permute-start.3 = (f32[544,128]{1,0:T(8,128)}, f32[544,128]{1,0:T(8,128)S(1)}, u32[]{:S(2)}, u32[]{:S(2)}) collective-permute-start(f32[544,128]{1,0:T(8,128)} %slice.15), channel_id=1, source_target_pairs={{0,16},{8,24},{16,0},{24,8},{1,17},{9,25},{17,1},{25,9},{2,18},{10... | collective-permute-start | bytes 835592 | tf_op jit(solution)/shard_map/ppermute | solution.py:603
  25.3 2.6 %all-to-all-done.in_ref = f32[8,152,128]{2,1,0:T(8,128)S(1)} async-done(((f32[8,152,128]{2,1,0:T(8,128)}), f32[8,152,128]{2,1,0:T(8,128)S(1)}, u32[]{:S(2)}, u32[]{:S(2)}) %all-to-all-start) | async-done | bytes 622624 | tf_op jit(solution)/shard_map/all_to_all | solution.py:694
  29.3 2.6 %collective-permute-start.5 = (f32[64,128]{1,0:T(8,128)S(1)}, f32[64,128]{1,0:T(8,128)S(1)}, u32[]{:S(2)}, u32[]{:S(2)}) collective-permute-start(f32[64,128]{1,0:T(8,128)S(1)} %get-tuple-element.56), channel_id=1, source_target_pairs={{0,4},{2,6},{4,0},{6,2},{1,5},{3,7},{5,1},{7,3},{8,12},{10,14},{12... | collective-permute-start | bytes 98312 | tf_op jit(solution)/shard_map/ppermute | solution.py:750
  33.6 4.0 %collective-permute-done.6.refs_3_ = f32[32,128]{1,0:T(8,128)S(1)} collective-permute-done((f32[32,128]{1,0:T(8,128)S(1)}, f32[32,128]{1,0:T(8,128)S(1)}, u32[]{:S(2)}, u32[]{:S(2)}) %collective-permute-start.6) | collective-permute-done | bytes 16416 | tf_op jit(solution)/shard_map/ppermute | solution.py:768
  37.5 1.7 %local.4.local_ref = f32[8,128,128]{2,1,0:T(8,128)S(1)} custom-call(f32[8,128,128]{2,1,0:T(8,128)S(1)} %get-tuple-element.57.y_ref.refs_5_.refs_1_), custom_call_target="tpu_custom_call" | custom-call | flops 7864320 | bytes 2097152 | tf_op jit(solution)/shard_map/local/pallas_call | solution.py:783
  44.9 5.3 %step.4 = (f32[8,128,128]{2,1,0:T(8,128)S(1)}, bf16[8,1024,256]{2,1,0:T(8,128)(2,1)S(1)}, f32[8,64,128]{2,1,0:T(8,128)S(1)}, f32[96,128]{1,0:T(8,128)S(1)}, f32[...) custom-call(f32[8,128,128]{2,1,0:T(8,128)S(1)} %local.4.local_ref, f32[96,128]{1,0:T(8,128)S(1)} %copy-done.5, ...), custom_call_target="tpu_custom_call" | custom-call | tf_op jit(solution)/shard_map/step/pallas_call | solution.py:847
  50.3 4.8 %collective-permute-start.13 = (f32[320,128]{1,0:T(8,128)S(1)}, f32[320,128]{1,0:T(8,128)S(1)}, u32[]{:S(2)}, u32[]{:S(2)}) collective-permute-start(f32[320,128]{1,0:T(8,128)S(1)} %get-tuple-element.75), channel_id=1, source_target_pairs={{0,2},{4,6},{2,0},{6,4},{1,3},{5,7},{3,1},{7,5},{8,10},{12,14},{10... | collective-permute-start | bytes 491528 | tf_op jit(solution)/shard_map/ppermute | solution.py:750
  55.7 2.8 %collective-permute-start.15 = (f32[32,128]{1,0:T(8,128)S(1)}, f32[32,128]{1,0:T(8,128)S(1)}, u32[]{:S(2)}, u32[]{:S(2)}) collective-permute-start(f32[32,128]{1,0:T(8,128)S(1)} %get-tuple-element.77), channel_id=1, source_target_pairs={{0,4},{2,6},{4,0},{6,2},{1,5},{3,7},{5,1},{7,3},{8,12},{10,14},{12... | collective-permute-start | bytes 49160 | tf_op jit(solution)/shard_map/ppermute | solution.py:750
  58.5 2.3 %local.5.local_ref = f32[8,128,128]{2,1,0:T(8,128)S(1)} custom-call(f32[8,128,128]{2,1,0:T(8,128)S(1)} %get-tuple-element.71.y_ref.refs_0_, s32[1]{0:T(128)} %get-tuple-element.72.refs_0_, f32[8,128,128]{2,1,0:T(8,128)S(1)} %get-tuple-element.57.y_ref.refs_5_.refs_1_, f32[8,64,128]{2,1,0:T(8,128)S(1)} %get-tuple-element.73.refs_2_.refs_1_), custom_call_target="tpu_custom_call" | custom-call | flops 7864320 | bytes 2097152 | tf_op jit(solution)/shard_map/local/pallas_call | solution.py:783
  62.5 3.6 %step.5 = (f32[8,128,128]{2,1,0:T(8,128)S(1)}, f32[96,128]{1,0:T(8,128)S(1)}, f32[320,128]{1,0:T(8,128)S(1)}, f32[320,128]{1,0:T(8,128)S(1)}, f32[32,128]{1,0:T(8,128)S(1)}) custom-call(f32[8,128,128]{2,1,0:T(8,128)S(1)} %local.5.local_ref, f32[96,128]{1,0:T(8,128)S(1)} %get-tuple-element.74.refs_0_, f32[320,128]{1,0:T(8,128)S(1)} %collective-permute-done.13.refs_1_, ...), custom_call_target="tpu_custom_call" | custom-call | tf_op jit(solution)/shard_map/step/pallas_call | solution.py:847
  67.4 4.4 %collective-permute-start.18 = (f32[32,128]{1,0:T(8,128)S(1)}, f32[32,128]{1,0:T(8,128)S(1)}, u32[]{:S(2)}, u32[]{:S(2)}) collective-permute-start(f32[32,128]{1,0:T(8,128)S(1)} %get-tuple-element.83), channel_id=1, source_target_pairs={{0,4},{2,6},{4,0},{6,2},{1,5},{3,7},{5,1},{7,3},{8,12},{10,14},{12... | collective-permute-start | bytes 49160 | tf_op jit(solution)/shard_map/ppermute | solution.py:750
  71.8 1.7 %local.6.local_ref = f32[8,128,128]{2,1,0:T(8,128)S(1)} custom-call(f32[8,128,128]{2,1,0:T(8,128)S(1)} %get-tuple-element.79.y_ref.refs_0_, f32[8,128,128]{2,1,0:T(8,128)S(1)} %get-tuple-element.71.y_ref.refs_0_, f32[8,64,128]{2,1,0:T(8,128)S(1)} %get-tuple-element.73.refs_2_.refs_1_), custom_call_target="tpu_custom_call" | custom-call | flops 7864320 | bytes 2097152 | tf_op jit(solution)/shard_map/local/pallas_call | solution.py:783
  73.4 1.7 %collective-permute-done.18.refs_3_ = f32[32,128]{1,0:T(8,128)S(1)} collective-permute-done((f32[32,128]{1,0:T(8,128)S(1)}, f32[32,128]{1,0:T(8,128)S(1)}, u32[]{:S(2)}, u32[]{:S(2)}) %collective-permute-start.18) | collective-permute-done | bytes 16416 | tf_op jit(solution)/shard_map/ppermute | solution.py:750
  75.2 3.6 %step.6 = (f32[8,128,128]{2,1,0:T(8,128)S(1)}, f32[96,128]{1,0:T(8,128)S(1)}, f32[320,128]{1,0:T(8,128)S(1)}, f32[320,128]{1,0:T(8,128)S(1)}, f32[32,128]{1,0:T(8,128)S(1)}) custom-call(f32[8,128,128]{2,1,0:T(8,128)S(1)} %local.6.local_ref, f32[96,128]{1,0:T(8,128)S(1)} %get-tuple-element.80.refs_0_, f32[320,128]{1,0:T(8,128)S(1)} %collective-permute-done.16.refs_1_, ...), custom_call_target="tpu_custom_call" | custom-call | tf_op jit(solution)/shard_map/step/pallas_call | solution.py:847
  79.9 4.4 %collective-permute-start.21 = (f32[32,128]{1,0:T(8,128)S(1)}, f32[32,128]{1,0:T(8,128)S(1)}, u32[]{:S(2)}, u32[]{:S(2)}) collective-permute-start(f32[32,128]{1,0:T(8,128)S(1)} %get-tuple-element.88), channel_id=1, source_target_pairs={{0,4},{2,6},{4,0},{6,2},{1,5},{3,7},{5,1},{7,3},{8,12},{10,14},{12... | collective-permute-start | bytes 49160 | tf_op jit(solution)/shard_map/ppermute | solution.py:750
  84.3 1.7 %local.7 = f32[8,128,128]{2,1,0:T(8,128)S(1)} custom-call(f32[8,128,128]{2,1,0:T(8,128)S(1)} %get-tuple-element.84.y_ref, f32[8,128,128]{2,1,0:T(8,128)S(1)} %get-tuple-element.79.y_ref.refs_0_, f32[8,64,128]{2,1,0:T(8,128)S(1)} %get-tuple-element.73.refs_2_.refs_1_), custom_call_target="tpu_custom_call" | custom-call | flops 7864320 | bytes 2097152 | tf_op jit(solution)/shard_map/local/pallas_call | solution.py:783
  86.0 1.9 %collective-permute-done.21 = f32[32,128]{1,0:T(8,128)S(1)} collective-permute-done((f32[32,128]{1,0:T(8,128)S(1)}, f32[32,128]{1,0:T(8,128)S(1)}, u32[]{:S(2)}, u32[]{:S(2)}) %collective-permute-start.21) | collective-permute-done | bytes 16416 | tf_op jit(solution)/shard_map/ppermute | solution.py:750
  87.9 3.8 %step.7 = (f32[8,128,128]{2,1,0:T(8,128)S(1)}, f32[1,128,128]{2,1,0:T(8,128)S(1)}, f32[1,128,128]{2,1,0:T(8,128)S(1)}, f32[1,128,128]{2,1,0:T(8,128)S(1)}, f32[1...) fusion(f32[8,128,128]{2,1,0:T(8,128)S(1)} %broadcast_in_dim.3, ...), kind=kCustom, calls=%fused_computation.29 | custom fusion | bytes 6275076 | tf_op jit(solution)/shard_map/step/pallas_call | solution.py:847
  92.0 1.8 %collective-permute-start.23 = (f32[1,128,128]{2,1,0:T(8,128)S(1)}, f32[1,128,128]{2,1,0:T(8,128)S(1)}, u32[]{:S(2)}, u32[]{:S(2)}) collective-permute-start(f32[1,128,128]{2,1,0:T(8,128)S(1)} %get-tuple-element.102), channel_id=1, source_target_pairs={{0,16},{1,17},{8,24},{9,25},{16,0},{17,1},{24,8},{25,9},{2,18},{3,... | collective-permute-start | bytes 196616 | tf_op jit(solution)/shard_map/ppermute | solution.py:874
  (88 shorter events, 29.2 us)
Async XLA Ops:
  2.9 16.6 %collective-permute-start = (f32[1088,128]{1,0:T(8,128)}, f32[1088,128]{1,0:T(8,128)S(1)}, u32[]{:S(2)}, u32[]{:S(2)}) collective-permute-start(f32[1088,128]{1,0:T(8,128)} %pack.1.payload_ref.refs_6_), channel_id=1, source_target_pairs={{0,1},{1,0},{2,3},{3,2},{4,5},{5,4},{6,7},{7,6},{8,9},{9,8},{10,11... | collective-permute-start | bytes 1671176 | tf_op jit(solution)/shard_map/ppermute | solution.py:603
  5.9 15.4 %collective-permute-start.1 = (f32[1088,128]{1,0:T(8,128)}, f32[1088,128]{1,0:T(8,128)S(1)}, u32[]{:S(2)}, u32[]{:S(2)}) collective-permute-start(f32[1088,128]{1,0:T(8,128)} %pack.1.payload_ref.refs_6_), channel_id=1, source_target_pairs={{0,16},{8,24},{16,0},{24,8},{1,17},{9,25},{17,1},{25,9},{2,18},{10... | collective-permute-start | bytes 1671176 | tf_op jit(solution)/shard_map/ppermute | solution.py:603
  7.4 13.9 %collective-permute-start.2 = (f32[1088,128]{1,0:T(8,128)}, f32[1088,128]{1,0:T(8,128)S(1)}, u32[]{:S(2)}, u32[]{:S(2)}) collective-permute-start(f32[1088,128]{1,0:T(8,128)} %pack.1.payload_ref.refs_6_), channel_id=1, source_target_pairs={{0,8},{8,0},{16,24},{24,16},{1,9},{9,1},{17,25},{25,17},{2,10},{10... | collective-permute-start | bytes 1671176 | tf_op jit(solution)/shard_map/ppermute | solution.py:603
  12.3 15.6 %all-to-all-start = ((f32[8,152,128]{2,1,0:T(8,128)}), f32[8,152,128]{2,1,0:T(8,128)S(1)}, u32[]{:S(2)}, u32[]{:S(2)}) async-start(f32[8,152,128]{2,1,0:T(8,128)} %get-tuple-element.54), calls=%async_computation | async-start | bytes 1245184 | tf_op jit(solution)/shard_map/all_to_all | solution.py:694
  22.0 17.2 %collective-permute-start.3 = (f32[544,128]{1,0:T(8,128)}, f32[544,128]{1,0:T(8,128)S(1)}, u32[]{:S(2)}, u32[]{:S(2)}) collective-permute-start(f32[544,128]{1,0:T(8,128)} %slice.15), channel_id=1, source_target_pairs={{0,16},{8,24},{16,0},{24,8},{1,17},{9,25},{17,1},{25,9},{2,18},{10... | collective-permute-start | bytes 835592 | tf_op jit(solution)/shard_map/ppermute | solution.py:603
  24.6 14.6 %collective-permute-start.4 = (f32[544,128]{1,0:T(8,128)}, f32[544,128]{1,0:T(8,128)}, u32[]{:S(2)}, u32[]{:S(2)}) collective-permute-start(f32[544,128]{1,0:T(8,128)} %slice.16), channel_id=1, source_target_pairs={{0,1},{1,0},{2,3},{3,2},{4,5},{5,4},{6,7},{7,6},{8,9},{9,8},{10,11... | collective-permute-start | bytes 835592 | tf_op jit(solution)/shard_map/ppermute | solution.py:603
  29.3 8.2 %collective-permute-start.5 = (f32[64,128]{1,0:T(8,128)S(1)}, f32[64,128]{1,0:T(8,128)S(1)}, u32[]{:S(2)}, u32[]{:S(2)}) collective-permute-start(f32[64,128]{1,0:T(8,128)S(1)} %get-tuple-element.56), channel_id=1, source_target_pairs={{0,4},{2,6},{4,0},{6,2},{1,5},{3,7},{5,1},{7,3},{8,12},{10,14},{12... | collective-permute-start | bytes 98312 | tf_op jit(solution)/shard_map/ppermute | solution.py:750
  31.9 5.6 %collective-permute-start.6 = (f32[32,128]{1,0:T(8,128)S(1)}, f32[32,128]{1,0:T(8,128)S(1)}, u32[]{:S(2)}, u32[]{:S(2)}) collective-permute-start(f32[32,128]{1,0:T(8,128)S(1)} %slice.17.refs_0_), channel_id=1, source_target_pairs={{0,6},{2,4},{4,2},{6,0},{1,7},{3,5},{5,3},{7,1},{8,14},{10,12},{12... | collective-permute-start | bytes 49160 | tf_op jit(solution)/shard_map/ppermute | solution.py:768
  33.3 7.4 %collective-permute-start.7 = (f32[352,128]{1,0:T(8,128)}, f32[352,128]{1,0:T(8,128)S(1)}, u32[]{:S(2)}, u32[]{:S(2)}) collective-permute-start(f32[352,128]{1,0:T(8,128)} %get-tuple-element.60), channel_id=1, source_target_pairs={{0,2},{4,6},{2,0},{6,4},{1,3},{5,7},{3,1},{7,5},{8,10},{12,14},{10... | collective-permute-start | bytes 540680 | tf_op jit(solution)/shard_map/ppermute | solution.py:750
  50.3 12.2 %collective-permute-start.13 = (f32[320,128]{1,0:T(8,128)S(1)}, f32[320,128]{1,0:T(8,128)S(1)}, u32[]{:S(2)}, u32[]{:S(2)}) collective-permute-start(f32[320,128]{1,0:T(8,128)S(1)} %get-tuple-element.75), channel_id=1, source_target_pairs={{0,2},{4,6},{2,0},{6,4},{1,3},{5,7},{3,1},{7,5},{8,10},{12,14},{10... | collective-permute-start | bytes 491528 | tf_op jit(solution)/shard_map/ppermute | solution.py:750
  55.1 7.4 %collective-permute-start.14 = (f32[320,128]{1,0:T(8,128)S(1)}, f32[320,128]{1,0:T(8,128)S(1)}, u32[]{:S(2)}, u32[]{:S(2)}) collective-permute-start(f32[320,128]{1,0:T(8,128)S(1)} %get-tuple-element.76), channel_id=1, source_target_pairs={{2,4},{4,2},{3,5},{5,3},{10,12},{12,10},{11,13},{13,11},{18,20},{2... | collective-permute-start | bytes 491528 | tf_op jit(solution)/shard_map/ppermute | solution.py:750
  55.7 6.7 %collective-permute-start.15 = (f32[32,128]{1,0:T(8,128)S(1)}, f32[32,128]{1,0:T(8,128)S(1)}, u32[]{:S(2)}, u32[]{:S(2)}) collective-permute-start(f32[32,128]{1,0:T(8,128)S(1)} %get-tuple-element.77), channel_id=1, source_target_pairs={{0,4},{2,6},{4,0},{6,2},{1,5},{3,7},{5,1},{7,3},{8,12},{10,14},{12... | collective-permute-start | bytes 49160 | tf_op jit(solution)/shard_map/ppermute | solution.py:750
  66.1 9.1 %collective-permute-start.16 = (f32[320,128]{1,0:T(8,128)S(1)}, f32[320,128]{1,0:T(8,128)S(1)}, u32[]{:S(2)}, u32[]{:S(2)}) collective-permute-start(f32[320,128]{1,0:T(8,128)S(1)} %get-tuple-element.81), channel_id=1, source_target_pairs={{0,2},{4,6},{2,0},{6,4},{1,3},{5,7},{3,1},{7,5},{8,10},{12,14},{10... | collective-permute-start | bytes 491528 | tf_op jit(solution)/shard_map/ppermute | solution.py:750
  66.5 8.6 %collective-permute-start.17 = (f32[320,128]{1,0:T(8,128)S(1)}, f32[320,128]{1,0:T(8,128)S(1)}, u32[]{:S(2)}, u32[]{:S(2)}) collective-permute-start(f32[320,128]{1,0:T(8,128)S(1)} %get-tuple-element.82), channel_id=1, source_target_pairs={{2,4},{4,2},{3,5},{5,3},{10,12},{12,10},{11,13},{13,11},{18,20},{2... | collective-permute-start | bytes 491528 | tf_op jit(solution)/shard_map/ppermute | solution.py:750
  67.4 7.8 %collective-permute-start.18 = (f32[32,128]{1,0:T(8,128)S(1)}, f32[32,128]{1,0:T(8,128)S(1)}, u32[]{:S(2)}, u32[]{:S(2)}) collective-permute-start(f32[32,128]{1,0:T(8,128)S(1)} %get-tuple-element.83), channel_id=1, source_target_pairs={{0,4},{2,6},{4,0},{6,2},{1,5},{3,7},{5,1},{7,3},{8,12},{10,14},{12... | collective-permute-start | bytes 49160 | tf_op jit(solution)/shard_map/ppermute | solution.py:750
  78.8 9.1 %collective-permute-start.19 = (f32[320,128]{1,0:T(8,128)S(1)}, f32[320,128]{1,0:T(8,128)S(1)}, u32[]{:S(2)}, u32[]{:S(2)}) collective-permute-start(f32[320,128]{1,0:T(8,128)S(1)} %get-tuple-element.86), channel_id=1, source_target_pairs={{0,2},{4,6},{2,0},{6,4},{1,3},{5,7},{3,1},{7,5},{8,10},{12,14},{10... | collective-permute-start | bytes 491528 | tf_op jit(solution)/shard_map/ppermute | solution.py:750
  79.3 8.6 %collective-permute-start.20 = (f32[320,128]{1,0:T(8,128)S(1)}, f32[320,128]{1,0:T(8,128)S(1)}, u32[]{:S(2)}, u32[]{:S(2)}) collective-permute-start(f32[320,128]{1,0:T(8,128)S(1)} %get-tuple-element.87), channel_id=1, source_target_pairs={{2,4},{4,2},{3,5},{5,3},{10,12},{12,10},{11,13},{13,11},{18,20},{2... | collective-permute-start | bytes 491528 | tf_op jit(solution)/shard_map/ppermute | solution.py:750
  79.9 7.9 %collective-permute-start.21 = (f32[32,128]{1,0:T(8,128)S(1)}, f32[32,128]{1,0:T(8,128)S(1)}, u32[]{:S(2)}, u32[]{:S(2)}) collective-permute-start(f32[32,128]{1,0:T(8,128)S(1)} %get-tuple-element.88), channel_id=1, source_target_pairs={{0,4},{2,6},{4,0},{6,2},{1,5},{3,7},{5,1},{7,3},{8,12},{10,14},{12... | collective-permute-start | bytes 49160 | tf_op jit(solution)/shard_map/ppermute | solution.py:750
  91.7 4.3 %collective-permute-start.22 = (f32[1,128,128]{2,1,0:T(8,128)S(1)}, f32[1,128,128]{2,1,0:T(8,128)S(1)}, u32[]{:S(2)}, u32[]{:S(2)}) collective-permute-start(f32[1,128,128]{2,1,0:T(8,128)S(1)} %get-tuple-element.100), channel_id=1, source_target_pairs={{0,1},{1,0},{8,9},{9,8},{16,17},{17,16},{24,25},{25,24},{2,3},{3,2... | collective-permute-start | bytes 196616 | tf_op jit(solution)/shard_map/ppermute | solution.py:874
  92.0 5.3 %collective-permute-start.23 = (f32[1,128,128]{2,1,0:T(8,128)S(1)}, f32[1,128,128]{2,1,0:T(8,128)S(1)}, u32[]{:S(2)}, u32[]{:S(2)}) collective-permute-start(f32[1,128,128]{2,1,0:T(8,128)S(1)} %get-tuple-element.102), channel_id=1, source_target_pairs={{0,16},{1,17},{8,24},{9,25},{16,0},{17,1},{24,8},{25,9},{2,18},{3,... | collective-permute-start | bytes 196616 | tf_op jit(solution)/shard_map/ppermute | solution.py:874
  93.8 5.3 %collective-permute-start.24 = (f32[1,128,128]{2,1,0:T(8,128)S(1)}, f32[1,128,128]{2,1,0:T(8,128)S(1)}, u32[]{:S(2)}, u32[]{:S(2)}) collective-permute-start(f32[1,128,128]{2,1,0:T(8,128)S(1)} %get-tuple-element.104), channel_id=1, source_target_pairs={{0,17},{1,16},{8,25},{9,24},{16,1},{17,0},{24,9},{25,8},{2,19},{3,... | collective-permute-start | bytes 196616 | tf_op jit(solution)/shard_map/ppermute | solution.py:874
  95.3 5.0 %collective-permute-start.26 = (f32[1,128,128]{2,1,0:T(8,128)S(1)}, f32[1,128,128]{2,1,0:T(8,128)S(1)}, u32[]{:S(2)}, u32[]{:S(2)}) collective-permute-start(f32[1,128,128]{2,1,0:T(8,128)S(1)} %get-tuple-element.108), channel_id=1, source_target_pairs={{0,9},{1,8},{8,1},{9,0},{16,25},{17,24},{24,17},{25,16},{2,11},{3,... | collective-permute-start | bytes 196616 | tf_op jit(solution)/shard_map/ppermute | solution.py:874
  96.1 4.4 %collective-permute-start.27 = (f32[1,128,128]{2,1,0:T(8,128)S(1)}, f32[1,128,128]{2,1,0:T(8,128)S(1)}, u32[]{:S(2)}, u32[]{:S(2)}) collective-permute-start(f32[1,128,128]{2,1,0:T(8,128)S(1)} %get-tuple-element.110), channel_id=1, source_target_pairs={{0,24},{1,25},{8,16},{9,17},{16,8},{17,9},{24,0},{25,1},{2,26},{3,... | collective-permute-start | bytes 196616 | tf_op jit(solution)/shard_map/ppermute | solution.py:874
  97.4 4.7 %collective-permute-start.28 = (f32[1,128,128]{2,1,0:T(8,128)S(1)}, f32[1,128,128]{2,1,0:T(8,128)S(1)}, u32[]{:S(2)}, u32[]{:S(2)}) collective-permute-start(f32[1,128,128]{2,1,0:T(8,128)S(1)} %get-tuple-element.112), channel_id=1, source_target_pairs={{0,25},{1,24},{8,17},{9,16},{16,9},{17,8},{24,1},{25,0},{2,27},{3,... | collective-permute-start | bytes 196616 | tf_op jit(solution)/shard_map/ppermute | solution.py:874
  (16 other events, 98.2 us)

commit v13 on v12

--- a/solution.py
+++ b/solution.py
@@ -763,15 +763,13 @@
         first, last = repeat == 0, repeat == DEGREE - 1
         received = list(swap(sends))
         if first:
+            current, received[3] = lax.optimization_barrier((current, received[3]))
             own_table = sends[3][plan.third :]
-            pairs = [(i, i ^ 3) for i in range(gy)]
-            last_table = [lax.ppermute(own_table, "gy", pairs)] if gy > 2 else []
-            current, received[3], *last_table = lax.optimization_barrier(
-                (current, received[3], *last_table)
-            )
             across = [own_table] * (gy > 1) + [received[1][message_rows:]] * (gy > 1)
             across += [received[3][plan.third :]] * (gy > 2)
-            across += last_table
+            if gy > 2:
+                pairs = [(i, i ^ 3) for i in range(gy)]
+                across.append(lax.ppermute(own_table, "gy", pairs))
             across = across or [own_table]
             scale = pl.pallas_call(
                 functools.partial(scale_kernel, plan),

time: 104 us -> 102 us (0.981)
  waiting for transfers between devices: 20.9 us -> 18.8 us
    ppermute x1, waiting for transfers between devices: 3.97 us -> 0.43 us  [turned_path(): across.append(lax.ppermute(own_table, 'gy', pairs))]
    ppermute x12, waiting for transfers between devices: 5.23 us -> 6.85 us  [pairwise(): return lax.ppermute(value, 'gy', pairs + [(b, a) for a, b in pairs])]
  transfers between devices with their start and end apart: 30 -> 30, of which waited for: 14 -> 15; matrix products, arithmetic and copies ran while one was open for 2% -> 2% of each run, Pallas kernels for 14% -> 14%
where the time goes in v13:
time: 102 us; the launch traced here: 101 us
  starting transfers between devices  43 us (42%)
  Pallas kernels  28.1 us (28%)
  waiting for transfers between devices  18.8 us (18%)
  local copies, waits for them, and re-layouts  10.1 us (10%)
    ppermute x12, starting transfers between devices, pairwise(): return lax.ppermute(value, 'gy', pairs + [(b, a) for a, b in pairs])  23.9 us
    pallas_call x3, Pallas kernels, turned_path(): pl.pallas_call(functools.partial(step_kernel, plan, first, last, base), o...  12.5 us
    ppermute x9, starting transfers between devices, exchange(): return lax.ppermute(value, axis, [(i, i ^ bit) for i in range(count)])  7.39 us
    pallas_call x4, Pallas kernels, turned_path(): pl.pallas_call(functools.partial(local_kernel, plan, first), out_shape=y_...  7.29 us
    ppermute x12, waiting for transfers between devices, pairwise(): return lax.ppermute(value, 'gy', pairs + [(b, a) for a, b in pairs])  6.85 us
    ppermute x7, starting transfers between devices, turned_path(): lax.ppermute(block, ('gx', 'gz'), [(i, i ^ moved) for i in range(blocks)])  6.72 us
    ppermute x9, waiting for transfers between devices, exchange(): return lax.ppermute(value, axis, [(i, i ^ bit) for i in range(count)])  5.46 us
    unnamed x22, local copies, waits for them, and re-layouts  4.48 us
  transfers between devices with their start and end apart: 30, of which 15 were waited for; matrix products, arithmetic and copies ran while one was open for 2% of the time, Pallas kernels for 14%

profile of v13, /device:TPU:0, one launch (start us, length us, event | category | flops | bytes accessed | tf_op | source)
XLA Modules:
  0.0 101.1 jit_solution(11405747409113576139)
XLA Ops:
  2.9 3.0 %collective-permute-start = (f32[1088,128]{1,0:T(8,128)}, f32[1088,128]{1,0:T(8,128)S(1)}, u32[]{:S(2)}, u32[]{:S(2)}) collective-permute-start(f32[1088,128]{1,0:T(8,128)} %pack.1.payload_ref.refs_6_), channel_id=1, source_target_pairs={{0,1},{1,0},{2,3},{3,2},{4,5},{5,4},{6,7},{7,6},{8,9},{9,8},{10,11... | collective-permute-start | bytes 1671176 | tf_op jit(solution)/shard_map/ppermute | solution.py:603
  8.0 4.3 %own_tiles.1 = (f32[8,152,128]{2,1,0:T(8,128)}, s32[1]{0:T(128)}) custom-call(s32[1]{0:T(128)S(6)} %copy.19.info_ref, f32[1088,128]{1,0:T(8,128)} %pack.1.payload_ref.refs_6_, s32[1,256]{1,0:T(1,128)} %bitcast.17, s32[1,256]{1,0:T(1,128)} %bitcast.18, f32[4,64]{1,0:T(4,128)} %bitcast.16, f32[8,128,128]{2,1,0:T(8,128)} %bitcast.12), custom_call_target="tpu_custom_call" | custom-call | tf_op jit(solution)/shard_map/own_tiles/pallas_call | solution.py:667
  12.3 3.6 %all-to-all-start = ((f32[8,152,128]{2,1,0:T(8,128)}), f32[8,152,128]{2,1,0:T(8,128)S(1)}, u32[]{:S(2)}, u32[]{:S(2)}) async-start(f32[8,152,128]{2,1,0:T(8,128)} %get-tuple-element.53), calls=%async_computation | async-start | bytes 1245184 | tf_op jit(solution)/shard_map/all_to_all | solution.py:694
  15.9 3.6 %collective-permute-done.refs_7_ = f32[1088,128]{1,0:T(8,128)S(1)} collective-permute-done((f32[1088,128]{1,0:T(8,128)}, f32[1088,128]{1,0:T(8,128)S(1)}, u32[]{:S(2)}, u32[]{:S(2)}) %collective-permute-start) | collective-permute-done | bytes 557088 | tf_op jit(solution)/shard_map/ppermute | solution.py:603
  19.4 1.8 %collective-permute-done.1.refs_8_ = f32[1088,128]{1,0:T(8,128)S(1)} collective-permute-done((f32[1088,128]{1,0:T(8,128)}, f32[1088,128]{1,0:T(8,128)S(1)}, u32[]{:S(2)}, u32[]{:S(2)}) %collective-permute-start.1) | collective-permute-done | bytes 557088 | tf_op jit(solution)/shard_map/ppermute | solution.py:603
  22.0 1.9 %collective-permute-start.3 = (f32[544,128]{1,0:T(8,128)}, f32[544,128]{1,0:T(8,128)S(1)}, u32[]{:S(2)}, u32[]{:S(2)}) collective-permute-start(f32[544,128]{1,0:T(8,128)} %slice.15), channel_id=1, source_target_pairs={{0,16},{8,24},{16,0},{24,8},{1,17},{9,25},{17,1},{25,9},{2,18},{10... | collective-permute-start | bytes 835592 | tf_op jit(solution)/shard_map/ppermute | solution.py:603
  25.3 2.6 %all-to-all-done.in_ref = f32[8,152,128]{2,1,0:T(8,128)S(1)} async-done(((f32[8,152,128]{2,1,0:T(8,128)}), f32[8,152,128]{2,1,0:T(8,128)S(1)}, u32[]{:S(2)}, u32[]{:S(2)}) %all-to-all-start) | async-done | bytes 622624 | tf_op jit(solution)/shard_map/all_to_all | solution.py:694
  29.3 2.6 %collective-permute-start.5 = (f32[64,128]{1,0:T(8,128)S(1)}, f32[64,128]{1,0:T(8,128)S(1)}, u32[]{:S(2)}, u32[]{:S(2)}) collective-permute-start(f32[64,128]{1,0:T(8,128)S(1)} %get-tuple-element.55), channel_id=1, source_target_pairs={{0,4},{2,6},{4,0},{6,2},{1,5},{3,7},{5,1},{7,3},{8,12},{10,14},{12... | collective-permute-start | bytes 98312 | tf_op jit(solution)/shard_map/ppermute | solution.py:750
  34.2 1.7 %local.4.local_ref = f32[8,128,128]{2,1,0:T(8,128)S(1)} custom-call(f32[8,128,128]{2,1,0:T(8,128)S(1)} %get-tuple-element.56.y_ref.refs_5_.refs_1_), custom_call_target="tpu_custom_call" | custom-call | flops 7864320 | bytes 2097152 | tf_op jit(solution)/shard_map/local/pallas_call | solution.py:781
  37.6 1.6 %collective-permute-done.6.refs_1_ = f32[352,128]{1,0:T(8,128)S(1)} collective-permute-done((f32[352,128]{1,0:T(8,128)}, f32[352,128]{1,0:T(8,128)S(1)}, u32[]{:S(2)}, u32[]{:S(2)}) %collective-permute-start.6) | collective-permute-done | bytes 180256 | tf_op jit(solution)/shard_map/ppermute | solution.py:750
  42.9 5.3 %step.4 = (f32[8,128,128]{2,1,0:T(8,128)S(1)}, bf16[8,1024,256]{2,1,0:T(8,128)(2,1)S(1)}, f32[8,64,128]{2,1,0:T(8,128)S(1)}, f32[96,128]{1,0:T(8,128)S(1)}, f32[...) custom-call(f32[8,128,128]{2,1,0:T(8,128)S(1)} %local.4.local_ref, f32[96,128]{1,0:T(8,128)S(1)} %copy-done.5, ...), custom_call_target="tpu_custom_call" | custom-call | tf_op jit(solution)/shard_map/step/pallas_call | solution.py:845
  48.2 5.7 %collective-permute-start.13 = (f32[320,128]{1,0:T(8,128)S(1)}, f32[320,128]{1,0:T(8,128)S(1)}, u32[]{:S(2)}, u32[]{:S(2)}) collective-permute-start(f32[320,128]{1,0:T(8,128)S(1)} %get-tuple-element.73), channel_id=1, source_target_pairs={{0,2},{4,6},{2,0},{6,4},{1,3},{5,7},{3,1},{7,5},{8,10},{12,14},{10... | collective-permute-start | bytes 491528 | tf_op jit(solution)/shard_map/ppermute | solution.py:750
  54.6 2.8 %collective-permute-start.15 = (f32[32,128]{1,0:T(8,128)S(1)}, f32[32,128]{1,0:T(8,128)S(1)}, u32[]{:S(2)}, u32[]{:S(2)}) collective-permute-start(f32[32,128]{1,0:T(8,128)S(1)} %get-tuple-element.75), channel_id=1, source_target_pairs={{0,4},{2,6},{4,0},{6,2},{1,5},{3,7},{5,1},{7,3},{8,12},{10,14},{12... | collective-permute-start | bytes 49160 | tf_op jit(solution)/shard_map/ppermute | solution.py:750
  57.4 2.3 %local.5.local_ref = f32[8,128,128]{2,1,0:T(8,128)S(1)} custom-call(f32[8,128,128]{2,1,0:T(8,128)S(1)} %get-tuple-element.69.y_ref.refs_0_, s32[1]{0:T(128)} %get-tuple-element.70.refs_0_, f32[8,128,128]{2,1,0:T(8,128)S(1)} %get-tuple-element.56.y_ref.refs_5_.refs_1_, f32[8,64,128]{2,1,0:T(8,128)S(1)} %get-tuple-element.71.refs_2_.refs_1_), custom_call_target="tpu_custom_call" | custom-call | flops 7864320 | bytes 2097152 | tf_op jit(solution)/shard_map/local/pallas_call | solution.py:781
  61.1 3.6 %step.5 = (f32[8,128,128]{2,1,0:T(8,128)S(1)}, f32[96,128]{1,0:T(8,128)S(1)}, f32[320,128]{1,0:T(8,128)S(1)}, f32[320,128]{1,0:T(8,128)S(1)}, f32[32,128]{1,0:T(8,128)S(1)}) custom-call(f32[8,128,128]{2,1,0:T(8,128)S(1)} %local.5.local_ref, f32[96,128]{1,0:T(8,128)S(1)} %get-tuple-element.72.refs_0_, f32[320,128]{1,0:T(8,128)S(1)} %collective-permute-done.13.refs_1_, ...), custom_call_target="tpu_custom_call" | custom-call | tf_op jit(solution)/shard_map/step/pallas_call | solution.py:845
  66.7 3.7 %collective-permute-start.18 = (f32[32,128]{1,0:T(8,128)S(1)}, f32[32,128]{1,0:T(8,128)S(1)}, u32[]{:S(2)}, u32[]{:S(2)}) collective-permute-start(f32[32,128]{1,0:T(8,128)S(1)} %get-tuple-element.81), channel_id=1, source_target_pairs={{0,4},{2,6},{4,0},{6,2},{1,5},{3,7},{5,1},{7,3},{8,12},{10,14},{12... | collective-permute-start | bytes 49160 | tf_op jit(solution)/shard_map/ppermute | solution.py:750
  70.4 1.7 %local.6.local_ref = f32[8,128,128]{2,1,0:T(8,128)S(1)} custom-call(f32[8,128,128]{2,1,0:T(8,128)S(1)} %get-tuple-element.77.y_ref.refs_0_, f32[8,128,128]{2,1,0:T(8,128)S(1)} %get-tuple-element.69.y_ref.refs_0_, f32[8,64,128]{2,1,0:T(8,128)S(1)} %get-tuple-element.71.refs_2_.refs_1_), custom_call_target="tpu_custom_call" | custom-call | flops 7864320 | bytes 2097152 | tf_op jit(solution)/shard_map/local/pallas_call | solution.py:781
  73.6 3.6 %step.6 = (f32[8,128,128]{2,1,0:T(8,128)S(1)}, f32[96,128]{1,0:T(8,128)S(1)}, f32[320,128]{1,0:T(8,128)S(1)}, f32[320,128]{1,0:T(8,128)S(1)}, f32[32,128]{1,0:T(8,128)S(1)}) custom-call(f32[8,128,128]{2,1,0:T(8,128)S(1)} %local.6.local_ref, f32[96,128]{1,0:T(8,128)S(1)} %get-tuple-element.78.refs_0_, f32[320,128]{1,0:T(8,128)S(1)} %collective-permute-done.16.refs_1_, ...), custom_call_target="tpu_custom_call" | custom-call | tf_op jit(solution)/shard_map/step/pallas_call | solution.py:845
  77.3 1.8 %collective-permute-start.19 = (f32[320,128]{1,0:T(8,128)S(1)}, f32[320,128]{1,0:T(8,128)S(1)}, u32[]{:S(2)}, u32[]{:S(2)}) collective-permute-start(f32[320,128]{1,0:T(8,128)S(1)} %get-tuple-element.84), channel_id=1, source_target_pairs={{0,2},{4,6},{2,0},{6,4},{1,3},{5,7},{3,1},{7,5},{8,10},{12,14},{10... | collective-permute-start | bytes 491528 | tf_op jit(solution)/shard_map/ppermute | solution.py:750
  79.8 3.0 %collective-permute-start.21 = (f32[32,128]{1,0:T(8,128)S(1)}, f32[32,128]{1,0:T(8,128)S(1)}, u32[]{:S(2)}, u32[]{:S(2)}) collective-permute-start(f32[32,128]{1,0:T(8,128)S(1)} %get-tuple-element.86), channel_id=1, source_target_pairs={{0,4},{2,6},{4,0},{6,2},{1,5},{3,7},{5,1},{7,3},{8,12},{10,14},{12... | collective-permute-start | bytes 49160 | tf_op jit(solution)/shard_map/ppermute | solution.py:750
  82.8 1.7 %local.7 = f32[8,128,128]{2,1,0:T(8,128)S(1)} custom-call(f32[8,128,128]{2,1,0:T(8,128)S(1)} %get-tuple-element.82.y_ref, f32[8,128,128]{2,1,0:T(8,128)S(1)} %get-tuple-element.77.y_ref.refs_0_, f32[8,64,128]{2,1,0:T(8,128)S(1)} %get-tuple-element.71.refs_2_.refs_1_), custom_call_target="tpu_custom_call" | custom-call | flops 7864320 | bytes 2097152 | tf_op jit(solution)/shard_map/local/pallas_call | solution.py:781
  84.5 1.7 %collective-permute-done.21 = f32[32,128]{1,0:T(8,128)S(1)} collective-permute-done((f32[32,128]{1,0:T(8,128)S(1)}, f32[32,128]{1,0:T(8,128)S(1)}, u32[]{:S(2)}, u32[]{:S(2)}) %collective-permute-start.21) | collective-permute-done | bytes 16416 | tf_op jit(solution)/shard_map/ppermute | solution.py:750
  86.2 3.8 %step.7 = (f32[8,128,128]{2,1,0:T(8,128)S(1)}, f32[1,128,128]{2,1,0:T(8,128)S(1)}, f32[1,128,128]{2,1,0:T(8,128)S(1)}, f32[1,128,128]{2,1,0:T(8,128)S(1)}, f32[1...) fusion(f32[8,128,128]{2,1,0:T(8,128)S(1)} %broadcast_in_dim.3, ...), kind=kCustom, calls=%fused_computation.29 | custom fusion | bytes 6275076 | tf_op jit(solution)/shard_map/step/pallas_call | solution.py:845
  90.4 1.7 %collective-permute-start.23 = (f32[1,128,128]{2,1,0:T(8,128)S(1)}, f32[1,128,128]{2,1,0:T(8,128)S(1)}, u32[]{:S(2)}, u32[]{:S(2)}) collective-permute-start(f32[1,128,128]{2,1,0:T(8,128)S(1)} %get-tuple-element.100), channel_id=1, source_target_pairs={{0,16},{1,17},{8,24},{9,25},{16,0},{17,1},{24,8},{25,9},{2,18},{3,... | collective-permute-start | bytes 196616 | tf_op jit(solution)/shard_map/ppermute | solution.py:872
  (88 shorter events, 31.1 us)
Async XLA Ops:
  2.9 16.6 %collective-permute-start = (f32[1088,128]{1,0:T(8,128)}, f32[1088,128]{1,0:T(8,128)S(1)}, u32[]{:S(2)}, u32[]{:S(2)}) collective-permute-start(f32[1088,128]{1,0:T(8,128)} %pack.1.payload_ref.refs_6_), channel_id=1, source_target_pairs={{0,1},{1,0},{2,3},{3,2},{4,5},{5,4},{6,7},{7,6},{8,9},{9,8},{10,11... | collective-permute-start | bytes 1671176 | tf_op jit(solution)/shard_map/ppermute | solution.py:603
  5.9 15.4 %collective-permute-start.1 = (f32[1088,128]{1,0:T(8,128)}, f32[1088,128]{1,0:T(8,128)S(1)}, u32[]{:S(2)}, u32[]{:S(2)}) collective-permute-start(f32[1088,128]{1,0:T(8,128)} %pack.1.payload_ref.refs_6_), channel_id=1, source_target_pairs={{0,16},{8,24},{16,0},{24,8},{1,17},{9,25},{17,1},{25,9},{2,18},{10... | collective-permute-start | bytes 1671176 | tf_op jit(solution)/shard_map/ppermute | solution.py:603
  7.4 13.9 %collective-permute-start.2 = (f32[1088,128]{1,0:T(8,128)}, f32[1088,128]{1,0:T(8,128)S(1)}, u32[]{:S(2)}, u32[]{:S(2)}) collective-permute-start(f32[1088,128]{1,0:T(8,128)} %pack.1.payload_ref.refs_6_), channel_id=1, source_target_pairs={{0,8},{8,0},{16,24},{24,16},{1,9},{9,1},{17,25},{25,17},{2,10},{10... | collective-permute-start | bytes 1671176 | tf_op jit(solution)/shard_map/ppermute | solution.py:603
  12.3 15.6 %all-to-all-start = ((f32[8,152,128]{2,1,0:T(8,128)}), f32[8,152,128]{2,1,0:T(8,128)S(1)}, u32[]{:S(2)}, u32[]{:S(2)}) async-start(f32[8,152,128]{2,1,0:T(8,128)} %get-tuple-element.53), calls=%async_computation | async-start | bytes 1245184 | tf_op jit(solution)/shard_map/all_to_all | solution.py:694
  22.0 13.9 %collective-permute-start.3 = (f32[544,128]{1,0:T(8,128)}, f32[544,128]{1,0:T(8,128)S(1)}, u32[]{:S(2)}, u32[]{:S(2)}) collective-permute-start(f32[544,128]{1,0:T(8,128)} %slice.15), channel_id=1, source_target_pairs={{0,16},{8,24},{16,0},{24,8},{1,17},{9,25},{17,1},{25,9},{2,18},{10... | collective-permute-start | bytes 835592 | tf_op jit(solution)/shard_map/ppermute | solution.py:603
  24.6 11.3 %collective-permute-start.4 = (f32[544,128]{1,0:T(8,128)}, f32[544,128]{1,0:T(8,128)}, u32[]{:S(2)}, u32[]{:S(2)}) collective-permute-start(f32[544,128]{1,0:T(8,128)} %slice.16), channel_id=1, source_target_pairs={{0,1},{1,0},{2,3},{3,2},{4,5},{5,4},{6,7},{7,6},{8,9},{9,8},{10,11... | collective-permute-start | bytes 835592 | tf_op jit(solution)/shard_map/ppermute | solution.py:603
  29.3 4.9 %collective-permute-start.5 = (f32[64,128]{1,0:T(8,128)S(1)}, f32[64,128]{1,0:T(8,128)S(1)}, u32[]{:S(2)}, u32[]{:S(2)}) collective-permute-start(f32[64,128]{1,0:T(8,128)S(1)} %get-tuple-element.55), channel_id=1, source_target_pairs={{0,4},{2,6},{4,0},{6,2},{1,5},{3,7},{5,1},{7,3},{8,12},{10,14},{12... | collective-permute-start | bytes 98312 | tf_op jit(solution)/shard_map/ppermute | solution.py:750
  31.9 5.7 %collective-permute-start.8 = (f32[32,128]{1,0:T(8,128)S(1)}, f32[32,128]{1,0:T(8,128)S(1)}, u32[]{:S(2)}, u32[]{:S(2)}) collective-permute-start(f32[32,128]{1,0:T(8,128)S(1)} %slice.17.refs_0_), channel_id=1, source_target_pairs={{0,6},{2,4},{4,2},{6,0},{1,7},{3,5},{5,3},{7,1},{8,14},{10,12},{12... | collective-permute-start | bytes 49160 | tf_op jit(solution)/shard_map/ppermute | solution.py:772
  33.3 5.9 %collective-permute-start.6 = (f32[352,128]{1,0:T(8,128)}, f32[352,128]{1,0:T(8,128)S(1)}, u32[]{:S(2)}, u32[]{:S(2)}) collective-permute-start(f32[352,128]{1,0:T(8,128)} %get-tuple-element.59), channel_id=1, source_target_pairs={{0,2},{4,6},{2,0},{6,4},{1,3},{5,7},{3,1},{7,5},{8,10},{12,14},{10... | collective-permute-start | bytes 540680 | tf_op jit(solution)/shard_map/ppermute | solution.py:750
  35.9 5.1 %collective-permute-start.10 = (f32[1088,128]{1,0:T(8,128)S(1)}, f32[1088,128]{1,0:T(8,128)}, u32[]{:S(2)}, u32[]{:S(2)}) collective-permute-start(f32[1088,128]{1,0:T(8,128)S(1)} %collective-permute-done.1.refs_8_), channel_id=1, source_target_pairs={{0,8},{8,0},{16,24},{24,16},{1,9},{9,1},{17,25},{25,17},{2,10},{10... | collective-permute-start | bytes 1671176 | tf_op jit(solution)/shard_map/ppermute | solution.py:603
  36.0 5.0 %collective-permute-start.9 = (f32[1088,128]{1,0:T(8,128)S(1)}, f32[1088,128]{1,0:T(8,128)}, u32[]{:S(2)}, u32[]{:S(2)}) collective-permute-start(f32[1088,128]{1,0:T(8,128)S(1)} %collective-permute-done.refs_7_), channel_id=1, source_target_pairs={{0,8},{8,0},{16,24},{24,16},{1,9},{9,1},{17,25},{25,17},{2,10},{10... | collective-permute-start | bytes 1671176 | tf_op jit(solution)/shard_map/ppermute | solution.py:603
  48.2 12.9 %collective-permute-start.13 = (f32[320,128]{1,0:T(8,128)S(1)}, f32[320,128]{1,0:T(8,128)S(1)}, u32[]{:S(2)}, u32[]{:S(2)}) collective-permute-start(f32[320,128]{1,0:T(8,128)S(1)} %get-tuple-element.73), channel_id=1, source_target_pairs={{0,2},{4,6},{2,0},{6,4},{1,3},{5,7},{3,1},{7,5},{8,10},{12,14},{10... | collective-permute-start | bytes 491528 | tf_op jit(solution)/shard_map/ppermute | solution.py:750
  53.9 7.2 %collective-permute-start.14 = (f32[320,128]{1,0:T(8,128)S(1)}, f32[320,128]{1,0:T(8,128)S(1)}, u32[]{:S(2)}, u32[]{:S(2)}) collective-permute-start(f32[320,128]{1,0:T(8,128)S(1)} %get-tuple-element.74), channel_id=1, source_target_pairs={{2,4},{4,2},{3,5},{5,3},{10,12},{12,10},{11,13},{13,11},{18,20},{2... | collective-permute-start | bytes 491528 | tf_op jit(solution)/shard_map/ppermute | solution.py:750
  54.6 6.5 %collective-permute-start.15 = (f32[32,128]{1,0:T(8,128)S(1)}, f32[32,128]{1,0:T(8,128)S(1)}, u32[]{:S(2)}, u32[]{:S(2)}) collective-permute-start(f32[32,128]{1,0:T(8,128)S(1)} %get-tuple-element.75), channel_id=1, source_target_pairs={{0,4},{2,6},{4,0},{6,2},{1,5},{3,7},{5,1},{7,3},{8,12},{10,14},{12... | collective-permute-start | bytes 49160 | tf_op jit(solution)/shard_map/ppermute | solution.py:750
  64.7 8.9 %collective-permute-start.16 = (f32[320,128]{1,0:T(8,128)S(1)}, f32[320,128]{1,0:T(8,128)S(1)}, u32[]{:S(2)}, u32[]{:S(2)}) collective-permute-start(f32[320,128]{1,0:T(8,128)S(1)} %get-tuple-element.79), channel_id=1, source_target_pairs={{0,2},{4,6},{2,0},{6,4},{1,3},{5,7},{3,1},{7,5},{8,10},{12,14},{10... | collective-permute-start | bytes 491528 | tf_op jit(solution)/shard_map/ppermute | solution.py:750
  65.8 7.8 %collective-permute-start.17 = (f32[320,128]{1,0:T(8,128)S(1)}, f32[320,128]{1,0:T(8,128)S(1)}, u32[]{:S(2)}, u32[]{:S(2)}) collective-permute-start(f32[320,128]{1,0:T(8,128)S(1)} %get-tuple-element.80), channel_id=1, source_target_pairs={{2,4},{4,2},{3,5},{5,3},{10,12},{12,10},{11,13},{13,11},{18,20},{2... | collective-permute-start | bytes 491528 | tf_op jit(solution)/shard_map/ppermute | solution.py:750
  66.7 6.9 %collective-permute-start.18 = (f32[32,128]{1,0:T(8,128)S(1)}, f32[32,128]{1,0:T(8,128)S(1)}, u32[]{:S(2)}, u32[]{:S(2)}) collective-permute-start(f32[32,128]{1,0:T(8,128)S(1)} %get-tuple-element.81), channel_id=1, source_target_pairs={{0,4},{2,6},{4,0},{6,2},{1,5},{3,7},{5,1},{7,3},{8,12},{10,14},{12... | collective-permute-start | bytes 49160 | tf_op jit(solution)/shard_map/ppermute | solution.py:750
  77.3 8.9 %collective-permute-start.19 = (f32[320,128]{1,0:T(8,128)S(1)}, f32[320,128]{1,0:T(8,128)S(1)}, u32[]{:S(2)}, u32[]{:S(2)}) collective-permute-start(f32[320,128]{1,0:T(8,128)S(1)} %get-tuple-element.84), channel_id=1, source_target_pairs={{0,2},{4,6},{2,0},{6,4},{1,3},{5,7},{3,1},{7,5},{8,10},{12,14},{10... | collective-permute-start | bytes 491528 | tf_op jit(solution)/shard_map/ppermute | solution.py:750
  79.1 7.1 %collective-permute-start.20 = (f32[320,128]{1,0:T(8,128)S(1)}, f32[320,128]{1,0:T(8,128)S(1)}, u32[]{:S(2)}, u32[]{:S(2)}) collective-permute-start(f32[320,128]{1,0:T(8,128)S(1)} %get-tuple-element.85), channel_id=1, source_target_pairs={{2,4},{4,2},{3,5},{5,3},{10,12},{12,10},{11,13},{13,11},{18,20},{2... | collective-permute-start | bytes 491528 | tf_op jit(solution)/shard_map/ppermute | solution.py:750
  79.8 6.4 %collective-permute-start.21 = (f32[32,128]{1,0:T(8,128)S(1)}, f32[32,128]{1,0:T(8,128)S(1)}, u32[]{:S(2)}, u32[]{:S(2)}) collective-permute-start(f32[32,128]{1,0:T(8,128)S(1)} %get-tuple-element.86), channel_id=1, source_target_pairs={{0,4},{2,6},{4,0},{6,2},{1,5},{3,7},{5,1},{7,3},{8,12},{10,14},{12... | collective-permute-start | bytes 49160 | tf_op jit(solution)/shard_map/ppermute | solution.py:750
  90.4 5.2 %collective-permute-start.23 = (f32[1,128,128]{2,1,0:T(8,128)S(1)}, f32[1,128,128]{2,1,0:T(8,128)S(1)}, u32[]{:S(2)}, u32[]{:S(2)}) collective-permute-start(f32[1,128,128]{2,1,0:T(8,128)S(1)} %get-tuple-element.100), channel_id=1, source_target_pairs={{0,16},{1,17},{8,24},{9,25},{16,0},{17,1},{24,8},{25,9},{2,18},{3,... | collective-permute-start | bytes 196616 | tf_op jit(solution)/shard_map/ppermute | solution.py:872
  92.1 5.2 %collective-permute-start.24 = (f32[1,128,128]{2,1,0:T(8,128)S(1)}, f32[1,128,128]{2,1,0:T(8,128)S(1)}, u32[]{:S(2)}, u32[]{:S(2)}) collective-permute-start(f32[1,128,128]{2,1,0:T(8,128)S(1)} %get-tuple-element.102), channel_id=1, source_target_pairs={{0,17},{1,16},{8,25},{9,24},{16,1},{17,0},{24,9},{25,8},{2,19},{3,... | collective-permute-start | bytes 196616 | tf_op jit(solution)/shard_map/ppermute | solution.py:872
  93.6 5.0 %collective-permute-start.26 = (f32[1,128,128]{2,1,0:T(8,128)S(1)}, f32[1,128,128]{2,1,0:T(8,128)S(1)}, u32[]{:S(2)}, u32[]{:S(2)}) collective-permute-start(f32[1,128,128]{2,1,0:T(8,128)S(1)} %get-tuple-element.106), channel_id=1, source_target_pairs={{0,9},{1,8},{8,1},{9,0},{16,25},{17,24},{24,17},{25,16},{2,11},{3,... | collective-permute-start | bytes 196616 | tf_op jit(solution)/shard_map/ppermute | solution.py:872
  95.6 4.7 %collective-permute-start.28 = (f32[1,128,128]{2,1,0:T(8,128)S(1)}, f32[1,128,128]{2,1,0:T(8,128)S(1)}, u32[]{:S(2)}, u32[]{:S(2)}) collective-permute-start(f32[1,128,128]{2,1,0:T(8,128)S(1)} %get-tuple-element.110), channel_id=1, source_target_pairs={{0,25},{1,24},{8,17},{9,16},{16,9},{17,8},{24,1},{25,0},{2,27},{3,... | collective-permute-start | bytes 196616 | tf_op jit(solution)/shard_map/ppermute | solution.py:872
  (16 other events, 96.4 us)
